TPU v7x, 512 devices: a whole 4x4x16 slice. The times are simulated.
512 devices in a mesh: dp: 64 (over z, y), tensor: 8 (over x, core).
Axes of the slice: x: 4, y: 4, z: 16, core: 2. Of those that a mesh axis runs over, the one named last changes fastest.
Arguments:
- normed: bfloat16 [32768, 4096], P('dp', 'tensor'), may hold values from -6 to 6
- output_gradient: bfloat16 [32768, 4096], P('dp', 'tensor'), may hold values from -480 to 480
- gate_preactivation: bfloat16 [32768, 7168], P('dp', 'tensor'), may hold values from -48 to 48
- upward_preactivation: bfloat16 [32768, 7168], P('dp', 'tensor'), may hold values from -48 to 48
- frozen_down_weight: bfloat16 [7168, 4096], P('tensor', 'dp'), may hold values from -0.0625 to 0.0625
- adapter_width_factors: bfloat16 [3, 16, 4096], replicated, may hold values from -0.09375 to 0.09375
- adapter_hidden_factors: bfloat16 [3, 16, 7168], P(None, None, 'tensor'), may hold values from -0.0625 to 0.0625
- clipping_limit: float32 [1], replicated, may hold values from 1000 to 3000
- width_noise_draw: float32 [3, 16, 4096], P(None, None, 'tensor'), may hold values from -0.3 to 0.3
- hidden_noise_draw: float32 [3, 16, 7168], P(None, None, 'tensor'), may hold values from -0.3 to 0.3
Outputs:
- grad_wide: float32 [3, 16, 4096], P(None, None, 'tensor')
- grad_hidden: float32 [3, 16, 7168], P(None, None, 'tensor')
All inputs are finite; a program needn't handle non-finite values.
Results may differ from a plain program's by a relative error of at most 0.0011.
The roundings to bfloat16 on the way count: a program that leaves them out, or rounds other values in their place, can miss the bound.
Values may be sent and summed in bfloat16 or wider, within the bound.
No kernel may reach another device: no remote copies, remote signals or barrier semaphores. Data moves between devices by JAX's collectives and lax.ppermute only.
A program may use at most 64 MiB of HBM per device.

v0:
```python
import jax
import jax.numpy as jnp
from jax import lax
from jax.sharding import PartitionSpec as P

SEQUENCE_TOKENS = 128


adapter_scale = 2.0


def silu_parts(gate_values):
    values = gate_values.astype(jnp.float32)
    sigmoid = jax.nn.sigmoid(values)
    return (values * sigmoid, sigmoid * (1.0 + values * (1.0 - sigmoid)))


def per_sequence(left_factor, right_factor):
    return adapter_scale * jnp.einsum(
        "bvt,bvk->btk", left_factor, right_factor, preferred_element_type=jnp.float32
    )


def per_device(
    normed,
    output_gradient,
    gate_preactivation,
    upward_preactivation,
    frozen_down_weight,
    adapter_width_factors,
    adapter_hidden_factors,
    clipping_limit,
    width_noise_draw,
    hidden_noise_draw,
):
    local_width = normed.shape[1]
    tokens_here = normed.shape[0]
    hidden_local = gate_preactivation.shape[1]
    example_list = tokens_here // SEQUENCE_TOKENS
    adapter_rank_size = adapter_width_factors.shape[1]
    shard_index = lax.axis_index("tensor")
    width_side_local = lax.dynamic_slice_in_dim(
        adapter_width_factors, shard_index * local_width, local_width, 2
    )
    in_partial = jnp.einsum(
        "op,hp->oh",
        normed,
        width_side_local[:2].reshape(2 * adapter_rank_size, local_width),
        preferred_element_type=jnp.float32,
    )
    in_summed = lax.psum(in_partial, "tensor")
    complete_gradient = lax.all_gather(output_gradient, "tensor", axis=1, tiled=True)
    adapter_backward = jnp.einsum(
        "op,hp->oh", complete_gradient, adapter_width_factors[2], preferred_element_type=jnp.float32
    ).astype(jnp.bfloat16)
    frozen = lax.all_gather(frozen_down_weight, "dp", axis=1, tiled=True)
    hidden_gradient = jnp.einsum(
        "td,hd->th", complete_gradient, frozen, preferred_element_type=jnp.float32
    )
    hidden_gradient = hidden_gradient + adapter_scale * jnp.dot(
        adapter_backward, adapter_hidden_factors[2], preferred_element_type=jnp.float32
    )
    silu_value, silu_slope = silu_parts(gate_preactivation)
    up_value = upward_preactivation.astype(jnp.float32)
    gated_activation = (silu_value * up_value).astype(jnp.bfloat16)
    gate_gradient = (hidden_gradient * up_value * silu_slope).astype(jnp.bfloat16)
    upward_gradient = (hidden_gradient * silu_value).astype(jnp.bfloat16)
    mid_partial = jnp.concatenate(
        [
            jnp.einsum(
                "yu,bu->yb",
                gated_activation,
                adapter_hidden_factors[2],
                preferred_element_type=jnp.float32,
            ),
            jnp.einsum(
                "yu,bu->yb",
                gate_gradient,
                adapter_hidden_factors[0],
                preferred_element_type=jnp.float32,
            ),
            jnp.einsum(
                "yu,bu->yb",
                upward_gradient,
                adapter_hidden_factors[1],
                preferred_element_type=jnp.float32,
            ),
        ],
        axis=1,
    )
    mid_summed = lax.psum(mid_partial, "tensor")
    in_round = in_summed.astype(jnp.bfloat16).reshape(
        example_list, SEQUENCE_TOKENS, 2 * adapter_rank_size
    )
    mid_round = mid_summed.astype(jnp.bfloat16).reshape(
        example_list, SEQUENCE_TOKENS, 3 * adapter_rank_size
    )
    backward_rows = adapter_backward.reshape(example_list, SEQUENCE_TOKENS, adapter_rank_size)
    hidden_norm_terms = jnp.stack(
        [
            per_sequence(
                in_round[:, :, :adapter_rank_size],
                gate_gradient.reshape(example_list, SEQUENCE_TOKENS, hidden_local),
            ),
            per_sequence(
                in_round[:, :, adapter_rank_size:],
                upward_gradient.reshape(example_list, SEQUENCE_TOKENS, hidden_local),
            ),
            per_sequence(
                backward_rows, gated_activation.reshape(example_list, SEQUENCE_TOKENS, hidden_local)
            ),
        ],
        axis=1,
    )
    normed_rows = normed.reshape(example_list, SEQUENCE_TOKENS, local_width)
    width_norm_terms = jnp.stack(
        [
            per_sequence(mid_round[:, :, adapter_rank_size : 2 * adapter_rank_size], normed_rows),
            per_sequence(mid_round[:, :, 2 * adapter_rank_size :], normed_rows),
            per_sequence(
                mid_round[:, :, :adapter_rank_size],
                output_gradient.reshape(example_list, SEQUENCE_TOKENS, local_width),
            ),
        ],
        axis=1,
    )
    squares = jnp.sum(hidden_norm_terms * hidden_norm_terms, axis=(1, 2, 3)) + jnp.sum(
        width_norm_terms * width_norm_terms, axis=(1, 2, 3)
    )
    norm_values = jnp.sqrt(lax.psum(squares, "tensor"))
    bound = clipping_limit[0]
    weights = bound / jnp.maximum(norm_values, bound)
    wide_sum = jnp.sum(weights[:, None, None, None] * width_norm_terms, axis=0)
    hidden_sum = jnp.sum(weights[:, None, None, None] * hidden_norm_terms, axis=0)
    wide_total, hidden_total = lax.psum((wide_sum, hidden_sum), "dp")
    sequence_count = example_list * lax.axis_size("dp")
    grad_wide = (wide_total + bound * width_noise_draw) / sequence_count
    grad_hidden = (hidden_total + bound * hidden_noise_draw) / sequence_count
    return (grad_wide, grad_hidden)


def solution(mesh):
    placed = (
        P("dp", "tensor"),
        P("dp", "tensor"),
        P("dp", "tensor"),
        P("dp", "tensor"),
        P("tensor", "dp"),
        P(),
        P(None, None, "tensor"),
        P(),
        P(None, None, "tensor"),
        P(None, None, "tensor"),
    )
    return jax.shard_map(
        per_device,
        mesh=mesh,
        in_specs=placed,
        out_specs=(P(None, None, "tensor"), P(None, None, "tensor")),
        check_vma=False,
    )
```

profile of v0, /device:TPU:2, one launch (start us, length us, event | category | flops | bytes accessed | tf_op | source)
XLA Modules:
  0.0 534.6 jit_solution(13533892030097967452)
XLA Ops:
  7.2 0.0 copy-start
  7.2 0.0 all-gather.3.cloned.1.call-start
  7.2 0.7 all-gather.3.cloned.1.call-update
  7.9 0.0 all-gather.5.cloned.1.call-start
  8.0 0.7 all-gather.5.cloned.1.call-update
  8.7 0.0 all-reduce.5.cloned.1.call-start
  8.7 0.8 constant_dynamic-slice_fusion
  9.5 0.0 copy-done
  9.5 0.2 convolution_bitcast_fusion
  9.7 43.7 %all-gather.3.cloned.1.call-done = bf16[512,4096]{1,0:T(8,128)(2,1)} async-done(((bf16[512,512]{1,0:T(8,128)(2,1)}), bf16[512,4096]{1,0:T(8,128)(2,1)}) %all-gather.3.cloned.1.call-update) | async-done | bytes 4194320 | tf_op jit(solution)/shard_map/all_gather | solution.py:52
  53.4 3.4 convolution_convert_fusion
  56.8 0.0 copy-start.5
  56.8 155.2 %all-gather.5.cloned.1.call-done = bf16[896,4096]{0,1:T(8,128)(2,1)} async-done(((bf16[896,64]{0,1:T(8,128)(2,1)}), bf16[896,4096]{0,1:T(8,128)(2,1)}) %all-gather.5.cloned.1.call-update) | async-done | bytes 7340048 | tf_op jit(solution)/shard_map/all_gather | solution.py:56
  212.0 0.0 copy-start.6
  212.0 0.0 copy-start.7
  212.0 9.9 %fusion.36 = f32[512,896]{1,0:T(8,128)S(1)} fusion(bf16[512,4096]{1,0:T(8,128)(2,1)} %all-gather.3.cloned.1.call-done, bf16[896,4096]{0,1:T(8,128)(2,1)} %all-gather.5.cloned.1.call-done), kind=kOutput, calls=%fused_computation.62 | convolution fusion | flops 3758096384 | bytes 13369344 | tf_op jit(solution)/shard_map/td,hd->th/dot_general | solution.py:57
  221.9 0.0 copy-done.5
  221.9 0.0 copy-done.6
  221.9 0.0 copy-done.7
  221.9 1.3 fusion.1
  223.2 0.3 fusion.16
  223.6 0.4 fusion.18
  223.9 0.4 fusion.20
  224.3 22.6 %all-reduce.6 = (bf16[512,48]{0,1:T(8,128)(2,1)S(1)}, bf16[512,32]{0,1:T(8,128)(2,1)}) all-reduce(f32[512,48]{0,1:T(8,128)S(1)} %pad_maximum_fusion.2, f32[512,32]{0,1:T(8,128)S(1)} %convolution_bitcast_fusion), channel_id=1, replica_groups=mesh['dp'=64,'tensor'=8] {'tensor'}, use_global_device_ids=true, to_apply=%region_2.0 | all-reduce | flops 40960 | bytes 245760 | tf_op jit(solution)/shard_map/psum | solution.py:91
  247.0 0.8 fusion.12
  247.8 0.8 fusion.13
  248.7 0.2 fusion.8
  248.9 0.8 reshape.33
  249.7 0.0 copy-start.1
  249.7 0.0 copy-start.2
  249.7 1.3 fusion.11
  251.0 0.3 fusion.9
  251.3 0.0 copy-start.4
  251.3 0.0 copy-start.3
  251.3 0.2 fusion.10
  251.5 0.2 multiply_reduce_fusion.1
  251.7 0.0 copy-done.1
  251.7 0.0 copy-done.2
  251.7 0.1 multiply_reduce_fusion.3
  252.5 12.6 %psum.37 = f32[4]{0:T(128)S(1)} all-reduce(f32[4]{0:T(128)S(1)} %add.35), channel_id=1, replica_groups=mesh['dp'=64,'tensor'=8] {'tensor'}, use_global_device_ids=true, to_apply=%region_4.0 | all-reduce | flops 4 | bytes 32 | tf_op jit(solution)/shard_map/psum | solution.py:130
  265.1 0.7 multiply_reduce_fusion.2
  265.8 0.8 multiply_reduce_fusion
  266.6 0.0 all-reduce.5.cloned.1.call-update
  266.6 258.2 %all-reduce.5.cloned.1.call-done = (f32[3,16,512]{2,1,0:T(8,128)}, f32[3,16,896]{2,1,0:T(8,128)}) async-done(((f32[3,16,512]{2,1,0:T(8,128)}, f32[3,16,896]{2,1,0:T(8,128)}), (f32[3,16,512]{2,1,0:T(8,128)}, f32[3,16,896]{2,1,0:T(8,128)})) %all-reduce.5.cloned.1.call-update) | async-done | bytes 270352 | tf_op jit(solution)/shard_map/psum | solution.py:135
  524.9 0.0 copy-done.4
  524.9 1.6 add_multiply_fusion.1
  526.4 0.0 copy-done.3
  526.4 1.6 add_multiply_fusion
  (6 shorter events, 0.1 us)
Async XLA Ops:
  7.2 2.3 copy-start
  7.2 46.2 %all-gather.3.cloned.1.call-start = ((), (), s32[]{:S(2)}) async-start(), calls=%async_computation | async-start | bytes 4718592 | tf_op jit(solution)/shard_map/all_gather | solution.py:52
  7.9 204.1 %all-gather.5.cloned.1.call-start = ((), (), s32[]{:S(2)}) async-start(), calls=%async_computation.1 | async-start | bytes 7454720 | tf_op jit(solution)/shard_map/all_gather | solution.py:56
  8.7 516.2 %all-reduce.5.cloned.1.call-start = ((), (), s32[]{:S(2)}) async-start(), calls=%async_computation.2 | async-start | bytes 540672 | tf_op jit(solution)/shard_map/psum | solution.py:135
  56.8 165.2 %copy-start.5 = (bf16[3,16,896]{2,1,0:T(8,128)(2,1)S(1)}, bf16[3,16,896]{2,1,0:T(8,128)(2,1)}, u32[]{:S(2)}) copy-start(bf16[3,16,896]{2,1,0:T(8,128)(2,1)} %param.16) | copy-start | bytes 258052
  212.0 9.9 %copy-start.6 = (bf16[512,896]{1,0:T(8,128)(2,1)S(1)}, bf16[512,896]{1,0:T(8,128)(2,1)}, u32[]{:S(2)}) copy-start(bf16[512,896]{1,0:T(8,128)(2,1)} %param.13) | copy-start | bytes 2752516
  212.0 9.9 %copy-start.7 = (bf16[512,896]{1,0:T(8,128)(2,1)S(1)}, bf16[512,896]{1,0:T(8,128)(2,1)}, u32[]{:S(2)}) copy-start(bf16[512,896]{1,0:T(8,128)(2,1)} %param.12) | copy-start | bytes 2752516
  249.7 2.0 copy-start.1
  249.7 2.0 copy-start.2
  251.3 273.6 %copy-start.4 = (f32[3,16,512]{2,1,0:T(8,128)S(1)}, f32[3,16,512]{2,1,0:T(8,128)}, u32[]{:S(2)}) copy-start(f32[3,16,512]{2,1,0:T(8,128)} %param.18) | copy-start | bytes 294916
  251.3 275.2 %copy-start.3 = (f32[3,16,896]{2,1,0:T(8,128)S(1)}, f32[3,16,896]{2,1,0:T(8,128)}, u32[]{:S(2)}) copy-start(f32[3,16,896]{2,1,0:T(8,128)} %param.19) | copy-start | bytes 516100
Sparse Core Ops, SparseCore 0:
  10.1 43.1 all-gather.2
  56.3 155.6 all-gather.4
  266.8 258.0 all-reduce.4
where the time goes:
time: 535 us
  waiting for transfers between devices  459 us (86%)
  blocking collectives  35.2 us (7%)
  matrix products  19.5 us (4%)
  between operations  14.5 us (3%)
    psum x1, waiting for transfers between devices, per_device(): wide_total, hidden_total = lax.psum((wide_sum, hidden_sum), 'dp')  258 us
    all_gather x1, waiting for transfers between devices, per_device(): frozen = lax.all_gather(frozen_down_weight, 'dp', axis=1, tiled=True)  155 us
    all_gather x1, waiting for transfers between devices, per_device(): lax.all_gather(output_gradient, 'tensor', axis=1, tiled=True)  43.7 us
    psum x1, blocking collectives, per_device(): mid_summed = lax.psum(mid_partial, 'tensor')  22.6 us
    psum x1, blocking collectives, per_device(): norm_values = jnp.sqrt(lax.psum(squares, 'tensor'))  12.6 us
  transfers between devices with their start and end apart: 3, of which 3 were waited for; matrix products, arithmetic and copies ran while one was open for 1% of the time, Pallas kernels for 0%

commit v1 on v0

v1 whole, which is shorter than its diff:
```python
import functools

import jax
import jax.numpy as jnp
from jax import lax
from jax.experimental import pallas as pl
from jax.experimental.pallas import tpu as pltpu
from jax.sharding import Mesh
from jax.sharding import PartitionSpec as P

SEQUENCE_TOKENS = 128
RANK = 16
SCALE = 2.0
F32 = jnp.float32
BF16 = jnp.bfloat16


def contract(left, right, left_dim, right_dim):
    return lax.dot_general(
        left, right, (((left_dim,), (right_dim,)), ((), ())), preferred_element_type=F32
    )


def hidden_kernel(
    n_blocks,
    place_ref,
    gradient_ref,
    *refs,
):
    block_refs = refs[:n_blocks]
    (gate_ref, up_ref, factors_ref, in_ref, lora_ref, lora_t_ref) = refs[n_blocks : n_blocks + 6]
    sums_ref, mids_ref = refs[n_blocks + 6 : n_blocks + 8]
    weight, gradient, total, sems = refs[n_blocks + 8 :]
    tokens, hidden = gate_ref.shape
    sequences = tokens // SEQUENCE_TOKENS

    copies = [pltpu.make_async_copy(gradient_ref, gradient, sems.at[n_blocks])]
    for i, block in enumerate(block_refs):
        rows = block.shape[0]
        start = pl.multiple_of(place_ref[i] * 128, 128)
        copies.append(
            pltpu.make_async_copy(block, weight.at[pl.ds(start, rows), :], sems.at[i])
        )
    for copy in copies:
        copy.start()
    mids_ref[...] = jnp.zeros_like(mids_ref)
    for copy in copies:
        copy.wait()

    def tile(start, width):
        cols = pl.ds(start, width)
        factors = factors_ref[:, cols]
        total[:, :width] = jnp.dot(
            gradient[...], weight[:, cols], preferred_element_type=F32
        ) + SCALE * jnp.dot(lora_ref[...], factors[2 * RANK :], preferred_element_type=F32)
        for e in range(sequences):
            rows = slice(e * SEQUENCE_TOKENS, (e + 1) * SEQUENCE_TOKENS)
            hidden_grad = total[rows, :width]
            gate = gate_ref[rows, cols].astype(F32)
            up = up_ref[rows, cols].astype(F32)
            sigmoid = jax.nn.sigmoid(gate)
            silu = gate * sigmoid
            slope = sigmoid * (1.0 + gate * (1.0 - sigmoid))
            activation = (silu * up).astype(BF16)
            gate_grad = (hidden_grad * up * slope).astype(BF16)
            up_grad = (hidden_grad * silu).astype(BF16)
            left = (in_ref[:RANK, rows], in_ref[RANK:, rows], lora_t_ref[:, rows])
            for j, right in enumerate((gate_grad, up_grad, activation)):
                part = slice(j * RANK, (j + 1) * RANK)
                sums_ref[e, part, cols] = SCALE * jnp.dot(
                    left[j], right, preferred_element_type=F32
                )
                mids_ref[part, rows] += contract(factors[part], right, 1, 1)

    step = 256
    whole = hidden // step

    def body(i, carry):
        tile(pl.multiple_of(i * step, step), step)
        return carry

    lax.fori_loop(0, whole, body, 0)
    if hidden > whole * step:
        tile(whole * step, hidden - whole * step)
    for e in range(sequences):
        square = sums_ref[e] * sums_ref[e]
        line = jnp.sum(jnp.sum(square, axis=0, keepdims=True), axis=1, keepdims=True)
        mids_ref[3 * RANK + e : 3 * RANK + e + 1, :] = jnp.broadcast_to(line, (1, tokens))


def clip_kernel(
    place_ref,
    clip_ref,
    mids_ref,
    sums_ref,
    normed_ref,
    gradient_ref,
    out_ref,
    wide,
):
    sequences, _, hidden = sums_ref.shape
    tokens, width = normed_ref.shape
    local = wide.shape[1]
    place = place_ref[0]
    bound = clip_ref[0]
    wide[...] = jnp.zeros_like(wide)
    weights = []
    for e in range(sequences):
        rows = slice(e * SEQUENCE_TOKENS, (e + 1) * SEQUENCE_TOKENS)
        mids = mids_ref[: 3 * RANK, rows].astype(BF16)
        squares = jnp.zeros((RANK, local), F32)

        def body(i, squares, rows=rows, mids=mids):
            cols = pl.ds(pl.multiple_of(i * local, local), local)
            first = SCALE * jnp.dot(
                mids[: 2 * RANK], normed_ref[rows, cols], preferred_element_type=F32
            )
            second = SCALE * jnp.dot(
                mids[2 * RANK :], gradient_ref[rows, cols], preferred_element_type=F32
            )
            return (
                squares
                + first[:RANK] * first[:RANK]
                + first[RANK:] * first[RANK:]
                + second * second
            )

        squares = lax.fori_loop(0, width // local, body, squares)
        total = jnp.sum(jnp.sum(squares, axis=0, keepdims=True), axis=1, keepdims=True)
        total = total + mids_ref[3 * RANK + e : 3 * RANK + e + 1, 0:1]
        weight = bound / jnp.maximum(jnp.sqrt(total), bound)
        weights.append(weight)
        cols = pl.ds(pl.multiple_of(place * local, local), local)
        wide[: 2 * RANK] += weight * (
            SCALE
            * jnp.dot(mids[: 2 * RANK], normed_ref[rows, cols], preferred_element_type=F32)
        )
        wide[2 * RANK :] += weight * (
            SCALE
            * jnp.dot(mids[2 * RANK :], gradient_ref[rows, cols], preferred_element_type=F32)
        )
    lanes = out_ref.shape[0] // 6
    for t in range(out_ref.shape[0]):
        r, c = divmod(t, lanes)
        rows = slice(8 * r, 8 * r + 8)
        at = c * 128
        if at < local:
            value = wide[rows, at : at + 128]
        elif at < local + hidden:
            at = at - local
            value = weights[0] * sums_ref[0, rows, at : at + 128]
            for e in range(1, sequences):
                value = value + weights[e] * sums_ref[e, rows, at : at + 128]
        else:
            value = jnp.zeros((8, 128), F32)
        out_ref[t] = value


def ring(size, by):
    return [(i, (i + by) % size) for i in range(size)]


def per_device(
    sizes,
    normed,
    output_gradient,
    gate_preactivation,
    upward_preactivation,
    frozen_down_weight,
    adapter_width_factors,
    adapter_hidden_factors,
    clipping_limit,
    width_noise_draw,
    hidden_noise_draw,
):
    tokens, local_width = normed.shape
    hidden = gate_preactivation.shape[1]
    sequences = tokens // SEQUENCE_TOKENS
    n_z = sizes["zh"] * sizes["zl"]
    n_tensor = sizes["x"] * sizes["c"]
    z_axes, tensor_axes = ("zh", "zl"), ("x", "c")
    z = lax.axis_index(z_axes)
    tensor = lax.axis_index(tensor_axes)

    gradient = lax.all_gather(output_gradient, tensor_axes, axis=1, tiled=True)
    block = lax.all_gather(frozen_down_weight.T, "y", axis=0, tiled=True)
    normed_all = lax.all_gather(normed, tensor_axes, axis=1, tiled=True)

    rows = block.shape[0]
    half = rows // 2
    units = rows // 128
    blocks, places = [block], [z * units]
    low = high = block
    for k in range(1, n_z // 2):
        low = lax.ppermute(low, z_axes, ring(n_z, 1))
        high = lax.ppermute(high, z_axes, ring(n_z, -1))
        blocks += [low, high]
        places += [((z + n_z - k) % n_z) * units, ((z + k) % n_z) * units]
    far = ((z + n_z // 2) % n_z) * units
    blocks.append(lax.ppermute(low[:half], z_axes, ring(n_z, 1)))
    blocks.append(lax.ppermute(high[half:], z_axes, ring(n_z, -1)))
    places += [far, far + units // 2]

    lora_t = contract(adapter_width_factors[2], gradient, 1, 1).astype(BF16)
    in_t = contract(
        adapter_width_factors[:2].reshape(2 * RANK, -1), normed_all, 1, 1
    ).astype(BF16)

    vmem = pl.BlockSpec(memory_space=pltpu.VMEM)
    smem = pl.BlockSpec(memory_space=pltpu.SMEM)
    anywhere = pl.BlockSpec(memory_space=pl.ANY)
    sums, mids = pl.pallas_call(
        functools.partial(hidden_kernel, len(blocks)),
        out_shape=(
            jax.ShapeDtypeStruct((sequences, 3 * RANK, hidden), F32),
            jax.ShapeDtypeStruct((8 * n_tensor, tokens), F32),
        ),
        in_specs=[smem, anywhere] + [anywhere] * len(blocks) + [vmem] * 6,
        out_specs=(vmem, vmem),
        scratch_shapes=[
            pltpu.VMEM((n_z * rows, hidden), BF16),
            pltpu.VMEM(gradient.shape, BF16),
            pltpu.VMEM((tokens, 256), F32),
            pltpu.SemaphoreType.DMA((len(blocks) + 1,)),
        ],
        compiler_params=pltpu.CompilerParams(vmem_limit_bytes=40 * 2**20),
        name="hidden_side",
    )(
        jnp.stack(places).astype(jnp.int32),
        gradient,
        *blocks,
        gate_preactivation,
        upward_preactivation,
        adapter_hidden_factors.reshape(3 * RANK, hidden),
        in_t,
        lora_t.T,
        lora_t,
    )

    pieces = lax.all_to_all(mids.reshape(n_tensor, 8, tokens), tensor_axes, 0, 0)
    piece = jnp.sum(pieces, axis=0)
    mids = lax.all_to_all(
        jnp.broadcast_to(piece, (n_tensor,) + piece.shape), tensor_axes, 0, 0
    ).reshape(8 * n_tensor, tokens)

    lanes = 12
    out = pl.pallas_call(
        clip_kernel,
        out_shape=jax.ShapeDtypeStruct((6 * lanes, 8, 128), F32),
        in_specs=[smem, smem, vmem, vmem, vmem, vmem],
        out_specs=vmem,
        scratch_shapes=[pltpu.VMEM((3 * RANK, local_width), F32)],
        compiler_params=pltpu.CompilerParams(vmem_limit_bytes=40 * 2**20),
        name="clip_side",
    )(tensor.reshape(1).astype(jnp.int32), clipping_limit, mids, sums, normed_all, gradient)

    first_axes, second_axes = ("zl", "y"), "zh"
    n_first, n_second = sizes["zl"] * sizes["y"], sizes["zh"]
    part = jnp.sum(
        lax.all_to_all(out.reshape(n_first, -1, 128), first_axes, 0, 0), axis=0
    )
    part = jnp.sum(
        lax.all_to_all(part.reshape(n_second, -1, 128), second_axes, 0, 0), axis=0
    )
    part = lax.all_to_all(
        jnp.broadcast_to(part, (n_second,) + part.shape), second_axes, 0, 0
    ).reshape(-1, 128)
    part = lax.all_to_all(
        jnp.broadcast_to(part, (n_first,) + part.shape), first_axes, 0, 0
    )
    total = (
        part.reshape(6, lanes, 8, 128)
        .transpose(0, 2, 1, 3)
        .reshape(3, RANK, lanes * 128)
    )
    count = sequences * n_z * sizes["y"]
    bound = clipping_limit[0]
    wide = total[:, :, :local_width]
    inner = total[:, :, local_width : local_width + hidden]
    return (
        (wide + bound * width_noise_draw) / count,
        (inner + bound * hidden_noise_draw) / count,
    )


def solution(mesh):
    names = ("zh", "zl", "y", "x", "c")
    extents = (8, 2, 4, 4, 2)
    fine = Mesh(mesh.devices.reshape(extents), names)
    dp, tensor = ("zh", "zl", "y"), ("x", "c")
    placed = (
        P(dp, tensor),
        P(dp, tensor),
        P(dp, tensor),
        P(dp, tensor),
        P(tensor, dp),
        P(),
        P(None, None, tensor),
        P(),
        P(None, None, tensor),
        P(None, None, tensor),
    )
    return jax.shard_map(
        functools.partial(per_device, dict(zip(names, extents, strict=True))),
        mesh=fine,
        in_specs=placed,
        out_specs=(P(None, None, tensor), P(None, None, tensor)),
        check_vma=False,
    )
```

time: 535 us -> 270 us (0.50)
  waiting for transfers between devices: 459 us -> 36 us
  starting transfers between devices: 0.11 us -> 68.7 us
  blocking collectives: 35.2 us -> 87.5 us
  local copies, waits for them, and re-layouts: 1.64 us -> 30.4 us
  Pallas kernels: 0 us -> 21.9 us
  matrix products: 19.5 us -> 7.22 us
    psum x1 -> x0, waiting for transfers between devices: 258 us -> none  [per_device(): wide_total, hidden_total = lax.psum((wide_sum, hidden_sum), 'dp')]
    all_gather x2, waiting for transfers between devices: 199 us -> 0.04 us  [the longest x1 0.02 us: per_device(): gradient = lax.all_gather(output_gradient, tensor_axes, axis=1, tiled=True)]
    all_to_all x0 -> x5, blocking collectives: none -> 74.1 us  [the longest x1 22.7 us: per_device(): lax.all_to_all(part.reshape(n_second, -1, 128), second_axes, 0, 0)]
    ppermute x0 -> x16, starting transfers between devices: none -> 63.9 us  [the longest x7 41 us: per_device(): high = lax.ppermute(high, z_axes, ring(n_z, -1))]
    psum x2 -> x0, blocking collectives: 35.2 us -> none  [the longest x1 22.6 us: per_device(): mid_summed = lax.psum(mid_partial, 'tensor')]
    ppermute x0 -> x16, waiting for transfers between devices: none -> 30.5 us  [the longest x7 29.6 us: per_device(): low = lax.ppermute(low, z_axes, ring(n_z, 1))]
    unnamed x16 -> x68, local copies, waits for them, and re-layouts: 0.04 us -> 26.3 us
    pallas_call x0 -> x2, Pallas kernels: none -> 21.9 us  [the longest x1 15.9 us: per_device(): pl.pallas_call(functools.partial(hidden_kernel, len(blocks)), out_shape=(...]
  transfers between devices with their start and end apart: 3 -> 19, of which waited for: 3 -> 10; matrix products, arithmetic and copies ran while one was open for 1% -> 4% of each run, Pallas kernels for 0% -> 0%
where the time goes in v1:
time: 270 us; the launch traced here: 268 us
  blocking collectives  87.5 us (32%)
  starting transfers between devices  68.7 us (25%)
  waiting for transfers between devices  36 us (13%)
  local copies, waits for them, and re-layouts  30.4 us (11%)
  Pallas kernels  21.9 us (8%)
  between operations  15.3 us (6%)
  matrix products  7.22 us (3%)
    ppermute x7, starting transfers between devices, per_device(): high = lax.ppermute(high, z_axes, ring(n_z, -1))  41 us
    ppermute x7, waiting for transfers between devices, per_device(): low = lax.ppermute(low, z_axes, ring(n_z, 1))  29.6 us
    unnamed x68, local copies, waits for them, and re-layouts  26.3 us
    all_to_all x1, blocking collectives, per_device(): lax.all_to_all(part.reshape(n_second, -1, 128), second_axes, 0, 0)  22.7 us
    all_to_all x1, blocking collectives, per_device(): lax.all_to_all(jnp.broadcast_to(part, (n_second,) + part.shape), second_a...  16.1 us
    all_to_all x1, blocking collectives, per_device(): lax.all_to_all(out.reshape(n_first, -1, 128), first_axes, 0, 0)  15.9 us
    pallas_call x1, Pallas kernels, per_device(): pl.pallas_call(functools.partial(hidden_kernel, len(blocks)), out_shape=(...  15.9 us
    ppermute x7, starting transfers between devices, per_device(): low = lax.ppermute(low, z_axes, ring(n_z, 1))  15.3 us
  transfers between devices with their start and end apart: 19, of which 10 were waited for; matrix products, arithmetic and copies ran while one was open for 4% of the time, Pallas kernels for 0%

profile of v1, /device:TPU:2, one launch (start us, length us, event | category | flops | bytes accessed | tf_op | source)
XLA Modules:
  0.0 268.4 jit_solution(13356604262856275611)
XLA Ops:
  8.6 13.4 %all_gather.10.refs_0_ = bf16[256,896]{1,0:T(8,128)(2,1)S(1)} all-gather(bf16[64,896]{1,0:T(8,128)(2,1)} %bitcast.49), channel_id=1, replica_groups=mesh['zh'=8,'zl'=2,'y'=4,'x'=4,'c'=2] {'y'}, dimensions={0}, use_global_device_ids=true | all-gather | bytes 573440 | tf_op jit(solution)/shard_map/all_gather | solution.py:186
  22.0 3.8 %collective-permute-start = (bf16[256,896]{1,0:T(8,128)(2,1)S(1)}, bf16[256,896]{1,0:T(8,128)(2,1)S(1)}, u32[]{:S(2)}, u32[]{:S(2)}) collective-permute-start(bf16[256,896]{1,0:T(8,128)(2,1)S(1)} %all_gather.10.refs_0_), channel_id=1, source_target_pairs={{0,32},{32,64},{64,96},{96,128},{128,160},{160,192},{192,224},{224... | collective-permute-start | bytes 1376264 | tf_op jit(solution)/shard_map/ppermute | solution.py:195
  25.9 9.5 %collective-permute-start.1 = (bf16[256,896]{1,0:T(8,128)(2,1)S(1)}, bf16[256,896]{1,0:T(8,128)(2,1)S(1)}, u32[]{:S(2)}, u32[]{:S(2)}) collective-permute-start(bf16[256,896]{1,0:T(8,128)(2,1)S(1)} %all_gather.10.refs_0_), channel_id=1, source_target_pairs={{0,480},{32,0},{64,32},{96,64},{128,96},{160,128},{192,160},{224,1... | collective-permute-start | bytes 1376264 | tf_op jit(solution)/shard_map/ppermute | solution.py:196
  35.4 6.9 %collective-permute-done.refs_1_ = bf16[256,896]{1,0:T(8,128)(2,1)S(1)} collective-permute-done((bf16[256,896]{1,0:T(8,128)(2,1)S(1)}, bf16[256,896]{1,0:T(8,128)(2,1)S(1)}, u32[]{:S(2)}, u32[]{:S(2)}) %collective-permute-start) | collective-permute-done | bytes 458784 | tf_op jit(solution)/shard_map/ppermute | solution.py:195
  42.2 1.9 collective-permute-start.2
  44.2 0.8 copy-done.7
  45.0 5.1 %collective-permute-start.3 = (bf16[256,896]{1,0:T(8,128)(2,1)S(1)}, bf16[256,896]{1,0:T(8,128)(2,1)S(1)}, u32[]{:S(2)}, u32[]{:S(2)}) collective-permute-start(bf16[256,896]{1,0:T(8,128)(2,1)S(1)} %collective-permute-done.1.refs_2_), channel_id=1, source_target_pairs={{0,480},{32,0},{64,32},{96,64},{128,96},{160,128},{192,160},{224,1... | collective-permute-start | bytes 1376264 | tf_op jit(solution)/shard_map/ppermute | solution.py:196
  50.1 0.8 copy-done.9
  50.9 4.4 %collective-permute-done.2.refs_3_ = bf16[256,896]{1,0:T(8,128)(2,1)S(1)} collective-permute-done((bf16[256,896]{1,0:T(8,128)(2,1)S(1)}, bf16[256,896]{1,0:T(8,128)(2,1)S(1)}, u32[]{:S(2)}, u32[]{:S(2)}) %collective-permute-start.2) | collective-permute-done | bytes 458784 | tf_op jit(solution)/shard_map/ppermute | solution.py:195
  55.3 1.9 collective-permute-start.4
  57.2 0.8 copy-done.11
  57.9 5.1 %collective-permute-start.5 = (bf16[256,896]{1,0:T(8,128)(2,1)S(1)}, bf16[256,896]{1,0:T(8,128)(2,1)S(1)}, u32[]{:S(2)}, u32[]{:S(2)}) collective-permute-start(bf16[256,896]{1,0:T(8,128)(2,1)S(1)} %collective-permute-done.3.refs_4_), channel_id=1, source_target_pairs={{0,480},{32,0},{64,32},{96,64},{128,96},{160,128},{192,160},{224,1... | collective-permute-start | bytes 1376264 | tf_op jit(solution)/shard_map/ppermute | solution.py:196
  63.1 0.8 copy-done.13
  63.9 3.5 %collective-permute-done.4.refs_5_ = bf16[256,896]{1,0:T(8,128)(2,1)S(1)} collective-permute-done((bf16[256,896]{1,0:T(8,128)(2,1)S(1)}, bf16[256,896]{1,0:T(8,128)(2,1)S(1)}, u32[]{:S(2)}, u32[]{:S(2)}) %collective-permute-start.4) | collective-permute-done | bytes 458784 | tf_op jit(solution)/shard_map/ppermute | solution.py:195
  67.4 1.9 collective-permute-start.6
  69.3 0.8 copy-done.15
  70.1 5.1 %collective-permute-start.7 = (bf16[256,896]{1,0:T(8,128)(2,1)S(1)}, bf16[256,896]{1,0:T(8,128)(2,1)S(1)}, u32[]{:S(2)}, u32[]{:S(2)}) collective-permute-start(bf16[256,896]{1,0:T(8,128)(2,1)S(1)} %collective-permute-done.5.refs_6_), channel_id=1, source_target_pairs={{0,480},{32,0},{64,32},{96,64},{128,96},{160,128},{192,160},{224,1... | collective-permute-start | bytes 1376264 | tf_op jit(solution)/shard_map/ppermute | solution.py:196
  75.2 0.8 copy-done.17
  76.0 2.9 %collective-permute-done.6.refs_7_ = bf16[256,896]{1,0:T(8,128)(2,1)S(1)} collective-permute-done((bf16[256,896]{1,0:T(8,128)(2,1)S(1)}, bf16[256,896]{1,0:T(8,128)(2,1)S(1)}, u32[]{:S(2)}, u32[]{:S(2)}) %collective-permute-start.6) | collective-permute-done | bytes 458784 | tf_op jit(solution)/shard_map/ppermute | solution.py:195
  78.9 1.9 collective-permute-start.8
  80.9 0.8 copy-done.19
  81.6 5.2 %collective-permute-start.9 = (bf16[256,896]{1,0:T(8,128)(2,1)S(1)}, bf16[256,896]{1,0:T(8,128)(2,1)S(1)}, u32[]{:S(2)}, u32[]{:S(2)}) collective-permute-start(bf16[256,896]{1,0:T(8,128)(2,1)S(1)} %collective-permute-done.7.refs_8_), channel_id=1, source_target_pairs={{0,480},{32,0},{64,32},{96,64},{128,96},{160,128},{192,160},{224,1... | collective-permute-start | bytes 1376264 | tf_op jit(solution)/shard_map/ppermute | solution.py:196
  86.8 0.8 copy-done.21
  87.6 3.8 %collective-permute-done.8.refs_9_ = bf16[256,896]{1,0:T(8,128)(2,1)S(1)} collective-permute-done((bf16[256,896]{1,0:T(8,128)(2,1)S(1)}, bf16[256,896]{1,0:T(8,128)(2,1)S(1)}, u32[]{:S(2)}, u32[]{:S(2)}) %collective-permute-start.8) | collective-permute-done | bytes 458784 | tf_op jit(solution)/shard_map/ppermute | solution.py:195
  91.4 1.9 collective-permute-start.10
  93.3 0.8 copy-done.23
  94.1 5.3 %collective-permute-start.11 = (bf16[256,896]{1,0:T(8,128)(2,1)S(1)}, bf16[256,896]{1,0:T(8,128)(2,1)S(1)}, u32[]{:S(2)}, u32[]{:S(2)}) collective-permute-start(bf16[256,896]{1,0:T(8,128)(2,1)S(1)} %collective-permute-done.9.refs_10_), channel_id=1, source_target_pairs={{0,480},{32,0},{64,32},{96,64},{128,96},{160,128},{192,160},{224,1... | collective-permute-start | bytes 1376264 | tf_op jit(solution)/shard_map/ppermute | solution.py:196
  99.5 0.8 copy-done.25
  100.2 4.7 %collective-permute-done.10.refs_11_ = bf16[256,896]{1,0:T(8,128)(2,1)S(1)} collective-permute-done((bf16[256,896]{1,0:T(8,128)(2,1)S(1)}, bf16[256,896]{1,0:T(8,128)(2,1)S(1)}, u32[]{:S(2)}, u32[]{:S(2)}) %collective-permute-start.10) | collective-permute-done | bytes 458784 | tf_op jit(solution)/shard_map/ppermute | solution.py:195
  104.9 1.9 collective-permute-start.12
  106.8 0.8 collective-permute-done.11.refs_12_
  107.6 5.6 %collective-permute-start.13 = (bf16[256,896]{1,0:T(8,128)(2,1)S(1)}, bf16[256,896]{1,0:T(8,128)(2,1)S(1)}, u32[]{:S(2)}, u32[]{:S(2)}) collective-permute-start(bf16[256,896]{1,0:T(8,128)(2,1)S(1)} %collective-permute-done.11.refs_12_), channel_id=1, source_target_pairs={{0,480},{32,0},{64,32},{96,64},{128,96},{160,128},{192,160},{224,1... | collective-permute-start | bytes 1376264 | tf_op jit(solution)/shard_map/ppermute | solution.py:196
  113.4 1.7 slice.20
  115.2 3.4 %collective-permute-done.12.refs_13_ = bf16[256,896]{1,0:T(8,128)(2,1)S(1)} collective-permute-done((bf16[256,896]{1,0:T(8,128)(2,1)S(1)}, bf16[256,896]{1,0:T(8,128)(2,1)S(1)}, u32[]{:S(2)}, u32[]{:S(2)}) %collective-permute-start.12) | collective-permute-done | bytes 458784 | tf_op jit(solution)/shard_map/ppermute | solution.py:195
  118.6 0.7 slice.24
  119.3 1.9 collective-permute-start.14
  122.1 5.7 %collective-permute-start.15 = (bf16[128,896]{1,0:T(8,128)(2,1)}, bf16[128,896]{1,0:T(8,128)(2,1)}, u32[]{:S(2)}, u32[]{:S(2)}) collective-permute-start(bf16[128,896]{1,0:T(8,128)(2,1)} %slice.25), channel_id=1, source_target_pairs={{0,480},{32,0},{64,32},{96,64},{128,96},{160,128},{192,160},{224,1... | collective-permute-start | bytes 688136 | tf_op jit(solution)/shard_map/ppermute | solution.py:201
  127.9 3.5 %fusion.1.refs_22_ = bf16[16,512]{1,0:T(8,128)(2,1)S(1)} fusion(bf16[512,4096]{1,0:T(8,128)(2,1)} %all-gather.3.cloned.1.call-done.gradient_ref, bf16[3,16,4096]{2,1,0:T(8,128)(2,1)} %param.15), kind=kOutput, calls=%fused_computation.4 | convolution fusion | flops 67108864 | bytes 4341760 | tf_op jit(solution)/shard_map/dot_general | solution.py:19
  131.5 3.8 %convolution_convert_fusion.refs_20_ = bf16[32,512]{1,0:T(8,128)(2,1)S(1)} fusion(bf16[32,4096]{1,0:T(8,128)(2,1)} %bitcast.48, bf16[512,4096]{1,0:T(8,128)(2,1)} %all-gather.5.cloned.1.call-done.normed_ref), kind=kOutput, calls=%fused_computation.1 | convolution fusion | flops 134234112 | bytes 4489216 | tf_op jit(solution)/shard_map/dot_general | solution.py:19
  135.3 1.0 copy-done.8
  136.3 1.0 copy-done.10
  137.4 1.0 copy-done.12
  138.4 1.0 copy-done.14
  139.4 1.0 copy-done.16
  140.4 1.0 copy-done.18
  141.4 1.0 copy-done.20
  142.5 1.0 copy-done.22
  143.5 1.0 copy-done.24
  144.5 1.0 copy-done.26
  145.5 1.0 copy-done.28
  146.5 1.0 copy-done.30
  147.6 15.9 %hidden_side.1 = (f32[4,48,896]{2,1,0:T(8,128)S(1)}, f32[64,512]{1,0:T(8,128)S(1)}) custom-call(s32[17]{0:T(128)S(1)} %stack.71.place_ref, bf16[512,4096]{1,0:T(8,128)(2,1)S(1)} %copy-done, bf16[256,896]{1,0:T(8,128)(2,1)S(1)} %all_gather.10.refs_0_, bf16[256,896]{1,0:T(8,128)(2,1)S(1)} %copy-done.8, bf16[256,896]{1,0:T(8,128)(2,1)S(1)} %copy-done.10, ...), custom_call_target="tpu_custom_call" | custom-call | tf_op jit(solution)/shard_map/hidden_side/pallas_call | solution.py:212
  163.4 0.9 copy-done.5
  164.3 9.3 %all_to_all.30 = f32[8,8,512]{2,1,0:T(8,128)S(1)} all-to-all(f32[8,8,512]{2,1,0:T(8,128)S(1)} %bitcast.44), channel_id=1, replica_groups=mesh['zh'=8,'zl'=2,'y'=4,'x'=4,'c'=2] {'x','c'}, dimensions={0} | all-to-all | bytes 262144 | tf_op jit(solution)/shard_map/all_to_all | solution.py:240
  174.3 4.7 %all-to-all-start.1 = ((f32[8,8,512]{2,1,0:T(8,128)}), f32[8,8,512]{2,1,0:T(8,128)S(1)}, u32[]{:S(2)}, u32[]{:S(2)}) async-start(f32[8,8,512]{2,1,0:T(8,128)} %broadcast_in_dim.9), calls=%async_computation.1 | async-start | bytes 262144 | tf_op jit(solution)/shard_map/all_to_all | solution.py:242
  179.7 4.1 %all-to-all-done.1 = f32[8,8,512]{2,1,0:T(8,128)S(1)} async-done(((f32[8,8,512]{2,1,0:T(8,128)}), f32[8,8,512]{2,1,0:T(8,128)S(1)}, u32[]{:S(2)}, u32[]{:S(2)}) %all-to-all-start.1) | async-done | bytes 131104 | tf_op jit(solution)/shard_map/all_to_all | solution.py:242
  183.7 2.2 copy-done.1
  185.9 2.2 copy-done.2
  188.1 1.1 copy-done.6
  189.2 6.1 %clip_side.1 = f32[72,8,128]{2,1,0:T(8,128)S(1)} custom-call(s32[1]{0:T(128)} %bitcast.place_ref, f32[1]{0:T(128)} %copy.14.clip_ref, f32[64,512]{1,0:T(8,128)S(1)} %bitcast.42, f32[4,48,896]{2,1,0:T(8,128)S(1)} %copy-done.6, bf16[512,4096]{1,0:T(8,128)(2,1)S(1)} %copy-done.2, bf16[512,4096]{1,0:T(8,128)(2,1)S(1)} %copy-done.1), custom_call_target="tpu_custom_call" | custom-call | tf_op jit(solution)/shard_map/clip_side/pallas_call | solution.py:247
  195.3 15.9 %all_to_all.31 = f32[8,72,128]{2,1,0:T(8,128)S(1)} all-to-all(f32[8,72,128]{2,1,0:T(8,128)S(1)} %bitcast.41), channel_id=1, replica_groups=mesh['zh'=8,'zl'=2,'y'=4,'x'=4,'c'=2] {'zl','y'}, dimensions={0} | all-to-all | bytes 589824 | tf_op jit(solution)/shard_map/all_to_all | solution.py:260
  211.2 22.7 %all_to_all.32 = f32[8,9,128]{2,1,0:T(8,128)S(1)} all-to-all(f32[8,9,128]{2,1,0:T(8,128)S(1)} %reshape.40), channel_id=1, replica_groups=mesh['zh'=8,'zl'=2,'y'=4,'x'=4,'c'=2] {'zh'}, dimensions={0} | all-to-all | bytes 73728 | tf_op jit(solution)/shard_map/all_to_all | solution.py:263
  233.9 16.1 %all_to_all.33 = f32[8,9,128]{2,1,0:T(8,128)S(1)} all-to-all(f32[8,9,128]{2,1,0:T(8,128)S(1)} %broadcast_in_dim.10), channel_id=1, replica_groups=mesh['zh'=8,'zl'=2,'y'=4,'x'=4,'c'=2] {'zh'}, dimensions={0} | all-to-all | bytes 73728 | tf_op jit(solution)/shard_map/all_to_all | solution.py:265
  250.0 10.2 %all_to_all.34 = f32[8,72,128]{2,1,0:T(8,128)S(1)} all-to-all(f32[8,72,128]{2,1,0:T(8,128)S(1)} %broadcast_in_dim.11), channel_id=1, replica_groups=mesh['zh'=8,'zl'=2,'y'=4,'x'=4,'c'=2] {'zl','y'}, dimensions={0} | all-to-all | bytes 589824 | tf_op jit(solution)/shard_map/all_to_all | solution.py:268
  (69 shorter events, 4.8 us)
Async XLA Ops:
  7.2 120.7 %all-gather.3.cloned.1.call-start = ((), (), s32[]{:S(2)}) async-start(), calls=%async_computation.6 | async-start | bytes 4718592 | tf_op jit(solution)/shard_map/all_gather | solution.py:185
  7.9 123.6 %all-gather.5.cloned.1.call-start = ((), (), s32[]{:S(2)}) async-start(), calls=%async_computation.7 | async-start | bytes 4718592 | tf_op jit(solution)/shard_map/all_gather | solution.py:187
  22.0 20.2 %collective-permute-start = (bf16[256,896]{1,0:T(8,128)(2,1)S(1)}, bf16[256,896]{1,0:T(8,128)(2,1)S(1)}, u32[]{:S(2)}, u32[]{:S(2)}) collective-permute-start(bf16[256,896]{1,0:T(8,128)(2,1)S(1)} %all_gather.10.refs_0_), channel_id=1, source_target_pairs={{0,32},{32,64},{64,96},{96,128},{128,160},{160,192},{192,224},{224... | collective-permute-start | bytes 1376264 | tf_op jit(solution)/shard_map/ppermute | solution.py:195
  25.9 19.1 %collective-permute-start.1 = (bf16[256,896]{1,0:T(8,128)(2,1)S(1)}, bf16[256,896]{1,0:T(8,128)(2,1)S(1)}, u32[]{:S(2)}, u32[]{:S(2)}) collective-permute-start(bf16[256,896]{1,0:T(8,128)(2,1)S(1)} %all_gather.10.refs_0_), channel_id=1, source_target_pairs={{0,480},{32,0},{64,32},{96,64},{128,96},{160,128},{192,160},{224,1... | collective-permute-start | bytes 1376264 | tf_op jit(solution)/shard_map/ppermute | solution.py:196
  42.2 13.0 %collective-permute-start.2 = (bf16[256,896]{1,0:T(8,128)(2,1)S(1)}, bf16[256,896]{1,0:T(8,128)(2,1)S(1)}, u32[]{:S(2)}, u32[]{:S(2)}) collective-permute-start(bf16[256,896]{1,0:T(8,128)(2,1)S(1)} %collective-permute-done.refs_1_), channel_id=1, source_target_pairs={{0,32},{32,64},{64,96},{96,128},{128,160},{160,192},{192,224},{224... | collective-permute-start | bytes 1376264 | tf_op jit(solution)/shard_map/ppermute | solution.py:195
  44.2 0.8 copy-start.7
  45.0 13.0 %collective-permute-start.3 = (bf16[256,896]{1,0:T(8,128)(2,1)S(1)}, bf16[256,896]{1,0:T(8,128)(2,1)S(1)}, u32[]{:S(2)}, u32[]{:S(2)}) collective-permute-start(bf16[256,896]{1,0:T(8,128)(2,1)S(1)} %collective-permute-done.1.refs_2_), channel_id=1, source_target_pairs={{0,480},{32,0},{64,32},{96,64},{128,96},{160,128},{192,160},{224,1... | collective-permute-start | bytes 1376264 | tf_op jit(solution)/shard_map/ppermute | solution.py:196
  50.1 0.8 copy-start.9
  55.3 12.1 %collective-permute-start.4 = (bf16[256,896]{1,0:T(8,128)(2,1)S(1)}, bf16[256,896]{1,0:T(8,128)(2,1)S(1)}, u32[]{:S(2)}, u32[]{:S(2)}) collective-permute-start(bf16[256,896]{1,0:T(8,128)(2,1)S(1)} %collective-permute-done.2.refs_3_), channel_id=1, source_target_pairs={{0,32},{32,64},{64,96},{96,128},{128,160},{160,192},{192,224},{224... | collective-permute-start | bytes 1376264 | tf_op jit(solution)/shard_map/ppermute | solution.py:195
  57.2 0.8 copy-start.11
  57.9 12.1 %collective-permute-start.5 = (bf16[256,896]{1,0:T(8,128)(2,1)S(1)}, bf16[256,896]{1,0:T(8,128)(2,1)S(1)}, u32[]{:S(2)}, u32[]{:S(2)}) collective-permute-start(bf16[256,896]{1,0:T(8,128)(2,1)S(1)} %collective-permute-done.3.refs_4_), channel_id=1, source_target_pairs={{0,480},{32,0},{64,32},{96,64},{128,96},{160,128},{192,160},{224,1... | collective-permute-start | bytes 1376264 | tf_op jit(solution)/shard_map/ppermute | solution.py:196
  63.1 0.8 copy-start.13
  67.4 11.6 %collective-permute-start.6 = (bf16[256,896]{1,0:T(8,128)(2,1)S(1)}, bf16[256,896]{1,0:T(8,128)(2,1)S(1)}, u32[]{:S(2)}, u32[]{:S(2)}) collective-permute-start(bf16[256,896]{1,0:T(8,128)(2,1)S(1)} %collective-permute-done.4.refs_5_), channel_id=1, source_target_pairs={{0,32},{32,64},{64,96},{96,128},{128,160},{160,192},{192,224},{224... | collective-permute-start | bytes 1376264 | tf_op jit(solution)/shard_map/ppermute | solution.py:195
  69.3 0.8 copy-start.15
  70.1 11.5 %collective-permute-start.7 = (bf16[256,896]{1,0:T(8,128)(2,1)S(1)}, bf16[256,896]{1,0:T(8,128)(2,1)S(1)}, u32[]{:S(2)}, u32[]{:S(2)}) collective-permute-start(bf16[256,896]{1,0:T(8,128)(2,1)S(1)} %collective-permute-done.5.refs_6_), channel_id=1, source_target_pairs={{0,480},{32,0},{64,32},{96,64},{128,96},{160,128},{192,160},{224,1... | collective-permute-start | bytes 1376264 | tf_op jit(solution)/shard_map/ppermute | solution.py:196
  75.2 0.8 copy-start.17
  78.9 12.5 %collective-permute-start.8 = (bf16[256,896]{1,0:T(8,128)(2,1)S(1)}, bf16[256,896]{1,0:T(8,128)(2,1)S(1)}, u32[]{:S(2)}, u32[]{:S(2)}) collective-permute-start(bf16[256,896]{1,0:T(8,128)(2,1)S(1)} %collective-permute-done.6.refs_7_), channel_id=1, source_target_pairs={{0,32},{32,64},{64,96},{96,128},{128,160},{160,192},{192,224},{224... | collective-permute-start | bytes 1376264 | tf_op jit(solution)/shard_map/ppermute | solution.py:195
  80.8 0.8 copy-start.19
  81.6 12.5 %collective-permute-start.9 = (bf16[256,896]{1,0:T(8,128)(2,1)S(1)}, bf16[256,896]{1,0:T(8,128)(2,1)S(1)}, u32[]{:S(2)}, u32[]{:S(2)}) collective-permute-start(bf16[256,896]{1,0:T(8,128)(2,1)S(1)} %collective-permute-done.7.refs_8_), channel_id=1, source_target_pairs={{0,480},{32,0},{64,32},{96,64},{128,96},{160,128},{192,160},{224,1... | collective-permute-start | bytes 1376264 | tf_op jit(solution)/shard_map/ppermute | solution.py:196
  86.8 0.8 copy-start.21
  91.4 13.5 %collective-permute-start.10 = (bf16[256,896]{1,0:T(8,128)(2,1)S(1)}, bf16[256,896]{1,0:T(8,128)(2,1)S(1)}, u32[]{:S(2)}, u32[]{:S(2)}) collective-permute-start(bf16[256,896]{1,0:T(8,128)(2,1)S(1)} %collective-permute-done.8.refs_9_), channel_id=1, source_target_pairs={{0,32},{32,64},{64,96},{96,128},{128,160},{160,192},{192,224},{224... | collective-permute-start | bytes 1376264 | tf_op jit(solution)/shard_map/ppermute | solution.py:195
  93.3 0.8 copy-start.23
  94.1 13.5 %collective-permute-start.11 = (bf16[256,896]{1,0:T(8,128)(2,1)S(1)}, bf16[256,896]{1,0:T(8,128)(2,1)S(1)}, u32[]{:S(2)}, u32[]{:S(2)}) collective-permute-start(bf16[256,896]{1,0:T(8,128)(2,1)S(1)} %collective-permute-done.9.refs_10_), channel_id=1, source_target_pairs={{0,480},{32,0},{64,32},{96,64},{128,96},{160,128},{192,160},{224,1... | collective-permute-start | bytes 1376264 | tf_op jit(solution)/shard_map/ppermute | solution.py:196
  99.5 0.8 copy-start.25
  104.9 16.5 %copy-start.27 = (bf16[256,896]{1,0:T(8,128)(2,1)}, bf16[256,896]{1,0:T(8,128)(2,1)S(1)}, u32[]{:S(2)}) copy-start(bf16[256,896]{1,0:T(8,128)(2,1)S(1)} %collective-permute-done.10.refs_11_) | copy-start | bytes 1376260
  104.9 13.7 %collective-permute-start.12 = (bf16[256,896]{1,0:T(8,128)(2,1)S(1)}, bf16[256,896]{1,0:T(8,128)(2,1)S(1)}, u32[]{:S(2)}, u32[]{:S(2)}) collective-permute-start(bf16[256,896]{1,0:T(8,128)(2,1)S(1)} %collective-permute-done.10.refs_11_), channel_id=1, source_target_pairs={{0,32},{32,64},{64,96},{96,128},{128,160},{160,192},{192,224},{224... | collective-permute-start | bytes 1376264 | tf_op jit(solution)/shard_map/ppermute | solution.py:195
  107.6 13.8 %copy-start.29 = (bf16[256,896]{1,0:T(8,128)(2,1)}, bf16[256,896]{1,0:T(8,128)(2,1)S(1)}, u32[]{:S(2)}) copy-start(bf16[256,896]{1,0:T(8,128)(2,1)S(1)} %collective-permute-done.11.refs_12_) | copy-start | bytes 1376260
  107.6 13.8 %collective-permute-start.13 = (bf16[256,896]{1,0:T(8,128)(2,1)S(1)}, bf16[256,896]{1,0:T(8,128)(2,1)S(1)}, u32[]{:S(2)}, u32[]{:S(2)}) collective-permute-start(bf16[256,896]{1,0:T(8,128)(2,1)S(1)} %collective-permute-done.11.refs_12_), channel_id=1, source_target_pairs={{0,480},{32,0},{64,32},{96,64},{128,96},{160,128},{192,160},{224,1... | collective-permute-start | bytes 1376264 | tf_op jit(solution)/shard_map/ppermute | solution.py:196
  119.3 15.9 %collective-permute-start.14 = (bf16[128,896]{1,0:T(8,128)(2,1)}, bf16[128,896]{1,0:T(8,128)(2,1)}, u32[]{:S(2)}, u32[]{:S(2)}) collective-permute-start(bf16[128,896]{1,0:T(8,128)(2,1)} %slice.24), channel_id=1, source_target_pairs={{0,32},{32,64},{64,96},{96,128},{128,160},{160,192},{192,224},{224... | collective-permute-start | bytes 688136 | tf_op jit(solution)/shard_map/ppermute | solution.py:200
  122.1 13.2 %copy-start.3 = (bf16[512,896]{1,0:T(8,128)(2,1)S(1)}, bf16[512,896]{1,0:T(8,128)(2,1)}, u32[]{:S(2)}) copy-start(bf16[512,896]{1,0:T(8,128)(2,1)} %refs_17_.1) | copy-start | bytes 2752516
  122.1 13.2 %copy-start.4 = (bf16[512,896]{1,0:T(8,128)(2,1)S(1)}, bf16[512,896]{1,0:T(8,128)(2,1)}, u32[]{:S(2)}) copy-start(bf16[512,896]{1,0:T(8,128)(2,1)} %refs_18_.1) | copy-start | bytes 2752516
  122.1 13.2 %copy-start.31 = (bf16[3,16,896]{2,1,0:T(8,128)(2,1)S(1)}, bf16[3,16,896]{2,1,0:T(8,128)(2,1)}, u32[]{:S(2)}) copy-start(bf16[3,16,896]{2,1,0:T(8,128)(2,1)} %param.16) | copy-start | bytes 258052
  122.1 13.2 %collective-permute-start.15 = (bf16[128,896]{1,0:T(8,128)(2,1)}, bf16[128,896]{1,0:T(8,128)(2,1)}, u32[]{:S(2)}, u32[]{:S(2)}) collective-permute-start(bf16[128,896]{1,0:T(8,128)(2,1)} %slice.25), channel_id=1, source_target_pairs={{0,480},{32,0},{64,32},{96,64},{128,96},{160,128},{192,160},{224,1... | collective-permute-start | bytes 688136 | tf_op jit(solution)/shard_map/ppermute | solution.py:201
  131.5 3.8 %copy-start = (bf16[512,4096]{1,0:T(8,128)(2,1)S(1)}, bf16[512,4096]{1,0:T(8,128)(2,1)}, u32[]{:S(2)}) copy-start(bf16[512,4096]{1,0:T(8,128)(2,1)} %all-gather.3.cloned.1.call-done.gradient_ref) | copy-start | bytes 12582916
  135.3 1.0 copy-start.8
  136.3 1.0 copy-start.10
  137.4 1.0 copy-start.12
  138.4 1.0 copy-start.14
  139.4 1.0 copy-start.16
  140.4 1.0 copy-start.18
  141.4 1.0 copy-start.20
  142.5 1.0 copy-start.22
  143.5 1.0 copy-start.24
  144.5 1.0 copy-start.26
  145.5 1.0 copy-start.28
  146.5 1.0 copy-start.30
  163.4 0.9 copy-start.5
  174.3 9.4 %all-to-all-start.1 = ((f32[8,8,512]{2,1,0:T(8,128)}), f32[8,8,512]{2,1,0:T(8,128)S(1)}, u32[]{:S(2)}, u32[]{:S(2)}) async-start(f32[8,8,512]{2,1,0:T(8,128)} %broadcast_in_dim.9), calls=%async_computation.1 | async-start | bytes 262144 | tf_op jit(solution)/shard_map/all_to_all | solution.py:242
  183.7 2.2 copy-start.1
  185.9 2.2 copy-start.2
  188.1 1.1 copy-start.6
  189.2 71.0 %copy-start.32 = (f32[3,16,896]{2,1,0:T(8,128)S(1)}, f32[3,16,896]{2,1,0:T(8,128)}, u32[]{:S(2)}) copy-start(f32[3,16,896]{2,1,0:T(8,128)} %param.19) | copy-start | bytes 516100
  189.2 71.7 %copy-start.33 = (f32[3,16,512]{2,1,0:T(8,128)S(1)}, f32[3,16,512]{2,1,0:T(8,128)}, u32[]{:S(2)}) copy-start(f32[3,16,512]{2,1,0:T(8,128)} %param.18) | copy-start | bytes 294916
Sparse Core Ops, SparseCore 0:
  10.1 43.1 all-gather.2
  55.5 39.7 all-gather.4

commit v2 on v1

v2 whole, which is shorter than its diff:
```python
import functools

import jax
import jax.numpy as jnp
from jax import lax
from jax.experimental import pallas as pl
from jax.experimental.pallas import tpu as pltpu
from jax.sharding import Mesh
from jax.sharding import PartitionSpec as P

SEQUENCE_TOKENS = 128
RANK = 16
SCALE = 2.0
F32 = jnp.float32
BF16 = jnp.bfloat16


def contract(left, right, left_dim, right_dim):
    return lax.dot_general(
        left, right, (((left_dim,), (right_dim,)), ((), ())), preferred_element_type=F32
    )


def column_tiles(hidden, step, tile):
    whole = hidden // step

    def body(i, carry):
        tile(pl.multiple_of(i * step, step), step)
        return carry

    lax.fori_loop(0, whole, body, 0)
    if hidden > whole * step:
        tile(whole * step, hidden - whole * step)


def block_product(place_ref, gradient_ref, block_refs, cols):
    left = jnp.concatenate(
        [
            gradient_ref[:, pl.ds(pl.multiple_of(place_ref[i] * 128, 128), block.shape[0])]
            for i, block in enumerate(block_refs)
        ],
        axis=1,
    )
    right = jnp.concatenate([block[:, cols] for block in block_refs], axis=0)
    return jnp.dot(left, right, preferred_element_type=F32)


def gram_of(rows_ref, out_ref):
    for e in range(out_ref.shape[0]):
        rows = rows_ref[e * SEQUENCE_TOKENS : (e + 1) * SEQUENCE_TOKENS, :]
        out_ref[e] = contract(rows, rows, 1, 1)


def first_kernel(n_blocks, place_ref, gradient_ref, *refs):
    block_refs = refs[:n_blocks]
    factor_ref, total_ref, lora_ref, gram_ref = refs[n_blocks:]

    def tile(start, width):
        cols = pl.ds(start, width)
        total_ref[:, cols] = block_product(place_ref, gradient_ref, block_refs, cols)

    column_tiles(total_ref.shape[1], 256, tile)
    lora_ref[...] = contract(factor_ref[...], gradient_ref[...], 1, 1).astype(BF16)
    gram_of(gradient_ref, gram_ref)


def more_kernel(n_blocks, place_ref, gradient_ref, *refs):
    block_refs = refs[:n_blocks]
    before_ref, total_ref = refs[n_blocks:]

    def tile(start, width):
        cols = pl.ds(start, width)
        total_ref[:, cols] = before_ref[:, cols] + block_product(
            place_ref, gradient_ref, block_refs, cols
        )

    column_tiles(total_ref.shape[1], 256, tile)


def normed_kernel(normed_ref, factors_ref, in_ref, gram_ref):
    in_ref[...] = contract(factors_ref[...], normed_ref[...], 1, 1).astype(BF16)
    gram_of(normed_ref, gram_ref)


def hidden_kernel(n_blocks, place_ref, gradient_ref, *refs):
    block_refs = refs[:n_blocks]
    (before_ref, gate_ref, up_ref, factors_ref, in_ref, lora_ref, lora_t_ref) = refs[
        n_blocks : n_blocks + 7
    ]
    sums_ref, mids_ref, total = refs[n_blocks + 7 :]
    tokens, hidden = gate_ref.shape
    sequences = tokens // SEQUENCE_TOKENS
    mids_ref[...] = jnp.zeros_like(mids_ref)

    def tile(start, width):
        cols = pl.ds(start, width)
        factors = factors_ref[:, cols]
        total[:, :width] = (
            before_ref[:, cols]
            + block_product(place_ref, gradient_ref, block_refs, cols)
            + SCALE * jnp.dot(lora_ref[...], factors[2 * RANK :], preferred_element_type=F32)
        )
        for e in range(sequences):
            rows = slice(e * SEQUENCE_TOKENS, (e + 1) * SEQUENCE_TOKENS)
            hidden_grad = total[rows, :width]
            gate = gate_ref[rows, cols].astype(F32)
            up = up_ref[rows, cols].astype(F32)
            sigmoid = jax.nn.sigmoid(gate)
            silu = gate * sigmoid
            slope = sigmoid * (1.0 + gate * (1.0 - sigmoid))
            activation = (silu * up).astype(BF16)
            gate_grad = (hidden_grad * up * slope).astype(BF16)
            up_grad = (hidden_grad * silu).astype(BF16)
            left = (in_ref[:RANK, rows], in_ref[RANK:, rows], lora_t_ref[:, rows])
            for j, right in enumerate((gate_grad, up_grad, activation)):
                part = slice(j * RANK, (j + 1) * RANK)
                sums_ref[e, part, cols] = SCALE * jnp.dot(
                    left[j], right, preferred_element_type=F32
                )
                mids_ref[part, rows] += contract(factors[part], right, 1, 1)

    column_tiles(hidden, 256, tile)
    for e in range(sequences):
        square = sums_ref[e] * sums_ref[e]
        line = jnp.sum(jnp.sum(square, axis=0, keepdims=True), axis=1, keepdims=True)
        mids_ref[3 * RANK + e : 3 * RANK + e + 1, :] = jnp.broadcast_to(line, (1, tokens))


def quadratic(left, gram):
    product = jnp.zeros((left.shape[0], gram.shape[1]), F32)
    rest = gram
    for _ in range(3):
        part = rest.astype(BF16)
        product = product + jnp.dot(left, part, preferred_element_type=F32)
        rest = rest - part.astype(F32)
    return product * left.astype(F32)


def total_of(values):
    return jnp.sum(jnp.sum(values, axis=0, keepdims=True), axis=1, keepdims=True)


def clip_kernel(
    clip_ref,
    mids_ref,
    sums_ref,
    normed_ref,
    gradient_ref,
    normed_gram_ref,
    gradient_gram_ref,
    out_ref,
    wide,
):
    sequences, _, hidden = sums_ref.shape
    local = wide.shape[1]
    bound = clip_ref[0]
    weights = []
    for e in range(sequences):
        rows = slice(e * SEQUENCE_TOKENS, (e + 1) * SEQUENCE_TOKENS)
        mids = mids_ref[: 3 * RANK, rows].astype(BF16)
        square = total_of(quadratic(mids[: 2 * RANK], normed_gram_ref[e])) + total_of(
            quadratic(mids[2 * RANK :], gradient_gram_ref[e])
        )
        square = SCALE * SCALE * jnp.maximum(square, 0.0)
        square = square + mids_ref[3 * RANK + e : 3 * RANK + e + 1, 0:1]
        weight = bound / jnp.maximum(jnp.sqrt(square), bound)
        weights.append(weight)
        first = weight * (
            SCALE * jnp.dot(mids[: 2 * RANK], normed_ref[rows, :], preferred_element_type=F32)
        )
        second = weight * (
            SCALE * jnp.dot(mids[2 * RANK :], gradient_ref[rows, :], preferred_element_type=F32)
        )
        if e == 0:
            wide[: 2 * RANK] = first
            wide[2 * RANK :] = second
        else:
            wide[: 2 * RANK] += first
            wide[2 * RANK :] += second
    lanes = out_ref.shape[0] // 6
    for t in range(out_ref.shape[0]):
        r, c = divmod(t, lanes)
        rows = slice(8 * r, 8 * r + 8)
        at = c * 128
        if at < local:
            value = wide[rows, at : at + 128]
        elif at < local + hidden:
            at = at - local
            value = weights[0] * sums_ref[0, rows, at : at + 128]
            for e in range(1, sequences):
                value = value + weights[e] * sums_ref[e, rows, at : at + 128]
        else:
            value = jnp.zeros((8, 128), F32)
        out_ref[t] = value


def ring(size, by):
    return [(i, (i + by) % size) for i in range(size)]


def per_device(
    sizes,
    normed,
    output_gradient,
    gate_preactivation,
    upward_preactivation,
    frozen_down_weight,
    adapter_width_factors,
    adapter_hidden_factors,
    clipping_limit,
    width_noise_draw,
    hidden_noise_draw,
):
    tokens, local_width = normed.shape
    hidden = gate_preactivation.shape[1]
    sequences = tokens // SEQUENCE_TOKENS
    n_z = sizes["z"]
    n_tensor = sizes["x"] * sizes["c"]
    z_axes, tensor_axes = "z", ("x", "c")
    z = lax.axis_index(z_axes)

    gradient = lax.all_gather(output_gradient, tensor_axes, axis=1, tiled=True)
    block = lax.all_gather(frozen_down_weight.T, "y", axis=0, tiled=True)
    normed_all = lax.all_gather(normed, tensor_axes, axis=1, tiled=True)

    rows = block.shape[0]
    half = rows // 2
    units = rows // 128
    vmem = pl.BlockSpec(memory_space=pltpu.VMEM)
    smem = pl.BlockSpec(memory_space=pltpu.SMEM)
    params = pltpu.CompilerParams(vmem_limit_bytes=32 * 2**20)

    def place(offsets):
        at = [((z + offset) % n_z) * units for offset in offsets]
        return jnp.stack(at).astype(jnp.int32)

    low, high = {0: block}, {0: block}

    def step(k, low_from, high_from):
        low[k] = lax.ppermute(low_from, z_axes, ring(n_z, 1))
        high[k] = lax.ppermute(high_from, z_axes, ring(n_z, -1))

    def product_cost(n_rows, read):
        return pl.CostEstimate(
            flops=2 * tokens * n_rows * hidden, bytes_accessed=read, transcendentals=0
        )

    last = n_z // 2
    for k in range(1, last - 2):
        step(k, low[k - 1], high[k - 1])
    offsets = [0] + [sign * k for k in range(1, last - 4) for sign in (-1, 1)]
    blocks = [block] + [side[k] for k in range(1, last - 4) for side in (low, high)]
    total, lora_t, gradient_gram = pl.pallas_call(
        functools.partial(first_kernel, len(blocks)),
        out_shape=(
            jax.ShapeDtypeStruct((tokens, hidden), F32),
            jax.ShapeDtypeStruct((RANK, tokens), BF16),
            jax.ShapeDtypeStruct((sequences, SEQUENCE_TOKENS, SEQUENCE_TOKENS), F32),
        ),
        in_specs=[smem] + [vmem] * (len(blocks) + 2),
        out_specs=(vmem, vmem, vmem),
        compiler_params=params,
        cost_estimate=product_cost(rows * len(blocks), 8 * 2**20),
        name="first_blocks",
    )(place(offsets), gradient, *blocks, adapter_width_factors[2])

    at = last - 3
    low_in, high_in, total = lax.optimization_barrier((low[at], high[at], total))
    step(last - 2, low_in, high_in)
    offsets = [sign * k for k in range(last - 4, last - 2) for sign in (-1, 1)]
    blocks = [side[k] for k in range(last - 4, last - 2) for side in (low, high)]
    total = pl.pallas_call(
        functools.partial(more_kernel, len(blocks)),
        out_shape=jax.ShapeDtypeStruct((tokens, hidden), F32),
        in_specs=[smem] + [vmem] * (len(blocks) + 2),
        out_specs=vmem,
        input_output_aliases={len(blocks) + 2: 0},
        compiler_params=params,
        cost_estimate=product_cost(rows * len(blocks), 6 * 2**20),
        name="more_blocks",
    )(place(offsets), gradient, *blocks, total)
    step(last - 1, low[last - 2], high[last - 2])

    in_t, normed_gram = pl.pallas_call(
        normed_kernel,
        out_shape=(
            jax.ShapeDtypeStruct((2 * RANK, tokens), BF16),
            jax.ShapeDtypeStruct((sequences, SEQUENCE_TOKENS, SEQUENCE_TOKENS), F32),
        ),
        in_specs=[vmem, vmem],
        out_specs=(vmem, vmem),
        compiler_params=params,
        cost_estimate=pl.CostEstimate(
            flops=2 * tokens * 4096 * 160, bytes_accessed=5 * 2**20, transcendentals=0
        ),
        name="normed_side",
    )(normed_all, adapter_width_factors[:2].reshape(2 * RANK, -1))

    low_in, high_in, total, in_t = lax.optimization_barrier(
        (low[last - 1], high[last - 1], total, in_t)
    )
    step(last, low_in[:half], high_in[half:])
    far = ((z + last) % n_z) * units
    offsets = [sign * k for k in range(last - 2, last) for sign in (-1, 1)]
    blocks = [side[k] for k in range(last - 2, last) for side in (low, high)]
    blocks += [low[last], high[last]]
    places = jnp.concatenate(
        [place(offsets), jnp.stack([far, far + units // 2]).astype(jnp.int32)]
    )
    sums, mids = pl.pallas_call(
        functools.partial(hidden_kernel, len(blocks)),
        out_shape=(
            jax.ShapeDtypeStruct((sequences, 3 * RANK, hidden), F32),
            jax.ShapeDtypeStruct((8 * n_tensor, tokens), F32),
        ),
        in_specs=[smem] + [vmem] * (len(blocks) + 8),
        out_specs=(vmem, vmem),
        scratch_shapes=[pltpu.VMEM((tokens, 256), F32)],
        compiler_params=params,
        name="hidden_side",
    )(
        places,
        gradient,
        *blocks,
        total,
        gate_preactivation,
        upward_preactivation,
        adapter_hidden_factors.reshape(3 * RANK, hidden),
        in_t,
        lora_t.T,
        lora_t,
    )

    pieces = lax.all_to_all(mids.reshape(n_tensor, 8, tokens), tensor_axes, 0, 0)
    piece = jnp.sum(pieces, axis=0)
    mids = lax.all_to_all(
        jnp.broadcast_to(piece, (n_tensor,) + piece.shape), tensor_axes, 0, 0
    ).reshape(8 * n_tensor, tokens)

    lanes = 12
    out = pl.pallas_call(
        clip_kernel,
        out_shape=jax.ShapeDtypeStruct((6 * lanes, 8, 128), F32),
        in_specs=[smem] + [vmem] * 6,
        out_specs=vmem,
        scratch_shapes=[pltpu.VMEM((3 * RANK, local_width), F32)],
        compiler_params=params,
        name="clip_side",
    )(
        clipping_limit,
        mids,
        sums,
        normed,
        output_gradient,
        normed_gram,
        gradient_gram,
    )

    n_y = sizes["y"]
    part = jnp.sum(lax.all_to_all(out.reshape(n_y, -1, 128), "y", 0, 0), axis=0)
    part = jnp.sum(lax.all_to_all(part.reshape(n_z, -1, 128), z_axes, 0, 0), axis=0)
    part = lax.all_to_all(
        jnp.broadcast_to(part, (n_z,) + part.shape), z_axes, 0, 0
    ).reshape(-1, 128)
    part = lax.all_gather(part, "y", axis=0)
    total = (
        part.reshape(6, lanes, 8, 128)
        .transpose(0, 2, 1, 3)
        .reshape(3, RANK, lanes * 128)
    )
    count = sequences * n_z * sizes["y"]
    bound = clipping_limit[0]
    wide = total[:, :, :local_width]
    inner = total[:, :, local_width : local_width + hidden]
    return (
        (wide + bound * width_noise_draw) / count,
        (inner + bound * hidden_noise_draw) / count,
    )


def solution(mesh):
    names = ("z", "y", "x", "c")
    extents = (16, 4, 4, 2)
    fine = Mesh(mesh.devices.reshape(extents), names)
    dp, tensor = ("z", "y"), ("x", "c")
    placed = (
        P(dp, tensor),
        P(dp, tensor),
        P(dp, tensor),
        P(dp, tensor),
        P(tensor, dp),
        P(),
        P(None, None, tensor),
        P(),
        P(None, None, tensor),
        P(None, None, tensor),
    )
    return jax.shard_map(
        functools.partial(per_device, dict(zip(names, extents, strict=True))),
        mesh=fine,
        in_specs=placed,
        out_specs=(P(None, None, tensor), P(None, None, tensor)),
        check_vma=False,
    )
```

time: 270 us -> 260 us (0.963)
  the two profiles are of different devices: /device:TPU:2 before, /device:TPU:32 now
where the time goes in v2:
time: 260 us; the launch traced here: 258 us
  blocking collectives  88.4 us (34%)
  starting transfers between devices  67.3 us (26%)
  local copies, waits for them, and re-layouts  36.2 us (14%)
  waiting for transfers between devices  31.2 us (12%)
  Pallas kernels  18.2 us (7%)
  between operations  15.3 us (6%)
    ppermute x8, starting transfers between devices, step(): high[k] = lax.ppermute(high_from, z_axes, ring(n_z, -1))  48.5 us
    unnamed x78, local copies, waits for them, and re-layouts  31.8 us
    all_to_all x1, blocking collectives, per_device(): lax.all_to_all(part.reshape(n_z, -1, 128), z_axes, 0, 0)  20.7 us
    all_to_all x1, blocking collectives, per_device(): lax.all_to_all(jnp.broadcast_to(part, (n_z,) + part.shape), z_axes, 0, 0)  17 us
    ppermute x8, starting transfers between devices, step(): low[k] = lax.ppermute(low_from, z_axes, ring(n_z, 1))  15.3 us
    all_to_all x1, blocking collectives, per_device(): part = jnp.sum(lax.all_to_all(out.reshape(n_y, -1, 128), 'y', 0, 0), axis=0)  13.9 us
    ppermute x8, waiting for transfers between devices, step(): high[k] = lax.ppermute(high_from, z_axes, ring(n_z, -1))  13.7 us
    all_gather x1, blocking collectives, per_device(): block = lax.all_gather(frozen_down_weight.T, 'y', axis=0, tiled=True)  13.4 us
  transfers between devices with their start and end apart: 19, of which 11 were waited for; matrix products, arithmetic and copies ran while one was open for 1% of the time, Pallas kernels for 4%

profile of v2, /device:TPU:32, one launch (start us, length us, event | category | flops | bytes accessed | tf_op | source)
XLA Modules:
  0.0 258.1 jit_solution(13628692026333395131)
XLA Ops:
  8.6 13.4 %all_gather.13.refs_0_ = bf16[256,896]{1,0:T(8,128)(2,1)S(1)} all-gather(bf16[64,896]{1,0:T(8,128)(2,1)} %bitcast.42), channel_id=1, replica_groups=mesh['z'=16,'y'=4,'x'=4,'c'=2] {'y'}, dimensions={0}, use_global_device_ids=true | all-gather | bytes 573440 | tf_op jit(solution)/shard_map/all_gather | solution.py:223
  22.0 6.9 %collective-permute-start.5 = (bf16[256,896]{1,0:T(8,128)(2,1)S(1)}, bf16[256,896]{1,0:T(8,128)(2,1)S(1)}, u32[]{:S(2)}, u32[]{:S(2)}) collective-permute-start(bf16[256,896]{1,0:T(8,128)(2,1)S(1)} %all_gather.13.refs_0_), channel_id=1, source_target_pairs={{0,480},{32,0},{64,32},{96,64},{128,96},{160,128},{192,160},{224,1... | collective-permute-start | bytes 1376264 | tf_op jit(solution)/shard_map/ppermute | solution.py:241
  28.9 1.9 collective-permute-start
  30.8 4.0 %collective-permute-done.5.refs_2_ = bf16[256,896]{1,0:T(8,128)(2,1)S(1)} collective-permute-done((bf16[256,896]{1,0:T(8,128)(2,1)S(1)}, bf16[256,896]{1,0:T(8,128)(2,1)S(1)}, u32[]{:S(2)}, u32[]{:S(2)}) %collective-permute-start.5) | collective-permute-done | bytes 458784 | tf_op jit(solution)/shard_map/ppermute | solution.py:241
  34.9 8.6 %collective-permute-start.6 = (bf16[256,896]{1,0:T(8,128)(2,1)S(1)}, bf16[256,896]{1,0:T(8,128)(2,1)S(1)}, u32[]{:S(2)}, u32[]{:S(2)}) collective-permute-start(bf16[256,896]{1,0:T(8,128)(2,1)S(1)} %collective-permute-done.5.refs_2_), channel_id=1, source_target_pairs={{0,480},{32,0},{64,32},{96,64},{128,96},{160,128},{192,160},{224,1... | collective-permute-start | bytes 1376264 | tf_op jit(solution)/shard_map/ppermute | solution.py:241
  43.5 0.8 copy-done.16
  44.3 1.9 collective-permute-start.1
  47.0 3.7 %collective-permute-done.6.refs_4_ = bf16[256,896]{1,0:T(8,128)(2,1)S(1)} collective-permute-done((bf16[256,896]{1,0:T(8,128)(2,1)S(1)}, bf16[256,896]{1,0:T(8,128)(2,1)S(1)}, u32[]{:S(2)}, u32[]{:S(2)}) %collective-permute-start.6) | collective-permute-done | bytes 458784 | tf_op jit(solution)/shard_map/ppermute | solution.py:241
  50.6 5.7 %collective-permute-start.7 = (bf16[256,896]{1,0:T(8,128)(2,1)S(1)}, bf16[256,896]{1,0:T(8,128)(2,1)S(1)}, u32[]{:S(2)}, u32[]{:S(2)}) collective-permute-start(bf16[256,896]{1,0:T(8,128)(2,1)S(1)} %collective-permute-done.6.refs_4_), channel_id=1, source_target_pairs={{0,480},{32,0},{64,32},{96,64},{128,96},{160,128},{192,160},{224,1... | collective-permute-start | bytes 1376264 | tf_op jit(solution)/shard_map/ppermute | solution.py:241
  56.4 0.8 copy-done.20
  57.6 1.9 collective-permute-start.2
  59.5 0.8 copy-done.22
  60.3 2.4 collective-permute-done.7.refs_6_
  62.7 5.7 %collective-permute-start.8 = (bf16[256,896]{1,0:T(8,128)(2,1)S(1)}, bf16[256,896]{1,0:T(8,128)(2,1)S(1)}, u32[]{:S(2)}, u32[]{:S(2)}) collective-permute-start(bf16[256,896]{1,0:T(8,128)(2,1)S(1)} %collective-permute-done.7.refs_6_), channel_id=1, source_target_pairs={{0,480},{32,0},{64,32},{96,64},{128,96},{160,128},{192,160},{224,1... | collective-permute-start | bytes 1376264 | tf_op jit(solution)/shard_map/ppermute | solution.py:241
  69.6 1.9 collective-permute-start.3
  71.6 0.8 copy-done.26
  72.4 2.0 collective-permute-done.8.refs_1_
  74.4 5.6 %collective-permute-start.9 = (bf16[256,896]{1,0:T(8,128)(2,1)S(1)}, bf16[256,896]{1,0:T(8,128)(2,1)}, u32[]{:S(2)}, u32[]{:S(2)}) collective-permute-start(bf16[256,896]{1,0:T(8,128)(2,1)S(1)} %collective-permute-done.8.refs_1_), channel_id=1, source_target_pairs={{0,480},{32,0},{64,32},{96,64},{128,96},{160,128},{192,160},{224,1... | collective-permute-start | bytes 1376264 | tf_op jit(solution)/shard_map/ppermute | solution.py:241
  79.9 1.2 collective-permute-done.3.refs_0_
  81.2 1.9 collective-permute-start.4
  83.1 0.9 slice_bitcast_fusion.refs_7_
  84.2 2.3 copy-done
  86.5 1.1 copy-done.17
  87.6 1.0 copy-done.19
  88.6 1.0 copy-done.21
  89.6 1.0 copy-done.23
  90.6 1.0 copy-done.25
  91.7 1.0 copy-done.27
  92.7 5.3 %first_blocks.1 = (f32[512,896]{1,0:T(8,128)S(1)}, bf16[16,512]{1,0:T(8,128)(2,1)S(1)}, f32[4,128,128]{2,1,0:T(8,128)S(1)}) custom-call(s32[7]{0:T(128)S(1)} %stack.70.place_ref, bf16[512,4096]{1,0:T(8,128)(2,1)S(1)} %copy-done, bf16[256,896]{1,0:T(8,128)(2,1)S(1)} %all_gather.13.refs_0_, bf16[256,896]{1,0:T(8,128)(2,1)S(1)} %copy-done.19, ...), custom_call_target="tpu_custom_call" | custom-call | flops 1644167168 | bytes 8388608 | tf_op jit(solution)/shard_map/first_blocks/pallas_call | solution.py:253
  98.6 1.9 collective-permute-start.10
  100.6 5.0 %collective-permute-start.11 = (bf16[256,896]{1,0:T(8,128)(2,1)}, bf16[256,896]{1,0:T(8,128)(2,1)}, u32[]{:S(2)}, u32[]{:S(2)}) collective-permute-start(bf16[256,896]{1,0:T(8,128)(2,1)} %collective-permute-done.9.refs_3_), channel_id=1, source_target_pairs={{0,480},{32,0},{64,32},{96,64},{128,96},{160,128},{192,160},{224,1... | collective-permute-start | bytes 1376264 | tf_op jit(solution)/shard_map/ppermute | solution.py:241
  105.6 5.0 %collective-permute-done.10.refs_0_ = bf16[256,896]{1,0:T(8,128)(2,1)} collective-permute-done((bf16[256,896]{1,0:T(8,128)(2,1)}, bf16[256,896]{1,0:T(8,128)(2,1)}, u32[]{:S(2)}, u32[]{:S(2)}) %collective-permute-start.10) | collective-permute-done | bytes 458784 | tf_op jit(solution)/shard_map/ppermute | solution.py:240
  110.6 1.9 collective-permute-start.12
  112.5 5.6 %collective-permute-start.13 = (bf16[256,896]{1,0:T(8,128)(2,1)}, bf16[256,896]{1,0:T(8,128)(2,1)S(1)}, u32[]{:S(2)}, u32[]{:S(2)}) collective-permute-start(bf16[256,896]{1,0:T(8,128)(2,1)} %collective-permute-done.11.refs_1_), channel_id=1, source_target_pairs={{0,480},{32,0},{64,32},{96,64},{128,96},{160,128},{192,160},{224,1... | collective-permute-start | bytes 1376264 | tf_op jit(solution)/shard_map/ppermute | solution.py:241
  118.2 1.0 slice.19
  119.3 2.3 copy-done.3
  121.6 2.5 normed_side.1
  124.1 1.0 copy-done.13
  125.1 1.0 copy-done.15
  126.2 3.1 %more_blocks.1.refs_6_ = f32[512,896]{1,0:T(8,128)S(1)} custom-call(s32[4]{0:T(128)S(1)} %pad_add_fusion.place_ref, bf16[512,4096]{1,0:T(8,128)(2,1)S(1)} %copy-done.1, bf16[256,896]{1,0:T(8,128)(2,1)S(1)} %copy-done.15, bf16[256,896]{1,0:T(8,128)(2,1)S(1)} %copy-done.13, ...), custom_call_target="tpu_custom_call", output_to_operand_aliasing={{}: (6, {})} | custom-call | flops 939524096 | bytes 6291456 | tf_op jit(solution)/shard_map/more_blocks/pallas_call | solution.py:272
  129.3 0.8 slice.20
  130.8 5.4 %collective-permute-start.15 = (bf16[128,896]{1,0:T(8,128)(2,1)}, bf16[128,896]{1,0:T(8,128)(2,1)S(1)}, u32[]{:S(2)}, u32[]{:S(2)}) collective-permute-start(bf16[128,896]{1,0:T(8,128)(2,1)} %slice.21), channel_id=1, source_target_pairs={{0,480},{32,0},{64,32},{96,64},{128,96},{160,128},{192,160},{224,1... | collective-permute-start | bytes 688136 | tf_op jit(solution)/shard_map/ppermute | solution.py:241
  136.2 1.9 collective-permute-start.14
  138.4 1.6 collective-permute-done.15.refs_5_
  140.8 3.6 %collective-permute-done.14.refs_4_ = bf16[128,896]{1,0:T(8,128)(2,1)S(1)} collective-permute-done((bf16[128,896]{1,0:T(8,128)(2,1)}, bf16[128,896]{1,0:T(8,128)(2,1)S(1)}, u32[]{:S(2)}, u32[]{:S(2)}) %collective-permute-start.14) | collective-permute-done | bytes 229408 | tf_op jit(solution)/shard_map/ppermute | solution.py:240
  145.1 2.2 copy-done.2
  147.2 1.0 copy-done.7
  148.3 1.2 copy-done.8
  149.4 1.2 copy-done.9
  150.6 0.9 copy-done.33
  151.6 0.9 copy-done.35
  152.5 0.9 copy-done.36
  153.4 6.8 %hidden_side.1 = (f32[4,48,896]{2,1,0:T(8,128)S(1)}, f32[64,512]{1,0:T(8,128)S(1)}) custom-call(s32[6]{0:T(128)S(1)} %concatenate.3.place_ref, bf16[512,4096]{1,0:T(8,128)(2,1)S(1)} %copy-done.2, bf16[256,896]{1,0:T(8,128)(2,1)} %collective-permute-done.10.refs_0_, bf16[256,896]{1,0:T(8,128)(2,1)} %collective-permute-done.11.refs_1_, ...), custom_call_target="tpu_custom_call" | custom-call | tf_op jit(solution)/shard_map/hidden_side/pallas_call | solution.py:310
  160.1 0.9 copy-done.10
  161.0 11.2 %all_to_all.25 = f32[8,8,512]{2,1,0:T(8,128)S(1)} all-to-all(f32[8,8,512]{2,1,0:T(8,128)S(1)} %bitcast.38), channel_id=1, replica_groups=mesh['z'=16,'y'=4,'x'=4,'c'=2] {'x','c'}, dimensions={0} | all-to-all | bytes 262144 | tf_op jit(solution)/shard_map/all_to_all | solution.py:334
  172.9 3.4 %all-to-all-start.1 = ((f32[8,8,512]{2,1,0:T(8,128)}), f32[8,8,512]{2,1,0:T(8,128)S(1)}, u32[]{:S(2)}, u32[]{:S(2)}) async-start(f32[8,8,512]{2,1,0:T(8,128)} %broadcast_in_dim.6), calls=%async_computation.1 | async-start | bytes 262144 | tf_op jit(solution)/shard_map/all_to_all | solution.py:336
  176.9 5.4 %all-to-all-done.1 = f32[8,8,512]{2,1,0:T(8,128)S(1)} async-done(((f32[8,8,512]{2,1,0:T(8,128)}), f32[8,8,512]{2,1,0:T(8,128)S(1)}, u32[]{:S(2)}, u32[]{:S(2)}) %all-to-all-start.1) | async-done | bytes 131104 | tf_op jit(solution)/shard_map/all_to_all | solution.py:336
  182.3 1.1 copy-done.11
  183.4 0.9 copy-done.29
  184.4 0.9 copy-done.31
  185.9 13.9 %all_to_all.26 = f32[4,144,128]{2,1,0:T(8,128)S(1)} all-to-all(f32[4,144,128]{2,1,0:T(8,128)S(1)} %bitcast.34), channel_id=1, replica_groups=mesh['z'=16,'y'=4,'x'=4,'c'=2] {'y'}, dimensions={0} | all-to-all | bytes 589824 | tf_op jit(solution)/shard_map/all_to_all | solution.py:360
  199.8 20.7 %all_to_all.27 = f32[16,9,128]{2,1,0:T(8,128)S(1)} all-to-all(f32[16,9,128]{2,1,0:T(8,128)S(1)} %reshape.33), channel_id=1, replica_groups=mesh['z'=16,'y'=4,'x'=4,'c'=2] {'z'}, dimensions={0} | all-to-all | bytes 147456 | tf_op jit(solution)/shard_map/all_to_all | solution.py:361
  220.5 17.0 %all_to_all.28 = f32[16,9,128]{2,1,0:T(8,128)S(1)} all-to-all(f32[16,9,128]{2,1,0:T(8,128)S(1)} %broadcast_in_dim.7), channel_id=1, replica_groups=mesh['z'=16,'y'=4,'x'=4,'c'=2] {'z'}, dimensions={0} | all-to-all | bytes 147456 | tf_op jit(solution)/shard_map/all_to_all | solution.py:362
  237.6 12.3 %all_gather.15 = f32[4,144,128]{2,1,0:T(8,128)S(1)} all-gather(f32[1,144,128]{2,1,0:T(8,128)S(1)} %all_gather_reshape.3), channel_id=1, replica_groups=mesh['z'=16,'y'=4,'x'=4,'c'=2] {'y'}, dimensions={0}, use_global_device_ids=true | all-gather | bytes 368640 | tf_op jit(solution)/shard_map/all_gather | solution.py:365
  (82 shorter events, 9.9 us)
Async XLA Ops:
  7.2 77.0 %all-gather.3.cloned.1.call-start = ((), (), s32[]{:S(2)}) async-start(), calls=%async_computation.5 | async-start | bytes 4718592 | tf_op jit(solution)/shard_map/all_gather | solution.py:222
  7.9 111.4 %all-gather.5.cloned.1.call-start = ((), (), s32[]{:S(2)}) async-start(), calls=%async_computation.6 | async-start | bytes 4718592 | tf_op jit(solution)/shard_map/all_gather | solution.py:224
  22.0 12.8 %collective-permute-start.5 = (bf16[256,896]{1,0:T(8,128)(2,1)S(1)}, bf16[256,896]{1,0:T(8,128)(2,1)S(1)}, u32[]{:S(2)}, u32[]{:S(2)}) collective-permute-start(bf16[256,896]{1,0:T(8,128)(2,1)S(1)} %all_gather.13.refs_0_), channel_id=1, source_target_pairs={{0,480},{32,0},{64,32},{96,64},{128,96},{160,128},{192,160},{224,1... | collective-permute-start | bytes 1376264 | tf_op jit(solution)/shard_map/ppermute | solution.py:241
  28.9 15.4 %collective-permute-start = (bf16[256,896]{1,0:T(8,128)(2,1)S(1)}, bf16[256,896]{1,0:T(8,128)(2,1)S(1)}, u32[]{:S(2)}, u32[]{:S(2)}) collective-permute-start(bf16[256,896]{1,0:T(8,128)(2,1)S(1)} %all_gather.13.refs_0_), channel_id=1, source_target_pairs={{0,32},{32,64},{64,96},{96,128},{128,160},{160,192},{192,224},{224... | collective-permute-start | bytes 1376264 | tf_op jit(solution)/shard_map/ppermute | solution.py:240
  34.9 15.8 %collective-permute-start.6 = (bf16[256,896]{1,0:T(8,128)(2,1)S(1)}, bf16[256,896]{1,0:T(8,128)(2,1)S(1)}, u32[]{:S(2)}, u32[]{:S(2)}) collective-permute-start(bf16[256,896]{1,0:T(8,128)(2,1)S(1)} %collective-permute-done.5.refs_2_), channel_id=1, source_target_pairs={{0,480},{32,0},{64,32},{96,64},{128,96},{160,128},{192,160},{224,1... | collective-permute-start | bytes 1376264 | tf_op jit(solution)/shard_map/ppermute | solution.py:241
  43.5 0.8 copy-start.16
  44.3 13.3 %collective-permute-start.1 = (bf16[256,896]{1,0:T(8,128)(2,1)S(1)}, bf16[256,896]{1,0:T(8,128)(2,1)S(1)}, u32[]{:S(2)}, u32[]{:S(2)}) collective-permute-start(bf16[256,896]{1,0:T(8,128)(2,1)S(1)} %collective-permute-done.refs_1_), channel_id=1, source_target_pairs={{0,32},{32,64},{64,96},{96,128},{128,160},{160,192},{192,224},{224... | collective-permute-start | bytes 1376264 | tf_op jit(solution)/shard_map/ppermute | solution.py:240
  46.2 0.8 copy-start.18
  50.6 12.0 %collective-permute-start.7 = (bf16[256,896]{1,0:T(8,128)(2,1)S(1)}, bf16[256,896]{1,0:T(8,128)(2,1)S(1)}, u32[]{:S(2)}, u32[]{:S(2)}) collective-permute-start(bf16[256,896]{1,0:T(8,128)(2,1)S(1)} %collective-permute-done.6.refs_4_), channel_id=1, source_target_pairs={{0,480},{32,0},{64,32},{96,64},{128,96},{160,128},{192,160},{224,1... | collective-permute-start | bytes 1376264 | tf_op jit(solution)/shard_map/ppermute | solution.py:241
  56.3 0.8 copy-start.20
  57.6 12.0 %collective-permute-start.2 = (bf16[256,896]{1,0:T(8,128)(2,1)S(1)}, bf16[256,896]{1,0:T(8,128)(2,1)S(1)}, u32[]{:S(2)}, u32[]{:S(2)}) collective-permute-start(bf16[256,896]{1,0:T(8,128)(2,1)S(1)} %collective-permute-done.1.refs_3_), channel_id=1, source_target_pairs={{0,32},{32,64},{64,96},{96,128},{128,160},{160,192},{192,224},{224... | collective-permute-start | bytes 1376264 | tf_op jit(solution)/shard_map/ppermute | solution.py:240
  59.5 0.8 copy-start.22
  62.7 11.7 %collective-permute-start.8 = (bf16[256,896]{1,0:T(8,128)(2,1)S(1)}, bf16[256,896]{1,0:T(8,128)(2,1)S(1)}, u32[]{:S(2)}, u32[]{:S(2)}) collective-permute-start(bf16[256,896]{1,0:T(8,128)(2,1)S(1)} %collective-permute-done.7.refs_6_), channel_id=1, source_target_pairs={{0,480},{32,0},{64,32},{96,64},{128,96},{160,128},{192,160},{224,1... | collective-permute-start | bytes 1376264 | tf_op jit(solution)/shard_map/ppermute | solution.py:241
  68.4 0.8 copy-start.24
  69.6 11.6 %collective-permute-start.3 = (bf16[256,896]{1,0:T(8,128)(2,1)S(1)}, bf16[256,896]{1,0:T(8,128)(2,1)S(1)}, u32[]{:S(2)}, u32[]{:S(2)}) collective-permute-start(bf16[256,896]{1,0:T(8,128)(2,1)S(1)} %collective-permute-done.2.refs_5_), channel_id=1, source_target_pairs={{0,32},{32,64},{64,96},{96,128},{128,160},{160,192},{192,224},{224... | collective-permute-start | bytes 1376264 | tf_op jit(solution)/shard_map/ppermute | solution.py:240
  71.6 0.8 copy-start.26
  74.3 38.2 %copy-start.12 = (bf16[256,896]{1,0:T(8,128)(2,1)}, bf16[256,896]{1,0:T(8,128)(2,1)S(1)}, u32[]{:S(2)}) copy-start(bf16[256,896]{1,0:T(8,128)(2,1)S(1)} %collective-permute-done.8.refs_1_) | copy-start | bytes 1376260
  74.4 24.3 %collective-permute-start.9 = (bf16[256,896]{1,0:T(8,128)(2,1)S(1)}, bf16[256,896]{1,0:T(8,128)(2,1)}, u32[]{:S(2)}, u32[]{:S(2)}) collective-permute-start(bf16[256,896]{1,0:T(8,128)(2,1)S(1)} %collective-permute-done.8.refs_1_), channel_id=1, source_target_pairs={{0,480},{32,0},{64,32},{96,64},{128,96},{160,128},{192,160},{224,1... | collective-permute-start | bytes 1376264 | tf_op jit(solution)/shard_map/ppermute | solution.py:241
  81.2 24.4 %copy-start.14 = (bf16[256,896]{1,0:T(8,128)(2,1)}, bf16[256,896]{1,0:T(8,128)(2,1)S(1)}, u32[]{:S(2)}) copy-start(bf16[256,896]{1,0:T(8,128)(2,1)S(1)} %collective-permute-done.3.refs_0_) | copy-start | bytes 1376260
  81.2 17.5 %collective-permute-start.4 = (bf16[256,896]{1,0:T(8,128)(2,1)S(1)}, bf16[256,896]{1,0:T(8,128)(2,1)}, u32[]{:S(2)}, u32[]{:S(2)}) collective-permute-start(bf16[256,896]{1,0:T(8,128)(2,1)S(1)} %collective-permute-done.3.refs_0_), channel_id=1, source_target_pairs={{0,32},{32,64},{64,96},{96,128},{128,160},{160,192},{192,224},{224... | collective-permute-start | bytes 1376264 | tf_op jit(solution)/shard_map/ppermute | solution.py:240
  84.2 2.3 copy-start
  86.5 1.1 copy-start.17
  87.6 1.0 copy-start.19
  88.6 1.0 copy-start.21
  89.6 1.0 copy-start.23
  90.6 1.0 copy-start.25
  91.7 1.0 copy-start.27
  97.9 0.7 copy-start.28
  98.6 11.9 %collective-permute-start.10 = (bf16[256,896]{1,0:T(8,128)(2,1)}, bf16[256,896]{1,0:T(8,128)(2,1)}, u32[]{:S(2)}, u32[]{:S(2)}) collective-permute-start(bf16[256,896]{1,0:T(8,128)(2,1)} %collective-permute-done.4.refs_2_), channel_id=1, source_target_pairs={{0,32},{32,64},{64,96},{96,128},{128,160},{160,192},{192,224},{224... | collective-permute-start | bytes 1376264 | tf_op jit(solution)/shard_map/ppermute | solution.py:240
  100.6 11.9 %collective-permute-start.11 = (bf16[256,896]{1,0:T(8,128)(2,1)}, bf16[256,896]{1,0:T(8,128)(2,1)}, u32[]{:S(2)}, u32[]{:S(2)}) collective-permute-start(bf16[256,896]{1,0:T(8,128)(2,1)} %collective-permute-done.9.refs_3_), channel_id=1, source_target_pairs={{0,480},{32,0},{64,32},{96,64},{128,96},{160,128},{192,160},{224,1... | collective-permute-start | bytes 1376264 | tf_op jit(solution)/shard_map/ppermute | solution.py:241
  110.6 18.7 %collective-permute-start.12 = (bf16[256,896]{1,0:T(8,128)(2,1)}, bf16[256,896]{1,0:T(8,128)(2,1)S(1)}, u32[]{:S(2)}, u32[]{:S(2)}) collective-permute-start(bf16[256,896]{1,0:T(8,128)(2,1)} %collective-permute-done.10.refs_0_), channel_id=1, source_target_pairs={{0,32},{32,64},{64,96},{96,128},{128,160},{160,192},{192,224},{224... | collective-permute-start | bytes 1376264 | tf_op jit(solution)/shard_map/ppermute | solution.py:240
  112.5 16.8 %collective-permute-start.13 = (bf16[256,896]{1,0:T(8,128)(2,1)}, bf16[256,896]{1,0:T(8,128)(2,1)S(1)}, u32[]{:S(2)}, u32[]{:S(2)}) collective-permute-start(bf16[256,896]{1,0:T(8,128)(2,1)} %collective-permute-done.11.refs_1_), channel_id=1, source_target_pairs={{0,480},{32,0},{64,32},{96,64},{128,96},{160,128},{192,160},{224,1... | collective-permute-start | bytes 1376264 | tf_op jit(solution)/shard_map/ppermute | solution.py:241
  119.3 4.8 %copy-start.1 = (bf16[512,4096]{1,0:T(8,128)(2,1)S(1)}, bf16[512,4096]{1,0:T(8,128)(2,1)}, u32[]{:S(2)}) copy-start(bf16[512,4096]{1,0:T(8,128)(2,1)} %all-gather.3.cloned.1.call-done.gradient_ref) | copy-start | bytes 12582916
  119.3 2.3 copy-start.3
  124.1 1.0 copy-start.13
  125.1 1.0 copy-start.15
  126.2 3.1 %copy-start.30 = (f32[4,128,128]{2,1,0:T(8,128)}, f32[4,128,128]{2,1,0:T(8,128)S(1)}, u32[]{:S(2)}) copy-start(f32[4,128,128]{2,1,0:T(8,128)S(1)} %get-tuple-element.28.normed_gram_ref) | copy-start | bytes 786436
  129.3 15.7 %copy-start.6 = (bf16[256,896]{1,0:T(8,128)(2,1)}, bf16[256,896]{1,0:T(8,128)(2,1)S(1)}, u32[]{:S(2)}) copy-start(bf16[256,896]{1,0:T(8,128)(2,1)S(1)} %collective-permute-done.13.refs_3_) | copy-start | bytes 1376260
  130.8 9.3 %collective-permute-start.15 = (bf16[128,896]{1,0:T(8,128)(2,1)}, bf16[128,896]{1,0:T(8,128)(2,1)S(1)}, u32[]{:S(2)}, u32[]{:S(2)}) collective-permute-start(bf16[128,896]{1,0:T(8,128)(2,1)} %slice.21), channel_id=1, source_target_pairs={{0,480},{32,0},{64,32},{96,64},{128,96},{160,128},{192,160},{224,1... | collective-permute-start | bytes 688136 | tf_op jit(solution)/shard_map/ppermute | solution.py:241
  136.2 8.1 %collective-permute-start.14 = (bf16[128,896]{1,0:T(8,128)(2,1)}, bf16[128,896]{1,0:T(8,128)(2,1)S(1)}, u32[]{:S(2)}, u32[]{:S(2)}) collective-permute-start(bf16[128,896]{1,0:T(8,128)(2,1)} %slice.20), channel_id=1, source_target_pairs={{0,32},{32,64},{64,96},{96,128},{128,160},{160,192},{192,224},{224... | collective-permute-start | bytes 688136 | tf_op jit(solution)/shard_map/ppermute | solution.py:240
  140.1 0.7 copy-start.32
  144.4 0.7 copy-start.34
  145.1 2.2 copy-start.2
  147.2 1.0 copy-start.7
  148.3 1.2 copy-start.8
  149.4 1.2 copy-start.9
  150.6 0.9 copy-start.33
  151.6 0.9 copy-start.35
  152.5 0.9 copy-start.36
  153.4 28.9 %copy-start.4 = (bf16[512,512]{1,0:T(8,128)(2,1)S(1)}, bf16[512,512]{1,0:T(8,128)(2,1)}, u32[]{:S(2)}) copy-start(bf16[512,512]{1,0:T(8,128)(2,1)} %gradient_ref.1) | copy-start | bytes 1572868
  153.4 28.9 %copy-start.5 = (bf16[512,512]{1,0:T(8,128)(2,1)S(1)}, bf16[512,512]{1,0:T(8,128)(2,1)}, u32[]{:S(2)}) copy-start(bf16[512,512]{1,0:T(8,128)(2,1)} %normed_ref.1) | copy-start | bytes 1572868
  160.1 0.9 copy-start.10
  161.0 88.9 %copy-start.38 = (f32[3,16,512]{2,1,0:T(8,128)S(1)}, f32[3,16,512]{2,1,0:T(8,128)}, u32[]{:S(2)}) copy-start(f32[3,16,512]{2,1,0:T(8,128)} %param.18) | copy-start | bytes 294916
  161.0 89.5 %copy-start.37 = (f32[3,16,896]{2,1,0:T(8,128)S(1)}, f32[3,16,896]{2,1,0:T(8,128)}, u32[]{:S(2)}) copy-start(f32[3,16,896]{2,1,0:T(8,128)} %param.19) | copy-start | bytes 516100
  172.9 9.4 %all-to-all-start.1 = ((f32[8,8,512]{2,1,0:T(8,128)}), f32[8,8,512]{2,1,0:T(8,128)S(1)}, u32[]{:S(2)}, u32[]{:S(2)}) async-start(f32[8,8,512]{2,1,0:T(8,128)} %broadcast_in_dim.6), calls=%async_computation.1 | async-start | bytes 262144 | tf_op jit(solution)/shard_map/all_to_all | solution.py:336
  182.3 1.1 copy-start.11
  183.4 0.9 copy-start.29
  184.4 0.9 copy-start.31
Sparse Core Ops, SparseCore 0:
  10.1 43.8 all-gather.2
  56.2 39.7 all-gather.4

commit v3 on v2

--- a/solution.py
+++ b/solution.py
@@ -33,73 +33,55 @@
         tile(whole * step, hidden - whole * step)
 
 
-def block_product(place_ref, gradient_ref, block_refs, cols):
-    left = jnp.concatenate(
-        [
-            gradient_ref[:, pl.ds(pl.multiple_of(place_ref[i] * 128, 128), block.shape[0])]
-            for i, block in enumerate(block_refs)
-        ],
-        axis=1,
-    )
-    right = jnp.concatenate([block[:, cols] for block in block_refs], axis=0)
-    return jnp.dot(left, right, preferred_element_type=F32)
-
-
 def gram_of(rows_ref, out_ref):
     for e in range(out_ref.shape[0]):
         rows = rows_ref[e * SEQUENCE_TOKENS : (e + 1) * SEQUENCE_TOKENS, :]
         out_ref[e] = contract(rows, rows, 1, 1)
 
 
-def first_kernel(n_blocks, place_ref, gradient_ref, *refs):
+def gather_kernel(rows_ref, factors_ref, projected_ref, gram_ref):
+    projected_ref[...] = contract(factors_ref[...], rows_ref[...], 1, 1).astype(BF16)
+    gram_of(rows_ref, gram_ref)
+
+
+def hidden_kernel(plan, n_blocks, spot_ref, gradient_ref, *refs):
     block_refs = refs[:n_blocks]
-    factor_ref, total_ref, lora_ref, gram_ref = refs[n_blocks:]
-
-    def tile(start, width):
-        cols = pl.ds(start, width)
-        total_ref[:, cols] = block_product(place_ref, gradient_ref, block_refs, cols)
-
-    column_tiles(total_ref.shape[1], 256, tile)
-    lora_ref[...] = contract(factor_ref[...], gradient_ref[...], 1, 1).astype(BF16)
-    gram_of(gradient_ref, gram_ref)
-
-
-def more_kernel(n_blocks, place_ref, gradient_ref, *refs):
-    block_refs = refs[:n_blocks]
-    before_ref, total_ref = refs[n_blocks:]
-
-    def tile(start, width):
-        cols = pl.ds(start, width)
-        total_ref[:, cols] = before_ref[:, cols] + block_product(
-            place_ref, gradient_ref, block_refs, cols
-        )
-
-    column_tiles(total_ref.shape[1], 256, tile)
-
-
-def normed_kernel(normed_ref, factors_ref, in_ref, gram_ref):
-    in_ref[...] = contract(factors_ref[...], normed_ref[...], 1, 1).astype(BF16)
-    gram_of(normed_ref, gram_ref)
-
-
-def hidden_kernel(n_blocks, place_ref, gradient_ref, *refs):
-    block_refs = refs[:n_blocks]
-    (before_ref, gate_ref, up_ref, factors_ref, in_ref, lora_ref, lora_t_ref) = refs[
-        n_blocks : n_blocks + 7
+    (gate_ref, up_ref, factors_ref, in_ref, lora_ref, lora_t_ref) = refs[
+        n_blocks : n_blocks + 6
     ]
-    sums_ref, mids_ref, total = refs[n_blocks + 7 :]
+    sums_ref, mids_ref, weight, gradient, total, sems = refs[n_blocks + 6 :]
     tokens, hidden = gate_ref.shape
     sequences = tokens // SEQUENCE_TOKENS
+    z, y, core = spot_ref[0], spot_ref[1], spot_ref[2]
+    n_z, n_y, piece = plan["n_z"], plan["n_y"], plan["piece"]
     mids_ref[...] = jnp.zeros_like(mids_ref)
+
+    def fetch(pieces):
+        copies = [pltpu.make_async_copy(gradient_ref, gradient, sems.at[0])]
+        for i, (block, row, off_z, off_y) in enumerate(pieces):
+            to = lax.rem(z + (off_z + n_z), n_z) * n_y + lax.rem(y + (off_y + n_y), n_y)
+            to = pl.multiple_of(to * piece, piece)
+            copies.append(
+                pltpu.make_async_copy(
+                    block_refs[block].at[pl.ds(row, piece), :],
+                    weight.at[pl.ds(to, piece), :],
+                    sems.at[i + 1],
+                )
+            )
+        for copy in copies:
+            copy.start()
+        for copy in copies:
+            copy.wait()
+
+    for c in range(2):
+        pl.when(core == c)(functools.partial(fetch, plan["pieces"][c]))
 
     def tile(start, width):
         cols = pl.ds(start, width)
         factors = factors_ref[:, cols]
-        total[:, :width] = (
-            before_ref[:, cols]
-            + block_product(place_ref, gradient_ref, block_refs, cols)
-            + SCALE * jnp.dot(lora_ref[...], factors[2 * RANK :], preferred_element_type=F32)
-        )
+        total[:, :width] = jnp.dot(
+            gradient[...], weight[:, cols], preferred_element_type=F32
+        ) + SCALE * jnp.dot(lora_ref[...], factors[2 * RANK :], preferred_element_type=F32)
         for e in range(sequences):
             rows = slice(e * SEQUENCE_TOKENS, (e + 1) * SEQUENCE_TOKENS)
             hidden_grad = total[rows, :width]
@@ -194,8 +176,78 @@
         out_ref[t] = value
 
 
-def ring(size, by):
-    return [(i, (i + by) % size) for i in range(size)]
+def core_ring(size, by, core):
+    return [(2 * i + core, 2 * ((i + by) % size) + core) for i in range(size)]
+
+
+def gather_weight(shard, n_z, n_y):
+    piece = shard.shape[0]
+
+    def along_z(block, by, core):
+        return lax.ppermute(block, ("z", "c"), core_ring(n_z, by, core))
+
+    def along_y(block, by, core):
+        return lax.ppermute(block, ("y", "c"), core_ring(n_y, by, core))
+
+    last = n_z // 2
+    blocks, pieces = [], ([], [])
+
+    def keep(block, core, places):
+        for row, (off_z, off_y) in enumerate(places):
+            pieces[core].append((len(blocks), row * piece, off_z, off_y))
+        blocks.append(block)
+
+    around = [0, -1, 1, 2]
+    column = jnp.concatenate(
+        [shard, along_y(shard, 1, 0), along_y(shard, -1, 0), along_y(shard, 2, 0)], axis=0
+    )
+    keep(column, 0, [(0, off) for off in around])
+    low0 = high0 = column
+    low1 = high1 = shard
+    singles, places = [shard], [0]
+    half = 2 * piece
+
+    def exchange(group, offs):
+        batch = jnp.concatenate(group, axis=0)
+        before, after = along_y(batch, 1, 1), along_y(batch, -1, 1)
+        return batch, before, after, offs
+
+    def forward(batch, before, after, offs):
+        middle = len(offs) // 2
+        opposite = (
+            along_y(before[: middle * piece], 1, 1),
+            along_y(after[middle * piece :], -1, 1),
+        )
+        keep(batch, 1, [(off, 0) for off in offs])
+        keep(before, 1, [(off, -1) for off in offs])
+        keep(after, 1, [(off, 1) for off in offs])
+        keep(opposite[0], 1, [(off, 2) for off in offs[:middle]])
+        keep(opposite[1], 1, [(off, 2) for off in offs[middle:]])
+
+    open_batches = []
+    for k in range(1, last + 1):
+        if k == last - 1:
+            batch, before, after, offs = open_batches.pop()
+            before, after, low1, high1 = lax.optimization_barrier((before, after, low1, high1))
+            forward(batch, before, after, offs)
+        low1 = along_z(low1, 1, 1)
+        singles, places = singles + [low1], places + [-k]
+        if k < last:
+            high1 = along_z(high1, -1, 1)
+            singles, places = singles + [high1], places + [k]
+        if len(singles) >= last:
+            open_batches.append(exchange(singles[:last], places[:last]))
+            singles, places = singles[last:], places[last:]
+        if k < last:
+            low0, high0 = along_z(low0, 1, 0), along_z(high0, -1, 0)
+            keep(low0, 0, [(-k, off) for off in around])
+            keep(high0, 0, [(k, off) for off in around])
+        else:
+            keep(along_z(low0[:half], 1, 0), 0, [(last, off) for off in around[:2]])
+            keep(along_z(high0[half:], -1, 0), 0, [(last, off) for off in around[2:]])
+    assert not singles
+    forward(*open_batches.pop())
+    return blocks, pieces
 
 
 def per_device(
@@ -220,109 +272,62 @@
     z = lax.axis_index(z_axes)
 
     gradient = lax.all_gather(output_gradient, tensor_axes, axis=1, tiled=True)
-    block = lax.all_gather(frozen_down_weight.T, "y", axis=0, tiled=True)
     normed_all = lax.all_gather(normed, tensor_axes, axis=1, tiled=True)
-
-    rows = block.shape[0]
-    half = rows // 2
-    units = rows // 128
+    shard = frozen_down_weight.T
+    blocks, pieces = gather_weight(shard, n_z, sizes["y"])
+
     vmem = pl.BlockSpec(memory_space=pltpu.VMEM)
     smem = pl.BlockSpec(memory_space=pltpu.SMEM)
+    hbm = pl.BlockSpec(memory_space=pltpu.HBM)
     params = pltpu.CompilerParams(vmem_limit_bytes=32 * 2**20)
 
-    def place(offsets):
-        at = [((z + offset) % n_z) * units for offset in offsets]
-        return jnp.stack(at).astype(jnp.int32)
-
-    low, high = {0: block}, {0: block}
-
-    def step(k, low_from, high_from):
-        low[k] = lax.ppermute(low_from, z_axes, ring(n_z, 1))
-        high[k] = lax.ppermute(high_from, z_axes, ring(n_z, -1))
-
-    def product_cost(n_rows, read):
-        return pl.CostEstimate(
-            flops=2 * tokens * n_rows * hidden, bytes_accessed=read, transcendentals=0
-        )
-
-    last = n_z // 2
-    for k in range(1, last - 2):
-        step(k, low[k - 1], high[k - 1])
-    offsets = [0] + [sign * k for k in range(1, last - 4) for sign in (-1, 1)]
-    blocks = [block] + [side[k] for k in range(1, last - 4) for side in (low, high)]
-    total, lora_t, gradient_gram = pl.pallas_call(
-        functools.partial(first_kernel, len(blocks)),
-        out_shape=(
-            jax.ShapeDtypeStruct((tokens, hidden), F32),
-            jax.ShapeDtypeStruct((RANK, tokens), BF16),
-            jax.ShapeDtypeStruct((sequences, SEQUENCE_TOKENS, SEQUENCE_TOKENS), F32),
-        ),
-        in_specs=[smem] + [vmem] * (len(blocks) + 2),
-        out_specs=(vmem, vmem, vmem),
-        compiler_params=params,
-        cost_estimate=product_cost(rows * len(blocks), 8 * 2**20),
-        name="first_blocks",
-    )(place(offsets), gradient, *blocks, adapter_width_factors[2])
-
-    at = last - 3
-    low_in, high_in, total = lax.optimization_barrier((low[at], high[at], total))
-    step(last - 2, low_in, high_in)
-    offsets = [sign * k for k in range(last - 4, last - 2) for sign in (-1, 1)]
-    blocks = [side[k] for k in range(last - 4, last - 2) for side in (low, high)]
-    total = pl.pallas_call(
-        functools.partial(more_kernel, len(blocks)),
-        out_shape=jax.ShapeDtypeStruct((tokens, hidden), F32),
-        in_specs=[smem] + [vmem] * (len(blocks) + 2),
-        out_specs=vmem,
-        input_output_aliases={len(blocks) + 2: 0},
-        compiler_params=params,
-        cost_estimate=product_cost(rows * len(blocks), 6 * 2**20),
-        name="more_blocks",
-    )(place(offsets), gradient, *blocks, total)
-    step(last - 1, low[last - 2], high[last - 2])
-
-    in_t, normed_gram = pl.pallas_call(
-        normed_kernel,
-        out_shape=(
-            jax.ShapeDtypeStruct((2 * RANK, tokens), BF16),
-            jax.ShapeDtypeStruct((sequences, SEQUENCE_TOKENS, SEQUENCE_TOKENS), F32),
-        ),
-        in_specs=[vmem, vmem],
-        out_specs=(vmem, vmem),
-        compiler_params=params,
-        cost_estimate=pl.CostEstimate(
-            flops=2 * tokens * 4096 * 160, bytes_accessed=5 * 2**20, transcendentals=0
-        ),
-        name="normed_side",
-    )(normed_all, adapter_width_factors[:2].reshape(2 * RANK, -1))
-
-    low_in, high_in, total, in_t = lax.optimization_barrier(
-        (low[last - 1], high[last - 1], total, in_t)
-    )
-    step(last, low_in[:half], high_in[half:])
-    far = ((z + last) % n_z) * units
-    offsets = [sign * k for k in range(last - 2, last) for sign in (-1, 1)]
-    blocks = [side[k] for k in range(last - 2, last) for side in (low, high)]
-    blocks += [low[last], high[last]]
-    places = jnp.concatenate(
-        [place(offsets), jnp.stack([far, far + units // 2]).astype(jnp.int32)]
-    )
+    def project(rows, factors, name):
+        return pl.pallas_call(
+            gather_kernel,
+            out_shape=(
+                jax.ShapeDtypeStruct((factors.shape[0], tokens), BF16),
+                jax.ShapeDtypeStruct((sequences, SEQUENCE_TOKENS, SEQUENCE_TOKENS), F32),
+            ),
+            in_specs=[vmem, vmem],
+            out_specs=(vmem, vmem),
+            compiler_params=params,
+            cost_estimate=pl.CostEstimate(
+                flops=2 * tokens * rows.shape[1] * (128 + factors.shape[0]),
+                bytes_accessed=5 * 2**20,
+                transcendentals=0,
+            ),
+            name=name,
+        )(rows, factors)
+
+    late = [i for i, _, off_z, _ in pieces[0] if off_z == n_z // 2 - 2][0]
+    gradient, blocks[late] = lax.optimization_barrier((gradient, blocks[late]))
+    lora_t, gradient_gram = project(gradient, adapter_width_factors[2], "gradient_side")
+    in_t, normed_gram = project(
+        normed_all, adapter_width_factors[:2].reshape(2 * RANK, -1), "normed_side"
+    )
+
+    n_copies = 1 + max(len(p) for p in pieces)
+    plan = dict(n_z=n_z, n_y=sizes["y"], piece=shard.shape[0], pieces=pieces)
     sums, mids = pl.pallas_call(
-        functools.partial(hidden_kernel, len(blocks)),
+        functools.partial(hidden_kernel, plan, len(blocks)),
         out_shape=(
             jax.ShapeDtypeStruct((sequences, 3 * RANK, hidden), F32),
             jax.ShapeDtypeStruct((8 * n_tensor, tokens), F32),
         ),
-        in_specs=[smem] + [vmem] * (len(blocks) + 8),
+        in_specs=[smem, hbm] + [hbm] * len(blocks) + [vmem] * 6,
         out_specs=(vmem, vmem),
-        scratch_shapes=[pltpu.VMEM((tokens, 256), F32)],
+        scratch_shapes=[
+            pltpu.VMEM((gradient.shape[1], hidden), BF16),
+            pltpu.VMEM(gradient.shape, BF16),
+            pltpu.VMEM((tokens, 256), F32),
+            pltpu.SemaphoreType.DMA((n_copies,)),
+        ],
         compiler_params=params,
         name="hidden_side",
     )(
-        places,
+        jnp.stack([z, lax.axis_index("y"), lax.axis_index("c")]).astype(jnp.int32),
         gradient,
         *blocks,
-        total,
         gate_preactivation,
         upward_preactivation,
         adapter_hidden_factors.reshape(3 * RANK, hidden),
@@ -331,10 +336,10 @@
         lora_t,
     )
 
-    pieces = lax.all_to_all(mids.reshape(n_tensor, 8, tokens), tensor_axes, 0, 0)
-    piece = jnp.sum(pieces, axis=0)
+    shares = lax.all_to_all(mids.reshape(n_tensor, 8, tokens), tensor_axes, 0, 0)
+    share = jnp.sum(shares, axis=0)
     mids = lax.all_to_all(
-        jnp.broadcast_to(piece, (n_tensor,) + piece.shape), tensor_axes, 0, 0
+        jnp.broadcast_to(share, (n_tensor,) + share.shape), tensor_axes, 0, 0
     ).reshape(8 * n_tensor, tokens)
 
     lanes = 12

time: 260 us -> 295 us (1.13)
  starting transfers between devices: 67.3 us -> 90.8 us
  Pallas kernels: 18.2 us -> 26.4 us
  local copies, waits for them, and re-layouts: 36.2 us -> 42.7 us
  blocking collectives: 88.4 us -> 83.3 us
    ppermute x16 -> x42, starting transfers between devices: 63.8 us -> 87.4 us  [the longest x31 67.7 us: along_z(): return lax.ppermute(block, ('z', 'c'), core_ring(n_z, by, core))]
    all_gather x1 -> x0, blocking collectives: 13.4 us -> none  [per_device(): block = lax.all_gather(frozen_down_weight.T, 'y', axis=0, tiled=True)]
    all_to_all x1, blocking collectives: 11.2 us -> 21.9 us  [per_device(): lax.all_to_all(mids.reshape(n_tensor, 8, tokens), tensor_axes, 0, 0)]
    pallas_call x4 -> x3, Pallas kernels: 17.6 us -> 25.8 us  [the longest x1 21 us: per_device(): pl.pallas_call(functools.partial(hidden_kernel, plan, len(blocks)), out_s...]
    unnamed x78 -> x112, local copies, waits for them, and re-layouts: 31.8 us -> 36.1 us
    slice x2 -> x6, local copies, waits for them, and re-layouts: 1.49 us -> 5.63 us  [the longest x2 1.67 us: forward(): after[middle * piece:]]
    all_to_all x1, blocking collectives: 13.9 us -> 10.9 us  [per_device(): part = jnp.sum(lax.all_to_all(out.reshape(n_y, -1, 128), 'y', 0, 0), axis=0)]
    ppermute x16 -> x42, waiting for transfers between devices: 24.4 us -> 25.2 us  [the longest x31 21.3 us: along_z(): return lax.ppermute(block, ('z', 'c'), core_ring(n_z, by, core))]
  transfers between devices with their start and end apart: 19 -> 45, of which waited for: 11 -> 11; matrix products, arithmetic and copies ran while one was open for 1% -> 3% of each run, Pallas kernels for 4% -> 2%
where the time goes in v3:
time: 295 us; the launch traced here: 293 us
  starting transfers between devices  90.8 us (31%)
  blocking collectives  83.3 us (28%)
  local copies, waits for them, and re-layouts  42.7 us (14%)
  waiting for transfers between devices  32 us (11%)
  Pallas kernels  26.4 us (9%)
  between operations  15.6 us (5%)
    ppermute x31, starting transfers between devices, along_z(): return lax.ppermute(block, ('z', 'c'), core_ring(n_z, by, core))  67.7 us
    unnamed x112, local copies, waits for them, and re-layouts  36.1 us
    all_to_all x1, blocking collectives, per_device(): lax.all_to_all(mids.reshape(n_tensor, 8, tokens), tensor_axes, 0, 0)  21.9 us
    ppermute x31, waiting for transfers between devices, along_z(): return lax.ppermute(block, ('z', 'c'), core_ring(n_z, by, core))  21.3 us
    all_to_all x1, blocking collectives, per_device(): lax.all_to_all(part.reshape(n_z, -1, 128), z_axes, 0, 0)  21.2 us
    pallas_call x1, Pallas kernels, per_device(): pl.pallas_call(functools.partial(hidden_kernel, plan, len(blocks)), out_s...  21 us
    ppermute x11, starting transfers between devices, along_y(): return lax.ppermute(block, ('y', 'c'), core_ring(n_y, by, core))  19.7 us
    all_to_all x1, blocking collectives, per_device(): lax.all_to_all(jnp.broadcast_to(part, (n_z,) + part.shape), z_axes, 0, 0)  17 us
  transfers between devices with their start and end apart: 45, of which 11 were waited for; matrix products, arithmetic and copies ran while one was open for 3% of the time, Pallas kernels for 2%

profile of v3, /device:TPU:32, one launch (start us, length us, event | category | flops | bytes accessed | tf_op | source)
XLA Modules:
  0.0 293.3 jit_solution(5850675642280654545)
XLA Ops:
  8.7 5.2 %collective-permute-start.2 = (bf16[64,896]{1,0:T(8,128)(2,1)}, bf16[64,896]{1,0:T(8,128)(2,1)S(1)}, u32[]{:S(2)}, u32[]{:S(2)}) collective-permute-start(bf16[64,896]{1,0:T(8,128)(2,1)} %bitcast.29), channel_id=1, source_target_pairs={{0,16},{8,24},{16,0},{24,8},{2,18},{10,26},{18,2},{26,10},{4,20},{... | collective-permute-start | bytes 344072 | tf_op jit(solution)/shard_map/ppermute | solution.py:190
  13.9 3.0 %collective-permute-start.1 = (bf16[64,896]{1,0:T(8,128)(2,1)}, bf16[64,896]{1,0:T(8,128)(2,1)S(1)}, u32[]{:S(2)}, u32[]{:S(2)}) collective-permute-start(bf16[64,896]{1,0:T(8,128)(2,1)} %bitcast.30), channel_id=1, source_target_pairs={{0,24},{8,0},{16,8},{24,16},{2,26},{10,2},{18,10},{26,18},{4,28},{... | collective-permute-start | bytes 344072 | tf_op jit(solution)/shard_map/ppermute | solution.py:190
  16.9 2.9 collective-permute-start
  21.1 3.8 %collective-permute-done = bf16[64,896]{1,0:T(8,128)(2,1)S(1)} collective-permute-done((bf16[64,896]{1,0:T(8,128)(2,1)}, bf16[64,896]{1,0:T(8,128)(2,1)S(1)}, u32[]{:S(2)}, u32[]{:S(2)}) %collective-permute-start) | collective-permute-done | bytes 114720 | tf_op jit(solution)/shard_map/ppermute | solution.py:190
  25.9 3.8 %collective-permute-start.9 = (bf16[256,896]{1,0:T(8,128)(2,1)S(1)}, bf16[256,896]{1,0:T(8,128)(2,1)S(1)}, u32[]{:S(2)}, u32[]{:S(2)}) collective-permute-start(bf16[256,896]{1,0:T(8,128)(2,1)S(1)} %pad_maximum_fusion.refs_0_), channel_id=1, source_target_pairs={{0,32},{32,64},{64,96},{96,128},{128,160},{160,192},{192,224},{224... | collective-permute-start | bytes 1376264 | tf_op jit(solution)/shard_map/ppermute | solution.py:187
  30.7 2.1 collective-permute-start.3
  35.6 2.0 collective-permute-done.9.refs_1_
  37.6 3.7 %collective-permute-start.10 = (bf16[256,896]{1,0:T(8,128)(2,1)S(1)}, bf16[256,896]{1,0:T(8,128)(2,1)S(1)}, u32[]{:S(2)}, u32[]{:S(2)}) collective-permute-start(bf16[256,896]{1,0:T(8,128)(2,1)S(1)} %collective-permute-done.9.refs_1_), channel_id=1, source_target_pairs={{0,32},{32,64},{64,96},{96,128},{128,160},{160,192},{192,224},{224... | collective-permute-start | bytes 1376264 | tf_op jit(solution)/shard_map/ppermute | solution.py:187
  42.2 6.4 %collective-permute-start.4 = (bf16[256,896]{1,0:T(8,128)(2,1)S(1)}, bf16[256,896]{1,0:T(8,128)(2,1)S(1)}, u32[]{:S(2)}, u32[]{:S(2)}) collective-permute-start(bf16[256,896]{1,0:T(8,128)(2,1)S(1)} %collective-permute-done.3.refs_2_), channel_id=1, source_target_pairs={{0,480},{32,0},{64,32},{96,64},{128,96},{160,128},{192,160},{224,1... | collective-permute-start | bytes 1376264 | tf_op jit(solution)/shard_map/ppermute | solution.py:187
  48.5 4.9 %collective-permute-done.10.refs_3_ = bf16[256,896]{1,0:T(8,128)(2,1)S(1)} collective-permute-done((bf16[256,896]{1,0:T(8,128)(2,1)S(1)}, bf16[256,896]{1,0:T(8,128)(2,1)S(1)}, u32[]{:S(2)}, u32[]{:S(2)}) %collective-permute-start.10) | collective-permute-done | bytes 458784 | tf_op jit(solution)/shard_map/ppermute | solution.py:187
  53.5 1.9 collective-permute-start.11
  58.3 5.2 %collective-permute-start.5 = (bf16[256,896]{1,0:T(8,128)(2,1)S(1)}, bf16[256,896]{1,0:T(8,128)(2,1)S(1)}, u32[]{:S(2)}, u32[]{:S(2)}) collective-permute-start(bf16[256,896]{1,0:T(8,128)(2,1)S(1)} %collective-permute-done.4.refs_4_), channel_id=1, source_target_pairs={{0,480},{32,0},{64,32},{96,64},{128,96},{160,128},{192,160},{224,1... | collective-permute-start | bytes 1376264 | tf_op jit(solution)/shard_map/ppermute | solution.py:187
  65.1 1.9 collective-permute-start.12
  70.6 5.1 %collective-permute-start.6 = (bf16[256,896]{1,0:T(8,128)(2,1)S(1)}, bf16[256,896]{1,0:T(8,128)(2,1)S(1)}, u32[]{:S(2)}, u32[]{:S(2)}) collective-permute-start(bf16[256,896]{1,0:T(8,128)(2,1)S(1)} %collective-permute-done.5.refs_6_), channel_id=1, source_target_pairs={{0,480},{32,0},{64,32},{96,64},{128,96},{160,128},{192,160},{224,1... | collective-permute-start | bytes 1376264 | tf_op jit(solution)/shard_map/ppermute | solution.py:187
  76.6 1.9 collective-permute-start.13
  81.7 5.1 %collective-permute-start.7 = (bf16[256,896]{1,0:T(8,128)(2,1)S(1)}, bf16[256,896]{1,0:T(8,128)(2,1)S(1)}, u32[]{:S(2)}, u32[]{:S(2)}) collective-permute-start(bf16[256,896]{1,0:T(8,128)(2,1)S(1)} %collective-permute-done.6.refs_8_), channel_id=1, source_target_pairs={{0,480},{32,0},{64,32},{96,64},{128,96},{160,128},{192,160},{224,1... | collective-permute-start | bytes 1376264 | tf_op jit(solution)/shard_map/ppermute | solution.py:187
  86.9 1.5 collective-permute-done.13.refs_9_
  88.4 1.9 collective-permute-start.14
  90.3 3.7 %collective-permute-done.7.refs_10_ = bf16[256,896]{1,0:T(8,128)(2,1)S(1)} collective-permute-done((bf16[256,896]{1,0:T(8,128)(2,1)S(1)}, bf16[256,896]{1,0:T(8,128)(2,1)S(1)}, u32[]{:S(2)}, u32[]{:S(2)}) %collective-permute-start.7) | collective-permute-done | bytes 458784 | tf_op jit(solution)/shard_map/ppermute | solution.py:187
  94.1 4.6 %collective-permute-start.8 = (bf16[256,896]{1,0:T(8,128)(2,1)S(1)}, bf16[256,896]{1,0:T(8,128)(2,1)}, u32[]{:S(2)}, u32[]{:S(2)}) collective-permute-start(bf16[256,896]{1,0:T(8,128)(2,1)S(1)} %collective-permute-done.7.refs_10_), channel_id=1, source_target_pairs={{0,480},{32,0},{64,32},{96,64},{128,96},{160,128},{192,160},{224,1... | collective-permute-start | bytes 1376264 | tf_op jit(solution)/shard_map/ppermute | solution.py:187
  99.4 1.6 collective-permute-done.14.refs_11_
  101.0 1.9 collective-permute-start.31
  105.3 1.4 collective-permute-start.30
  106.8 1.4 collective-permute-start.29
  109.1 1.0 copy-done.5
  110.0 1.4 collective-permute-start.41
  112.3 1.0 copy-done.7
  113.2 1.4 collective-permute-start.40
  114.7 5.1 %collective-permute-start.32 = (bf16[256,896]{1,0:T(8,128)(2,1)}, bf16[256,896]{1,0:T(8,128)(2,1)}, u32[]{:S(2)}, u32[]{:S(2)}) collective-permute-start(bf16[256,896]{1,0:T(8,128)(2,1)} %collective-permute-done.8.refs_12_), channel_id=1, source_target_pairs={{0,480},{32,0},{64,32},{96,64},{128,96},{160,128},{192,160},{224,1... | collective-permute-start | bytes 1376264 | tf_op jit(solution)/shard_map/ppermute | solution.py:187
  120.6 5.5 %collective-permute-done.32.refs_19_ = bf16[256,896]{1,0:T(8,128)(2,1)} collective-permute-done((bf16[256,896]{1,0:T(8,128)(2,1)}, bf16[256,896]{1,0:T(8,128)(2,1)}, u32[]{:S(2)}, u32[]{:S(2)}) %collective-permute-start.32) | collective-permute-done | bytes 458784 | tf_op jit(solution)/shard_map/ppermute | solution.py:187
  126.1 1.9 collective-permute-start.33
  128.0 1.6 slice.41
  129.7 5.1 %collective-permute-start.34 = (bf16[128,896]{1,0:T(8,128)(2,1)}, bf16[128,896]{1,0:T(8,128)(2,1)}, u32[]{:S(2)}, u32[]{:S(2)}) collective-permute-start(bf16[128,896]{1,0:T(8,128)(2,1)} %slice.41), channel_id=1, source_target_pairs={{0,480},{32,0},{64,32},{96,64},{128,96},{160,128},{192,160},{224,1... | collective-permute-start | bytes 688136 | tf_op jit(solution)/shard_map/ppermute | solution.py:187
  134.9 2.2 copy-done
  137.1 2.3 gradient_side.1
  140.3 2.3 copy-done.2
  142.6 2.5 normed_side.1
  145.8 1.2 copy-done.6
  147.0 1.2 copy-done.8
  148.2 1.2 copy-done.10
  149.4 1.2 copy-done.12
  150.6 1.0 copy-done.14
  151.6 1.2 copy-done.15
  152.8 1.2 copy-done.16
  153.9 1.0 copy-done.20
  155.0 1.0 copy-done.22
  156.0 1.0 copy-done.24
  157.0 1.0 copy-done.26
  158.0 1.0 copy-done.28
  159.0 1.0 copy-done.30
  160.1 1.0 copy-done.32
  161.1 1.0 copy-done.34
  162.1 1.0 copy-done.36
  163.1 1.0 copy-done.38
  164.1 1.0 copy-done.40
  166.0 21.0 %hidden_side.1 = (f32[4,48,896]{2,1,0:T(8,128)S(1)}, f32[64,512]{1,0:T(8,128)S(1)}) custom-call(s32[3]{0:T(128)S(1)} %pad_add_fusion.spot_ref, bf16[512,4096]{1,0:T(8,128)(2,1)S(1)} %copy-done.1, bf16[256,896]{1,0:T(8,128)(2,1)S(1)} %pad_maximum_fusion.refs_0_, bf16[256,896]{1,0:T(8,128)(2,1)S(1)} %copy-done.20, bf16[256,896]{1,0:T(8,128)(2,1)S(1)} %copy-done.22, ...), custom_call_target="tpu_custom_call" | custom-call | tf_op jit(solution)/shard_map/hidden_side/pallas_call | solution.py:311
  187.9 21.9 %all_to_all.25 = f32[8,8,512]{2,1,0:T(8,128)S(1)} all-to-all(f32[8,8,512]{2,1,0:T(8,128)S(1)} %bitcast.25), channel_id=1, replica_groups=mesh['z'=16,'y'=4,'x'=4,'c'=2] {'x','c'}, dimensions={0} | all-to-all | bytes 262144 | tf_op jit(solution)/shard_map/all_to_all | solution.py:339
  210.5 3.4 %all-to-all-start.1 = ((f32[8,8,512]{2,1,0:T(8,128)}), f32[8,8,512]{2,1,0:T(8,128)S(1)}, u32[]{:S(2)}, u32[]{:S(2)}) async-start(f32[8,8,512]{2,1,0:T(8,128)} %broadcast_in_dim.6), calls=%async_computation.1 | async-start | bytes 262144 | tf_op jit(solution)/shard_map/all_to_all | solution.py:341
  214.5 5.4 %all-to-all-done.1 = f32[8,8,512]{2,1,0:T(8,128)S(1)} async-done(((f32[8,8,512]{2,1,0:T(8,128)}), f32[8,8,512]{2,1,0:T(8,128)S(1)}, u32[]{:S(2)}, u32[]{:S(2)}) %all-to-all-start.1) | async-done | bytes 131104 | tf_op jit(solution)/shard_map/all_to_all | solution.py:341
  219.9 1.1 copy-done.18
  223.5 10.9 %all_to_all.26 = f32[4,144,128]{2,1,0:T(8,128)S(1)} all-to-all(f32[4,144,128]{2,1,0:T(8,128)S(1)} %bitcast.21), channel_id=1, replica_groups=mesh['z'=16,'y'=4,'x'=4,'c'=2] {'y'}, dimensions={0} | all-to-all | bytes 589824 | tf_op jit(solution)/shard_map/all_to_all | solution.py:365
  234.4 21.2 %all_to_all.27 = f32[16,9,128]{2,1,0:T(8,128)S(1)} all-to-all(f32[16,9,128]{2,1,0:T(8,128)S(1)} %reshape.33), channel_id=1, replica_groups=mesh['z'=16,'y'=4,'x'=4,'c'=2] {'z'}, dimensions={0} | all-to-all | bytes 147456 | tf_op jit(solution)/shard_map/all_to_all | solution.py:366
  255.7 17.0 %all_to_all.28 = f32[16,9,128]{2,1,0:T(8,128)S(1)} all-to-all(f32[16,9,128]{2,1,0:T(8,128)S(1)} %broadcast_in_dim.7), channel_id=1, replica_groups=mesh['z'=16,'y'=4,'x'=4,'c'=2] {'z'}, dimensions={0} | all-to-all | bytes 147456 | tf_op jit(solution)/shard_map/all_to_all | solution.py:367
  272.7 12.3 %all_gather.11 = f32[4,144,128]{2,1,0:T(8,128)S(1)} all-gather(f32[1,144,128]{2,1,0:T(8,128)S(1)} %all_gather_reshape.3), channel_id=1, replica_groups=mesh['z'=16,'y'=4,'x'=4,'c'=2] {'y'}, dimensions={0}, use_global_device_ids=true | all-gather | bytes 368640 | tf_op jit(solution)/shard_map/all_gather | solution.py:370
  (171 shorter events, 33.7 us)
Async XLA Ops:
  7.2 127.7 %all-gather.3.cloned.1.call-start = ((), (), s32[]{:S(2)}) async-start(), calls=%async_computation.5 | async-start | bytes 4718592 | tf_op jit(solution)/shard_map/all_gather | solution.py:274
  7.9 132.3 %all-gather.5.cloned.1.call-start = ((), (), s32[]{:S(2)}) async-start(), calls=%async_computation.6 | async-start | bytes 4718592 | tf_op jit(solution)/shard_map/all_gather | solution.py:275
  8.6 111.2 %copy-start.46 = (bf16[3,16,4096]{2,1,0:T(8,128)(2,1)S(1)}, bf16[3,16,4096]{2,1,0:T(8,128)(2,1)}, u32[]{:S(2)}) copy-start(bf16[3,16,4096]{2,1,0:T(8,128)(2,1)} %param.15) | copy-start | bytes 1179652
  8.7 12.5 %collective-permute-start.2 = (bf16[64,896]{1,0:T(8,128)(2,1)}, bf16[64,896]{1,0:T(8,128)(2,1)S(1)}, u32[]{:S(2)}, u32[]{:S(2)}) collective-permute-start(bf16[64,896]{1,0:T(8,128)(2,1)} %bitcast.29), channel_id=1, source_target_pairs={{0,16},{8,24},{16,0},{24,8},{2,18},{10,26},{18,2},{26,10},{4,20},{... | collective-permute-start | bytes 344072 | tf_op jit(solution)/shard_map/ppermute | solution.py:190
  13.9 7.2 %collective-permute-start.1 = (bf16[64,896]{1,0:T(8,128)(2,1)}, bf16[64,896]{1,0:T(8,128)(2,1)S(1)}, u32[]{:S(2)}, u32[]{:S(2)}) collective-permute-start(bf16[64,896]{1,0:T(8,128)(2,1)} %bitcast.30), channel_id=1, source_target_pairs={{0,24},{8,0},{16,8},{24,16},{2,26},{10,2},{18,10},{26,18},{4,28},{... | collective-permute-start | bytes 344072 | tf_op jit(solution)/shard_map/ppermute | solution.py:190
  16.9 8.1 %collective-permute-start = (bf16[64,896]{1,0:T(8,128)(2,1)}, bf16[64,896]{1,0:T(8,128)(2,1)S(1)}, u32[]{:S(2)}, u32[]{:S(2)}) collective-permute-start(bf16[64,896]{1,0:T(8,128)(2,1)} %bitcast.31), channel_id=1, source_target_pairs={{0,8},{8,16},{16,24},{24,0},{2,10},{10,18},{18,26},{26,2},{4,12},{... | collective-permute-start | bytes 344072 | tf_op jit(solution)/shard_map/ppermute | solution.py:190
  19.8 13.0 %collective-permute-start.16 = (bf16[64,896]{1,0:T(8,128)(2,1)}, bf16[64,896]{1,0:T(8,128)(2,1)S(1)}, u32[]{:S(2)}, u32[]{:S(2)}) collective-permute-start(bf16[64,896]{1,0:T(8,128)(2,1)} %bitcast.32), channel_id=1, source_target_pairs={{1,481},{33,1},{65,33},{97,65},{129,97},{161,129},{193,161},{225,1... | collective-permute-start | bytes 344072 | tf_op jit(solution)/shard_map/ppermute | solution.py:187
  20.4 13.0 %collective-permute-start.15 = (bf16[64,896]{1,0:T(8,128)(2,1)}, bf16[64,896]{1,0:T(8,128)(2,1)S(1)}, u32[]{:S(2)}, u32[]{:S(2)}) collective-permute-start(bf16[64,896]{1,0:T(8,128)(2,1)} %bitcast.33), channel_id=1, source_target_pairs={{1,33},{33,65},{65,97},{97,129},{129,161},{161,193},{193,225},{225... | collective-permute-start | bytes 344072 | tf_op jit(solution)/shard_map/ppermute | solution.py:187
  25.9 11.7 %collective-permute-start.9 = (bf16[256,896]{1,0:T(8,128)(2,1)S(1)}, bf16[256,896]{1,0:T(8,128)(2,1)S(1)}, u32[]{:S(2)}, u32[]{:S(2)}) collective-permute-start(bf16[256,896]{1,0:T(8,128)(2,1)S(1)} %pad_maximum_fusion.refs_0_), channel_id=1, source_target_pairs={{0,32},{32,64},{64,96},{96,128},{128,160},{160,192},{192,224},{224... | collective-permute-start | bytes 1376264 | tf_op jit(solution)/shard_map/ppermute | solution.py:187
  30.7 11.5 %collective-permute-start.3 = (bf16[256,896]{1,0:T(8,128)(2,1)S(1)}, bf16[256,896]{1,0:T(8,128)(2,1)S(1)}, u32[]{:S(2)}, u32[]{:S(2)}) collective-permute-start(bf16[256,896]{1,0:T(8,128)(2,1)S(1)} %pad_maximum_fusion.refs_0_), channel_id=1, source_target_pairs={{0,480},{32,0},{64,32},{96,64},{128,96},{160,128},{192,160},{224,1... | collective-permute-start | bytes 1376264 | tf_op jit(solution)/shard_map/ppermute | solution.py:187
  32.8 1.4 collective-permute-start.18
  33.5 1.4 collective-permute-start.17
  34.2 7.9 %collective-permute-start.20 = (bf16[64,896]{1,0:T(8,128)(2,1)S(1)}, bf16[64,896]{1,0:T(8,128)(2,1)S(1)}, u32[]{:S(2)}, u32[]{:S(2)}) collective-permute-start(bf16[64,896]{1,0:T(8,128)(2,1)S(1)} %collective-permute-done.18), channel_id=1, source_target_pairs={{1,481},{33,1},{65,33},{97,65},{129,97},{161,129},{193,161},{225,1... | collective-permute-start | bytes 344072 | tf_op jit(solution)/shard_map/ppermute | solution.py:187
  34.9 6.5 %collective-permute-start.19 = (bf16[64,896]{1,0:T(8,128)(2,1)S(1)}, bf16[64,896]{1,0:T(8,128)(2,1)S(1)}, u32[]{:S(2)}, u32[]{:S(2)}) collective-permute-start(bf16[64,896]{1,0:T(8,128)(2,1)S(1)} %collective-permute-done.17), channel_id=1, source_target_pairs={{1,33},{33,65},{65,97},{97,129},{129,161},{161,193},{193,225},{225... | collective-permute-start | bytes 344072 | tf_op jit(solution)/shard_map/ppermute | solution.py:187
  37.6 61.0 %copy-start.19 = (bf16[256,896]{1,0:T(8,128)(2,1)}, bf16[256,896]{1,0:T(8,128)(2,1)S(1)}, u32[]{:S(2)}) copy-start(bf16[256,896]{1,0:T(8,128)(2,1)S(1)} %collective-permute-done.9.refs_1_) | copy-start | bytes 1376260
  37.6 15.9 %collective-permute-start.10 = (bf16[256,896]{1,0:T(8,128)(2,1)S(1)}, bf16[256,896]{1,0:T(8,128)(2,1)S(1)}, u32[]{:S(2)}, u32[]{:S(2)}) collective-permute-start(bf16[256,896]{1,0:T(8,128)(2,1)S(1)} %collective-permute-done.9.refs_1_), channel_id=1, source_target_pairs={{0,32},{32,64},{64,96},{96,128},{128,160},{160,192},{192,224},{224... | collective-permute-start | bytes 1376264 | tf_op jit(solution)/shard_map/ppermute | solution.py:187
  41.4 14.0 %collective-permute-start.21 = (bf16[64,896]{1,0:T(8,128)(2,1)S(1)}, bf16[64,896]{1,0:T(8,128)(2,1)S(1)}, u32[]{:S(2)}, u32[]{:S(2)}) collective-permute-start(bf16[64,896]{1,0:T(8,128)(2,1)S(1)} %collective-permute-done.19), channel_id=1, source_target_pairs={{1,33},{33,65},{65,97},{97,129},{129,161},{161,193},{193,225},{225... | collective-permute-start | bytes 344072 | tf_op jit(solution)/shard_map/ppermute | solution.py:187
  42.1 37.9 %copy-start.21 = (bf16[256,896]{1,0:T(8,128)(2,1)}, bf16[256,896]{1,0:T(8,128)(2,1)S(1)}, u32[]{:S(2)}) copy-start(bf16[256,896]{1,0:T(8,128)(2,1)S(1)} %collective-permute-done.3.refs_2_) | copy-start | bytes 1376260
  42.2 16.1 %collective-permute-start.4 = (bf16[256,896]{1,0:T(8,128)(2,1)S(1)}, bf16[256,896]{1,0:T(8,128)(2,1)S(1)}, u32[]{:S(2)}, u32[]{:S(2)}) collective-permute-start(bf16[256,896]{1,0:T(8,128)(2,1)S(1)} %collective-permute-done.3.refs_2_), channel_id=1, source_target_pairs={{0,480},{32,0},{64,32},{96,64},{128,96},{160,128},{192,160},{224,1... | collective-permute-start | bytes 1376264 | tf_op jit(solution)/shard_map/ppermute | solution.py:187
  53.5 26.5 %copy-start.23 = (bf16[256,896]{1,0:T(8,128)(2,1)}, bf16[256,896]{1,0:T(8,128)(2,1)S(1)}, u32[]{:S(2)}) copy-start(bf16[256,896]{1,0:T(8,128)(2,1)S(1)} %collective-permute-done.10.refs_3_) | copy-start | bytes 1376260
  53.5 11.6 %collective-permute-start.11 = (bf16[256,896]{1,0:T(8,128)(2,1)S(1)}, bf16[256,896]{1,0:T(8,128)(2,1)S(1)}, u32[]{:S(2)}, u32[]{:S(2)}) collective-permute-start(bf16[256,896]{1,0:T(8,128)(2,1)S(1)} %collective-permute-done.10.refs_3_), channel_id=1, source_target_pairs={{0,32},{32,64},{64,96},{96,128},{128,160},{160,192},{192,224},{224... | collective-permute-start | bytes 1376264 | tf_op jit(solution)/shard_map/ppermute | solution.py:187
  55.4 24.6 %copy-start.9 = (bf16[512,896]{1,0:T(8,128)(2,1)}, bf16[512,896]{1,0:T(8,128)(2,1)S(1)}, u32[]{:S(2)}) copy-start(bf16[512,896]{1,0:T(8,128)(2,1)S(1)} %constant_dynamic-update-slice_fusion.refs_13_) | copy-start | bytes 2752516
  55.4 14.5 %collective-permute-start.23 = (bf16[512,896]{1,0:T(8,128)(2,1)S(1)}, bf16[512,896]{1,0:T(8,128)(2,1)S(1)}, u32[]{:S(2)}, u32[]{:S(2)}) collective-permute-start(bf16[512,896]{1,0:T(8,128)(2,1)S(1)} %constant_dynamic-update-slice_fusion.refs_13_), channel_id=1, source_target_pairs={{1,25},{9,1},{17,9},{25,17},{3,27},{11,3},{19,11},{27,19},{5,29},{... | collective-permute-start | bytes 2752520 | tf_op jit(solution)/shard_map/ppermute | solution.py:190
  56.2 13.8 %collective-permute-start.22 = (bf16[512,896]{1,0:T(8,128)(2,1)S(1)}, bf16[512,896]{1,0:T(8,128)(2,1)S(1)}, u32[]{:S(2)}, u32[]{:S(2)}) collective-permute-start(bf16[512,896]{1,0:T(8,128)(2,1)S(1)} %constant_dynamic-update-slice_fusion.refs_13_), channel_id=1, source_target_pairs={{1,9},{9,17},{17,25},{25,1},{3,11},{11,19},{19,27},{27,3},{5,13},{... | collective-permute-start | bytes 2752520 | tf_op jit(solution)/shard_map/ppermute | solution.py:190
  56.9 0.7 collective-permute-start.26
  57.6 10.2 %collective-permute-start.24 = (bf16[64,896]{1,0:T(8,128)(2,1)S(1)}, bf16[64,896]{1,0:T(8,128)(2,1)S(1)}, u32[]{:S(2)}, u32[]{:S(2)}) collective-permute-start(bf16[64,896]{1,0:T(8,128)(2,1)S(1)} %collective-permute-done.21), channel_id=1, source_target_pairs={{1,33},{33,65},{65,97},{97,129},{129,161},{161,193},{193,225},{225... | collective-permute-start | bytes 344072 | tf_op jit(solution)/shard_map/ppermute | solution.py:187
  58.3 12.3 %collective-permute-start.5 = (bf16[256,896]{1,0:T(8,128)(2,1)S(1)}, bf16[256,896]{1,0:T(8,128)(2,1)S(1)}, u32[]{:S(2)}, u32[]{:S(2)}) collective-permute-start(bf16[256,896]{1,0:T(8,128)(2,1)S(1)} %collective-permute-done.4.refs_4_), channel_id=1, source_target_pairs={{0,480},{32,0},{64,32},{96,64},{128,96},{160,128},{192,160},{224,1... | collective-permute-start | bytes 1376264 | tf_op jit(solution)/shard_map/ppermute | solution.py:187
  65.1 11.6 %collective-permute-start.12 = (bf16[256,896]{1,0:T(8,128)(2,1)S(1)}, bf16[256,896]{1,0:T(8,128)(2,1)S(1)}, u32[]{:S(2)}, u32[]{:S(2)}) collective-permute-start(bf16[256,896]{1,0:T(8,128)(2,1)S(1)} %collective-permute-done.11.refs_5_), channel_id=1, source_target_pairs={{0,32},{32,64},{64,96},{96,128},{128,160},{160,192},{192,224},{224... | collective-permute-start | bytes 1376264 | tf_op jit(solution)/shard_map/ppermute | solution.py:187
  67.8 0.7 collective-permute-start.27
  68.5 0.7 collective-permute-start.25
  69.2 0.7 collective-permute-start.28
  69.9 9.3 %collective-permute-start.35 = (bf16[64,896]{1,0:T(8,128)(2,1)S(1)}, bf16[64,896]{1,0:T(8,128)(2,1)S(1)}, u32[]{:S(2)}, u32[]{:S(2)}) collective-permute-start(bf16[64,896]{1,0:T(8,128)(2,1)S(1)} %collective-permute-done.25), channel_id=1, source_target_pairs={{1,33},{33,65},{65,97},{97,129},{129,161},{161,193},{193,225},{225... | collective-permute-start | bytes 344072 | tf_op jit(solution)/shard_map/ppermute | solution.py:187
  70.6 49.2 %copy-start.29 = (bf16[256,896]{1,0:T(8,128)(2,1)}, bf16[256,896]{1,0:T(8,128)(2,1)S(1)}, u32[]{:S(2)}) copy-start(bf16[256,896]{1,0:T(8,128)(2,1)S(1)} %collective-permute-done.5.refs_6_) | copy-start | bytes 1376260
  70.6 11.1 %collective-permute-start.6 = (bf16[256,896]{1,0:T(8,128)(2,1)S(1)}, bf16[256,896]{1,0:T(8,128)(2,1)S(1)}, u32[]{:S(2)}, u32[]{:S(2)}) collective-permute-start(bf16[256,896]{1,0:T(8,128)(2,1)S(1)} %collective-permute-done.5.refs_6_), channel_id=1, source_target_pairs={{0,480},{32,0},{64,32},{96,64},{128,96},{160,128},{192,160},{224,1... | collective-permute-start | bytes 1376264 | tf_op jit(solution)/shard_map/ppermute | solution.py:187
  76.6 43.2 %copy-start.31 = (bf16[256,896]{1,0:T(8,128)(2,1)}, bf16[256,896]{1,0:T(8,128)(2,1)S(1)}, u32[]{:S(2)}) copy-start(bf16[256,896]{1,0:T(8,128)(2,1)S(1)} %collective-permute-done.12.refs_7_) | copy-start | bytes 1376260
  76.6 11.8 %collective-permute-start.13 = (bf16[256,896]{1,0:T(8,128)(2,1)S(1)}, bf16[256,896]{1,0:T(8,128)(2,1)S(1)}, u32[]{:S(2)}, u32[]{:S(2)}) collective-permute-start(bf16[256,896]{1,0:T(8,128)(2,1)S(1)} %collective-permute-done.12.refs_7_), channel_id=1, source_target_pairs={{0,32},{32,64},{64,96},{96,128},{128,160},{160,192},{192,224},{224... | collective-permute-start | bytes 1376264 | tf_op jit(solution)/shard_map/ppermute | solution.py:187
  78.6 1.4 collective-permute-start.36
  79.3 0.7 collective-permute-start.37
  80.1 32.2 %copy-start.11 = (bf16[512,896]{1,0:T(8,128)(2,1)}, bf16[512,896]{1,0:T(8,128)(2,1)S(1)}, u32[]{:S(2)}) copy-start(bf16[512,896]{1,0:T(8,128)(2,1)S(1)} %constant_dynamic-update-slice_fusion.8.refs_22_) | copy-start | bytes 2752516
  80.1 26.7 %collective-permute-start.39 = (bf16[512,896]{1,0:T(8,128)(2,1)S(1)}, bf16[512,896]{1,0:T(8,128)(2,1)S(1)}, u32[]{:S(2)}, u32[]{:S(2)}) collective-permute-start(bf16[512,896]{1,0:T(8,128)(2,1)S(1)} %constant_dynamic-update-slice_fusion.8.refs_22_), channel_id=1, source_target_pairs={{1,25},{9,1},{17,9},{25,17},{3,27},{11,3},{19,11},{27,19},{5,29},{... | collective-permute-start | bytes 2752520 | tf_op jit(solution)/shard_map/ppermute | solution.py:190
  80.8 29.2 %collective-permute-start.38 = (bf16[512,896]{1,0:T(8,128)(2,1)S(1)}, bf16[512,896]{1,0:T(8,128)(2,1)S(1)}, u32[]{:S(2)}, u32[]{:S(2)}) collective-permute-start(bf16[512,896]{1,0:T(8,128)(2,1)S(1)} %constant_dynamic-update-slice_fusion.8.refs_22_), channel_id=1, source_target_pairs={{1,9},{9,17},{17,25},{25,1},{3,11},{11,19},{19,27},{27,3},{5,13},{... | collective-permute-start | bytes 2752520 | tf_op jit(solution)/shard_map/ppermute | solution.py:190
  81.7 38.1 %copy-start.33 = (bf16[256,896]{1,0:T(8,128)(2,1)}, bf16[256,896]{1,0:T(8,128)(2,1)S(1)}, u32[]{:S(2)}) copy-start(bf16[256,896]{1,0:T(8,128)(2,1)S(1)} %collective-permute-done.6.refs_8_) | copy-start | bytes 1376260
  81.7 12.3 %collective-permute-start.7 = (bf16[256,896]{1,0:T(8,128)(2,1)S(1)}, bf16[256,896]{1,0:T(8,128)(2,1)S(1)}, u32[]{:S(2)}, u32[]{:S(2)}) collective-permute-start(bf16[256,896]{1,0:T(8,128)(2,1)S(1)} %collective-permute-done.6.refs_8_), channel_id=1, source_target_pairs={{0,480},{32,0},{64,32},{96,64},{128,96},{160,128},{192,160},{224,1... | collective-permute-start | bytes 1376264 | tf_op jit(solution)/shard_map/ppermute | solution.py:187
  88.4 31.5 %copy-start.35 = (bf16[256,896]{1,0:T(8,128)(2,1)}, bf16[256,896]{1,0:T(8,128)(2,1)S(1)}, u32[]{:S(2)}) copy-start(bf16[256,896]{1,0:T(8,128)(2,1)S(1)} %collective-permute-done.13.refs_9_) | copy-start | bytes 1376260
  88.4 12.6 %collective-permute-start.14 = (bf16[256,896]{1,0:T(8,128)(2,1)S(1)}, bf16[256,896]{1,0:T(8,128)(2,1)S(1)}, u32[]{:S(2)}, u32[]{:S(2)}) collective-permute-start(bf16[256,896]{1,0:T(8,128)(2,1)S(1)} %collective-permute-done.13.refs_9_), channel_id=1, source_target_pairs={{0,32},{32,64},{64,96},{96,128},{128,160},{160,192},{192,224},{224... | collective-permute-start | bytes 1376264 | tf_op jit(solution)/shard_map/ppermute | solution.py:187
  94.1 19.2 %collective-permute-start.8 = (bf16[256,896]{1,0:T(8,128)(2,1)S(1)}, bf16[256,896]{1,0:T(8,128)(2,1)}, u32[]{:S(2)}, u32[]{:S(2)}) collective-permute-start(bf16[256,896]{1,0:T(8,128)(2,1)S(1)} %collective-permute-done.7.refs_10_), channel_id=1, source_target_pairs={{0,480},{32,0},{64,32},{96,64},{128,96},{160,128},{192,160},{224,1... | collective-permute-start | bytes 1376264 | tf_op jit(solution)/shard_map/ppermute | solution.py:187
  101.0 13.7 %collective-permute-start.31 = (bf16[256,896]{1,0:T(8,128)(2,1)S(1)}, bf16[256,896]{1,0:T(8,128)(2,1)S(1)}, u32[]{:S(2)}, u32[]{:S(2)}) collective-permute-start(bf16[256,896]{1,0:T(8,128)(2,1)S(1)} %collective-permute-done.14.refs_11_), channel_id=1, source_target_pairs={{0,32},{32,64},{64,96},{96,128},{128,160},{160,192},{192,224},{224... | collective-permute-start | bytes 1376264 | tf_op jit(solution)/shard_map/ppermute | solution.py:187
  105.3 24.3 %collective-permute-start.30 = (bf16[256,896]{1,0:T(8,128)(2,1)}, bf16[256,896]{1,0:T(8,128)(2,1)}, u32[]{:S(2)}, u32[]{:S(2)}) collective-permute-start(bf16[256,896]{1,0:T(8,128)(2,1)} %slice.31), channel_id=1, source_target_pairs={{1,25},{9,1},{17,9},{25,17},{3,27},{11,3},{19,11},{27,19},{5,29},{... | collective-permute-start | bytes 1376264 | tf_op jit(solution)/shard_map/ppermute | solution.py:190
  106.8 39.0 %collective-permute-start.29 = (bf16[256,896]{1,0:T(8,128)(2,1)}, bf16[256,896]{1,0:T(8,128)(2,1)}, u32[]{:S(2)}, u32[]{:S(2)}) collective-permute-start(bf16[256,896]{1,0:T(8,128)(2,1)} %slice.30), channel_id=1, source_target_pairs={{1,9},{9,17},{17,25},{25,1},{3,11},{11,19},{19,27},{27,3},{5,13},{... | collective-permute-start | bytes 1376264 | tf_op jit(solution)/shard_map/ppermute | solution.py:190
  110.0 35.8 %collective-permute-start.41 = (bf16[256,896]{1,0:T(8,128)(2,1)}, bf16[256,896]{1,0:T(8,128)(2,1)}, u32[]{:S(2)}, u32[]{:S(2)}) collective-permute-start(bf16[256,896]{1,0:T(8,128)(2,1)} %slice.43), channel_id=1, source_target_pairs={{1,25},{9,1},{17,9},{25,17},{3,27},{11,3},{19,11},{27,19},{5,29},{... | collective-permute-start | bytes 1376264 | tf_op jit(solution)/shard_map/ppermute | solution.py:190
  113.2 32.6 %collective-permute-start.40 = (bf16[256,896]{1,0:T(8,128)(2,1)}, bf16[256,896]{1,0:T(8,128)(2,1)}, u32[]{:S(2)}, u32[]{:S(2)}) collective-permute-start(bf16[256,896]{1,0:T(8,128)(2,1)} %slice.42), channel_id=1, source_target_pairs={{1,9},{9,17},{17,25},{25,1},{3,11},{11,19},{19,27},{27,3},{5,13},{... | collective-permute-start | bytes 1376264 | tf_op jit(solution)/shard_map/ppermute | solution.py:190
  114.7 30.4 %copy-start.13 = (bf16[256,896]{1,0:T(8,128)(2,1)}, bf16[256,896]{1,0:T(8,128)(2,1)S(1)}, u32[]{:S(2)}) copy-start(bf16[256,896]{1,0:T(8,128)(2,1)S(1)} %collective-permute-done.31.refs_18_) | copy-start | bytes 1376260
  114.7 11.4 %collective-permute-start.32 = (bf16[256,896]{1,0:T(8,128)(2,1)}, bf16[256,896]{1,0:T(8,128)(2,1)}, u32[]{:S(2)}, u32[]{:S(2)}) collective-permute-start(bf16[256,896]{1,0:T(8,128)(2,1)} %collective-permute-done.8.refs_12_), channel_id=1, source_target_pairs={{0,480},{32,0},{64,32},{96,64},{128,96},{160,128},{192,160},{224,1... | collective-permute-start | bytes 1376264 | tf_op jit(solution)/shard_map/ppermute | solution.py:187
  126.1 19.7 %collective-permute-start.33 = (bf16[128,896]{1,0:T(8,128)(2,1)}, bf16[128,896]{1,0:T(8,128)(2,1)}, u32[]{:S(2)}, u32[]{:S(2)}) collective-permute-start(bf16[128,896]{1,0:T(8,128)(2,1)} %slice.40), channel_id=1, source_target_pairs={{0,32},{32,64},{64,96},{96,128},{128,160},{160,192},{192,224},{224... | collective-permute-start | bytes 688136 | tf_op jit(solution)/shard_map/ppermute | solution.py:187
  129.7 16.2 %collective-permute-start.34 = (bf16[128,896]{1,0:T(8,128)(2,1)}, bf16[128,896]{1,0:T(8,128)(2,1)}, u32[]{:S(2)}, u32[]{:S(2)}) collective-permute-start(bf16[128,896]{1,0:T(8,128)(2,1)} %slice.41), channel_id=1, source_target_pairs={{0,480},{32,0},{64,32},{96,64},{128,96},{160,128},{192,160},{224,1... | collective-permute-start | bytes 688136 | tf_op jit(solution)/shard_map/ppermute | solution.py:187
  134.9 2.2 copy-start
  140.2 5.6 %copy-start.1 = (bf16[512,4096]{1,0:T(8,128)(2,1)S(1)}, bf16[512,4096]{1,0:T(8,128)(2,1)}, u32[]{:S(2)}) copy-start(bf16[512,4096]{1,0:T(8,128)(2,1)} %all-gather.3.cloned.1.call-done.rows_ref.gradient_ref) | copy-start | bytes 12582916
  140.3 2.3 copy-start.2
  145.8 1.2 copy-start.6
  166.0 53.9 %copy-start.3 = (bf16[512,512]{1,0:T(8,128)(2,1)S(1)}, bf16[512,512]{1,0:T(8,128)(2,1)}, u32[]{:S(2)}) copy-start(bf16[512,512]{1,0:T(8,128)(2,1)} %gradient_ref.1) | copy-start | bytes 1572868
  166.0 53.9 %copy-start.4 = (bf16[512,512]{1,0:T(8,128)(2,1)S(1)}, bf16[512,512]{1,0:T(8,128)(2,1)}, u32[]{:S(2)}) copy-start(bf16[512,512]{1,0:T(8,128)(2,1)} %normed_ref.1) | copy-start | bytes 1572868
  187.9 97.1 %copy-start.48 = (f32[3,16,512]{2,1,0:T(8,128)S(1)}, f32[3,16,512]{2,1,0:T(8,128)}, u32[]{:S(2)}) copy-start(f32[3,16,512]{2,1,0:T(8,128)} %param.18) | copy-start | bytes 294916
  187.9 97.8 %copy-start.47 = (f32[3,16,896]{2,1,0:T(8,128)S(1)}, f32[3,16,896]{2,1,0:T(8,128)}, u32[]{:S(2)}) copy-start(f32[3,16,896]{2,1,0:T(8,128)} %param.19) | copy-start | bytes 516100
  210.5 9.4 %all-to-all-start.1 = ((f32[8,8,512]{2,1,0:T(8,128)}), f32[8,8,512]{2,1,0:T(8,128)S(1)}, u32[]{:S(2)}, u32[]{:S(2)}) async-start(f32[8,8,512]{2,1,0:T(8,128)} %broadcast_in_dim.6), calls=%async_computation.1 | async-start | bytes 262144 | tf_op jit(solution)/shard_map/all_to_all | solution.py:341
  (30 other events, 29.3 us)
Sparse Core Ops, SparseCore 0:
  10.1 43.8 all-gather.2
  56.2 39.7 all-gather.4

commit v4 on v2

--- a/solution.py
+++ b/solution.py
@@ -33,53 +33,61 @@
         tile(whole * step, hidden - whole * step)
 
 
-def block_product(place_ref, gradient_ref, block_refs, cols):
-    left = jnp.concatenate(
-        [
-            gradient_ref[:, pl.ds(pl.multiple_of(place_ref[i] * 128, 128), block.shape[0])]
-            for i, block in enumerate(block_refs)
-        ],
-        axis=1,
-    )
-    right = jnp.concatenate([block[:, cols] for block in block_refs], axis=0)
-    return jnp.dot(left, right, preferred_element_type=F32)
-
-
-def gram_of(rows_ref, out_ref):
-    for e in range(out_ref.shape[0]):
+def fetch_blocks(place_ref, gradient_ref, block_refs, left, right, sems):
+    copies, row = [], 0
+    for i, block in enumerate(block_refs):
+        rows = block.shape[0]
+        at = pl.ds(pl.multiple_of(place_ref[i] * 128, 128), rows)
+        copies.append(
+            pltpu.make_async_copy(
+                gradient_ref.at[:, at], left.at[:, pl.ds(row, rows)], sems.at[2 * i]
+            )
+        )
+        copies.append(
+            pltpu.make_async_copy(block, right.at[pl.ds(row, rows), :], sems.at[2 * i + 1])
+        )
+        row += rows
+    for copy in copies:
+        copy.start()
+    return copies
+
+
+def side_kernel(rows_ref, factors_ref, projected_ref, gram_ref, total):
+    step = pl.program_id(0)
+
+    @pl.when(step == 0)
+    def _():
+        total[...] = jnp.zeros_like(total)
+        gram_ref[...] = jnp.zeros_like(gram_ref)
+
+    total[...] += contract(factors_ref[...], rows_ref[...], 1, 1)
+    for e in range(gram_ref.shape[0]):
         rows = rows_ref[e * SEQUENCE_TOKENS : (e + 1) * SEQUENCE_TOKENS, :]
-        out_ref[e] = contract(rows, rows, 1, 1)
-
-
-def first_kernel(n_blocks, place_ref, gradient_ref, *refs):
+        gram_ref[e] += contract(rows, rows, 1, 1)
+
+    @pl.when(step == pl.num_programs(0) - 1)
+    def _():
+        projected_ref[...] = total[...].astype(BF16)
+
+
+def part_kernel(n_blocks, first, place_ref, gradient_ref, *refs):
     block_refs = refs[:n_blocks]
-    factor_ref, total_ref, lora_ref, gram_ref = refs[n_blocks:]
+    if first:
+        total_ref, left, right, sems = refs[n_blocks:]
+    else:
+        before_ref, total_ref, left, right, sems = refs[n_blocks:]
+    for copy in fetch_blocks(place_ref, gradient_ref, block_refs, left, right, sems):
+        copy.wait()
 
     def tile(start, width):
         cols = pl.ds(start, width)
-        total_ref[:, cols] = block_product(place_ref, gradient_ref, block_refs, cols)
+        product = jnp.dot(left[...], right[:, cols], preferred_element_type=F32)
+        if first:
+            total_ref[:, cols] = product
+        else:
+            total_ref[:, cols] = before_ref[:, cols] + product
 
     column_tiles(total_ref.shape[1], 256, tile)
-    lora_ref[...] = contract(factor_ref[...], gradient_ref[...], 1, 1).astype(BF16)
-    gram_of(gradient_ref, gram_ref)
-
-
-def more_kernel(n_blocks, place_ref, gradient_ref, *refs):
-    block_refs = refs[:n_blocks]
-    before_ref, total_ref = refs[n_blocks:]
-
-    def tile(start, width):
-        cols = pl.ds(start, width)
-        total_ref[:, cols] = before_ref[:, cols] + block_product(
-            place_ref, gradient_ref, block_refs, cols
-        )
-
-    column_tiles(total_ref.shape[1], 256, tile)
-
-
-def normed_kernel(normed_ref, factors_ref, in_ref, gram_ref):
-    in_ref[...] = contract(factors_ref[...], normed_ref[...], 1, 1).astype(BF16)
-    gram_of(normed_ref, gram_ref)
 
 
 def hidden_kernel(n_blocks, place_ref, gradient_ref, *refs):
@@ -87,17 +95,20 @@
     (before_ref, gate_ref, up_ref, factors_ref, in_ref, lora_ref, lora_t_ref) = refs[
         n_blocks : n_blocks + 7
     ]
-    sums_ref, mids_ref, total = refs[n_blocks + 7 :]
+    sums_ref, mids_ref, total, left_rows, right_rows, sems = refs[n_blocks + 7 :]
     tokens, hidden = gate_ref.shape
     sequences = tokens // SEQUENCE_TOKENS
+    copies = fetch_blocks(place_ref, gradient_ref, block_refs, left_rows, right_rows, sems)
     mids_ref[...] = jnp.zeros_like(mids_ref)
+    for copy in copies:
+        copy.wait()
 
     def tile(start, width):
         cols = pl.ds(start, width)
         factors = factors_ref[:, cols]
         total[:, :width] = (
             before_ref[:, cols]
-            + block_product(place_ref, gradient_ref, block_refs, cols)
+            + jnp.dot(left_rows[...], right_rows[:, cols], preferred_element_type=F32)
             + SCALE * jnp.dot(lora_ref[...], factors[2 * RANK :], preferred_element_type=F32)
         )
         for e in range(sequences):
@@ -177,20 +188,20 @@
         else:
             wide[: 2 * RANK] += first
             wide[2 * RANK :] += second
-    lanes = out_ref.shape[0] // 6
+    lanes = (local + hidden) // 128
     for t in range(out_ref.shape[0]):
         r, c = divmod(t, lanes)
         rows = slice(8 * r, 8 * r + 8)
         at = c * 128
-        if at < local:
+        if r >= 3 * RANK // 8:
+            value = jnp.zeros((8, 128), F32)
+        elif at < local:
             value = wide[rows, at : at + 128]
-        elif at < local + hidden:
+        else:
             at = at - local
             value = weights[0] * sums_ref[0, rows, at : at + 128]
             for e in range(1, sequences):
                 value = value + weights[e] * sums_ref[e, rows, at : at + 128]
-        else:
-            value = jnp.zeros((8, 128), F32)
         out_ref[t] = value
 
 
@@ -228,7 +239,8 @@
     units = rows // 128
     vmem = pl.BlockSpec(memory_space=pltpu.VMEM)
     smem = pl.BlockSpec(memory_space=pltpu.SMEM)
-    params = pltpu.CompilerParams(vmem_limit_bytes=32 * 2**20)
+    hbm = pl.BlockSpec(memory_space=pl.ANY)
+    params = pltpu.CompilerParams(vmem_limit_bytes=60 * 2**20)
 
     def place(offsets):
         at = [((z + offset) % n_z) * units for offset in offsets]
@@ -240,72 +252,88 @@
         low[k] = lax.ppermute(low_from, z_axes, ring(n_z, 1))
         high[k] = lax.ppermute(high_from, z_axes, ring(n_z, -1))
 
-    def product_cost(n_rows, read):
-        return pl.CostEstimate(
-            flops=2 * tokens * n_rows * hidden, bytes_accessed=read, transcendentals=0
-        )
+    def side(values, factors, name):
+        width = values.shape[1]
+        chunk = 1024
+        return pl.pallas_call(
+            side_kernel,
+            out_shape=(
+                jax.ShapeDtypeStruct((factors.shape[0], tokens), BF16),
+                jax.ShapeDtypeStruct((sequences, SEQUENCE_TOKENS, SEQUENCE_TOKENS), F32),
+            ),
+            grid=(width // chunk,),
+            in_specs=[
+                pl.BlockSpec((tokens, chunk), lambda i: (0, i)),
+                pl.BlockSpec((factors.shape[0], chunk), lambda i: (0, i)),
+            ],
+            out_specs=(
+                pl.BlockSpec((factors.shape[0], tokens), lambda i: (0, 0)),
+                pl.BlockSpec((sequences, SEQUENCE_TOKENS, SEQUENCE_TOKENS), lambda i: (0, 0, 0)),
+            ),
+            scratch_shapes=[pltpu.VMEM((factors.shape[0], tokens), F32)],
+            compiler_params=params,
+            cost_estimate=pl.CostEstimate(
+                flops=2 * tokens * width * (128 + factors.shape[0]),
+                bytes_accessed=5 * 2**20,
+                transcendentals=0,
+            ),
+            name=name,
+        )(values, factors)
+
+    def scratch(n_rows, n_blocks):
+        return [
+            pltpu.VMEM((tokens, n_rows), BF16),
+            pltpu.VMEM((n_rows, hidden), BF16),
+            pltpu.SemaphoreType.DMA((2 * n_blocks,)),
+        ]
+
+    def part(offsets, before=None):
+        blocks = [(low if offset < 0 else high)[abs(offset)] for offset in offsets]
+        n = len(blocks)
+        given = [] if before is None else [before]
+        return pl.pallas_call(
+            functools.partial(part_kernel, n, before is None),
+            out_shape=jax.ShapeDtypeStruct((tokens, hidden), F32),
+            in_specs=[smem] + [hbm] * (n + 1) + [vmem] * len(given),
+            out_specs=vmem,
+            scratch_shapes=scratch(n * rows, n),
+            compiler_params=params,
+            cost_estimate=pl.CostEstimate(
+                flops=2 * tokens * n * rows * hidden,
+                bytes_accessed=6 * 2**20,
+                transcendentals=0,
+            ),
+            name="part_product",
+        )(place(offsets), gradient, *blocks, *given)
+
+    def pairs(first, end):
+        return [sign * k for k in range(first, end) for sign in (-1, 1)]
 
     last = n_z // 2
     for k in range(1, last - 2):
         step(k, low[k - 1], high[k - 1])
-    offsets = [0] + [sign * k for k in range(1, last - 4) for sign in (-1, 1)]
-    blocks = [block] + [side[k] for k in range(1, last - 4) for side in (low, high)]
-    total, lora_t, gradient_gram = pl.pallas_call(
-        functools.partial(first_kernel, len(blocks)),
-        out_shape=(
-            jax.ShapeDtypeStruct((tokens, hidden), F32),
-            jax.ShapeDtypeStruct((RANK, tokens), BF16),
-            jax.ShapeDtypeStruct((sequences, SEQUENCE_TOKENS, SEQUENCE_TOKENS), F32),
-        ),
-        in_specs=[smem] + [vmem] * (len(blocks) + 2),
-        out_specs=(vmem, vmem, vmem),
-        compiler_params=params,
-        cost_estimate=product_cost(rows * len(blocks), 8 * 2**20),
-        name="first_blocks",
-    )(place(offsets), gradient, *blocks, adapter_width_factors[2])
-
+    total = part([0] + pairs(1, last - 5))
     at = last - 3
     low_in, high_in, total = lax.optimization_barrier((low[at], high[at], total))
     step(last - 2, low_in, high_in)
-    offsets = [sign * k for k in range(last - 4, last - 2) for sign in (-1, 1)]
-    blocks = [side[k] for k in range(last - 4, last - 2) for side in (low, high)]
-    total = pl.pallas_call(
-        functools.partial(more_kernel, len(blocks)),
-        out_shape=jax.ShapeDtypeStruct((tokens, hidden), F32),
-        in_specs=[smem] + [vmem] * (len(blocks) + 2),
-        out_specs=vmem,
-        input_output_aliases={len(blocks) + 2: 0},
-        compiler_params=params,
-        cost_estimate=product_cost(rows * len(blocks), 6 * 2**20),
-        name="more_blocks",
-    )(place(offsets), gradient, *blocks, total)
-    step(last - 1, low[last - 2], high[last - 2])
-
-    in_t, normed_gram = pl.pallas_call(
-        normed_kernel,
-        out_shape=(
-            jax.ShapeDtypeStruct((2 * RANK, tokens), BF16),
-            jax.ShapeDtypeStruct((sequences, SEQUENCE_TOKENS, SEQUENCE_TOKENS), F32),
-        ),
-        in_specs=[vmem, vmem],
-        out_specs=(vmem, vmem),
-        compiler_params=params,
-        cost_estimate=pl.CostEstimate(
-            flops=2 * tokens * 4096 * 160, bytes_accessed=5 * 2**20, transcendentals=0
-        ),
-        name="normed_side",
-    )(normed_all, adapter_width_factors[:2].reshape(2 * RANK, -1))
-
-    low_in, high_in, total, in_t = lax.optimization_barrier(
-        (low[last - 1], high[last - 1], total, in_t)
-    )
+    total = part(pairs(last - 5, last - 3), total)
+    lora_t, gradient_gram = side(gradient, adapter_width_factors[2], "gradient_side")
+    at = last - 2
+    low_in, high_in, total, lora_t = lax.optimization_barrier(
+        (low[at], high[at], total, lora_t)
+    )
+    step(last - 1, low_in, high_in)
+    total = part(pairs(last - 3, last - 1), total)
+    at = last - 1
+    low_in, high_in, total = lax.optimization_barrier((low[at], high[at], total))
     step(last, low_in[:half], high_in[half:])
+    in_t, normed_gram = side(
+        normed_all, adapter_width_factors[:2].reshape(2 * RANK, -1), "normed_side"
+    )
     far = ((z + last) % n_z) * units
-    offsets = [sign * k for k in range(last - 2, last) for sign in (-1, 1)]
-    blocks = [side[k] for k in range(last - 2, last) for side in (low, high)]
-    blocks += [low[last], high[last]]
+    blocks = [low[last - 1], high[last - 1], low[last], high[last]]
     places = jnp.concatenate(
-        [place(offsets), jnp.stack([far, far + units // 2]).astype(jnp.int32)]
+        [place(pairs(last - 1, last)), jnp.stack([far, far + units // 2]).astype(jnp.int32)]
     )
     sums, mids = pl.pallas_call(
         functools.partial(hidden_kernel, len(blocks)),
@@ -313,9 +341,9 @@
             jax.ShapeDtypeStruct((sequences, 3 * RANK, hidden), F32),
             jax.ShapeDtypeStruct((8 * n_tensor, tokens), F32),
         ),
-        in_specs=[smem] + [vmem] * (len(blocks) + 8),
+        in_specs=[smem] + [hbm] * (len(blocks) + 1) + [vmem] * 7,
         out_specs=(vmem, vmem),
-        scratch_shapes=[pltpu.VMEM((tokens, 256), F32)],
+        scratch_shapes=[pltpu.VMEM((tokens, 256), F32)] + scratch(3 * rows, len(blocks)),
         compiler_params=params,
         name="hidden_side",
     )(
@@ -337,10 +365,12 @@
         jnp.broadcast_to(piece, (n_tensor,) + piece.shape), tensor_axes, 0, 0
     ).reshape(8 * n_tensor, tokens)
 
-    lanes = 12
+    lanes = (local_width + hidden) // 128
+    tiles = 6 * lanes
+    padded = -(-tiles // n_z) * n_z
     out = pl.pallas_call(
         clip_kernel,
-        out_shape=jax.ShapeDtypeStruct((6 * lanes, 8, 128), F32),
+        out_shape=jax.ShapeDtypeStruct((padded, 8, 128), F32),
         in_specs=[smem] + [vmem] * 6,
         out_specs=vmem,
         scratch_shapes=[pltpu.VMEM((3 * RANK, local_width), F32)],
@@ -356,15 +386,14 @@
         gradient_gram,
     )
 
-    n_y = sizes["y"]
-    part = jnp.sum(lax.all_to_all(out.reshape(n_y, -1, 128), "y", 0, 0), axis=0)
-    part = jnp.sum(lax.all_to_all(part.reshape(n_z, -1, 128), z_axes, 0, 0), axis=0)
-    part = lax.all_to_all(
-        jnp.broadcast_to(part, (n_z,) + part.shape), z_axes, 0, 0
-    ).reshape(-1, 128)
-    part = lax.all_gather(part, "y", axis=0)
+    part_sum = jnp.sum(lax.all_to_all(out.reshape(n_z, -1, 128), z_axes, 0, 0), axis=0)
+    part_sum = jnp.sum(lax.all_gather(part_sum, "y", axis=0), axis=0)
+    whole = lax.all_to_all(
+        jnp.broadcast_to(part_sum, (n_z,) + part_sum.shape), z_axes, 0, 0
+    )
     total = (
-        part.reshape(6, lanes, 8, 128)
+        whole.reshape(padded, 8, 128)[:tiles]
+        .reshape(6, lanes, 8, 128)
         .transpose(0, 2, 1, 3)
         .reshape(3, RANK, lanes * 128)
     )

time: 260 us -> 256 us (0.985)
  local copies, waits for them, and re-layouts: 36.2 us -> 5.97 us
  Pallas kernels: 18.2 us -> 41.5 us
  blocking collectives: 88.4 us -> 92.6 us
    unnamed x78 -> x44, local copies, waits for them, and re-layouts: 31.8 us -> 1.49 us
    pallas_call x4 -> x6, Pallas kernels: 11.5 us -> 32.9 us  [the longest x3 18.9 us: part(): pl.pallas_call(functools.partial(part_kernel, n, before is None), out_sha...]
    ppermute x8, waiting for transfers between devices: 10.8 us -> 5.22 us  [step(): low[k] = lax.ppermute(low_from, z_axes, ring(n_z, 1))]
    all_to_all x3 -> x2, blocking collectives: 51.5 us -> 56.4 us  [the longest x1 30.7 us: per_device(): lax.all_to_all(out.reshape(n_z, -1, 128), z_axes, 0, 0)]
    ppermute x8, waiting for transfers between devices: 13.7 us -> 17 us  [step(): high[k] = lax.ppermute(high_from, z_axes, ring(n_z, -1))]
  transfers between devices with their start and end apart: 19 -> 19, of which waited for: 11 -> 11; matrix products, arithmetic and copies ran while one was open for 1% -> 2% of each run, Pallas kernels for 4% -> 12%
where the time goes in v4:
time: 256 us; the launch traced here: 255 us
  blocking collectives  92.6 us (36%)
  starting transfers between devices  67.5 us (26%)
  Pallas kernels  41.5 us (16%)
  waiting for transfers between devices  29 us (11%)
  between operations  15.2 us (6%)
  local copies, waits for them, and re-layouts  5.97 us (2%)
  other arithmetic  3.12 us (1%)
    ppermute x8, starting transfers between devices, step(): high[k] = lax.ppermute(high_from, z_axes, ring(n_z, -1))  48.7 us
    all_to_all x1, blocking collectives, per_device(): lax.all_to_all(out.reshape(n_z, -1, 128), z_axes, 0, 0)  30.7 us
    all_to_all x1, blocking collectives, per_device(): lax.all_to_all(jnp.broadcast_to(part_sum, (n_z,) + part_sum.shape), z_axe...  25.7 us
    pallas_call x3, Pallas kernels, part(): pl.pallas_call(functools.partial(part_kernel, n, before is None), out_sha...  18.9 us
    ppermute x8, waiting for transfers between devices, step(): high[k] = lax.ppermute(high_from, z_axes, ring(n_z, -1))  17 us
    ppermute x8, starting transfers between devices, step(): low[k] = lax.ppermute(low_from, z_axes, ring(n_z, 1))  15.3 us
    all_gather x1, blocking collectives, per_device(): block = lax.all_gather(frozen_down_weight.T, 'y', axis=0, tiled=True)  13.4 us
    all_gather x1, blocking collectives, per_device(): part_sum = jnp.sum(lax.all_gather(part_sum, 'y', axis=0), axis=0)  11.9 us
  transfers between devices with their start and end apart: 19, of which 11 were waited for; matrix products, arithmetic and copies ran while one was open for 2% of the time, Pallas kernels for 12%

profile of v4, /device:TPU:32, one launch (start us, length us, event | category | flops | bytes accessed | tf_op | source)
XLA Modules:
  0.0 254.9 jit_solution(1422750262689641354)
XLA Ops:
  7.2 0.0 all-gather.4.cloned.1.call-start
  7.2 0.7 all-gather.4.cloned.1.call-update
  7.9 0.0 all-gather.6.cloned.1.call-start
  7.9 0.7 all-gather.6.cloned.1.call-update
  8.6 13.4 %all_gather.16.refs_0_ = bf16[256,896]{1,0:T(8,128)(2,1)S(1)} all-gather(bf16[64,896]{1,0:T(8,128)(2,1)} %bitcast.45), channel_id=1, replica_groups=mesh['z'=16,'y'=4,'x'=4,'c'=2] {'y'}, dimensions={0}, use_global_device_ids=true | all-gather | bytes 573440 | tf_op jit(solution)/shard_map/all_gather | solution.py:234
  22.0 6.9 %collective-permute-start.5 = (bf16[256,896]{1,0:T(8,128)(2,1)S(1)}, bf16[256,896]{1,0:T(8,128)(2,1)S(1)}, u32[]{:S(2)}, u32[]{:S(2)}) collective-permute-start(bf16[256,896]{1,0:T(8,128)(2,1)S(1)} %all_gather.16.refs_0_), channel_id=1, source_target_pairs={{0,480},{32,0},{64,32},{96,64},{128,96},{160,128},{192,160},{224,1... | collective-permute-start | bytes 1376264 | tf_op jit(solution)/shard_map/ppermute | solution.py:253
  28.9 1.9 collective-permute-start
  30.8 4.0 %collective-permute-done.5.refs_2_ = bf16[256,896]{1,0:T(8,128)(2,1)S(1)} collective-permute-done((bf16[256,896]{1,0:T(8,128)(2,1)S(1)}, bf16[256,896]{1,0:T(8,128)(2,1)S(1)}, u32[]{:S(2)}, u32[]{:S(2)}) %collective-permute-start.5) | collective-permute-done | bytes 458784 | tf_op jit(solution)/shard_map/ppermute | solution.py:253
  34.9 8.6 %collective-permute-start.6 = (bf16[256,896]{1,0:T(8,128)(2,1)S(1)}, bf16[256,896]{1,0:T(8,128)(2,1)S(1)}, u32[]{:S(2)}, u32[]{:S(2)}) collective-permute-start(bf16[256,896]{1,0:T(8,128)(2,1)S(1)} %collective-permute-done.5.refs_2_), channel_id=1, source_target_pairs={{0,480},{32,0},{64,32},{96,64},{128,96},{160,128},{192,160},{224,1... | collective-permute-start | bytes 1376264 | tf_op jit(solution)/shard_map/ppermute | solution.py:253
  43.5 0.5 collective-permute-done.refs_1_
  44.0 1.9 collective-permute-start.1
  45.9 4.7 %collective-permute-done.6.refs_4_ = bf16[256,896]{1,0:T(8,128)(2,1)S(1)} collective-permute-done((bf16[256,896]{1,0:T(8,128)(2,1)S(1)}, bf16[256,896]{1,0:T(8,128)(2,1)S(1)}, u32[]{:S(2)}, u32[]{:S(2)}) %collective-permute-start.6) | collective-permute-done | bytes 458784 | tf_op jit(solution)/shard_map/ppermute | solution.py:253
  50.7 5.7 %collective-permute-start.7 = (bf16[256,896]{1,0:T(8,128)(2,1)S(1)}, bf16[256,896]{1,0:T(8,128)(2,1)S(1)}, u32[]{:S(2)}, u32[]{:S(2)}) collective-permute-start(bf16[256,896]{1,0:T(8,128)(2,1)S(1)} %collective-permute-done.6.refs_4_), channel_id=1, source_target_pairs={{0,480},{32,0},{64,32},{96,64},{128,96},{160,128},{192,160},{224,1... | collective-permute-start | bytes 1376264 | tf_op jit(solution)/shard_map/ppermute | solution.py:253
  56.4 0.5 collective-permute-done.1.refs_3_
  56.9 1.9 collective-permute-start.2
  58.8 3.9 %collective-permute-done.7.refs_1_ = bf16[256,896]{1,0:T(8,128)(2,1)S(1)} collective-permute-done((bf16[256,896]{1,0:T(8,128)(2,1)S(1)}, bf16[256,896]{1,0:T(8,128)(2,1)S(1)}, u32[]{:S(2)}, u32[]{:S(2)}) %collective-permute-start.7) | collective-permute-done | bytes 458784 | tf_op jit(solution)/shard_map/ppermute | solution.py:253
  62.7 5.7 %collective-permute-start.8 = (bf16[256,896]{1,0:T(8,128)(2,1)S(1)}, bf16[256,896]{1,0:T(8,128)(2,1)S(1)}, u32[]{:S(2)}, u32[]{:S(2)}) collective-permute-start(bf16[256,896]{1,0:T(8,128)(2,1)S(1)} %collective-permute-done.7.refs_1_), channel_id=1, source_target_pairs={{0,480},{32,0},{64,32},{96,64},{128,96},{160,128},{192,160},{224,1... | collective-permute-start | bytes 1376264 | tf_op jit(solution)/shard_map/ppermute | solution.py:253
  68.4 0.5 collective-permute-done.2.refs_0_
  68.9 1.9 collective-permute-start.3
  70.8 3.5 %collective-permute-done.8.refs_3_ = bf16[256,896]{1,0:T(8,128)(2,1)S(1)} collective-permute-done((bf16[256,896]{1,0:T(8,128)(2,1)S(1)}, bf16[256,896]{1,0:T(8,128)(2,1)S(1)}, u32[]{:S(2)}, u32[]{:S(2)}) %collective-permute-start.8) | collective-permute-done | bytes 458784 | tf_op jit(solution)/shard_map/ppermute | solution.py:253
  74.4 5.6 %collective-permute-start.9 = (bf16[256,896]{1,0:T(8,128)(2,1)S(1)}, bf16[256,896]{1,0:T(8,128)(2,1)S(1)}, u32[]{:S(2)}, u32[]{:S(2)}) collective-permute-start(bf16[256,896]{1,0:T(8,128)(2,1)S(1)} %collective-permute-done.8.refs_3_), channel_id=1, source_target_pairs={{0,480},{32,0},{64,32},{96,64},{128,96},{160,128},{192,160},{224,1... | collective-permute-start | bytes 1376264 | tf_op jit(solution)/shard_map/ppermute | solution.py:253
  80.0 0.5 collective-permute-done.3.refs_2_
  80.5 1.9 collective-permute-start.4
  82.4 0.7 stack.69.place_ref
  83.1 0.0 copy-done
  83.1 6.1 %part_product.3.refs_4_ = f32[512,896]{1,0:T(8,128)} custom-call(s32[5]{0:T(128)} %stack.69.place_ref, bf16[512,4096]{1,0:T(8,128)(2,1)} %all-gather.4.cloned.1.call-done.gradient_ref.rows_ref, bf16[256,896]{1,0:T(8,128)(2,1)} %copy-done, bf16[256,896]{1,0:T(8,128)(2,1)} %copy-done.13, bf16[256,896]{1,0:T(8,128)(2,1)} %copy-done.12, ...), custom_call_target="tpu_custom_call" | custom-call | flops 1174405120 | bytes 6291456 | tf_op jit(solution)/shard_map/part_product/pallas_call | solution.py:294
  89.3 0.0 collective-permute-done.9.refs_1_
  89.3 3.3 %collective-permute-done.4.refs_0_ = bf16[256,896]{1,0:T(8,128)(2,1)S(1)} collective-permute-done((bf16[256,896]{1,0:T(8,128)(2,1)S(1)}, bf16[256,896]{1,0:T(8,128)(2,1)S(1)}, u32[]{:S(2)}, u32[]{:S(2)}) %collective-permute-start.4) | collective-permute-done | bytes 458784 | tf_op jit(solution)/shard_map/ppermute | solution.py:252
  92.6 1.9 collective-permute-start.10
  94.5 5.4 %collective-permute-start.11 = (bf16[256,896]{1,0:T(8,128)(2,1)S(1)}, bf16[256,896]{1,0:T(8,128)(2,1)S(1)}, u32[]{:S(2)}, u32[]{:S(2)}) collective-permute-start(bf16[256,896]{1,0:T(8,128)(2,1)S(1)} %collective-permute-done.9.refs_1_), channel_id=1, source_target_pairs={{0,480},{32,0},{64,32},{96,64},{128,96},{160,128},{192,160},{224,1... | collective-permute-start | bytes 1376264 | tf_op jit(solution)/shard_map/ppermute | solution.py:253
  99.9 1.6 slice_bitcast_fusion.factors_ref
  101.5 0.6 pad_add_fusion.1.place_ref
  102.0 5.4 %gradient_side.1 = (bf16[16,512]{1,0:T(8,128)(2,1)}, f32[4,128,128]{2,1,0:T(8,128)}) custom-call(bf16[512,4096]{1,0:T(8,128)(2,1)} %all-gather.4.cloned.1.call-done.gradient_ref.rows_ref, bf16[16,4096]{1,0:T(8,128)(2,1)} %slice_bitcast_fusion.factors_ref), custom_call_target="tpu_custom_call" | custom-call | flops 603979776 | bytes 5242880 | tf_op jit(solution)/shard_map/gradient_side/pallas_call | solution.py:258
  107.5 6.4 %part_product.4.refs_4_ = f32[512,896]{1,0:T(8,128)} custom-call(s32[4]{0:T(128)} %pad_add_fusion.1.place_ref, bf16[512,4096]{1,0:T(8,128)(2,1)} %all-gather.4.cloned.1.call-done.gradient_ref.rows_ref, bf16[256,896]{1,0:T(8,128)(2,1)} %copy-done.7, bf16[256,896]{1,0:T(8,128)(2,1)} %copy-done.6, bf16[256,896]{1,0:T(8,128)(2,1)} %copy-done.9, ...), custom_call_target="tpu_custom_call" | custom-call | flops 939524096 | bytes 6291456 | tf_op jit(solution)/shard_map/part_product/pallas_call | solution.py:294
  113.8 0.0 collective-permute-done.10.refs_2_
  113.9 0.0 collective-permute-done.11.refs_3_
  113.9 1.9 collective-permute-start.12
  115.8 5.1 %collective-permute-start.13 = (bf16[256,896]{1,0:T(8,128)(2,1)S(1)}, bf16[256,896]{1,0:T(8,128)(2,1)S(1)}, u32[]{:S(2)}, u32[]{:S(2)}) collective-permute-start(bf16[256,896]{1,0:T(8,128)(2,1)S(1)} %collective-permute-done.11.refs_3_), channel_id=1, source_target_pairs={{0,480},{32,0},{64,32},{96,64},{128,96},{160,128},{192,160},{224,1... | collective-permute-start | bytes 1376264 | tf_op jit(solution)/shard_map/ppermute | solution.py:253
  121.0 0.6 pad_add_fusion.2.place_ref
  121.6 6.4 %part_product.5.refs_4_ = f32[512,896]{1,0:T(8,128)} custom-call(s32[4]{0:T(128)} %pad_add_fusion.2.place_ref, bf16[512,4096]{1,0:T(8,128)(2,1)} %all-gather.4.cloned.1.call-done.gradient_ref.rows_ref, bf16[256,896]{1,0:T(8,128)(2,1)} %copy-done.5, bf16[256,896]{1,0:T(8,128)(2,1)} %copy-done.4, bf16[256,896]{1,0:T(8,128)(2,1)} %copy-done.10, ...), custom_call_target="tpu_custom_call" | custom-call | flops 939524096 | bytes 6291456 | tf_op jit(solution)/shard_map/part_product/pallas_call | solution.py:294
  128.0 0.0 collective-permute-done.12.refs_0_
  128.1 0.8 collective-permute-done.13.refs_1_
  128.9 5.7 %collective-permute-start.15 = (bf16[128,896]{1,0:T(8,128)(2,1)S(1)}, bf16[128,896]{1,0:T(8,128)(2,1)S(1)}, u32[]{:S(2)}, u32[]{:S(2)}) collective-permute-start(bf16[128,896]{1,0:T(8,128)(2,1)S(1)} %slice.23), channel_id=1, source_target_pairs={{0,480},{32,0},{64,32},{96,64},{128,96},{160,128},{192,160},{224,1... | collective-permute-start | bytes 688136 | tf_op jit(solution)/shard_map/ppermute | solution.py:253
  134.6 1.9 collective-permute-start.14
  136.5 0.7 slice.24
  137.3 0.6 pad_add_fusion.place_ref
  137.9 5.6 %normed_side.1 = (bf16[32,512]{1,0:T(8,128)(2,1)}, f32[4,128,128]{2,1,0:T(8,128)}) custom-call(bf16[512,4096]{1,0:T(8,128)(2,1)} %all-gather.6.cloned.1.call-done.rows_ref, bf16[32,4096]{1,0:T(8,128)(2,1)} %bitcast.40), custom_call_target="tpu_custom_call" | custom-call | flops 671088640 | bytes 5242880 | tf_op jit(solution)/shard_map/normed_side/pallas_call | solution.py:258
  143.4 0.8 copy.13
  144.2 0.0 collective-permute-done.15.refs_3_
  144.2 0.0 collective-permute-done.14.refs_2_
  144.2 0.7 copy-done.17
  144.9 0.1 copy-done.18
  145.0 8.7 %hidden_side.1 = (f32[4,48,896]{2,1,0:T(8,128)}, f32[64,512]{1,0:T(8,128)}) custom-call(s32[4]{0:T(128)} %pad_add_fusion.place_ref, bf16[512,4096]{1,0:T(8,128)(2,1)} %all-gather.4.cloned.1.call-done.gradient_ref.rows_ref, bf16[256,896]{1,0:T(8,128)(2,1)} %copy-done.1, bf16[256,896]{1,0:T(8,128)(2,1)} %copy-done.2, bf16[128,896]{1,0:T(8,128)(2,1)} %copy-done.18, ...), custom_call_target="tpu_custom_call" | custom-call | tf_op jit(solution)/shard_map/hidden_side/pallas_call | solution.py:338
  153.6 10.9 %all_to_all.20 = f32[8,8,512]{2,1,0:T(8,128)S(1)} all-to-all(f32[8,8,512]{2,1,0:T(8,128)} %bitcast.44), channel_id=1, replica_groups=mesh['z'=16,'y'=4,'x'=4,'c'=2] {'x','c'}, dimensions={0} | all-to-all | bytes 262144 | tf_op jit(solution)/shard_map/all_to_all | solution.py:362
  164.6 0.7 broadcast_in_dim.6
  165.3 3.4 %all-to-all-start.1 = ((f32[8,8,512]{2,1,0:T(8,128)}), f32[8,8,512]{2,1,0:T(8,128)S(1)}, u32[]{:S(2)}, u32[]{:S(2)}) async-start(f32[8,8,512]{2,1,0:T(8,128)} %broadcast_in_dim.6), calls=%async_computation.1 | async-start | bytes 262144 | tf_op jit(solution)/shard_map/all_to_all | solution.py:364
  169.3 5.4 %all-to-all-done.1 = f32[8,8,512]{2,1,0:T(8,128)S(1)} async-done(((f32[8,8,512]{2,1,0:T(8,128)}), f32[8,8,512]{2,1,0:T(8,128)S(1)}, u32[]{:S(2)}, u32[]{:S(2)}) %all-to-all-start.1) | async-done | bytes 131104 | tf_op jit(solution)/shard_map/all_to_all | solution.py:364
  174.7 0.7 copy-done.3
  175.4 3.0 %clip_side.1 = f32[80,8,128]{2,1,0:T(8,128)} custom-call(f32[1]{0:T(128)} %copy.14.clip_ref, f32[64,512]{1,0:T(8,128)} %bitcast.42, f32[4,48,896]{2,1,0:T(8,128)} %get-tuple-element.31.sums_ref, bf16[512,512]{1,0:T(8,128)(2,1)} %normed_ref.1, bf16[512,512]{1,0:T(8,128)(2,1)} %gradient_ref.1, f32[4,128,128]{2,1,0:T(8,128)} %get-tuple-element.32.normed_gram_ref, ...), custom_call_target="tpu_custom_call" | custom-call | tf_op jit(solution)/shard_map/clip_side/pallas_call | solution.py:371
  178.3 30.7 %all_to_all.21 = f32[16,40,128]{2,1,0:T(8,128)S(1)} all-to-all(f32[16,40,128]{2,1,0:T(8,128)} %bitcast.36), channel_id=1, replica_groups=mesh['z'=16,'y'=4,'x'=4,'c'=2] {'z'}, dimensions={0} | all-to-all | bytes 655360 | tf_op jit(solution)/shard_map/all_to_all | solution.py:389
  209.0 11.9 %all-gather = f32[160,128]{1,0:T(8,128)S(1)} all-gather(f32[40,128]{1,0:T(8,128)S(1)} %reduce_sum.28), channel_id=2, replica_groups=mesh['z'=16,'y'=4,'x'=4,'c'=2] {'y'}, dimensions={0}, use_global_device_ids=true | all-gather | bytes 102400 | tf_op jit(solution)/shard_map/all_gather | solution.py:390
  221.0 25.7 %all_to_all.22 = f32[16,40,128]{2,1,0:T(8,128)S(1)} all-to-all(f32[16,40,128]{2,1,0:T(8,128)S(1)} %broadcast_in_dim.7), channel_id=1, replica_groups=mesh['z'=16,'y'=4,'x'=4,'c'=2] {'z'}, dimensions={0} | all-to-all | bytes 655360 | tf_op jit(solution)/shard_map/all_to_all | solution.py:391
  246.7 0.7 fusion.1
  247.4 0.7 fusion
  (49 shorter events, 0.2 us)
Async XLA Ops:
  7.2 76.0 %all-gather.4.cloned.1.call-start = ((), (), s32[]{:S(2)}) async-start(), calls=%async_computation.4 | async-start | bytes 4718592 | tf_op jit(solution)/shard_map/all_gather | solution.py:233
  7.9 130.0 %all-gather.6.cloned.1.call-start = ((), (), s32[]{:S(2)}) async-start(), calls=%async_computation.5 | async-start | bytes 4718592 | tf_op jit(solution)/shard_map/all_gather | solution.py:235
  22.0 61.1 %copy-start = (bf16[256,896]{1,0:T(8,128)(2,1)}, bf16[256,896]{1,0:T(8,128)(2,1)S(1)}, u32[]{:S(2)}) copy-start(bf16[256,896]{1,0:T(8,128)(2,1)S(1)} %all_gather.16.refs_0_) | copy-start | bytes 1376260
  22.0 12.8 %collective-permute-start.5 = (bf16[256,896]{1,0:T(8,128)(2,1)S(1)}, bf16[256,896]{1,0:T(8,128)(2,1)S(1)}, u32[]{:S(2)}, u32[]{:S(2)}) collective-permute-start(bf16[256,896]{1,0:T(8,128)(2,1)S(1)} %all_gather.16.refs_0_), channel_id=1, source_target_pairs={{0,480},{32,0},{64,32},{96,64},{128,96},{160,128},{192,160},{224,1... | collective-permute-start | bytes 1376264 | tf_op jit(solution)/shard_map/ppermute | solution.py:253
  28.9 15.1 %collective-permute-start = (bf16[256,896]{1,0:T(8,128)(2,1)S(1)}, bf16[256,896]{1,0:T(8,128)(2,1)S(1)}, u32[]{:S(2)}, u32[]{:S(2)}) collective-permute-start(bf16[256,896]{1,0:T(8,128)(2,1)S(1)} %all_gather.16.refs_0_), channel_id=1, source_target_pairs={{0,32},{32,64},{64,96},{96,128},{128,160},{160,192},{192,224},{224... | collective-permute-start | bytes 1376264 | tf_op jit(solution)/shard_map/ppermute | solution.py:252
  34.9 45.6 %copy-start.12 = (bf16[256,896]{1,0:T(8,128)(2,1)}, bf16[256,896]{1,0:T(8,128)(2,1)S(1)}, u32[]{:S(2)}) copy-start(bf16[256,896]{1,0:T(8,128)(2,1)S(1)} %collective-permute-done.5.refs_2_) | copy-start | bytes 1376260
  34.9 15.8 %collective-permute-start.6 = (bf16[256,896]{1,0:T(8,128)(2,1)S(1)}, bf16[256,896]{1,0:T(8,128)(2,1)S(1)}, u32[]{:S(2)}, u32[]{:S(2)}) collective-permute-start(bf16[256,896]{1,0:T(8,128)(2,1)S(1)} %collective-permute-done.5.refs_2_), channel_id=1, source_target_pairs={{0,480},{32,0},{64,32},{96,64},{128,96},{160,128},{192,160},{224,1... | collective-permute-start | bytes 1376264 | tf_op jit(solution)/shard_map/ppermute | solution.py:253
  44.0 38.4 %copy-start.13 = (bf16[256,896]{1,0:T(8,128)(2,1)}, bf16[256,896]{1,0:T(8,128)(2,1)S(1)}, u32[]{:S(2)}) copy-start(bf16[256,896]{1,0:T(8,128)(2,1)S(1)} %collective-permute-done.refs_1_) | copy-start | bytes 1376260
  44.0 12.9 %collective-permute-start.1 = (bf16[256,896]{1,0:T(8,128)(2,1)S(1)}, bf16[256,896]{1,0:T(8,128)(2,1)S(1)}, u32[]{:S(2)}, u32[]{:S(2)}) collective-permute-start(bf16[256,896]{1,0:T(8,128)(2,1)S(1)} %collective-permute-done.refs_1_), channel_id=1, source_target_pairs={{0,32},{32,64},{64,96},{96,128},{128,160},{160,192},{192,224},{224... | collective-permute-start | bytes 1376264 | tf_op jit(solution)/shard_map/ppermute | solution.py:252
  50.7 20.1 %copy-start.14 = (bf16[256,896]{1,0:T(8,128)(2,1)}, bf16[256,896]{1,0:T(8,128)(2,1)S(1)}, u32[]{:S(2)}) copy-start(bf16[256,896]{1,0:T(8,128)(2,1)S(1)} %collective-permute-done.6.refs_4_) | copy-start | bytes 1376260
  50.7 12.0 %collective-permute-start.7 = (bf16[256,896]{1,0:T(8,128)(2,1)S(1)}, bf16[256,896]{1,0:T(8,128)(2,1)S(1)}, u32[]{:S(2)}, u32[]{:S(2)}) collective-permute-start(bf16[256,896]{1,0:T(8,128)(2,1)S(1)} %collective-permute-done.6.refs_4_), channel_id=1, source_target_pairs={{0,480},{32,0},{64,32},{96,64},{128,96},{160,128},{192,160},{224,1... | collective-permute-start | bytes 1376264 | tf_op jit(solution)/shard_map/ppermute | solution.py:253
  56.9 23.1 %copy-start.15 = (bf16[256,896]{1,0:T(8,128)(2,1)}, bf16[256,896]{1,0:T(8,128)(2,1)S(1)}, u32[]{:S(2)}) copy-start(bf16[256,896]{1,0:T(8,128)(2,1)S(1)} %collective-permute-done.1.refs_3_) | copy-start | bytes 1376260
  56.9 12.0 %collective-permute-start.2 = (bf16[256,896]{1,0:T(8,128)(2,1)S(1)}, bf16[256,896]{1,0:T(8,128)(2,1)S(1)}, u32[]{:S(2)}, u32[]{:S(2)}) collective-permute-start(bf16[256,896]{1,0:T(8,128)(2,1)S(1)} %collective-permute-done.1.refs_3_), channel_id=1, source_target_pairs={{0,32},{32,64},{64,96},{96,128},{128,160},{160,192},{192,224},{224... | collective-permute-start | bytes 1376264 | tf_op jit(solution)/shard_map/ppermute | solution.py:252
  62.7 26.6 %copy-start.6 = (bf16[256,896]{1,0:T(8,128)(2,1)}, bf16[256,896]{1,0:T(8,128)(2,1)S(1)}, u32[]{:S(2)}) copy-start(bf16[256,896]{1,0:T(8,128)(2,1)S(1)} %collective-permute-done.7.refs_1_) | copy-start | bytes 1376260
  62.7 11.7 %collective-permute-start.8 = (bf16[256,896]{1,0:T(8,128)(2,1)S(1)}, bf16[256,896]{1,0:T(8,128)(2,1)S(1)}, u32[]{:S(2)}, u32[]{:S(2)}) collective-permute-start(bf16[256,896]{1,0:T(8,128)(2,1)S(1)} %collective-permute-done.7.refs_1_), channel_id=1, source_target_pairs={{0,480},{32,0},{64,32},{96,64},{128,96},{160,128},{192,160},{224,1... | collective-permute-start | bytes 1376264 | tf_op jit(solution)/shard_map/ppermute | solution.py:253
  68.9 20.4 %copy-start.7 = (bf16[256,896]{1,0:T(8,128)(2,1)}, bf16[256,896]{1,0:T(8,128)(2,1)S(1)}, u32[]{:S(2)}) copy-start(bf16[256,896]{1,0:T(8,128)(2,1)S(1)} %collective-permute-done.2.refs_0_) | copy-start | bytes 1376260
  68.9 11.6 %collective-permute-start.3 = (bf16[256,896]{1,0:T(8,128)(2,1)S(1)}, bf16[256,896]{1,0:T(8,128)(2,1)S(1)}, u32[]{:S(2)}, u32[]{:S(2)}) collective-permute-start(bf16[256,896]{1,0:T(8,128)(2,1)S(1)} %collective-permute-done.2.refs_0_), channel_id=1, source_target_pairs={{0,32},{32,64},{64,96},{96,128},{128,160},{160,192},{192,224},{224... | collective-permute-start | bytes 1376264 | tf_op jit(solution)/shard_map/ppermute | solution.py:252
  74.4 14.9 %copy-start.8 = (bf16[256,896]{1,0:T(8,128)(2,1)}, bf16[256,896]{1,0:T(8,128)(2,1)S(1)}, u32[]{:S(2)}) copy-start(bf16[256,896]{1,0:T(8,128)(2,1)S(1)} %collective-permute-done.8.refs_3_) | copy-start | bytes 1376260
  74.4 14.9 %collective-permute-start.9 = (bf16[256,896]{1,0:T(8,128)(2,1)S(1)}, bf16[256,896]{1,0:T(8,128)(2,1)S(1)}, u32[]{:S(2)}, u32[]{:S(2)}) collective-permute-start(bf16[256,896]{1,0:T(8,128)(2,1)S(1)} %collective-permute-done.8.refs_3_), channel_id=1, source_target_pairs={{0,480},{32,0},{64,32},{96,64},{128,96},{160,128},{192,160},{224,1... | collective-permute-start | bytes 1376264 | tf_op jit(solution)/shard_map/ppermute | solution.py:253
  80.5 8.8 %copy-start.9 = (bf16[256,896]{1,0:T(8,128)(2,1)}, bf16[256,896]{1,0:T(8,128)(2,1)S(1)}, u32[]{:S(2)}) copy-start(bf16[256,896]{1,0:T(8,128)(2,1)S(1)} %collective-permute-done.3.refs_2_) | copy-start | bytes 1376260
  80.5 12.1 %collective-permute-start.4 = (bf16[256,896]{1,0:T(8,128)(2,1)S(1)}, bf16[256,896]{1,0:T(8,128)(2,1)S(1)}, u32[]{:S(2)}, u32[]{:S(2)}) collective-permute-start(bf16[256,896]{1,0:T(8,128)(2,1)S(1)} %collective-permute-done.3.refs_2_), channel_id=1, source_target_pairs={{0,32},{32,64},{64,96},{96,128},{128,160},{160,192},{192,224},{224... | collective-permute-start | bytes 1376264 | tf_op jit(solution)/shard_map/ppermute | solution.py:252
  89.3 18.2 %copy-start.4 = (bf16[256,896]{1,0:T(8,128)(2,1)}, bf16[256,896]{1,0:T(8,128)(2,1)S(1)}, u32[]{:S(2)}) copy-start(bf16[256,896]{1,0:T(8,128)(2,1)S(1)} %collective-permute-done.9.refs_1_) | copy-start | bytes 1376260
  92.6 14.9 %copy-start.5 = (bf16[256,896]{1,0:T(8,128)(2,1)}, bf16[256,896]{1,0:T(8,128)(2,1)S(1)}, u32[]{:S(2)}) copy-start(bf16[256,896]{1,0:T(8,128)(2,1)S(1)} %collective-permute-done.4.refs_0_) | copy-start | bytes 1376260
  92.6 21.3 %collective-permute-start.10 = (bf16[256,896]{1,0:T(8,128)(2,1)S(1)}, bf16[256,896]{1,0:T(8,128)(2,1)S(1)}, u32[]{:S(2)}, u32[]{:S(2)}) collective-permute-start(bf16[256,896]{1,0:T(8,128)(2,1)S(1)} %collective-permute-done.4.refs_0_), channel_id=1, source_target_pairs={{0,32},{32,64},{64,96},{96,128},{128,160},{160,192},{192,224},{224... | collective-permute-start | bytes 1376264 | tf_op jit(solution)/shard_map/ppermute | solution.py:252
  94.5 19.4 %collective-permute-start.11 = (bf16[256,896]{1,0:T(8,128)(2,1)S(1)}, bf16[256,896]{1,0:T(8,128)(2,1)S(1)}, u32[]{:S(2)}, u32[]{:S(2)}) collective-permute-start(bf16[256,896]{1,0:T(8,128)(2,1)S(1)} %collective-permute-done.9.refs_1_), channel_id=1, source_target_pairs={{0,480},{32,0},{64,32},{96,64},{128,96},{160,128},{192,160},{224,1... | collective-permute-start | bytes 1376264 | tf_op jit(solution)/shard_map/ppermute | solution.py:253
  113.9 7.7 %copy-start.10 = (bf16[256,896]{1,0:T(8,128)(2,1)}, bf16[256,896]{1,0:T(8,128)(2,1)S(1)}, u32[]{:S(2)}) copy-start(bf16[256,896]{1,0:T(8,128)(2,1)S(1)} %collective-permute-done.10.refs_2_) | copy-start | bytes 1376260
  113.9 7.7 %copy-start.11 = (bf16[256,896]{1,0:T(8,128)(2,1)}, bf16[256,896]{1,0:T(8,128)(2,1)S(1)}, u32[]{:S(2)}) copy-start(bf16[256,896]{1,0:T(8,128)(2,1)S(1)} %collective-permute-done.11.refs_3_) | copy-start | bytes 1376260
  113.9 14.2 %collective-permute-start.12 = (bf16[256,896]{1,0:T(8,128)(2,1)S(1)}, bf16[256,896]{1,0:T(8,128)(2,1)S(1)}, u32[]{:S(2)}, u32[]{:S(2)}) collective-permute-start(bf16[256,896]{1,0:T(8,128)(2,1)S(1)} %collective-permute-done.10.refs_2_), channel_id=1, source_target_pairs={{0,32},{32,64},{64,96},{96,128},{128,160},{160,192},{192,224},{224... | collective-permute-start | bytes 1376264 | tf_op jit(solution)/shard_map/ppermute | solution.py:252
  115.8 13.0 %collective-permute-start.13 = (bf16[256,896]{1,0:T(8,128)(2,1)S(1)}, bf16[256,896]{1,0:T(8,128)(2,1)S(1)}, u32[]{:S(2)}, u32[]{:S(2)}) collective-permute-start(bf16[256,896]{1,0:T(8,128)(2,1)S(1)} %collective-permute-done.11.refs_3_), channel_id=1, source_target_pairs={{0,480},{32,0},{64,32},{96,64},{128,96},{160,128},{192,160},{224,1... | collective-permute-start | bytes 1376264 | tf_op jit(solution)/shard_map/ppermute | solution.py:253
  121.6 15.0 %copy-start.16 = (bf16[3,16,4096]{2,1,0:T(8,128)(2,1)S(1)}, bf16[3,16,4096]{2,1,0:T(8,128)(2,1)}, u32[]{:S(2)}) copy-start(bf16[3,16,4096]{2,1,0:T(8,128)(2,1)} %param.15) | copy-start | bytes 1179652
  128.0 15.4 %copy-start.1 = (bf16[256,896]{1,0:T(8,128)(2,1)}, bf16[256,896]{1,0:T(8,128)(2,1)S(1)}, u32[]{:S(2)}) copy-start(bf16[256,896]{1,0:T(8,128)(2,1)S(1)} %collective-permute-done.12.refs_0_) | copy-start | bytes 1376260
  128.8 14.6 %copy-start.2 = (bf16[256,896]{1,0:T(8,128)(2,1)}, bf16[256,896]{1,0:T(8,128)(2,1)S(1)}, u32[]{:S(2)}) copy-start(bf16[256,896]{1,0:T(8,128)(2,1)S(1)} %collective-permute-done.13.refs_1_) | copy-start | bytes 1376260
  128.9 15.3 %collective-permute-start.15 = (bf16[128,896]{1,0:T(8,128)(2,1)S(1)}, bf16[128,896]{1,0:T(8,128)(2,1)S(1)}, u32[]{:S(2)}, u32[]{:S(2)}) collective-permute-start(bf16[128,896]{1,0:T(8,128)(2,1)S(1)} %slice.23), channel_id=1, source_target_pairs={{0,480},{32,0},{64,32},{96,64},{128,96},{160,128},{192,160},{224,1... | collective-permute-start | bytes 688136 | tf_op jit(solution)/shard_map/ppermute | solution.py:253
  134.6 9.6 %collective-permute-start.14 = (bf16[128,896]{1,0:T(8,128)(2,1)S(1)}, bf16[128,896]{1,0:T(8,128)(2,1)S(1)}, u32[]{:S(2)}, u32[]{:S(2)}) collective-permute-start(bf16[128,896]{1,0:T(8,128)(2,1)S(1)} %slice.22), channel_id=1, source_target_pairs={{0,32},{32,64},{64,96},{96,128},{128,160},{160,192},{192,224},{224... | collective-permute-start | bytes 688136 | tf_op jit(solution)/shard_map/ppermute | solution.py:252
  137.9 5.6 %copy-start.21 = (bf16[16,512]{1,0:T(8,128)(2,1)S(1)}, bf16[16,512]{1,0:T(8,128)(2,1)}, u32[]{:S(2)}) copy-start(bf16[16,512]{1,0:T(8,128)(2,1)} %get-tuple-element.29.refs_10_) | copy-start | bytes 49156
  144.2 0.7 copy-start.17
  144.2 0.8 copy-start.18
  165.3 9.4 %all-to-all-start.1 = ((f32[8,8,512]{2,1,0:T(8,128)}), f32[8,8,512]{2,1,0:T(8,128)S(1)}, u32[]{:S(2)}, u32[]{:S(2)}) async-start(f32[8,8,512]{2,1,0:T(8,128)} %broadcast_in_dim.6), calls=%async_computation.1 | async-start | bytes 262144 | tf_op jit(solution)/shard_map/all_to_all | solution.py:364
  174.7 0.7 copy-start.3
  178.3 68.4 %copy-start.20 = (f32[3,16,512]{2,1,0:T(8,128)S(1)}, f32[3,16,512]{2,1,0:T(8,128)}, u32[]{:S(2)}) copy-start(f32[3,16,512]{2,1,0:T(8,128)} %param.18) | copy-start | bytes 294916
  178.3 69.0 %copy-start.19 = (f32[3,16,896]{2,1,0:T(8,128)S(1)}, f32[3,16,896]{2,1,0:T(8,128)}, u32[]{:S(2)}) copy-start(f32[3,16,896]{2,1,0:T(8,128)} %param.19) | copy-start | bytes 516100
Sparse Core Ops, SparseCore 0:
  10.1 43.8 all-gather.3
  56.2 39.7 all-gather.5

commit v5 on v4

--- a/solution.py
+++ b/solution.py
@@ -25,12 +25,26 @@
     whole = hidden // step
 
     def body(i, carry):
-        tile(pl.multiple_of(i * step, step), step)
+        tile(i, pl.multiple_of(i * step, step), step)
         return carry
 
     lax.fori_loop(0, whole, body, 0)
+    spans = [(i * step, step) for i in range(whole)]
     if hidden > whole * step:
-        tile(whole * step, hidden - whole * step)
+        spans.append((whole * step, hidden - whole * step))
+        tile(whole, *spans[-1])
+    return spans
+
+
+def copy_rows(source, target, sems, at, parts):
+    rows = source.shape[0] // parts
+    copies = []
+    for i in range(parts):
+        span = pl.ds(i * rows, rows)
+        copies.append(
+            pltpu.make_async_copy(source.at[span, :], target.at[span, :], sems.at[at + i])
+        )
+    return copies
 
 
 def fetch_blocks(place_ref, gradient_ref, block_refs, left, right, sems):
@@ -38,21 +52,16 @@
     for i, block in enumerate(block_refs):
         rows = block.shape[0]
         at = pl.ds(pl.multiple_of(place_ref[i] * 128, 128), rows)
-        copies.append(
-            pltpu.make_async_copy(
-                gradient_ref.at[:, at], left.at[:, pl.ds(row, rows)], sems.at[2 * i]
-            )
-        )
-        copies.append(
-            pltpu.make_async_copy(block, right.at[pl.ds(row, rows), :], sems.at[2 * i + 1])
-        )
+        span = pl.ds(row, rows)
+        copies += copy_rows(gradient_ref.at[:, at], left.at[:, span], sems, 4 * i, 2)
+        copies += copy_rows(block, right.at[span, :], sems, 4 * i + 2, 2)
         row += rows
-    for copy in copies:
-        copy.start()
     return copies
 
 
-def side_kernel(rows_ref, factors_ref, projected_ref, gram_ref, total):
+def side_kernel(n_rows, *refs):
+    row_refs = refs[:n_rows]
+    factors_ref, projected_ref, gram_ref, total = refs[n_rows:]
     step = pl.program_id(0)
 
     @pl.when(step == 0)
@@ -60,9 +69,10 @@
         total[...] = jnp.zeros_like(total)
         gram_ref[...] = jnp.zeros_like(gram_ref)
 
-    total[...] += contract(factors_ref[...], rows_ref[...], 1, 1)
-    for e in range(gram_ref.shape[0]):
-        rows = rows_ref[e * SEQUENCE_TOKENS : (e + 1) * SEQUENCE_TOKENS, :]
+    for e, rows_ref in enumerate(row_refs):
+        rows = rows_ref[...]
+        span = slice(e * SEQUENCE_TOKENS, (e + 1) * SEQUENCE_TOKENS)
+        total[:, span] += contract(factors_ref[...], rows, 1, 1)
         gram_ref[e] += contract(rows, rows, 1, 1)
 
     @pl.when(step == pl.num_programs(0) - 1)
@@ -72,38 +82,59 @@
 
 def part_kernel(n_blocks, first, place_ref, gradient_ref, *refs):
     block_refs = refs[:n_blocks]
-    if first:
-        total_ref, left, right, sems = refs[n_blocks:]
-    else:
-        before_ref, total_ref, left, right, sems = refs[n_blocks:]
-    for copy in fetch_blocks(place_ref, gradient_ref, block_refs, left, right, sems):
+    refs = refs[n_blocks:]
+    if not first:
+        before_ref, refs = refs[0], refs[1:]
+    out_ref, total, left, right, sems, out_sems = refs
+    copies = fetch_blocks(place_ref, gradient_ref, block_refs, left, right, sems)
+    if not first:
+        copies += copy_rows(before_ref, total, sems, 4 * n_blocks, 4)
+    for copy in copies:
+        copy.start()
+    for copy in copies:
         copy.wait()
 
-    def tile(start, width):
+    def write(i, cols):
+        return pltpu.make_async_copy(total.at[:, cols], out_ref.at[:, cols], out_sems.at[i])
+
+    def tile(i, start, width):
         cols = pl.ds(start, width)
         product = jnp.dot(left[...], right[:, cols], preferred_element_type=F32)
-        if first:
-            total_ref[:, cols] = product
-        else:
-            total_ref[:, cols] = before_ref[:, cols] + product
-
-    column_tiles(total_ref.shape[1], 256, tile)
+        total[:, cols] = product if first else total[:, cols] + product
+        write(i, cols).start()
+
+    for i, (start, width) in enumerate(column_tiles(total.shape[1], 256, tile)):
+        write(i, pl.ds(start, width)).wait()
 
 
 def hidden_kernel(n_blocks, place_ref, gradient_ref, *refs):
     block_refs = refs[:n_blocks]
-    (before_ref, gate_ref, up_ref, factors_ref, in_ref, lora_ref, lora_t_ref) = refs[
+    (before_hbm, gate_hbm, up_hbm, factors_ref, in_ref, lora_ref, lora_t_ref) = refs[
         n_blocks : n_blocks + 7
     ]
-    sums_ref, mids_ref, total, left_rows, right_rows, sems = refs[n_blocks + 7 :]
+    (sums_hbm, mids_ref, total, before_ref, gate_ref, up_ref, sums_ref, left_rows, right_rows) = (
+        refs[n_blocks + 7 : -2]
+    )
+    sems, out_sems = refs[-2:]
     tokens, hidden = gate_ref.shape
     sequences = tokens // SEQUENCE_TOKENS
     copies = fetch_blocks(place_ref, gradient_ref, block_refs, left_rows, right_rows, sems)
+    at = 4 * n_blocks
+    for source, target in ((before_hbm, before_ref), (gate_hbm, gate_ref), (up_hbm, up_ref)):
+        copies += copy_rows(source, target, sems, at, 4)
+        at += 4
+    for copy in copies:
+        copy.start()
     mids_ref[...] = jnp.zeros_like(mids_ref)
     for copy in copies:
         copy.wait()
 
-    def tile(start, width):
+    def write(i, cols):
+        return pltpu.make_async_copy(
+            sums_ref.at[:, :, cols], sums_hbm.at[:, :, cols], out_sems.at[i]
+        )
+
+    def tile(i, start, width):
         cols = pl.ds(start, width)
         factors = factors_ref[:, cols]
         total[:, :width] = (
@@ -129,12 +160,15 @@
                     left[j], right, preferred_element_type=F32
                 )
                 mids_ref[part, rows] += contract(factors[part], right, 1, 1)
-
-    column_tiles(hidden, 256, tile)
+        write(i, cols).start()
+
+    spans = column_tiles(hidden, 256, tile)
     for e in range(sequences):
         square = sums_ref[e] * sums_ref[e]
         line = jnp.sum(jnp.sum(square, axis=0, keepdims=True), axis=1, keepdims=True)
         mids_ref[3 * RANK + e : 3 * RANK + e + 1, :] = jnp.broadcast_to(line, (1, tokens))
+    for i, (start, width) in enumerate(spans):
+        write(i, pl.ds(start, width)).wait()
 
 
 def quadratic(left, gram):
@@ -256,16 +290,17 @@
         width = values.shape[1]
         chunk = 1024
         return pl.pallas_call(
-            side_kernel,
+            functools.partial(side_kernel, sequences),
             out_shape=(
                 jax.ShapeDtypeStruct((factors.shape[0], tokens), BF16),
                 jax.ShapeDtypeStruct((sequences, SEQUENCE_TOKENS, SEQUENCE_TOKENS), F32),
             ),
             grid=(width // chunk,),
             in_specs=[
-                pl.BlockSpec((tokens, chunk), lambda i: (0, i)),
-                pl.BlockSpec((factors.shape[0], chunk), lambda i: (0, i)),
-            ],
+                pl.BlockSpec((SEQUENCE_TOKENS, chunk), functools.partial(lambda e, i: (e, i), e))
+                for e in range(sequences)
+            ]
+            + [pl.BlockSpec((factors.shape[0], chunk), lambda i: (0, i))],
             out_specs=(
                 pl.BlockSpec((factors.shape[0], tokens), lambda i: (0, 0)),
                 pl.BlockSpec((sequences, SEQUENCE_TOKENS, SEQUENCE_TOKENS), lambda i: (0, 0, 0)),
@@ -278,13 +313,14 @@
                 transcendentals=0,
             ),
             name=name,
-        )(values, factors)
-
-    def scratch(n_rows, n_blocks):
+        )(*[values] * sequences, factors)
+
+    def scratch(n_rows, n_sems):
         return [
             pltpu.VMEM((tokens, n_rows), BF16),
             pltpu.VMEM((n_rows, hidden), BF16),
-            pltpu.SemaphoreType.DMA((2 * n_blocks,)),
+            pltpu.SemaphoreType.DMA((n_sems,)),
+            pltpu.SemaphoreType.DMA((-(-hidden // 256),)),
         ]
 
     def part(offsets, before=None):
@@ -294,9 +330,9 @@
         return pl.pallas_call(
             functools.partial(part_kernel, n, before is None),
             out_shape=jax.ShapeDtypeStruct((tokens, hidden), F32),
-            in_specs=[smem] + [hbm] * (n + 1) + [vmem] * len(given),
-            out_specs=vmem,
-            scratch_shapes=scratch(n * rows, n),
+            in_specs=[smem] + [hbm] * (n + 1 + len(given)),
+            out_specs=hbm,
+            scratch_shapes=[pltpu.VMEM((tokens, hidden), F32)] + scratch(n * rows, 4 * n + 4),
             compiler_params=params,
             cost_estimate=pl.CostEstimate(
                 flops=2 * tokens * n * rows * hidden,
@@ -314,19 +350,17 @@
         step(k, low[k - 1], high[k - 1])
     total = part([0] + pairs(1, last - 5))
     at = last - 3
-    low_in, high_in, total = lax.optimization_barrier((low[at], high[at], total))
-    step(last - 2, low_in, high_in)
+    high_in, total = lax.optimization_barrier((high[at], total))
+    step(last - 2, low[at], high_in)
     total = part(pairs(last - 5, last - 3), total)
     lora_t, gradient_gram = side(gradient, adapter_width_factors[2], "gradient_side")
     at = last - 2
-    low_in, high_in, total, lora_t = lax.optimization_barrier(
-        (low[at], high[at], total, lora_t)
-    )
-    step(last - 1, low_in, high_in)
+    high_in, total, lora_t = lax.optimization_barrier((high[at], total, lora_t))
+    step(last - 1, low[at], high_in)
     total = part(pairs(last - 3, last - 1), total)
     at = last - 1
-    low_in, high_in, total = lax.optimization_barrier((low[at], high[at], total))
-    step(last, low_in[:half], high_in[half:])
+    high_in, total = lax.optimization_barrier((high[at], total))
+    step(last, low[at][:half], high_in[half:])
     in_t, normed_gram = side(
         normed_all, adapter_width_factors[:2].reshape(2 * RANK, -1), "normed_side"
     )
@@ -341,9 +375,16 @@
             jax.ShapeDtypeStruct((sequences, 3 * RANK, hidden), F32),
             jax.ShapeDtypeStruct((8 * n_tensor, tokens), F32),
         ),
-        in_specs=[smem] + [hbm] * (len(blocks) + 1) + [vmem] * 7,
-        out_specs=(vmem, vmem),
-        scratch_shapes=[pltpu.VMEM((tokens, 256), F32)] + scratch(3 * rows, len(blocks)),
+        in_specs=[smem] + [hbm] * (len(blocks) + 4) + [vmem] * 4,
+        out_specs=(hbm, vmem),
+        scratch_shapes=[
+            pltpu.VMEM((tokens, 256), F32),
+            pltpu.VMEM((tokens, hidden), F32),
+            pltpu.VMEM((tokens, hidden), BF16),
+            pltpu.VMEM((tokens, hidden), BF16),
+            pltpu.VMEM((sequences, 3 * RANK, hidden), F32),
+        ]
+        + scratch(3 * rows, 4 * len(blocks) + 12),
         compiler_params=params,
         name="hidden_side",
     )(
@@ -367,7 +408,7 @@
 
     lanes = (local_width + hidden) // 128
     tiles = 6 * lanes
-    padded = -(-tiles // n_z) * n_z
+    padded = -(-tiles // 8) * 8
     out = pl.pallas_call(
         clip_kernel,
         out_shape=jax.ShapeDtypeStruct((padded, 8, 128), F32),
@@ -386,11 +427,13 @@
         gradient_gram,
     )
 
-    part_sum = jnp.sum(lax.all_to_all(out.reshape(n_z, -1, 128), z_axes, 0, 0), axis=0)
-    part_sum = jnp.sum(lax.all_gather(part_sum, "y", axis=0), axis=0)
-    whole = lax.all_to_all(
-        jnp.broadcast_to(part_sum, (n_z,) + part_sum.shape), z_axes, 0, 0
-    )
+    n_y = sizes["y"]
+    share = jnp.sum(lax.all_to_all(out.reshape(n_y, -1, 128), "y", 0, 0), axis=0)
+    share = jnp.sum(lax.all_to_all(share.reshape(n_z, -1, 128), z_axes, 0, 0), axis=0)
+    share = lax.all_to_all(
+        jnp.broadcast_to(share, (n_z,) + share.shape), z_axes, 0, 0
+    ).reshape(-1, 128)
+    whole = lax.all_to_all(jnp.broadcast_to(share, (n_y,) + share.shape), "y", 0, 0)
     total = (
         whole.reshape(padded, 8, 128)[:tiles]
         .reshape(6, lanes, 8, 128)

time: 256 us -> 251 us (0.980)
  blocking collectives: 92.6 us -> 87.6 us
    ppermute x8, waiting for transfers between devices: 5.22 us -> 24.7 us  [step(): low[k] = lax.ppermute(low_from, z_axes, ring(n_z, 1))]
    ppermute x8, waiting for transfers between devices: 17 us -> 0.02 us  [step(): high[k] = lax.ppermute(high_from, z_axes, ring(n_z, -1))]
    all_gather x1 -> x0, blocking collectives: 11.9 us -> none  [per_device(): part_sum = jnp.sum(lax.all_gather(part_sum, 'y', axis=0), axis=0)]
    all_to_all x2 -> x4, blocking collectives: 56.4 us -> 63.5 us  [the longest x1 25 us: per_device(): lax.all_to_all(share.reshape(n_z, -1, 128), z_axes, 0, 0)]
    ppermute x8, starting transfers between devices: 48.7 us -> 43.3 us  [step(): high[k] = lax.ppermute(high_from, z_axes, ring(n_z, -1))]
    ppermute x8, starting transfers between devices: 15.3 us -> 18.4 us  [step(): low[k] = lax.ppermute(low_from, z_axes, ring(n_z, 1))]
  transfers between devices with their start and end apart: 19 -> 19, of which waited for: 11 -> 6; matrix products, arithmetic and copies ran while one was open for 2% -> 2% of each run, Pallas kernels for 12% -> 12%
where the time goes in v5:
time: 251 us; the launch traced here: 250 us
  blocking collectives  87.6 us (35%)
  starting transfers between devices  65.1 us (26%)
  Pallas kernels  41.1 us (16%)
  waiting for transfers between devices  31.5 us (13%)
  between operations  15.3 us (6%)
  local copies, waits for them, and re-layouts  5.91 us (2%)
  other arithmetic  3.34 us (1%)
    ppermute x8, starting transfers between devices, step(): high[k] = lax.ppermute(high_from, z_axes, ring(n_z, -1))  43.3 us
    all_to_all x1, blocking collectives, per_device(): lax.all_to_all(share.reshape(n_z, -1, 128), z_axes, 0, 0)  25 us
    ppermute x8, waiting for transfers between devices, step(): low[k] = lax.ppermute(low_from, z_axes, ring(n_z, 1))  24.7 us
    ppermute x8, starting transfers between devices, step(): low[k] = lax.ppermute(low_from, z_axes, ring(n_z, 1))  18.4 us
    pallas_call x3, Pallas kernels, part(): pl.pallas_call(functools.partial(part_kernel, n, before is None), out_sha...  17.4 us
    all_to_all x1, blocking collectives, per_device(): lax.all_to_all(jnp.broadcast_to(share, (n_z,) + share.shape), z_axes, 0, 0)  17 us
    all_gather x1, blocking collectives, per_device(): block = lax.all_gather(frozen_down_weight.T, 'y', axis=0, tiled=True)  13.4 us
    all_to_all x1, blocking collectives, per_device(): lax.all_to_all(out.reshape(n_y, -1, 128), 'y', 0, 0)  12.3 us
  transfers between devices with their start and end apart: 19, of which 6 were waited for; matrix products, arithmetic and copies ran while one was open for 2% of the time, Pallas kernels for 12%

profile of v5, /device:TPU:32, one launch (start us, length us, event | category | flops | bytes accessed | tf_op | source)
XLA Modules:
  0.0 249.9 jit_solution(17960510597331073440)
XLA Ops:
  7.2 0.0 all-gather.3.cloned.1.call-start
  7.2 0.7 all-gather.3.cloned.1.call-update
  7.9 0.0 all-gather.5.cloned.1.call-start
  7.9 0.7 all-gather.5.cloned.1.call-update
  8.6 13.4 %all_gather.10.refs_0_ = bf16[256,896]{1,0:T(8,128)(2,1)S(1)} all-gather(bf16[64,896]{1,0:T(8,128)(2,1)} %bitcast.43), channel_id=1, replica_groups=mesh['z'=16,'y'=4,'x'=4,'c'=2] {'y'}, dimensions={0}, use_global_device_ids=true | all-gather | bytes 573440 | tf_op jit(solution)/shard_map/all_gather | solution.py:268
  22.0 3.8 %collective-permute-start = (bf16[256,896]{1,0:T(8,128)(2,1)S(1)}, bf16[256,896]{1,0:T(8,128)(2,1)S(1)}, u32[]{:S(2)}, u32[]{:S(2)}) collective-permute-start(bf16[256,896]{1,0:T(8,128)(2,1)S(1)} %all_gather.10.refs_0_), channel_id=1, source_target_pairs={{0,32},{32,64},{64,96},{96,128},{128,160},{160,192},{192,224},{224... | collective-permute-start | bytes 1376264 | tf_op jit(solution)/shard_map/ppermute | solution.py:286
  25.9 5.0 %collective-permute-start.7 = (bf16[256,896]{1,0:T(8,128)(2,1)S(1)}, bf16[256,896]{1,0:T(8,128)(2,1)S(1)}, u32[]{:S(2)}, u32[]{:S(2)}) collective-permute-start(bf16[256,896]{1,0:T(8,128)(2,1)S(1)} %all_gather.10.refs_0_), channel_id=1, source_target_pairs={{0,480},{32,0},{64,32},{96,64},{128,96},{160,128},{192,160},{224,1... | collective-permute-start | bytes 1376264 | tf_op jit(solution)/shard_map/ppermute | solution.py:287
  30.8 4.5 %collective-permute-done.refs_1_ = bf16[256,896]{1,0:T(8,128)(2,1)S(1)} collective-permute-done((bf16[256,896]{1,0:T(8,128)(2,1)S(1)}, bf16[256,896]{1,0:T(8,128)(2,1)S(1)}, u32[]{:S(2)}, u32[]{:S(2)}) %collective-permute-start) | collective-permute-done | bytes 458784 | tf_op jit(solution)/shard_map/ppermute | solution.py:286
  35.3 3.0 %collective-permute-start.1 = (bf16[256,896]{1,0:T(8,128)(2,1)S(1)}, bf16[256,896]{1,0:T(8,128)(2,1)S(1)}, u32[]{:S(2)}, u32[]{:S(2)}) collective-permute-start(bf16[256,896]{1,0:T(8,128)(2,1)S(1)} %collective-permute-done.refs_1_), channel_id=1, source_target_pairs={{0,32},{32,64},{64,96},{96,128},{128,160},{160,192},{192,224},{224... | collective-permute-start | bytes 1376264 | tf_op jit(solution)/shard_map/ppermute | solution.py:286
  38.3 0.0 collective-permute-done.7.refs_2_
  38.3 7.9 %collective-permute-start.8 = (bf16[256,896]{1,0:T(8,128)(2,1)S(1)}, bf16[256,896]{1,0:T(8,128)(2,1)S(1)}, u32[]{:S(2)}, u32[]{:S(2)}) collective-permute-start(bf16[256,896]{1,0:T(8,128)(2,1)S(1)} %collective-permute-done.7.refs_2_), channel_id=1, source_target_pairs={{0,480},{32,0},{64,32},{96,64},{128,96},{160,128},{192,160},{224,1... | collective-permute-start | bytes 1376264 | tf_op jit(solution)/shard_map/ppermute | solution.py:287
  46.2 6.3 %collective-permute-done.1.refs_3_ = bf16[256,896]{1,0:T(8,128)(2,1)S(1)} collective-permute-done((bf16[256,896]{1,0:T(8,128)(2,1)S(1)}, bf16[256,896]{1,0:T(8,128)(2,1)S(1)}, u32[]{:S(2)}, u32[]{:S(2)}) %collective-permute-start.1) | collective-permute-done | bytes 458784 | tf_op jit(solution)/shard_map/ppermute | solution.py:286
  52.5 1.9 collective-permute-start.2
  54.5 0.0 collective-permute-done.8.refs_4_
  54.5 4.9 %collective-permute-start.9 = (bf16[256,896]{1,0:T(8,128)(2,1)S(1)}, bf16[256,896]{1,0:T(8,128)(2,1)S(1)}, u32[]{:S(2)}, u32[]{:S(2)}) collective-permute-start(bf16[256,896]{1,0:T(8,128)(2,1)S(1)} %collective-permute-done.8.refs_4_), channel_id=1, source_target_pairs={{0,480},{32,0},{64,32},{96,64},{128,96},{160,128},{192,160},{224,1... | collective-permute-start | bytes 1376264 | tf_op jit(solution)/shard_map/ppermute | solution.py:287
  59.3 5.5 %collective-permute-done.2.refs_0_ = bf16[256,896]{1,0:T(8,128)(2,1)S(1)} collective-permute-done((bf16[256,896]{1,0:T(8,128)(2,1)S(1)}, bf16[256,896]{1,0:T(8,128)(2,1)S(1)}, u32[]{:S(2)}, u32[]{:S(2)}) %collective-permute-start.2) | collective-permute-done | bytes 458784 | tf_op jit(solution)/shard_map/ppermute | solution.py:286
  64.8 1.9 collective-permute-start.3
  66.8 0.0 collective-permute-done.9.refs_1_
  66.8 4.9 %collective-permute-start.10 = (bf16[256,896]{1,0:T(8,128)(2,1)S(1)}, bf16[256,896]{1,0:T(8,128)(2,1)S(1)}, u32[]{:S(2)}, u32[]{:S(2)}) collective-permute-start(bf16[256,896]{1,0:T(8,128)(2,1)S(1)} %collective-permute-done.9.refs_1_), channel_id=1, source_target_pairs={{0,480},{32,0},{64,32},{96,64},{128,96},{160,128},{192,160},{224,1... | collective-permute-start | bytes 1376264 | tf_op jit(solution)/shard_map/ppermute | solution.py:287
  71.6 4.6 %collective-permute-done.3.refs_2_ = bf16[256,896]{1,0:T(8,128)(2,1)S(1)} collective-permute-done((bf16[256,896]{1,0:T(8,128)(2,1)S(1)}, bf16[256,896]{1,0:T(8,128)(2,1)S(1)}, u32[]{:S(2)}, u32[]{:S(2)}) %collective-permute-start.3) | collective-permute-done | bytes 458784 | tf_op jit(solution)/shard_map/ppermute | solution.py:286
  76.2 1.9 collective-permute-start.4
  78.2 0.0 collective-permute-done.10.refs_3_
  78.2 5.0 %collective-permute-start.11 = (bf16[256,896]{1,0:T(8,128)(2,1)S(1)}, bf16[256,896]{1,0:T(8,128)(2,1)S(1)}, u32[]{:S(2)}, u32[]{:S(2)}) collective-permute-start(bf16[256,896]{1,0:T(8,128)(2,1)S(1)} %collective-permute-done.10.refs_3_), channel_id=1, source_target_pairs={{0,480},{32,0},{64,32},{96,64},{128,96},{160,128},{192,160},{224,1... | collective-permute-start | bytes 1376264 | tf_op jit(solution)/shard_map/ppermute | solution.py:287
  83.3 0.6 stack.69.place_ref
  83.9 3.8 %collective-permute-done.4.refs_0_ = bf16[256,896]{1,0:T(8,128)(2,1)S(1)} collective-permute-done((bf16[256,896]{1,0:T(8,128)(2,1)S(1)}, bf16[256,896]{1,0:T(8,128)(2,1)S(1)}, u32[]{:S(2)}, u32[]{:S(2)}) %collective-permute-start.4) | collective-permute-done | bytes 458784 | tf_op jit(solution)/shard_map/ppermute | solution.py:286
  87.7 1.9 collective-permute-start.5
  89.6 0.0 all-gather.3.cloned.1.call-done.gradient_ref.refs_0_.refs_1_.refs_2_.refs_3_
  89.7 5.8 %part_product.3.refs_4_ = f32[512,896]{1,0:T(8,128)} custom-call(s32[5]{0:T(128)} %stack.69.place_ref, bf16[512,4096]{1,0:T(8,128)(2,1)} %all-gather.3.cloned.1.call-done.gradient_ref.refs_0_.refs_1_.refs_2_.refs_3_, bf16[256,896]{1,0:T(8,128)(2,1)} %copy-done, bf16[256,896]{1,0:T(8,128)(2,1)} %copy-done.11, bf16[256,896]{1,0:T(8,128)(2,1)} %copy-done.12, ...), custom_call_target="tpu_custom_call" | custom-call | flops 1174405120 | bytes 6291456 | tf_op jit(solution)/shard_map/part_product/pallas_call | solution.py:330
  95.5 0.0 collective-permute-done.11.refs_1_
  95.5 5.4 %collective-permute-start.12 = (bf16[256,896]{1,0:T(8,128)(2,1)S(1)}, bf16[256,896]{1,0:T(8,128)(2,1)S(1)}, u32[]{:S(2)}, u32[]{:S(2)}) collective-permute-start(bf16[256,896]{1,0:T(8,128)(2,1)S(1)} %collective-permute-done.11.refs_1_), channel_id=1, source_target_pairs={{0,480},{32,0},{64,32},{96,64},{128,96},{160,128},{192,160},{224,1... | collective-permute-start | bytes 1376264 | tf_op jit(solution)/shard_map/ppermute | solution.py:287
  101.0 1.6 slice_bitcast_fusion.refs_4_
  102.5 0.7 pad_add_fusion.1.place_ref
  103.2 0.0 collective-permute-done.5.refs_2_
  103.2 1.9 collective-permute-start.6
  105.1 5.6 %gradient_side.1 = (bf16[16,512]{1,0:T(8,128)(2,1)}, f32[4,128,128]{2,1,0:T(8,128)}) custom-call(bf16[512,4096]{1,0:T(8,128)(2,1)} %all-gather.3.cloned.1.call-done.gradient_ref.refs_0_.refs_1_.refs_2_.refs_3_, bf16[512,4096]{1,0:T(8,128)(2,1)} %all-gather.3.cloned.1.call-done.gradient_ref.refs_0_.refs_1_.refs_2_.refs_3_, ...), custom_call_target="tpu_custom_call" | custom-call | flops 603979776 | bytes 5242880 | tf_op jit(solution)/shard_map/gradient_side/pallas_call | solution.py:292
  110.7 5.8 %part_product.4.refs_4_ = f32[512,896]{1,0:T(8,128)} custom-call(s32[4]{0:T(128)} %pad_add_fusion.1.place_ref, bf16[512,4096]{1,0:T(8,128)(2,1)} %all-gather.3.cloned.1.call-done.gradient_ref.refs_0_.refs_1_.refs_2_.refs_3_, bf16[256,896]{1,0:T(8,128)(2,1)} %copy-done.6, bf16[256,896]{1,0:T(8,128)(2,1)} %copy-done.7, bf16[256,896]{1,0:T(8,128)(2,1)} %copy-done.8, ...), custom_call_target="tpu_custom_call" | custom-call | flops 939524096 | bytes 6291456 | tf_op jit(solution)/shard_map/part_product/pallas_call | solution.py:330
  116.6 0.0 collective-permute-done.12.refs_3_
  116.6 5.1 %collective-permute-start.13 = (bf16[256,896]{1,0:T(8,128)(2,1)S(1)}, bf16[256,896]{1,0:T(8,128)(2,1)S(1)}, u32[]{:S(2)}, u32[]{:S(2)}) collective-permute-start(bf16[256,896]{1,0:T(8,128)(2,1)S(1)} %collective-permute-done.12.refs_3_), channel_id=1, source_target_pairs={{0,480},{32,0},{64,32},{96,64},{128,96},{160,128},{192,160},{224,1... | collective-permute-start | bytes 1376264 | tf_op jit(solution)/shard_map/ppermute | solution.py:287
  121.8 0.6 pad_add_fusion.2.place_ref
  122.4 0.0 copy-start.15
  122.4 2.1 collective-permute-start.14
  124.5 5.8 %part_product.5.refs_4_ = f32[512,896]{1,0:T(8,128)} custom-call(s32[4]{0:T(128)} %pad_add_fusion.2.place_ref, bf16[512,4096]{1,0:T(8,128)(2,1)} %all-gather.3.cloned.1.call-done.gradient_ref.refs_0_.refs_1_.refs_2_.refs_3_, bf16[256,896]{1,0:T(8,128)(2,1)} %copy-done.4, bf16[256,896]{1,0:T(8,128)(2,1)} %copy-done.5, ...), custom_call_target="tpu_custom_call" | custom-call | flops 939524096 | bytes 6291456 | tf_op jit(solution)/shard_map/part_product/pallas_call | solution.py:330
  130.3 0.0 collective-permute-done.13.refs_1_
  130.4 5.1 %collective-permute-start.15 = (bf16[128,896]{1,0:T(8,128)(2,1)S(1)}, bf16[128,896]{1,0:T(8,128)(2,1)S(1)}, u32[]{:S(2)}, u32[]{:S(2)}) collective-permute-start(bf16[128,896]{1,0:T(8,128)(2,1)S(1)} %slice.23), channel_id=1, source_target_pairs={{0,480},{32,0},{64,32},{96,64},{128,96},{160,128},{192,160},{224,1... | collective-permute-start | bytes 688136 | tf_op jit(solution)/shard_map/ppermute | solution.py:287
  135.6 0.7 slice.24
  136.3 0.7 pad_add_fusion.place_ref
  137.0 5.8 %normed_side.1 = (bf16[32,512]{1,0:T(8,128)(2,1)}, f32[4,128,128]{2,1,0:T(8,128)}) custom-call(bf16[512,4096]{1,0:T(8,128)(2,1)} %all-gather.5.cloned.1.call-done.refs_0_.refs_1_.refs_2_.refs_3_, bf16[512,4096]{1,0:T(8,128)(2,1)} %all-gather.5.cloned.1.call-done.refs_0_.refs_1_.refs_2_.refs_3_, ...), custom_call_target="tpu_custom_call" | custom-call | flops 671088640 | bytes 5242880 | tf_op jit(solution)/shard_map/normed_side/pallas_call | solution.py:292
  142.7 0.8 copy.13
  143.5 0.0 collective-permute-done.15.refs_3_
  143.5 0.7 copy-done.16
  144.2 0.1 copy-done.17
  144.2 9.4 %hidden_side.1 = (f32[4,48,896]{2,1,0:T(8,128)}, f32[64,512]{1,0:T(8,128)}) custom-call(s32[4]{0:T(128)} %pad_add_fusion.place_ref, bf16[512,4096]{1,0:T(8,128)(2,1)} %all-gather.3.cloned.1.call-done.gradient_ref.refs_0_.refs_1_.refs_2_.refs_3_, bf16[256,896]{1,0:T(8,128)(2,1)} %copy-done.1, bf16[256,896]{1,0:T(8,128)(2,1)} %copy-done.2, ...), custom_call_target="tpu_custom_call" | custom-call | tf_op jit(solution)/shard_map/hidden_side/pallas_call | solution.py:372
  153.6 10.7 %all_to_all.30 = f32[8,8,512]{2,1,0:T(8,128)S(1)} all-to-all(f32[8,8,512]{2,1,0:T(8,128)} %bitcast.42), channel_id=1, replica_groups=mesh['z'=16,'y'=4,'x'=4,'c'=2] {'x','c'}, dimensions={0} | all-to-all | bytes 262144 | tf_op jit(solution)/shard_map/all_to_all | solution.py:403
  164.4 0.7 broadcast_in_dim.9
  165.0 3.4 %all-to-all-start.1 = ((f32[8,8,512]{2,1,0:T(8,128)}), f32[8,8,512]{2,1,0:T(8,128)S(1)}, u32[]{:S(2)}, u32[]{:S(2)}) async-start(f32[8,8,512]{2,1,0:T(8,128)} %broadcast_in_dim.9), calls=%async_computation.1 | async-start | bytes 262144 | tf_op jit(solution)/shard_map/all_to_all | solution.py:405
  169.1 5.4 %all-to-all-done.1 = f32[8,8,512]{2,1,0:T(8,128)S(1)} async-done(((f32[8,8,512]{2,1,0:T(8,128)}), f32[8,8,512]{2,1,0:T(8,128)S(1)}, u32[]{:S(2)}, u32[]{:S(2)}) %all-to-all-start.1) | async-done | bytes 131104 | tf_op jit(solution)/shard_map/all_to_all | solution.py:405
  174.5 0.7 copy-done.3
  175.1 2.9 %clip_side.1 = f32[72,8,128]{2,1,0:T(8,128)} custom-call(f32[1]{0:T(128)} %copy.14.clip_ref, f32[64,512]{1,0:T(8,128)} %bitcast.41, f32[4,48,896]{2,1,0:T(8,128)} %get-tuple-element.25.sums_ref, bf16[512,512]{1,0:T(8,128)(2,1)} %normed_ref.1, bf16[512,512]{1,0:T(8,128)(2,1)} %gradient_ref.1, f32[4,128,128]{2,1,0:T(8,128)} %get-tuple-element.26.normed_gram_ref, ...), custom_call_target="tpu_custom_call" | custom-call | tf_op jit(solution)/shard_map/clip_side/pallas_call | solution.py:412
  178.1 12.3 %all_to_all.31 = f32[4,144,128]{2,1,0:T(8,128)S(1)} all-to-all(f32[4,144,128]{2,1,0:T(8,128)} %bitcast.35), channel_id=1, replica_groups=mesh['z'=16,'y'=4,'x'=4,'c'=2] {'y'}, dimensions={0} | all-to-all | bytes 589824 | tf_op jit(solution)/shard_map/all_to_all | solution.py:431
  190.4 25.0 %all_to_all.32 = f32[16,9,128]{2,1,0:T(8,128)S(1)} all-to-all(f32[16,9,128]{2,1,0:T(8,128)S(1)} %reshape.39), channel_id=1, replica_groups=mesh['z'=16,'y'=4,'x'=4,'c'=2] {'z'}, dimensions={0} | all-to-all | bytes 147456 | tf_op jit(solution)/shard_map/all_to_all | solution.py:432
  215.4 17.0 %all_to_all.33 = f32[16,9,128]{2,1,0:T(8,128)S(1)} all-to-all(f32[16,9,128]{2,1,0:T(8,128)S(1)} %broadcast_in_dim.10), channel_id=1, replica_groups=mesh['z'=16,'y'=4,'x'=4,'c'=2] {'z'}, dimensions={0} | all-to-all | bytes 147456 | tf_op jit(solution)/shard_map/all_to_all | solution.py:433
  232.5 9.2 %all_to_all.34 = f32[4,144,128]{2,1,0:T(8,128)S(1)} all-to-all(f32[4,144,128]{2,1,0:T(8,128)S(1)} %broadcast_in_dim.11), channel_id=1, replica_groups=mesh['z'=16,'y'=4,'x'=4,'c'=2] {'y'}, dimensions={0} | all-to-all | bytes 589824 | tf_op jit(solution)/shard_map/all_to_all | solution.py:436
  241.7 0.7 fusion.1
  242.4 0.7 fusion
  (51 shorter events, 0.2 us)
Async XLA Ops:
  7.2 82.5 %all-gather.3.cloned.1.call-start = ((), (), s32[]{:S(2)}) async-start(), calls=%async_computation.6 | async-start | bytes 4718592 | tf_op jit(solution)/shard_map/all_gather | solution.py:267
  7.9 129.1 %all-gather.5.cloned.1.call-start = ((), (), s32[]{:S(2)}) async-start(), calls=%async_computation.7 | async-start | bytes 4718592 | tf_op jit(solution)/shard_map/all_gather | solution.py:269
  22.0 67.6 %copy-start = (bf16[256,896]{1,0:T(8,128)(2,1)}, bf16[256,896]{1,0:T(8,128)(2,1)S(1)}, u32[]{:S(2)}) copy-start(bf16[256,896]{1,0:T(8,128)(2,1)S(1)} %all_gather.10.refs_0_) | copy-start | bytes 1376260
  22.0 13.3 %collective-permute-start = (bf16[256,896]{1,0:T(8,128)(2,1)S(1)}, bf16[256,896]{1,0:T(8,128)(2,1)S(1)}, u32[]{:S(2)}, u32[]{:S(2)}) collective-permute-start(bf16[256,896]{1,0:T(8,128)(2,1)S(1)} %all_gather.10.refs_0_), channel_id=1, source_target_pairs={{0,32},{32,64},{64,96},{96,128},{128,160},{160,192},{192,224},{224... | collective-permute-start | bytes 1376264 | tf_op jit(solution)/shard_map/ppermute | solution.py:286
  25.9 12.5 %collective-permute-start.7 = (bf16[256,896]{1,0:T(8,128)(2,1)S(1)}, bf16[256,896]{1,0:T(8,128)(2,1)S(1)}, u32[]{:S(2)}, u32[]{:S(2)}) collective-permute-start(bf16[256,896]{1,0:T(8,128)(2,1)S(1)} %all_gather.10.refs_0_), channel_id=1, source_target_pairs={{0,480},{32,0},{64,32},{96,64},{128,96},{160,128},{192,160},{224,1... | collective-permute-start | bytes 1376264 | tf_op jit(solution)/shard_map/ppermute | solution.py:287
  35.3 42.8 %copy-start.11 = (bf16[256,896]{1,0:T(8,128)(2,1)}, bf16[256,896]{1,0:T(8,128)(2,1)S(1)}, u32[]{:S(2)}) copy-start(bf16[256,896]{1,0:T(8,128)(2,1)S(1)} %collective-permute-done.refs_1_) | copy-start | bytes 1376260
  35.3 17.2 %collective-permute-start.1 = (bf16[256,896]{1,0:T(8,128)(2,1)S(1)}, bf16[256,896]{1,0:T(8,128)(2,1)S(1)}, u32[]{:S(2)}, u32[]{:S(2)}) collective-permute-start(bf16[256,896]{1,0:T(8,128)(2,1)S(1)} %collective-permute-done.refs_1_), channel_id=1, source_target_pairs={{0,32},{32,64},{64,96},{96,128},{128,160},{160,192},{192,224},{224... | collective-permute-start | bytes 1376264 | tf_op jit(solution)/shard_map/ppermute | solution.py:286
  38.3 44.9 %copy-start.12 = (bf16[256,896]{1,0:T(8,128)(2,1)}, bf16[256,896]{1,0:T(8,128)(2,1)S(1)}, u32[]{:S(2)}) copy-start(bf16[256,896]{1,0:T(8,128)(2,1)S(1)} %collective-permute-done.7.refs_2_) | copy-start | bytes 1376260
  38.3 16.1 %collective-permute-start.8 = (bf16[256,896]{1,0:T(8,128)(2,1)S(1)}, bf16[256,896]{1,0:T(8,128)(2,1)S(1)}, u32[]{:S(2)}, u32[]{:S(2)}) collective-permute-start(bf16[256,896]{1,0:T(8,128)(2,1)S(1)} %collective-permute-done.7.refs_2_), channel_id=1, source_target_pairs={{0,480},{32,0},{64,32},{96,64},{128,96},{160,128},{192,160},{224,1... | collective-permute-start | bytes 1376264 | tf_op jit(solution)/shard_map/ppermute | solution.py:287
  52.5 19.1 %copy-start.13 = (bf16[256,896]{1,0:T(8,128)(2,1)}, bf16[256,896]{1,0:T(8,128)(2,1)S(1)}, u32[]{:S(2)}) copy-start(bf16[256,896]{1,0:T(8,128)(2,1)S(1)} %collective-permute-done.1.refs_3_) | copy-start | bytes 1376260
  52.5 12.3 %collective-permute-start.2 = (bf16[256,896]{1,0:T(8,128)(2,1)S(1)}, bf16[256,896]{1,0:T(8,128)(2,1)S(1)}, u32[]{:S(2)}, u32[]{:S(2)}) collective-permute-start(bf16[256,896]{1,0:T(8,128)(2,1)S(1)} %collective-permute-done.1.refs_3_), channel_id=1, source_target_pairs={{0,32},{32,64},{64,96},{96,128},{128,160},{160,192},{192,224},{224... | collective-permute-start | bytes 1376264 | tf_op jit(solution)/shard_map/ppermute | solution.py:286
  54.5 23.7 %copy-start.14 = (bf16[256,896]{1,0:T(8,128)(2,1)}, bf16[256,896]{1,0:T(8,128)(2,1)S(1)}, u32[]{:S(2)}) copy-start(bf16[256,896]{1,0:T(8,128)(2,1)S(1)} %collective-permute-done.8.refs_4_) | copy-start | bytes 1376260
  54.5 12.3 %collective-permute-start.9 = (bf16[256,896]{1,0:T(8,128)(2,1)S(1)}, bf16[256,896]{1,0:T(8,128)(2,1)S(1)}, u32[]{:S(2)}, u32[]{:S(2)}) collective-permute-start(bf16[256,896]{1,0:T(8,128)(2,1)S(1)} %collective-permute-done.8.refs_4_), channel_id=1, source_target_pairs={{0,480},{32,0},{64,32},{96,64},{128,96},{160,128},{192,160},{224,1... | collective-permute-start | bytes 1376264 | tf_op jit(solution)/shard_map/ppermute | solution.py:287
  64.8 30.6 %copy-start.6 = (bf16[256,896]{1,0:T(8,128)(2,1)}, bf16[256,896]{1,0:T(8,128)(2,1)S(1)}, u32[]{:S(2)}) copy-start(bf16[256,896]{1,0:T(8,128)(2,1)S(1)} %collective-permute-done.2.refs_0_) | copy-start | bytes 1376260
  64.8 11.4 %collective-permute-start.3 = (bf16[256,896]{1,0:T(8,128)(2,1)S(1)}, bf16[256,896]{1,0:T(8,128)(2,1)S(1)}, u32[]{:S(2)}, u32[]{:S(2)}) collective-permute-start(bf16[256,896]{1,0:T(8,128)(2,1)S(1)} %collective-permute-done.2.refs_0_), channel_id=1, source_target_pairs={{0,32},{32,64},{64,96},{96,128},{128,160},{160,192},{192,224},{224... | collective-permute-start | bytes 1376264 | tf_op jit(solution)/shard_map/ppermute | solution.py:286
  66.8 28.7 %copy-start.7 = (bf16[256,896]{1,0:T(8,128)(2,1)}, bf16[256,896]{1,0:T(8,128)(2,1)S(1)}, u32[]{:S(2)}) copy-start(bf16[256,896]{1,0:T(8,128)(2,1)S(1)} %collective-permute-done.9.refs_1_) | copy-start | bytes 1376260
  66.8 11.4 %collective-permute-start.10 = (bf16[256,896]{1,0:T(8,128)(2,1)S(1)}, bf16[256,896]{1,0:T(8,128)(2,1)S(1)}, u32[]{:S(2)}, u32[]{:S(2)}) collective-permute-start(bf16[256,896]{1,0:T(8,128)(2,1)S(1)} %collective-permute-done.9.refs_1_), channel_id=1, source_target_pairs={{0,480},{32,0},{64,32},{96,64},{128,96},{160,128},{192,160},{224,1... | collective-permute-start | bytes 1376264 | tf_op jit(solution)/shard_map/ppermute | solution.py:287
  76.2 19.3 %copy-start.8 = (bf16[256,896]{1,0:T(8,128)(2,1)}, bf16[256,896]{1,0:T(8,128)(2,1)S(1)}, u32[]{:S(2)}) copy-start(bf16[256,896]{1,0:T(8,128)(2,1)S(1)} %collective-permute-done.3.refs_2_) | copy-start | bytes 1376260
  76.2 11.5 %collective-permute-start.4 = (bf16[256,896]{1,0:T(8,128)(2,1)S(1)}, bf16[256,896]{1,0:T(8,128)(2,1)S(1)}, u32[]{:S(2)}, u32[]{:S(2)}) collective-permute-start(bf16[256,896]{1,0:T(8,128)(2,1)S(1)} %collective-permute-done.3.refs_2_), channel_id=1, source_target_pairs={{0,32},{32,64},{64,96},{96,128},{128,160},{160,192},{192,224},{224... | collective-permute-start | bytes 1376264 | tf_op jit(solution)/shard_map/ppermute | solution.py:286
  78.2 17.3 %copy-start.9 = (bf16[256,896]{1,0:T(8,128)(2,1)}, bf16[256,896]{1,0:T(8,128)(2,1)S(1)}, u32[]{:S(2)}) copy-start(bf16[256,896]{1,0:T(8,128)(2,1)S(1)} %collective-permute-done.10.refs_3_) | copy-start | bytes 1376260
  78.2 17.3 %collective-permute-start.11 = (bf16[256,896]{1,0:T(8,128)(2,1)S(1)}, bf16[256,896]{1,0:T(8,128)(2,1)S(1)}, u32[]{:S(2)}, u32[]{:S(2)}) collective-permute-start(bf16[256,896]{1,0:T(8,128)(2,1)S(1)} %collective-permute-done.10.refs_3_), channel_id=1, source_target_pairs={{0,480},{32,0},{64,32},{96,64},{128,96},{160,128},{192,160},{224,1... | collective-permute-start | bytes 1376264 | tf_op jit(solution)/shard_map/ppermute | solution.py:287
  87.7 7.8 %copy-start.4 = (bf16[256,896]{1,0:T(8,128)(2,1)}, bf16[256,896]{1,0:T(8,128)(2,1)S(1)}, u32[]{:S(2)}) copy-start(bf16[256,896]{1,0:T(8,128)(2,1)S(1)} %collective-permute-done.4.refs_0_) | copy-start | bytes 1376260
  87.7 15.5 %collective-permute-start.5 = (bf16[256,896]{1,0:T(8,128)(2,1)S(1)}, bf16[256,896]{1,0:T(8,128)(2,1)}, u32[]{:S(2)}, u32[]{:S(2)}) collective-permute-start(bf16[256,896]{1,0:T(8,128)(2,1)S(1)} %collective-permute-done.4.refs_0_), channel_id=1, source_target_pairs={{0,32},{32,64},{64,96},{96,128},{128,160},{160,192},{192,224},{224... | collective-permute-start | bytes 1376264 | tf_op jit(solution)/shard_map/ppermute | solution.py:286
  95.5 15.2 %copy-start.5 = (bf16[256,896]{1,0:T(8,128)(2,1)}, bf16[256,896]{1,0:T(8,128)(2,1)S(1)}, u32[]{:S(2)}) copy-start(bf16[256,896]{1,0:T(8,128)(2,1)S(1)} %collective-permute-done.11.refs_1_) | copy-start | bytes 1376260
  95.5 21.0 %collective-permute-start.12 = (bf16[256,896]{1,0:T(8,128)(2,1)S(1)}, bf16[256,896]{1,0:T(8,128)(2,1)S(1)}, u32[]{:S(2)}, u32[]{:S(2)}) collective-permute-start(bf16[256,896]{1,0:T(8,128)(2,1)S(1)} %collective-permute-done.11.refs_1_), channel_id=1, source_target_pairs={{0,480},{32,0},{64,32},{96,64},{128,96},{160,128},{192,160},{224,1... | collective-permute-start | bytes 1376264 | tf_op jit(solution)/shard_map/ppermute | solution.py:287
  103.2 19.2 %collective-permute-start.6 = (bf16[256,896]{1,0:T(8,128)(2,1)}, bf16[256,896]{1,0:T(8,128)(2,1)S(1)}, u32[]{:S(2)}, u32[]{:S(2)}) collective-permute-start(bf16[256,896]{1,0:T(8,128)(2,1)} %collective-permute-done.5.refs_2_), channel_id=1, source_target_pairs={{0,32},{32,64},{64,96},{96,128},{128,160},{160,192},{192,224},{224... | collective-permute-start | bytes 1376264 | tf_op jit(solution)/shard_map/ppermute | solution.py:286
  116.6 7.9 %copy-start.10 = (bf16[256,896]{1,0:T(8,128)(2,1)}, bf16[256,896]{1,0:T(8,128)(2,1)S(1)}, u32[]{:S(2)}) copy-start(bf16[256,896]{1,0:T(8,128)(2,1)S(1)} %collective-permute-done.12.refs_3_) | copy-start | bytes 1376260
  116.6 13.7 %collective-permute-start.13 = (bf16[256,896]{1,0:T(8,128)(2,1)S(1)}, bf16[256,896]{1,0:T(8,128)(2,1)S(1)}, u32[]{:S(2)}, u32[]{:S(2)}) collective-permute-start(bf16[256,896]{1,0:T(8,128)(2,1)S(1)} %collective-permute-done.12.refs_3_), channel_id=1, source_target_pairs={{0,480},{32,0},{64,32},{96,64},{128,96},{160,128},{192,160},{224,1... | collective-permute-start | bytes 1376264 | tf_op jit(solution)/shard_map/ppermute | solution.py:287
  122.4 7.9 %copy-start.1 = (bf16[256,896]{1,0:T(8,128)(2,1)}, bf16[256,896]{1,0:T(8,128)(2,1)S(1)}, u32[]{:S(2)}) copy-start(bf16[256,896]{1,0:T(8,128)(2,1)S(1)} %collective-permute-done.6.refs_0_) | copy-start | bytes 1376260
  122.4 13.1 %copy-start.15 = (bf16[3,16,4096]{2,1,0:T(8,128)(2,1)S(1)}, bf16[3,16,4096]{2,1,0:T(8,128)(2,1)}, u32[]{:S(2)}) copy-start(bf16[3,16,4096]{2,1,0:T(8,128)(2,1)} %param.15) | copy-start | bytes 1179652
  122.4 21.1 %collective-permute-start.14 = (bf16[128,896]{1,0:T(8,128)(2,1)S(1)}, bf16[128,896]{1,0:T(8,128)(2,1)S(1)}, u32[]{:S(2)}, u32[]{:S(2)}) collective-permute-start(bf16[128,896]{1,0:T(8,128)(2,1)S(1)} %slice.28), channel_id=1, source_target_pairs={{0,32},{32,64},{64,96},{96,128},{128,160},{160,192},{192,224},{224... | collective-permute-start | bytes 688136 | tf_op jit(solution)/shard_map/ppermute | solution.py:286
  130.3 12.4 %copy-start.2 = (bf16[256,896]{1,0:T(8,128)(2,1)}, bf16[256,896]{1,0:T(8,128)(2,1)S(1)}, u32[]{:S(2)}) copy-start(bf16[256,896]{1,0:T(8,128)(2,1)S(1)} %collective-permute-done.13.refs_1_) | copy-start | bytes 1376260
  130.4 13.1 %collective-permute-start.15 = (bf16[128,896]{1,0:T(8,128)(2,1)S(1)}, bf16[128,896]{1,0:T(8,128)(2,1)S(1)}, u32[]{:S(2)}, u32[]{:S(2)}) collective-permute-start(bf16[128,896]{1,0:T(8,128)(2,1)S(1)} %slice.23), channel_id=1, source_target_pairs={{0,480},{32,0},{64,32},{96,64},{128,96},{160,128},{192,160},{224,1... | collective-permute-start | bytes 688136 | tf_op jit(solution)/shard_map/ppermute | solution.py:287
  137.0 5.8 %copy-start.20 = (bf16[16,512]{1,0:T(8,128)(2,1)S(1)}, bf16[16,512]{1,0:T(8,128)(2,1)}, u32[]{:S(2)}) copy-start(bf16[16,512]{1,0:T(8,128)(2,1)} %get-tuple-element.23.refs_10_) | copy-start | bytes 49156
  143.5 0.7 copy-start.16
  143.5 0.7 copy-start.17
  165.0 9.4 %all-to-all-start.1 = ((f32[8,8,512]{2,1,0:T(8,128)}), f32[8,8,512]{2,1,0:T(8,128)S(1)}, u32[]{:S(2)}, u32[]{:S(2)}) async-start(f32[8,8,512]{2,1,0:T(8,128)} %broadcast_in_dim.9), calls=%async_computation.1 | async-start | bytes 262144 | tf_op jit(solution)/shard_map/all_to_all | solution.py:405
  174.5 0.7 copy-start.3
  178.1 63.7 %copy-start.19 = (f32[3,16,512]{2,1,0:T(8,128)S(1)}, f32[3,16,512]{2,1,0:T(8,128)}, u32[]{:S(2)}) copy-start(f32[3,16,512]{2,1,0:T(8,128)} %param.18) | copy-start | bytes 294916
  190.3 52.1 %copy-start.18 = (f32[3,16,896]{2,1,0:T(8,128)S(1)}, f32[3,16,896]{2,1,0:T(8,128)}, u32[]{:S(2)}) copy-start(f32[3,16,896]{2,1,0:T(8,128)} %param.19) | copy-start | bytes 516100
Sparse Core Ops, SparseCore 0:
  10.1 43.8 all-gather.2
  56.2 39.7 all-gather.4

commit v6 on v5

--- a/solution.py
+++ b/solution.py
@@ -59,25 +59,27 @@
     return copies
 
 
-def side_kernel(n_rows, *refs):
-    row_refs = refs[:n_rows]
-    factors_ref, projected_ref, gram_ref, total = refs[n_rows:]
+def side_kernel(n_pairs, *refs):
+    row_refs = refs[:n_pairs]
+    factors_ref, projected_ref, gram_ref, total = refs[n_pairs:]
     step = pl.program_id(0)
+    size = SEQUENCE_TOKENS
 
     @pl.when(step == 0)
     def _():
         total[...] = jnp.zeros_like(total)
-        gram_ref[...] = jnp.zeros_like(gram_ref)
-
-    for e, rows_ref in enumerate(row_refs):
+
+    for p, rows_ref in enumerate(row_refs):
         rows = rows_ref[...]
-        span = slice(e * SEQUENCE_TOKENS, (e + 1) * SEQUENCE_TOKENS)
-        total[:, span] += contract(factors_ref[...], rows, 1, 1)
-        gram_ref[e] += contract(rows, rows, 1, 1)
+        stacked = jnp.concatenate([rows, factors_ref[...]], axis=0)
+        total[p] += contract(stacked, rows, 1, 1)
 
     @pl.when(step == pl.num_programs(0) - 1)
     def _():
-        projected_ref[...] = total[...].astype(BF16)
+        for p in range(n_pairs):
+            gram_ref[2 * p] = total[p, :size, :size]
+            gram_ref[2 * p + 1] = total[p, size : 2 * size, size:]
+            projected_ref[:, 2 * size * p : 2 * size * (p + 1)] = total[p, 2 * size :].astype(BF16)
 
 
 def part_kernel(n_blocks, first, place_ref, gradient_ref, *refs):
@@ -94,17 +96,17 @@
     for copy in copies:
         copy.wait()
 
-    def write(i, cols):
-        return pltpu.make_async_copy(total.at[:, cols], out_ref.at[:, cols], out_sems.at[i])
-
-    def tile(i, start, width):
-        cols = pl.ds(start, width)
+    writes = []
+    hidden = total.shape[1]
+    for i, start in enumerate(range(0, hidden, 512)):
+        cols = slice(start, min(start + 512, hidden))
         product = jnp.dot(left[...], right[:, cols], preferred_element_type=F32)
         total[:, cols] = product if first else total[:, cols] + product
-        write(i, cols).start()
-
-    for i, (start, width) in enumerate(column_tiles(total.shape[1], 256, tile)):
-        write(i, pl.ds(start, width)).wait()
+        write = pltpu.make_async_copy(total.at[:, cols], out_ref.at[:, cols], out_sems.at[i])
+        write.start()
+        writes.append(write)
+    for write in writes:
+        write.wait()
 
 
 def hidden_kernel(n_blocks, place_ref, gradient_ref, *refs):
@@ -118,14 +120,17 @@
     sems, out_sems = refs[-2:]
     tokens, hidden = gate_ref.shape
     sequences = tokens // SEQUENCE_TOKENS
-    copies = fetch_blocks(place_ref, gradient_ref, block_refs, left_rows, right_rows, sems)
-    at = 4 * n_blocks
+    blocks = fetch_blocks(place_ref, gradient_ref, block_refs, left_rows, right_rows, sems)
+    copies, at = [], 4 * n_blocks
     for source, target in ((before_hbm, before_ref), (gate_hbm, gate_ref), (up_hbm, up_ref)):
         copies += copy_rows(source, target, sems, at, 4)
         at += 4
-    for copy in copies:
+    for copy in blocks + copies:
         copy.start()
     mids_ref[...] = jnp.zeros_like(mids_ref)
+    for copy in blocks:
+        copy.wait()
+    total[...] = jnp.dot(left_rows[...], right_rows[...], preferred_element_type=F32)
     for copy in copies:
         copy.wait()
 
@@ -137,14 +142,14 @@
     def tile(i, start, width):
         cols = pl.ds(start, width)
         factors = factors_ref[:, cols]
-        total[:, :width] = (
-            before_ref[:, cols]
-            + jnp.dot(left_rows[...], right_rows[:, cols], preferred_element_type=F32)
-            + SCALE * jnp.dot(lora_ref[...], factors[2 * RANK :], preferred_element_type=F32)
-        )
         for e in range(sequences):
             rows = slice(e * SEQUENCE_TOKENS, (e + 1) * SEQUENCE_TOKENS)
-            hidden_grad = total[rows, :width]
+            hidden_grad = (
+                total[rows, cols]
+                + before_ref[rows, cols]
+                + SCALE
+                * jnp.dot(lora_ref[rows, :], factors[2 * RANK :], preferred_element_type=F32)
+            )
             gate = gate_ref[rows, cols].astype(F32)
             up = up_ref[rows, cols].astype(F32)
             sigmoid = jax.nn.sigmoid(gate)
@@ -290,22 +295,26 @@
         width = values.shape[1]
         chunk = 1024
         return pl.pallas_call(
-            functools.partial(side_kernel, sequences),
+            functools.partial(side_kernel, sequences // 2),
             out_shape=(
                 jax.ShapeDtypeStruct((factors.shape[0], tokens), BF16),
                 jax.ShapeDtypeStruct((sequences, SEQUENCE_TOKENS, SEQUENCE_TOKENS), F32),
             ),
             grid=(width // chunk,),
             in_specs=[
-                pl.BlockSpec((SEQUENCE_TOKENS, chunk), functools.partial(lambda e, i: (e, i), e))
-                for e in range(sequences)
+                pl.BlockSpec((2 * SEQUENCE_TOKENS, chunk), functools.partial(lambda p, i: (p, i), p))
+                for p in range(sequences // 2)
             ]
             + [pl.BlockSpec((factors.shape[0], chunk), lambda i: (0, i))],
             out_specs=(
                 pl.BlockSpec((factors.shape[0], tokens), lambda i: (0, 0)),
                 pl.BlockSpec((sequences, SEQUENCE_TOKENS, SEQUENCE_TOKENS), lambda i: (0, 0, 0)),
             ),
-            scratch_shapes=[pltpu.VMEM((factors.shape[0], tokens), F32)],
+            scratch_shapes=[
+                pltpu.VMEM(
+                    (sequences // 2, 2 * SEQUENCE_TOKENS + factors.shape[0], 2 * SEQUENCE_TOKENS), F32
+                )
+            ],
             compiler_params=params,
             cost_estimate=pl.CostEstimate(
                 flops=2 * tokens * width * (128 + factors.shape[0]),
@@ -313,7 +322,7 @@
                 transcendentals=0,
             ),
             name=name,
-        )(*[values] * sequences, factors)
+        )(*[values] * (sequences // 2), factors)
 
     def scratch(n_rows, n_sems):
         return [
@@ -342,32 +351,33 @@
             name="part_product",
         )(place(offsets), gradient, *blocks, *given)
 
+    def after(value, other):
+        return lax.optimization_barrier((value, other))[0]
+
     def pairs(first, end):
         return [sign * k for k in range(first, end) for sign in (-1, 1)]
 
     last = n_z // 2
-    for k in range(1, last - 2):
+    for k in range(1, last - 3):
         step(k, low[k - 1], high[k - 1])
     total = part([0] + pairs(1, last - 5))
+    at = last - 4
+    step(at + 1, after(low[at], total), after(high[at], total))
+    lora_t, gradient_gram = side(gradient, adapter_width_factors[2], "gradient_side")
     at = last - 3
-    high_in, total = lax.optimization_barrier((high[at], total))
-    step(last - 2, low[at], high_in)
-    total = part(pairs(last - 5, last - 3), total)
-    lora_t, gradient_gram = side(gradient, adapter_width_factors[2], "gradient_side")
+    step(at + 1, after(low[at], lora_t), after(high[at], lora_t))
+    total = part(pairs(last - 5, last - 2), total)
     at = last - 2
-    high_in, total, lora_t = lax.optimization_barrier((high[at], total, lora_t))
-    step(last - 1, low[at], high_in)
-    total = part(pairs(last - 3, last - 1), total)
+    step(at + 1, after(low[at], total), after(high[at], total))
     at = last - 1
-    high_in, total = lax.optimization_barrier((high[at], total))
-    step(last, low[at][:half], high_in[half:])
+    step(last, low[at][:half], high[at][half:])
     in_t, normed_gram = side(
         normed_all, adapter_width_factors[:2].reshape(2 * RANK, -1), "normed_side"
     )
     far = ((z + last) % n_z) * units
-    blocks = [low[last - 1], high[last - 1], low[last], high[last]]
+    blocks = [side_of[k] for k in range(last - 2, last + 1) for side_of in (low, high)]
     places = jnp.concatenate(
-        [place(pairs(last - 1, last)), jnp.stack([far, far + units // 2]).astype(jnp.int32)]
+        [place(pairs(last - 2, last)), jnp.stack([far, far + units // 2]).astype(jnp.int32)]
     )
     sums, mids = pl.pallas_call(
         functools.partial(hidden_kernel, len(blocks)),
@@ -378,13 +388,13 @@
         in_specs=[smem] + [hbm] * (len(blocks) + 4) + [vmem] * 4,
         out_specs=(hbm, vmem),
         scratch_shapes=[
-            pltpu.VMEM((tokens, 256), F32),
+            pltpu.VMEM((tokens, hidden), F32),
             pltpu.VMEM((tokens, hidden), F32),
             pltpu.VMEM((tokens, hidden), BF16),
             pltpu.VMEM((tokens, hidden), BF16),
             pltpu.VMEM((sequences, 3 * RANK, hidden), F32),
         ]
-        + scratch(3 * rows, 4 * len(blocks) + 12),
+        + scratch(5 * rows, 4 * len(blocks) + 12),
         compiler_params=params,
         name="hidden_side",
     )(

time: 251 us -> 242 us (0.964)
  Pallas kernels: 41.1 us -> 35.2 us
  blocking collectives: 87.6 us -> 83.6 us
    ppermute x8, waiting for transfers between devices: 24.7 us -> 11.9 us  [step(): low[k] = lax.ppermute(low_from, z_axes, ring(n_z, 1))]
    ppermute x8, waiting for transfers between devices: 0.02 us -> 12.7 us  [step(): high[k] = lax.ppermute(high_from, z_axes, ring(n_z, -1))]
    pallas_call x3 -> x2, Pallas kernels: 17.4 us -> 12.5 us  [part(): pl.pallas_call(functools.partial(part_kernel, n, before is None), out_sha...]
    ppermute x8, starting transfers between devices: 43.3 us -> 47.9 us  [step(): high[k] = lax.ppermute(high_from, z_axes, ring(n_z, -1))]
    all_to_all x1, blocking collectives: 25 us -> 20.6 us  [per_device(): lax.all_to_all(share.reshape(n_z, -1, 128), z_axes, 0, 0)]
    ppermute x8, starting transfers between devices: 18.4 us -> 15.3 us  [step(): low[k] = lax.ppermute(low_from, z_axes, ring(n_z, 1))]
  transfers between devices with their start and end apart: 19 -> 19, of which waited for: 6 -> 9; matrix products, arithmetic and copies ran while one was open for 2% -> 2% of each run, Pallas kernels for 12% -> 9%
where the time goes in v6:
time: 242 us; the launch traced here: 241 us
  blocking collectives  83.6 us (35%)
  starting transfers between devices  66.7 us (28%)
  Pallas kernels  35.2 us (15%)
  waiting for transfers between devices  31.4 us (13%)
  between operations  15.3 us (6%)
  local copies, waits for them, and re-layouts  7.24 us (3%)
    ppermute x8, starting transfers between devices, step(): high[k] = lax.ppermute(high_from, z_axes, ring(n_z, -1))  47.9 us
    all_to_all x1, blocking collectives, per_device(): lax.all_to_all(share.reshape(n_z, -1, 128), z_axes, 0, 0)  20.6 us
    all_to_all x1, blocking collectives, per_device(): lax.all_to_all(jnp.broadcast_to(share, (n_z,) + share.shape), z_axes, 0, 0)  17 us
    ppermute x8, starting transfers between devices, step(): low[k] = lax.ppermute(low_from, z_axes, ring(n_z, 1))  15.3 us
    all_gather x1, blocking collectives, per_device(): block = lax.all_gather(frozen_down_weight.T, 'y', axis=0, tiled=True)  13.4 us
    ppermute x8, waiting for transfers between devices, step(): high[k] = lax.ppermute(high_from, z_axes, ring(n_z, -1))  12.7 us
    pallas_call x2, Pallas kernels, part(): pl.pallas_call(functools.partial(part_kernel, n, before is None), out_sha...  12.5 us
    all_to_all x1, blocking collectives, per_device(): lax.all_to_all(out.reshape(n_y, -1, 128), 'y', 0, 0)  12.3 us
  transfers between devices with their start and end apart: 19, of which 9 were waited for; matrix products, arithmetic and copies ran while one was open for 2% of the time, Pallas kernels for 9%

profile of v6, /device:TPU:32, one launch (start us, length us, event | category | flops | bytes accessed | tf_op | source)
XLA Modules:
  0.0 240.8 jit_solution(17268315175877710333)
XLA Ops:
  7.2 0.0 all-gather.3.cloned.1.call-start
  7.2 0.7 all-gather.3.cloned.1.call-update
  7.9 0.0 all-gather.5.cloned.1.call-start
  7.9 0.7 all-gather.5.cloned.1.call-update
  8.6 13.4 %all_gather.10.refs_0_ = bf16[256,896]{1,0:T(8,128)(2,1)S(1)} all-gather(bf16[64,896]{1,0:T(8,128)(2,1)} %bitcast.43), channel_id=1, replica_groups=mesh['z'=16,'y'=4,'x'=4,'c'=2] {'y'}, dimensions={0}, use_global_device_ids=true | all-gather | bytes 573440 | tf_op jit(solution)/shard_map/all_gather | solution.py:273
  22.0 6.9 %collective-permute-start.4 = (bf16[256,896]{1,0:T(8,128)(2,1)S(1)}, bf16[256,896]{1,0:T(8,128)(2,1)S(1)}, u32[]{:S(2)}, u32[]{:S(2)}) collective-permute-start(bf16[256,896]{1,0:T(8,128)(2,1)S(1)} %all_gather.10.refs_0_), channel_id=1, source_target_pairs={{0,480},{32,0},{64,32},{96,64},{128,96},{160,128},{192,160},{224,1... | collective-permute-start | bytes 1376264 | tf_op jit(solution)/shard_map/ppermute | solution.py:292
  28.9 1.9 collective-permute-start
  30.8 4.0 %collective-permute-done.4.refs_2_ = bf16[256,896]{1,0:T(8,128)(2,1)S(1)} collective-permute-done((bf16[256,896]{1,0:T(8,128)(2,1)S(1)}, bf16[256,896]{1,0:T(8,128)(2,1)S(1)}, u32[]{:S(2)}, u32[]{:S(2)}) %collective-permute-start.4) | collective-permute-done | bytes 458784 | tf_op jit(solution)/shard_map/ppermute | solution.py:292
  34.9 8.6 %collective-permute-start.5 = (bf16[256,896]{1,0:T(8,128)(2,1)S(1)}, bf16[256,896]{1,0:T(8,128)(2,1)S(1)}, u32[]{:S(2)}, u32[]{:S(2)}) collective-permute-start(bf16[256,896]{1,0:T(8,128)(2,1)S(1)} %collective-permute-done.4.refs_2_), channel_id=1, source_target_pairs={{0,480},{32,0},{64,32},{96,64},{128,96},{160,128},{192,160},{224,1... | collective-permute-start | bytes 1376264 | tf_op jit(solution)/shard_map/ppermute | solution.py:292
  43.5 0.5 collective-permute-done.refs_1_
  44.0 1.9 collective-permute-start.1
  45.9 4.7 %collective-permute-done.5.refs_4_ = bf16[256,896]{1,0:T(8,128)(2,1)S(1)} collective-permute-done((bf16[256,896]{1,0:T(8,128)(2,1)S(1)}, bf16[256,896]{1,0:T(8,128)(2,1)S(1)}, u32[]{:S(2)}, u32[]{:S(2)}) %collective-permute-start.5) | collective-permute-done | bytes 458784 | tf_op jit(solution)/shard_map/ppermute | solution.py:292
  50.7 5.7 %collective-permute-start.8 = (bf16[256,896]{1,0:T(8,128)(2,1)S(1)}, bf16[256,896]{1,0:T(8,128)(2,1)S(1)}, u32[]{:S(2)}, u32[]{:S(2)}) collective-permute-start(bf16[256,896]{1,0:T(8,128)(2,1)S(1)} %collective-permute-done.5.refs_4_), channel_id=1, source_target_pairs={{0,480},{32,0},{64,32},{96,64},{128,96},{160,128},{192,160},{224,1... | collective-permute-start | bytes 1376264 | tf_op jit(solution)/shard_map/ppermute | solution.py:292
  56.4 0.5 collective-permute-done.1.refs_3_
  56.9 1.9 collective-permute-start.2
  58.8 3.9 %collective-permute-done.8.refs_1_ = bf16[256,896]{1,0:T(8,128)(2,1)S(1)} collective-permute-done((bf16[256,896]{1,0:T(8,128)(2,1)S(1)}, bf16[256,896]{1,0:T(8,128)(2,1)S(1)}, u32[]{:S(2)}, u32[]{:S(2)}) %collective-permute-start.8) | collective-permute-done | bytes 458784 | tf_op jit(solution)/shard_map/ppermute | solution.py:292
  62.7 5.7 %collective-permute-start.9 = (bf16[256,896]{1,0:T(8,128)(2,1)S(1)}, bf16[256,896]{1,0:T(8,128)(2,1)}, u32[]{:S(2)}, u32[]{:S(2)}) collective-permute-start(bf16[256,896]{1,0:T(8,128)(2,1)S(1)} %collective-permute-done.8.refs_1_), channel_id=1, source_target_pairs={{0,480},{32,0},{64,32},{96,64},{128,96},{160,128},{192,160},{224,1... | collective-permute-start | bytes 1376264 | tf_op jit(solution)/shard_map/ppermute | solution.py:292
  68.4 0.5 collective-permute-done.2.refs_0_
  68.9 1.9 collective-permute-start.3
  70.9 0.7 stack.68.place_ref
  71.6 5.8 %part_product.2.refs_6_ = f32[512,896]{1,0:T(8,128)} custom-call(s32[5]{0:T(128)} %stack.68.place_ref, bf16[512,4096]{1,0:T(8,128)(2,1)} %all-gather.3.cloned.1.call-done.gradient_ref.refs_0_.refs_1_, bf16[256,896]{1,0:T(8,128)(2,1)} %copy-done, bf16[256,896]{1,0:T(8,128)(2,1)} %copy-done.7, bf16[256,896]{1,0:T(8,128)(2,1)} %copy-done.6, ...), custom_call_target="tpu_custom_call" | custom-call | flops 1174405120 | bytes 6291456 | tf_op jit(solution)/shard_map/part_product/pallas_call | solution.py:339
  77.4 0.0 collective-permute-done.9.refs_3_
  77.4 5.2 %collective-permute-start.10 = (bf16[256,896]{1,0:T(8,128)(2,1)}, bf16[256,896]{1,0:T(8,128)(2,1)S(1)}, u32[]{:S(2)}, u32[]{:S(2)}) collective-permute-start(bf16[256,896]{1,0:T(8,128)(2,1)} %collective-permute-done.9.refs_3_), channel_id=1, source_target_pairs={{0,480},{32,0},{64,32},{96,64},{128,96},{160,128},{192,160},{224,1... | collective-permute-start | bytes 1376264 | tf_op jit(solution)/shard_map/ppermute | solution.py:292
  82.6 0.0 collective-permute-done.3.refs_2_
  82.6 1.9 collective-permute-start.6
  84.5 1.6 slice_bitcast_fusion.refs_2_
  86.1 4.8 %gradient_side.1 = (bf16[16,512]{1,0:T(8,128)(2,1)}, f32[4,128,128]{2,1,0:T(8,128)}) custom-call(bf16[512,4096]{1,0:T(8,128)(2,1)} %all-gather.3.cloned.1.call-done.gradient_ref.refs_0_.refs_1_, bf16[512,4096]{1,0:T(8,128)(2,1)} %all-gather.3.cloned.1.call-done.gradient_ref.refs_0_.refs_1_, bf16[16,4096]{1,0:T(8,128)(2,1)} %slice_bitcast_fusion.refs_2_), custom_call_target="tpu_custom_call" | custom-call | flops 603979776 | bytes 5242880 | tf_op jit(solution)/shard_map/gradient_side/pallas_call | solution.py:297
  90.9 3.6 %collective-permute-done.6.refs_4_ = bf16[256,896]{1,0:T(8,128)(2,1)S(1)} collective-permute-done((bf16[256,896]{1,0:T(8,128)(2,1)}, bf16[256,896]{1,0:T(8,128)(2,1)S(1)}, u32[]{:S(2)}, u32[]{:S(2)}) %collective-permute-start.6) | collective-permute-done | bytes 458784 | tf_op jit(solution)/shard_map/ppermute | solution.py:291
  94.5 1.9 collective-permute-start.7
  96.4 0.0 collective-permute-done.10.refs_5_
  96.4 5.4 %collective-permute-start.11 = (bf16[256,896]{1,0:T(8,128)(2,1)S(1)}, bf16[256,896]{1,0:T(8,128)(2,1)S(1)}, u32[]{:S(2)}, u32[]{:S(2)}) collective-permute-start(bf16[256,896]{1,0:T(8,128)(2,1)S(1)} %collective-permute-done.10.refs_5_), channel_id=1, source_target_pairs={{0,480},{32,0},{64,32},{96,64},{128,96},{160,128},{192,160},{224,1... | collective-permute-start | bytes 1376264 | tf_op jit(solution)/shard_map/ppermute | solution.py:292
  101.9 0.6 stack.75.place_ref
  102.6 6.7 %part_product.3.refs_6_ = f32[512,896]{1,0:T(8,128)} custom-call(s32[6]{0:T(128)} %stack.75.place_ref, bf16[512,4096]{1,0:T(8,128)(2,1)} %all-gather.3.cloned.1.call-done.gradient_ref.refs_0_.refs_1_, bf16[256,896]{1,0:T(8,128)(2,1)} %copy-done.11, bf16[256,896]{1,0:T(8,128)(2,1)} %copy-done.10, bf16[256,896]{1,0:T(8,128)(2,1)} %collective-permute-done.3.refs_2_, ...), custom_call_target="tpu_custom_call" | custom-call | flops 1409286144 | bytes 6291456 | tf_op jit(solution)/shard_map/part_product/pallas_call | solution.py:339
  109.3 0.0 collective-permute-done.7.refs_0_
  109.3 1.9 collective-permute-start.12
  111.3 0.0 collective-permute-done.11.refs_1_
  111.3 5.1 %collective-permute-start.13 = (bf16[256,896]{1,0:T(8,128)(2,1)S(1)}, bf16[256,896]{1,0:T(8,128)(2,1)S(1)}, u32[]{:S(2)}, u32[]{:S(2)}) collective-permute-start(bf16[256,896]{1,0:T(8,128)(2,1)S(1)} %collective-permute-done.11.refs_1_), channel_id=1, source_target_pairs={{0,480},{32,0},{64,32},{96,64},{128,96},{160,128},{192,160},{224,1... | collective-permute-start | bytes 1376264 | tf_op jit(solution)/shard_map/ppermute | solution.py:292
  116.4 6.8 %collective-permute-done.12.refs_2_ = bf16[256,896]{1,0:T(8,128)(2,1)S(1)} collective-permute-done((bf16[256,896]{1,0:T(8,128)(2,1)S(1)}, bf16[256,896]{1,0:T(8,128)(2,1)S(1)}, u32[]{:S(2)}, u32[]{:S(2)}) %collective-permute-start.12) | collective-permute-done | bytes 458784 | tf_op jit(solution)/shard_map/ppermute | solution.py:291
  123.3 1.9 collective-permute-start.14
  125.2 0.0 collective-permute-done.13.refs_3_
  125.2 5.3 %collective-permute-start.15 = (bf16[128,896]{1,0:T(8,128)(2,1)S(1)}, bf16[128,896]{1,0:T(8,128)(2,1)S(1)}, u32[]{:S(2)}, u32[]{:S(2)}) collective-permute-start(bf16[128,896]{1,0:T(8,128)(2,1)S(1)} %slice.29), channel_id=1, source_target_pairs={{0,480},{32,0},{64,32},{96,64},{128,96},{160,128},{192,160},{224,1... | collective-permute-start | bytes 688136 | tf_op jit(solution)/shard_map/ppermute | solution.py:292
  130.6 0.7 slice.24
  131.3 0.6 concatenate.3.place_ref
  131.9 0.8 copy.13
  132.7 4.8 %normed_side.1 = (bf16[32,512]{1,0:T(8,128)(2,1)}, f32[4,128,128]{2,1,0:T(8,128)}) custom-call(bf16[512,4096]{1,0:T(8,128)(2,1)} %all-gather.5.cloned.1.call-done.refs_0_.refs_1_, bf16[512,4096]{1,0:T(8,128)(2,1)} %all-gather.5.cloned.1.call-done.refs_0_.refs_1_, bf16[32,4096]{1,0:T(8,128)(2,1)} %bitcast.39), custom_call_target="tpu_custom_call" | custom-call | flops 671088640 | bytes 5242880 | tf_op jit(solution)/shard_map/normed_side/pallas_call | solution.py:297
  137.5 0.0 collective-permute-done.14.refs_4_
  137.5 0.0 collective-permute-done.15.refs_5_
  137.5 0.7 copy-done.15
  138.2 0.1 copy-done.16
  138.3 10.1 %hidden_side.1 = (f32[4,48,896]{2,1,0:T(8,128)}, f32[64,512]{1,0:T(8,128)}) custom-call(s32[6]{0:T(128)} %concatenate.3.place_ref, bf16[512,4096]{1,0:T(8,128)(2,1)} %all-gather.3.cloned.1.call-done.gradient_ref.refs_0_.refs_1_, bf16[256,896]{1,0:T(8,128)(2,1)} %copy-done.4, bf16[256,896]{1,0:T(8,128)(2,1)} %copy-done.5, bf16[256,896]{1,0:T(8,128)(2,1)} %copy-done.1, ...), custom_call_target="tpu_custom_call" | custom-call | tf_op jit(solution)/shard_map/hidden_side/pallas_call | solution.py:382
  148.5 0.0 copy-start.18
  148.5 0.0 copy-start.17
  148.5 11.1 %all_to_all.30 = f32[8,8,512]{2,1,0:T(8,128)S(1)} all-to-all(f32[8,8,512]{2,1,0:T(8,128)} %bitcast.42), channel_id=1, replica_groups=mesh['z'=16,'y'=4,'x'=4,'c'=2] {'x','c'}, dimensions={0} | all-to-all | bytes 262144 | tf_op jit(solution)/shard_map/all_to_all | solution.py:413
  159.6 0.7 broadcast_in_dim.9
  160.3 3.4 %all-to-all-start.1 = ((f32[8,8,512]{2,1,0:T(8,128)}), f32[8,8,512]{2,1,0:T(8,128)S(1)}, u32[]{:S(2)}, u32[]{:S(2)}) async-start(f32[8,8,512]{2,1,0:T(8,128)} %broadcast_in_dim.9), calls=%async_computation.1 | async-start | bytes 262144 | tf_op jit(solution)/shard_map/all_to_all | solution.py:415
  164.3 5.4 %all-to-all-done.1 = f32[8,8,512]{2,1,0:T(8,128)S(1)} async-done(((f32[8,8,512]{2,1,0:T(8,128)}), f32[8,8,512]{2,1,0:T(8,128)S(1)}, u32[]{:S(2)}, u32[]{:S(2)}) %all-to-all-start.1) | async-done | bytes 131104 | tf_op jit(solution)/shard_map/all_to_all | solution.py:415
  169.7 0.7 copy-done.3
  170.4 2.9 %clip_side.1 = f32[72,8,128]{2,1,0:T(8,128)} custom-call(f32[1]{0:T(128)} %copy.14.clip_ref, f32[64,512]{1,0:T(8,128)} %bitcast.41, f32[4,48,896]{2,1,0:T(8,128)} %get-tuple-element.23.sums_ref, bf16[512,512]{1,0:T(8,128)(2,1)} %normed_ref.1, bf16[512,512]{1,0:T(8,128)(2,1)} %gradient_ref.1, f32[4,128,128]{2,1,0:T(8,128)} %get-tuple-element.24.normed_gram_ref, ...), custom_call_target="tpu_custom_call" | custom-call | tf_op jit(solution)/shard_map/clip_side/pallas_call | solution.py:422
  173.3 12.3 %all_to_all.31 = f32[4,144,128]{2,1,0:T(8,128)S(1)} all-to-all(f32[4,144,128]{2,1,0:T(8,128)} %bitcast.35), channel_id=1, replica_groups=mesh['z'=16,'y'=4,'x'=4,'c'=2] {'y'}, dimensions={0} | all-to-all | bytes 589824 | tf_op jit(solution)/shard_map/all_to_all | solution.py:441
  185.7 20.6 %all_to_all.32 = f32[16,9,128]{2,1,0:T(8,128)S(1)} all-to-all(f32[16,9,128]{2,1,0:T(8,128)S(1)} %reshape.39), channel_id=1, replica_groups=mesh['z'=16,'y'=4,'x'=4,'c'=2] {'z'}, dimensions={0} | all-to-all | bytes 147456 | tf_op jit(solution)/shard_map/all_to_all | solution.py:442
  206.3 17.0 %all_to_all.33 = f32[16,9,128]{2,1,0:T(8,128)S(1)} all-to-all(f32[16,9,128]{2,1,0:T(8,128)S(1)} %broadcast_in_dim.10), channel_id=1, replica_groups=mesh['z'=16,'y'=4,'x'=4,'c'=2] {'z'}, dimensions={0} | all-to-all | bytes 147456 | tf_op jit(solution)/shard_map/all_to_all | solution.py:443
  223.3 9.2 %all_to_all.34 = f32[4,144,128]{2,1,0:T(8,128)S(1)} all-to-all(f32[4,144,128]{2,1,0:T(8,128)S(1)} %broadcast_in_dim.11), channel_id=1, replica_groups=mesh['z'=16,'y'=4,'x'=4,'c'=2] {'y'}, dimensions={0} | all-to-all | bytes 589824 | tf_op jit(solution)/shard_map/all_to_all | solution.py:446
  232.6 0.7 fusion.1
  233.3 0.7 fusion
  (47 shorter events, 0.2 us)
Async XLA Ops:
  7.2 64.4 %all-gather.3.cloned.1.call-start = ((), (), s32[]{:S(2)}) async-start(), calls=%async_computation.6 | async-start | bytes 4718592 | tf_op jit(solution)/shard_map/all_gather | solution.py:272
  7.9 124.8 %all-gather.5.cloned.1.call-start = ((), (), s32[]{:S(2)}) async-start(), calls=%async_computation.7 | async-start | bytes 4718592 | tf_op jit(solution)/shard_map/all_gather | solution.py:274
  22.0 49.5 %copy-start = (bf16[256,896]{1,0:T(8,128)(2,1)}, bf16[256,896]{1,0:T(8,128)(2,1)S(1)}, u32[]{:S(2)}) copy-start(bf16[256,896]{1,0:T(8,128)(2,1)S(1)} %all_gather.10.refs_0_) | copy-start | bytes 1376260
  22.0 12.8 %collective-permute-start.4 = (bf16[256,896]{1,0:T(8,128)(2,1)S(1)}, bf16[256,896]{1,0:T(8,128)(2,1)S(1)}, u32[]{:S(2)}, u32[]{:S(2)}) collective-permute-start(bf16[256,896]{1,0:T(8,128)(2,1)S(1)} %all_gather.10.refs_0_), channel_id=1, source_target_pairs={{0,480},{32,0},{64,32},{96,64},{128,96},{160,128},{192,160},{224,1... | collective-permute-start | bytes 1376264 | tf_op jit(solution)/shard_map/ppermute | solution.py:292
  28.9 15.1 %collective-permute-start = (bf16[256,896]{1,0:T(8,128)(2,1)S(1)}, bf16[256,896]{1,0:T(8,128)(2,1)S(1)}, u32[]{:S(2)}, u32[]{:S(2)}) collective-permute-start(bf16[256,896]{1,0:T(8,128)(2,1)S(1)} %all_gather.10.refs_0_), channel_id=1, source_target_pairs={{0,32},{32,64},{64,96},{96,128},{128,160},{160,192},{192,224},{224... | collective-permute-start | bytes 1376264 | tf_op jit(solution)/shard_map/ppermute | solution.py:291
  34.9 36.7 %copy-start.6 = (bf16[256,896]{1,0:T(8,128)(2,1)}, bf16[256,896]{1,0:T(8,128)(2,1)S(1)}, u32[]{:S(2)}) copy-start(bf16[256,896]{1,0:T(8,128)(2,1)S(1)} %collective-permute-done.4.refs_2_) | copy-start | bytes 1376260
  34.9 15.8 %collective-permute-start.5 = (bf16[256,896]{1,0:T(8,128)(2,1)S(1)}, bf16[256,896]{1,0:T(8,128)(2,1)S(1)}, u32[]{:S(2)}, u32[]{:S(2)}) collective-permute-start(bf16[256,896]{1,0:T(8,128)(2,1)S(1)} %collective-permute-done.4.refs_2_), channel_id=1, source_target_pairs={{0,480},{32,0},{64,32},{96,64},{128,96},{160,128},{192,160},{224,1... | collective-permute-start | bytes 1376264 | tf_op jit(solution)/shard_map/ppermute | solution.py:292
  44.0 27.6 %copy-start.7 = (bf16[256,896]{1,0:T(8,128)(2,1)}, bf16[256,896]{1,0:T(8,128)(2,1)S(1)}, u32[]{:S(2)}) copy-start(bf16[256,896]{1,0:T(8,128)(2,1)S(1)} %collective-permute-done.refs_1_) | copy-start | bytes 1376260
  44.0 12.9 %collective-permute-start.1 = (bf16[256,896]{1,0:T(8,128)(2,1)S(1)}, bf16[256,896]{1,0:T(8,128)(2,1)S(1)}, u32[]{:S(2)}, u32[]{:S(2)}) collective-permute-start(bf16[256,896]{1,0:T(8,128)(2,1)S(1)} %collective-permute-done.refs_1_), channel_id=1, source_target_pairs={{0,32},{32,64},{64,96},{96,128},{128,160},{160,192},{192,224},{224... | collective-permute-start | bytes 1376264 | tf_op jit(solution)/shard_map/ppermute | solution.py:291
  50.7 20.9 %copy-start.8 = (bf16[256,896]{1,0:T(8,128)(2,1)}, bf16[256,896]{1,0:T(8,128)(2,1)S(1)}, u32[]{:S(2)}) copy-start(bf16[256,896]{1,0:T(8,128)(2,1)S(1)} %collective-permute-done.5.refs_4_) | copy-start | bytes 1376260
  50.7 12.0 %collective-permute-start.8 = (bf16[256,896]{1,0:T(8,128)(2,1)S(1)}, bf16[256,896]{1,0:T(8,128)(2,1)S(1)}, u32[]{:S(2)}, u32[]{:S(2)}) collective-permute-start(bf16[256,896]{1,0:T(8,128)(2,1)S(1)} %collective-permute-done.5.refs_4_), channel_id=1, source_target_pairs={{0,480},{32,0},{64,32},{96,64},{128,96},{160,128},{192,160},{224,1... | collective-permute-start | bytes 1376264 | tf_op jit(solution)/shard_map/ppermute | solution.py:292
  56.9 14.7 %copy-start.9 = (bf16[256,896]{1,0:T(8,128)(2,1)}, bf16[256,896]{1,0:T(8,128)(2,1)S(1)}, u32[]{:S(2)}) copy-start(bf16[256,896]{1,0:T(8,128)(2,1)S(1)} %collective-permute-done.1.refs_3_) | copy-start | bytes 1376260
  56.9 12.0 %collective-permute-start.2 = (bf16[256,896]{1,0:T(8,128)(2,1)S(1)}, bf16[256,896]{1,0:T(8,128)(2,1)S(1)}, u32[]{:S(2)}, u32[]{:S(2)}) collective-permute-start(bf16[256,896]{1,0:T(8,128)(2,1)S(1)} %collective-permute-done.1.refs_3_), channel_id=1, source_target_pairs={{0,32},{32,64},{64,96},{96,128},{128,160},{160,192},{192,224},{224... | collective-permute-start | bytes 1376264 | tf_op jit(solution)/shard_map/ppermute | solution.py:291
  62.7 14.7 %copy-start.10 = (bf16[256,896]{1,0:T(8,128)(2,1)}, bf16[256,896]{1,0:T(8,128)(2,1)S(1)}, u32[]{:S(2)}) copy-start(bf16[256,896]{1,0:T(8,128)(2,1)S(1)} %collective-permute-done.8.refs_1_) | copy-start | bytes 1376260
  62.7 14.7 %collective-permute-start.9 = (bf16[256,896]{1,0:T(8,128)(2,1)S(1)}, bf16[256,896]{1,0:T(8,128)(2,1)}, u32[]{:S(2)}, u32[]{:S(2)}) collective-permute-start(bf16[256,896]{1,0:T(8,128)(2,1)S(1)} %collective-permute-done.8.refs_1_), channel_id=1, source_target_pairs={{0,480},{32,0},{64,32},{96,64},{128,96},{160,128},{192,160},{224,1... | collective-permute-start | bytes 1376264 | tf_op jit(solution)/shard_map/ppermute | solution.py:292
  68.9 8.5 %copy-start.11 = (bf16[256,896]{1,0:T(8,128)(2,1)}, bf16[256,896]{1,0:T(8,128)(2,1)S(1)}, u32[]{:S(2)}) copy-start(bf16[256,896]{1,0:T(8,128)(2,1)S(1)} %collective-permute-done.2.refs_0_) | copy-start | bytes 1376260
  68.9 13.7 %collective-permute-start.3 = (bf16[256,896]{1,0:T(8,128)(2,1)S(1)}, bf16[256,896]{1,0:T(8,128)(2,1)}, u32[]{:S(2)}, u32[]{:S(2)}) collective-permute-start(bf16[256,896]{1,0:T(8,128)(2,1)S(1)} %collective-permute-done.2.refs_0_), channel_id=1, source_target_pairs={{0,32},{32,64},{64,96},{96,128},{128,160},{160,192},{192,224},{224... | collective-permute-start | bytes 1376264 | tf_op jit(solution)/shard_map/ppermute | solution.py:291
  77.4 19.0 %collective-permute-start.10 = (bf16[256,896]{1,0:T(8,128)(2,1)}, bf16[256,896]{1,0:T(8,128)(2,1)S(1)}, u32[]{:S(2)}, u32[]{:S(2)}) collective-permute-start(bf16[256,896]{1,0:T(8,128)(2,1)} %collective-permute-done.9.refs_3_), channel_id=1, source_target_pairs={{0,480},{32,0},{64,32},{96,64},{128,96},{160,128},{192,160},{224,1... | collective-permute-start | bytes 1376264 | tf_op jit(solution)/shard_map/ppermute | solution.py:292
  82.6 11.9 %collective-permute-start.6 = (bf16[256,896]{1,0:T(8,128)(2,1)}, bf16[256,896]{1,0:T(8,128)(2,1)S(1)}, u32[]{:S(2)}, u32[]{:S(2)}) collective-permute-start(bf16[256,896]{1,0:T(8,128)(2,1)} %collective-permute-done.3.refs_2_), channel_id=1, source_target_pairs={{0,32},{32,64},{64,96},{96,128},{128,160},{160,192},{192,224},{224... | collective-permute-start | bytes 1376264 | tf_op jit(solution)/shard_map/ppermute | solution.py:291
  94.5 8.1 %copy-start.13 = (bf16[256,896]{1,0:T(8,128)(2,1)}, bf16[256,896]{1,0:T(8,128)(2,1)S(1)}, u32[]{:S(2)}) copy-start(bf16[256,896]{1,0:T(8,128)(2,1)S(1)} %collective-permute-done.6.refs_4_) | copy-start | bytes 1376260
  94.5 14.8 %collective-permute-start.7 = (bf16[256,896]{1,0:T(8,128)(2,1)S(1)}, bf16[256,896]{1,0:T(8,128)(2,1)S(1)}, u32[]{:S(2)}, u32[]{:S(2)}) collective-permute-start(bf16[256,896]{1,0:T(8,128)(2,1)S(1)} %collective-permute-done.6.refs_4_), channel_id=1, source_target_pairs={{0,32},{32,64},{64,96},{96,128},{128,160},{160,192},{192,224},{224... | collective-permute-start | bytes 1376264 | tf_op jit(solution)/shard_map/ppermute | solution.py:291
  96.4 6.1 %copy-start.12 = (bf16[256,896]{1,0:T(8,128)(2,1)}, bf16[256,896]{1,0:T(8,128)(2,1)S(1)}, u32[]{:S(2)}) copy-start(bf16[256,896]{1,0:T(8,128)(2,1)S(1)} %collective-permute-done.10.refs_5_) | copy-start | bytes 1376260
  96.4 14.8 %collective-permute-start.11 = (bf16[256,896]{1,0:T(8,128)(2,1)S(1)}, bf16[256,896]{1,0:T(8,128)(2,1)S(1)}, u32[]{:S(2)}, u32[]{:S(2)}) collective-permute-start(bf16[256,896]{1,0:T(8,128)(2,1)S(1)} %collective-permute-done.10.refs_5_), channel_id=1, source_target_pairs={{0,480},{32,0},{64,32},{96,64},{128,96},{160,128},{192,160},{224,1... | collective-permute-start | bytes 1376264 | tf_op jit(solution)/shard_map/ppermute | solution.py:292
  102.5 28.0 %copy-start.14 = (bf16[3,16,4096]{2,1,0:T(8,128)(2,1)S(1)}, bf16[3,16,4096]{2,1,0:T(8,128)(2,1)}, u32[]{:S(2)}) copy-start(bf16[3,16,4096]{2,1,0:T(8,128)(2,1)} %param.15) | copy-start | bytes 1179652
  102.5 29.4 %copy-start.19 = (bf16[16,512]{1,0:T(8,128)(2,1)S(1)}, bf16[16,512]{1,0:T(8,128)(2,1)}, u32[]{:S(2)}) copy-start(bf16[16,512]{1,0:T(8,128)(2,1)} %get-tuple-element.15.refs_12_) | copy-start | bytes 49156
  109.3 28.2 %copy-start.4 = (bf16[256,896]{1,0:T(8,128)(2,1)}, bf16[256,896]{1,0:T(8,128)(2,1)S(1)}, u32[]{:S(2)}) copy-start(bf16[256,896]{1,0:T(8,128)(2,1)S(1)} %collective-permute-done.7.refs_0_) | copy-start | bytes 1376260
  109.3 13.9 %collective-permute-start.12 = (bf16[256,896]{1,0:T(8,128)(2,1)S(1)}, bf16[256,896]{1,0:T(8,128)(2,1)S(1)}, u32[]{:S(2)}, u32[]{:S(2)}) collective-permute-start(bf16[256,896]{1,0:T(8,128)(2,1)S(1)} %collective-permute-done.7.refs_0_), channel_id=1, source_target_pairs={{0,32},{32,64},{64,96},{96,128},{128,160},{160,192},{192,224},{224... | collective-permute-start | bytes 1376264 | tf_op jit(solution)/shard_map/ppermute | solution.py:291
  111.3 26.2 %copy-start.5 = (bf16[256,896]{1,0:T(8,128)(2,1)}, bf16[256,896]{1,0:T(8,128)(2,1)S(1)}, u32[]{:S(2)}) copy-start(bf16[256,896]{1,0:T(8,128)(2,1)S(1)} %collective-permute-done.11.refs_1_) | copy-start | bytes 1376260
  111.3 13.9 %collective-permute-start.13 = (bf16[256,896]{1,0:T(8,128)(2,1)S(1)}, bf16[256,896]{1,0:T(8,128)(2,1)S(1)}, u32[]{:S(2)}, u32[]{:S(2)}) collective-permute-start(bf16[256,896]{1,0:T(8,128)(2,1)S(1)} %collective-permute-done.11.refs_1_), channel_id=1, source_target_pairs={{0,480},{32,0},{64,32},{96,64},{128,96},{160,128},{192,160},{224,1... | collective-permute-start | bytes 1376264 | tf_op jit(solution)/shard_map/ppermute | solution.py:292
  123.2 14.3 %copy-start.1 = (bf16[256,896]{1,0:T(8,128)(2,1)}, bf16[256,896]{1,0:T(8,128)(2,1)S(1)}, u32[]{:S(2)}) copy-start(bf16[256,896]{1,0:T(8,128)(2,1)S(1)} %collective-permute-done.12.refs_2_) | copy-start | bytes 1376260
  123.3 14.3 %collective-permute-start.14 = (bf16[128,896]{1,0:T(8,128)(2,1)S(1)}, bf16[128,896]{1,0:T(8,128)(2,1)S(1)}, u32[]{:S(2)}, u32[]{:S(2)}) collective-permute-start(bf16[128,896]{1,0:T(8,128)(2,1)S(1)} %slice.28), channel_id=1, source_target_pairs={{0,32},{32,64},{64,96},{96,128},{128,160},{160,192},{192,224},{224... | collective-permute-start | bytes 688136 | tf_op jit(solution)/shard_map/ppermute | solution.py:291
  125.2 12.3 %copy-start.2 = (bf16[256,896]{1,0:T(8,128)(2,1)}, bf16[256,896]{1,0:T(8,128)(2,1)S(1)}, u32[]{:S(2)}) copy-start(bf16[256,896]{1,0:T(8,128)(2,1)S(1)} %collective-permute-done.13.refs_3_) | copy-start | bytes 1376260
  125.2 12.3 %collective-permute-start.15 = (bf16[128,896]{1,0:T(8,128)(2,1)S(1)}, bf16[128,896]{1,0:T(8,128)(2,1)S(1)}, u32[]{:S(2)}, u32[]{:S(2)}) collective-permute-start(bf16[128,896]{1,0:T(8,128)(2,1)S(1)} %slice.29), channel_id=1, source_target_pairs={{0,480},{32,0},{64,32},{96,64},{128,96},{160,128},{192,160},{224,1... | collective-permute-start | bytes 688136 | tf_op jit(solution)/shard_map/ppermute | solution.py:292
  137.5 0.7 copy-start.15
  137.5 0.8 copy-start.16
  148.5 84.1 %copy-start.18 = (f32[3,16,512]{2,1,0:T(8,128)S(1)}, f32[3,16,512]{2,1,0:T(8,128)}, u32[]{:S(2)}) copy-start(f32[3,16,512]{2,1,0:T(8,128)} %param.18) | copy-start | bytes 294916
  148.5 84.8 %copy-start.17 = (f32[3,16,896]{2,1,0:T(8,128)S(1)}, f32[3,16,896]{2,1,0:T(8,128)}, u32[]{:S(2)}) copy-start(f32[3,16,896]{2,1,0:T(8,128)} %param.19) | copy-start | bytes 516100
  160.3 9.4 %all-to-all-start.1 = ((f32[8,8,512]{2,1,0:T(8,128)}), f32[8,8,512]{2,1,0:T(8,128)S(1)}, u32[]{:S(2)}, u32[]{:S(2)}) async-start(f32[8,8,512]{2,1,0:T(8,128)} %broadcast_in_dim.9), calls=%async_computation.1 | async-start | bytes 262144 | tf_op jit(solution)/shard_map/all_to_all | solution.py:415
  169.7 0.7 copy-start.3
Sparse Core Ops, SparseCore 0:
  10.1 43.8 all-gather.2
  56.2 39.7 all-gather.4

commit v7 on v6

--- a/solution.py
+++ b/solution.py
@@ -47,15 +47,26 @@
     return copies
 
 
-def fetch_blocks(place_ref, gradient_ref, block_refs, left, right, sems):
-    copies, row = [], 0
-    for i, block in enumerate(block_refs):
-        rows = block.shape[0]
-        at = pl.ds(pl.multiple_of(place_ref[i] * 128, 128), rows)
-        span = pl.ds(row, rows)
-        copies += copy_rows(gradient_ref.at[:, at], left.at[:, span], sems, 4 * i, 2)
-        copies += copy_rows(block, right.at[span, :], sems, 4 * i + 2, 2)
-        row += rows
+def fetch_blocks(plan, place_ref, gradient_ref, block_refs, left, right, sems):
+    copies, at = [], 0
+    for i, sources in enumerate(plan):
+        n = len(sources)
+        rows = right.shape[0] // len(plan)
+        piece = rows // n
+        span = pl.ds(i * rows, rows)
+        columns = pl.ds(pl.multiple_of(place_ref[i] * rows, rows), rows)
+        copies += copy_rows(gradient_ref.at[:, columns], left.at[:, span], sems, at, 2)
+        at += 2
+        for j, (block, row) in enumerate(sources):
+            to = i * rows + lax.rem(place_ref[len(plan)] + j, n) * piece
+            copies.append(
+                pltpu.make_async_copy(
+                    block_refs[block].at[pl.ds(row, piece), :],
+                    right.at[pl.ds(pl.multiple_of(to, piece), piece), :],
+                    sems.at[at],
+                )
+            )
+            at += 1
     return copies
 
 
@@ -82,15 +93,15 @@
             projected_ref[:, 2 * size * p : 2 * size * (p + 1)] = total[p, 2 * size :].astype(BF16)
 
 
-def part_kernel(n_blocks, first, place_ref, gradient_ref, *refs):
+def part_kernel(plan, n_blocks, first, place_ref, gradient_ref, *refs):
     block_refs = refs[:n_blocks]
     refs = refs[n_blocks:]
     if not first:
         before_ref, refs = refs[0], refs[1:]
     out_ref, total, left, right, sems, out_sems = refs
-    copies = fetch_blocks(place_ref, gradient_ref, block_refs, left, right, sems)
+    copies = fetch_blocks(plan, place_ref, gradient_ref, block_refs, left, right, sems)
     if not first:
-        copies += copy_rows(before_ref, total, sems, 4 * n_blocks, 4)
+        copies += copy_rows(before_ref, total, sems, len(copies), 4)
     for copy in copies:
         copy.start()
     for copy in copies:
@@ -109,7 +120,7 @@
         write.wait()
 
 
-def hidden_kernel(n_blocks, place_ref, gradient_ref, *refs):
+def hidden_kernel(plan, n_blocks, place_ref, gradient_ref, *refs):
     block_refs = refs[:n_blocks]
     (before_hbm, gate_hbm, up_hbm, factors_ref, in_ref, lora_ref, lora_t_ref) = refs[
         n_blocks : n_blocks + 7
@@ -120,8 +131,8 @@
     sems, out_sems = refs[-2:]
     tokens, hidden = gate_ref.shape
     sequences = tokens // SEQUENCE_TOKENS
-    blocks = fetch_blocks(place_ref, gradient_ref, block_refs, left_rows, right_rows, sems)
-    copies, at = [], 4 * n_blocks
+    blocks = fetch_blocks(plan, place_ref, gradient_ref, block_refs, left_rows, right_rows, sems)
+    copies, at = [], len(blocks)
     for source, target in ((before_hbm, before_ref), (gate_hbm, gate_ref), (up_hbm, up_ref)):
         copies += copy_rows(source, target, sems, at, 4)
         at += 4
@@ -270,26 +281,54 @@
     z = lax.axis_index(z_axes)
 
     gradient = lax.all_gather(output_gradient, tensor_axes, axis=1, tiled=True)
-    block = lax.all_gather(frozen_down_weight.T, "y", axis=0, tiled=True)
+    shard = frozen_down_weight.T
     normed_all = lax.all_gather(normed, tensor_axes, axis=1, tiled=True)
 
-    rows = block.shape[0]
-    half = rows // 2
-    units = rows // 128
+    n_y = sizes["y"]
+    piece = shard.shape[0]
+    rows = n_y * piece
+    y = lax.axis_index("y")
     vmem = pl.BlockSpec(memory_space=pltpu.VMEM)
     smem = pl.BlockSpec(memory_space=pltpu.SMEM)
     hbm = pl.BlockSpec(memory_space=pl.ANY)
     params = pltpu.CompilerParams(vmem_limit_bytes=60 * 2**20)
 
     def place(offsets):
-        at = [((z + offset) % n_z) * units for offset in offsets]
-        return jnp.stack(at).astype(jnp.int32)
-
+        at = [(z + offset + n_z) % n_z for offset in offsets]
+        return jnp.stack(at + [y]).astype(jnp.int32)
+
+    block = jnp.concatenate([shard, lax.ppermute(shard, "y", ring(n_y, -1))], axis=0)
     low, high = {0: block}, {0: block}
+    last = n_z // 2
 
     def step(k, low_from, high_from):
         low[k] = lax.ppermute(low_from, z_axes, ring(n_z, 1))
         high[k] = lax.ppermute(high_from, z_axes, ring(n_z, -1))
+
+    def pair_of(offset):
+        if offset == last:
+            return low[last], high[last]
+        whole = (low if offset < 0 else high)[abs(offset)]
+        return whole[:piece], whole[piece:]
+
+    def exchange(offsets):
+        own, following = zip(*(pair_of(offset) for offset in offsets), strict=True)
+        return (
+            lax.ppermute(jnp.concatenate(following, axis=0), "y", ring(n_y, -1)),
+            lax.ppermute(jnp.concatenate(own, axis=0), "y", ring(n_y, 1)),
+        )
+
+    def blocks_of(offsets, others):
+        blocks, plan = list(others), []
+        for i, offset in enumerate(offsets):
+            if offset == last:
+                here = [(len(blocks), 0), (len(blocks) + 1, 0)]
+                blocks += [low[last], high[last]]
+            else:
+                here = [(len(blocks), 0), (len(blocks), piece)]
+                blocks.append((low if offset < 0 else high)[abs(offset)])
+            plan.append(here + [(0, i * piece), (1, i * piece)])
+        return blocks, plan
 
     def side(values, factors, name):
         width = values.shape[1]
@@ -332,16 +371,17 @@
             pltpu.SemaphoreType.DMA((-(-hidden // 256),)),
         ]
 
-    def part(offsets, before=None):
-        blocks = [(low if offset < 0 else high)[abs(offset)] for offset in offsets]
-        n = len(blocks)
+    def part(offsets, others, before=None):
+        blocks, plan = blocks_of(offsets, others)
+        n = len(offsets)
         given = [] if before is None else [before]
         return pl.pallas_call(
-            functools.partial(part_kernel, n, before is None),
+            functools.partial(part_kernel, plan, len(blocks), before is None),
             out_shape=jax.ShapeDtypeStruct((tokens, hidden), F32),
-            in_specs=[smem] + [hbm] * (n + 1 + len(given)),
+            in_specs=[smem] + [hbm] * (len(blocks) + 1 + len(given)),
             out_specs=hbm,
-            scratch_shapes=[pltpu.VMEM((tokens, hidden), F32)] + scratch(n * rows, 4 * n + 4),
+            scratch_shapes=[pltpu.VMEM((tokens, hidden), F32)]
+            + scratch(n * rows, (2 + n_y) * n + 4),
             compiler_params=params,
             cost_estimate=pl.CostEstimate(
                 flops=2 * tokens * n * rows * hidden,
@@ -358,29 +398,29 @@
         return [sign * k for k in range(first, end) for sign in (-1, 1)]
 
     last = n_z // 2
-    for k in range(1, last - 3):
+    for k in range(1, last - 4):
         step(k, low[k - 1], high[k - 1])
-    total = part([0] + pairs(1, last - 5))
-    at = last - 4
-    step(at + 1, after(low[at], total), after(high[at], total))
+    groups = [[0] + pairs(1, last - 4), pairs(last - 4, last - 1), pairs(last - 1, last) + [last]]
+    others = [exchange(groups[0])]
+    for k in range(last - 4, last - 2):
+        step(k, low[k - 1], high[k - 1])
     lora_t, gradient_gram = side(gradient, adapter_width_factors[2], "gradient_side")
     at = last - 3
     step(at + 1, after(low[at], lora_t), after(high[at], lora_t))
-    total = part(pairs(last - 5, last - 2), total)
+    others.append(exchange(groups[1]))
+    total = part(groups[0], others[0])
     at = last - 2
     step(at + 1, after(low[at], total), after(high[at], total))
     at = last - 1
-    step(last, low[at][:half], high[at][half:])
+    step(last, low[at][:piece], high[at][piece:])
+    others.append(exchange(groups[2]))
+    total = part(groups[1], others[1], after(total, low[last]))
     in_t, normed_gram = side(
         normed_all, adapter_width_factors[:2].reshape(2 * RANK, -1), "normed_side"
     )
-    far = ((z + last) % n_z) * units
-    blocks = [side_of[k] for k in range(last - 2, last + 1) for side_of in (low, high)]
-    places = jnp.concatenate(
-        [place(pairs(last - 2, last)), jnp.stack([far, far + units // 2]).astype(jnp.int32)]
-    )
+    blocks, plan = blocks_of(groups[2], others[2])
     sums, mids = pl.pallas_call(
-        functools.partial(hidden_kernel, len(blocks)),
+        functools.partial(hidden_kernel, plan, len(blocks)),
         out_shape=(
             jax.ShapeDtypeStruct((sequences, 3 * RANK, hidden), F32),
             jax.ShapeDtypeStruct((8 * n_tensor, tokens), F32),
@@ -394,11 +434,11 @@
             pltpu.VMEM((tokens, hidden), BF16),
             pltpu.VMEM((sequences, 3 * RANK, hidden), F32),
         ]
-        + scratch(5 * rows, 4 * len(blocks) + 12),
+        + scratch(len(plan) * rows, (2 + n_y) * len(plan) + 12),
         compiler_params=params,
         name="hidden_side",
     )(
-        places,
+        place(groups[2]),
         gradient,
         *blocks,
         total,
@@ -437,7 +477,6 @@
         gradient_gram,
     )
 
-    n_y = sizes["y"]
     share = jnp.sum(lax.all_to_all(out.reshape(n_y, -1, 128), "y", 0, 0), axis=0)
     share = jnp.sum(lax.all_to_all(share.reshape(n_z, -1, 128), z_axes, 0, 0), axis=0)
     share = lax.all_to_all(

time: 242 us -> 252 us (1.041)
  starting transfers between devices: 66.7 us -> 87.7 us
  waiting for transfers between devices: 31.4 us -> 15.8 us
  local copies, waits for them, and re-layouts: 7.24 us -> 20 us
  blocking collectives: 83.6 us -> 72.1 us
  other arithmetic: 1.41 us -> 4.54 us
    ppermute x0 -> x7, starting transfers between devices: none -> 26.3 us  [the longest x3 15.7 us: exchange(): lax.ppermute(jnp.concatenate(following, axis=0), 'y', ring(n_y, -1))]
    all_gather x1 -> x0, blocking collectives: 13.4 us -> none  [per_device(): block = lax.all_gather(frozen_down_weight.T, 'y', axis=0, tiled=True)]
    unnamed x40 -> x64, local copies, waits for them, and re-layouts: 1.51 us -> 13.5 us
    ppermute x8, waiting for transfers between devices: 12.7 us -> 1.55 us  [step(): high[k] = lax.ppermute(high_from, z_axes, ring(n_z, -1))]
    ppermute x8, waiting for transfers between devices: 11.9 us -> 6.27 us  [step(): low[k] = lax.ppermute(low_from, z_axes, ring(n_z, 1))]
    ppermute x8, starting transfers between devices: 47.9 us -> 42.5 us  [step(): high[k] = lax.ppermute(high_from, z_axes, ring(n_z, -1))]
  transfers between devices with their start and end apart: 19 -> 26, of which waited for: 9 -> 7; matrix products, arithmetic and copies ran while one was open for 2% -> 7% of each run, Pallas kernels for 9% -> 9%
where the time goes in v7:
time: 252 us; the launch traced here: 250 us
  starting transfers between devices  87.7 us (35%)
  blocking collectives  72.1 us (29%)
  Pallas kernels  35 us (14%)
  local copies, waits for them, and re-layouts  20 us (8%)
  waiting for transfers between devices  15.8 us (6%)
  between operations  15.4 us (6%)
  other arithmetic  4.54 us (2%)
    ppermute x8, starting transfers between devices, step(): high[k] = lax.ppermute(high_from, z_axes, ring(n_z, -1))  42.5 us
    all_to_all x1, blocking collectives, per_device(): lax.all_to_all(share.reshape(n_z, -1, 128), z_axes, 0, 0)  22.2 us
    all_to_all x1, blocking collectives, per_device(): lax.all_to_all(jnp.broadcast_to(share, (n_z,) + share.shape), z_axes, 0, 0)  17 us
    ppermute x3, starting transfers between devices, exchange(): lax.ppermute(jnp.concatenate(following, axis=0), 'y', ring(n_y, -1))  15.7 us
    ppermute x8, starting transfers between devices, step(): low[k] = lax.ppermute(low_from, z_axes, ring(n_z, 1))  15.4 us
    unnamed x64, local copies, waits for them, and re-layouts  13.5 us
    pallas_call x2, Pallas kernels, part(): pl.pallas_call(functools.partial(part_kernel, plan, len(blocks), before i...  13.3 us
    all_to_all x1, blocking collectives, per_device(): lax.all_to_all(out.reshape(n_y, -1, 128), 'y', 0, 0)  12.5 us
  transfers between devices with their start and end apart: 26, of which 7 were waited for; matrix products, arithmetic and copies ran while one was open for 7% of the time, Pallas kernels for 9%

profile of v7, /device:TPU:32, one launch (start us, length us, event | category | flops | bytes accessed | tf_op | source)
XLA Modules:
  0.0 250.5 jit_solution(16335467517680050588)
XLA Ops:
  7.9 0.7 all-gather.5.cloned.1.call-update
  8.6 4.9 %collective-permute-start = (bf16[64,896]{1,0:T(8,128)(2,1)}, bf16[64,896]{1,0:T(8,128)(2,1)S(1)}, u32[]{:S(2)}, u32[]{:S(2)}) collective-permute-start(bf16[64,896]{1,0:T(8,128)(2,1)} %bitcast.43), channel_id=1, source_target_pairs={{0,24},{8,0},{16,8},{24,16},{1,25},{9,1},{17,9},{25,17},{2,26},{10... | collective-permute-start | bytes 344072 | tf_op jit(solution)/shard_map/ppermute | solution.py:300
  13.6 1.6 slice_bitcast_fusion.refs_2_
  15.2 1.1 collective-permute-done
  16.3 0.9 pad_maximum_fusion.2.refs_2_
  17.2 6.7 %collective-permute-start.7 = (bf16[128,896]{1,0:T(8,128)(2,1)S(1)}, bf16[128,896]{1,0:T(8,128)(2,1)S(1)}, u32[]{:S(2)}, u32[]{:S(2)}) collective-permute-start(bf16[128,896]{1,0:T(8,128)(2,1)S(1)} %pad_maximum_fusion.2.refs_2_), channel_id=1, source_target_pairs={{0,480},{32,0},{64,32},{96,64},{128,96},{160,128},{192,160},{224,1... | collective-permute-start | bytes 688136 | tf_op jit(solution)/shard_map/ppermute | solution.py:306
  23.9 1.9 collective-permute-start.1
  25.8 1.6 constant_dynamic-update-slice_fusion.1
  28.6 6.7 %collective-permute-start.8 = (bf16[128,896]{1,0:T(8,128)(2,1)S(1)}, bf16[128,896]{1,0:T(8,128)(2,1)S(1)}, u32[]{:S(2)}, u32[]{:S(2)}) collective-permute-start(bf16[128,896]{1,0:T(8,128)(2,1)S(1)} %collective-permute-done.7.refs_4_), channel_id=1, source_target_pairs={{0,480},{32,0},{64,32},{96,64},{128,96},{160,128},{192,160},{224,1... | collective-permute-start | bytes 688136 | tf_op jit(solution)/shard_map/ppermute | solution.py:306
  35.4 1.9 collective-permute-start.2
  37.3 0.7 slice_dynamic-update-slice_fusion.17
  38.0 0.7 slice_dynamic-update-slice_fusion.16
  39.0 5.0 %collective-permute-start.9 = (bf16[128,896]{1,0:T(8,128)(2,1)S(1)}, bf16[128,896]{1,0:T(8,128)(2,1)S(1)}, u32[]{:S(2)}, u32[]{:S(2)}) collective-permute-start(bf16[128,896]{1,0:T(8,128)(2,1)S(1)} %collective-permute-done.8.refs_6_), channel_id=1, source_target_pairs={{0,480},{32,0},{64,32},{96,64},{128,96},{160,128},{192,160},{224,1... | collective-permute-start | bytes 688136 | tf_op jit(solution)/shard_map/ppermute | solution.py:306
  44.5 1.9 collective-permute-start.3
  46.4 0.7 slice_dynamic-update-slice_fusion.15
  47.1 0.7 slice_dynamic-update-slice_fusion.14
  47.9 5.8 %collective-permute-done.3.refs_7_ = bf16[128,896]{1,0:T(8,128)(2,1)S(1)} collective-permute-done((bf16[128,896]{1,0:T(8,128)(2,1)S(1)}, bf16[128,896]{1,0:T(8,128)(2,1)S(1)}, u32[]{:S(2)}, u32[]{:S(2)}) %collective-permute-start.3) | collective-permute-done | bytes 229408 | tf_op jit(solution)/shard_map/ppermute | solution.py:305
  53.6 1.9 collective-permute-start.4
  55.5 0.7 slice_dynamic-update-slice_fusion.13
  56.3 0.7 slice_dynamic-update-slice_fusion.12
  57.0 5.5 %collective-permute-start.10 = (bf16[448,896]{1,0:T(8,128)(2,1)}, bf16[448,896]{1,0:T(8,128)(2,1)S(1)}, u32[]{:S(2)}, u32[]{:S(2)}) collective-permute-start(bf16[448,896]{1,0:T(8,128)(2,1)} %get-tuple-element.41), channel_id=1, source_target_pairs={{0,24},{8,0},{16,8},{24,16},{1,25},{9,1},{17,9},{25,17},{2,26},{10... | collective-permute-start | bytes 2408456 | tf_op jit(solution)/shard_map/ppermute | solution.py:317
  62.5 1.9 collective-permute-start.11
  64.4 5.1 %collective-permute-start.13 = (bf16[128,896]{1,0:T(8,128)(2,1)S(1)}, bf16[128,896]{1,0:T(8,128)(2,1)S(1)}, u32[]{:S(2)}, u32[]{:S(2)}) collective-permute-start(bf16[128,896]{1,0:T(8,128)(2,1)S(1)} %collective-permute-done.9.refs_8_), channel_id=1, source_target_pairs={{0,480},{32,0},{64,32},{96,64},{128,96},{160,128},{192,160},{224,1... | collective-permute-start | bytes 688136 | tf_op jit(solution)/shard_map/ppermute | solution.py:306
  69.6 1.9 collective-permute-start.5
  71.5 0.7 slice_dynamic-update-slice_fusion.5
  72.2 0.9 collective-permute-done.13.refs_3_
  73.1 5.1 %collective-permute-start.14 = (bf16[128,896]{1,0:T(8,128)(2,1)S(1)}, bf16[128,896]{1,0:T(8,128)(2,1)S(1)}, u32[]{:S(2)}, u32[]{:S(2)}) collective-permute-start(bf16[128,896]{1,0:T(8,128)(2,1)S(1)} %collective-permute-done.13.refs_3_), channel_id=1, source_target_pairs={{0,480},{32,0},{64,32},{96,64},{128,96},{160,128},{192,160},{224,1... | collective-permute-start | bytes 688136 | tf_op jit(solution)/shard_map/ppermute | solution.py:306
  78.2 0.7 slice_dynamic-update-slice_fusion.4
  78.9 0.8 slice_dynamic-update-slice_fusion.3
  79.7 4.8 %gradient_side.1 = (bf16[16,512]{1,0:T(8,128)(2,1)}, f32[4,128,128]{2,1,0:T(8,128)}) custom-call(bf16[512,4096]{1,0:T(8,128)(2,1)} %all-gather.3.cloned.1.call-done.refs_0_.refs_1_.gradient_ref, bf16[512,4096]{1,0:T(8,128)(2,1)} %all-gather.3.cloned.1.call-done.refs_0_.refs_1_.gradient_ref, bf16[16,4096]{1,0:T(8,128)(2,1)} %slice_bitcast_fusion.refs_2_), custom_call_target="tpu_custom_call" | custom-call | flops 603979776 | bytes 5242880 | tf_op jit(solution)/shard_map/gradient_side/pallas_call | solution.py:336
  84.6 5.6 %collective-permute-start.15 = (bf16[128,896]{1,0:T(8,128)(2,1)S(1)}, bf16[128,896]{1,0:T(8,128)(2,1)S(1)}, u32[]{:S(2)}, u32[]{:S(2)}) collective-permute-start(bf16[128,896]{1,0:T(8,128)(2,1)S(1)} %collective-permute-done.14.refs_5_), channel_id=1, source_target_pairs={{0,480},{32,0},{64,32},{96,64},{128,96},{160,128},{192,160},{224,1... | collective-permute-start | bytes 688136 | tf_op jit(solution)/shard_map/ppermute | solution.py:306
  90.2 1.9 collective-permute-start.6
  92.1 0.7 slice_dynamic-update-slice_fusion.2
  92.9 0.9 copy-done.15
  93.8 6.7 %part_product.2.refs_8_ = f32[512,896]{1,0:T(8,128)} custom-call(s32[8]{0:T(128)} %stack.74.place_ref, bf16[512,4096]{1,0:T(8,128)(2,1)} %all-gather.3.cloned.1.call-done.refs_0_.refs_1_.gradient_ref, bf16[448,896]{1,0:T(8,128)(2,1)} %copy-done.15, bf16[448,896]{1,0:T(8,128)(2,1)} %collective-permute-done.11.refs_1_, bf16[128,896]{1,0:T(8,128)(2,1)} %copy-done.6, ...), custom_call_target="tpu_custom_call" | custom-call | flops 1644167168 | bytes 6291456 | tf_op jit(solution)/shard_map/part_product/pallas_call | solution.py:378
  100.5 3.9 %collective-permute-start.16 = (bf16[128,896]{1,0:T(8,128)(2,1)S(1)}, bf16[128,896]{1,0:T(8,128)(2,1)S(1)}, u32[]{:S(2)}, u32[]{:S(2)}) collective-permute-start(bf16[128,896]{1,0:T(8,128)(2,1)S(1)} %collective-permute-done.15.refs_7_), channel_id=1, source_target_pairs={{0,480},{32,0},{64,32},{96,64},{128,96},{160,128},{192,160},{224,1... | collective-permute-start | bytes 688136 | tf_op jit(solution)/shard_map/ppermute | solution.py:306
  104.4 2.0 collective-permute-start.12
  106.3 0.7 slice_dynamic-update-slice_fusion.1
  107.0 0.7 slice_dynamic-update-slice_fusion
  107.8 5.1 %collective-permute-start.21 = (bf16[384,896]{1,0:T(8,128)(2,1)}, bf16[384,896]{1,0:T(8,128)(2,1)S(1)}, u32[]{:S(2)}, u32[]{:S(2)}) collective-permute-start(bf16[384,896]{1,0:T(8,128)(2,1)} %get-tuple-element.25), channel_id=1, source_target_pairs={{0,24},{8,0},{16,8},{24,16},{1,25},{9,1},{17,9},{25,17},{2,26},{10... | collective-permute-start | bytes 2064392 | tf_op jit(solution)/shard_map/ppermute | solution.py:317
  112.8 1.9 collective-permute-start.22
  114.8 4.4 %collective-permute-start.17 = (bf16[64,896]{1,0:T(8,128)(2,1)S(1)}, bf16[64,896]{1,0:T(8,128)(2,1)S(1)}, u32[]{:S(2)}, u32[]{:S(2)}) collective-permute-start(bf16[64,896]{1,0:T(8,128)(2,1)S(1)} %get-tuple-element.37), channel_id=1, source_target_pairs={{0,480},{32,0},{64,32},{96,64},{128,96},{160,128},{192,160},{224,1... | collective-permute-start | bytes 344072 | tf_op jit(solution)/shard_map/ppermute | solution.py:306
  119.3 1.9 collective-permute-start.19
  121.5 0.8 pad_maximum_fusion
  122.3 5.1 %collective-permute-start.18 = (bf16[192,896]{1,0:T(8,128)(2,1)}, bf16[192,896]{1,0:T(8,128)(2,1)S(1)}, u32[]{:S(2)}, u32[]{:S(2)}) collective-permute-start(bf16[192,896]{1,0:T(8,128)(2,1)} %pad_maximum_fusion), channel_id=1, source_target_pairs={{0,24},{8,0},{16,8},{24,16},{1,25},{9,1},{17,9},{25,17},{2,26},{10... | collective-permute-start | bytes 1032200 | tf_op jit(solution)/shard_map/ppermute | solution.py:317
  127.5 0.8 pad_maximum_fusion.1
  128.3 1.9 collective-permute-start.20
  130.3 0.7 slice.130
  132.3 0.8 copy.13
  133.1 4.8 %normed_side.1 = (bf16[32,512]{1,0:T(8,128)(2,1)}, f32[4,128,128]{2,1,0:T(8,128)}) custom-call(bf16[512,4096]{1,0:T(8,128)(2,1)} %all-gather.5.cloned.1.call-done.refs_0_.refs_1_, bf16[512,4096]{1,0:T(8,128)(2,1)} %all-gather.5.cloned.1.call-done.refs_0_.refs_1_, bf16[32,4096]{1,0:T(8,128)(2,1)} %bitcast.40), custom_call_target="tpu_custom_call" | custom-call | flops 671088640 | bytes 5242880 | tf_op jit(solution)/shard_map/normed_side/pallas_call | solution.py:336
  138.0 0.8 copy-done.16
  138.8 0.9 copy-done.17
  139.7 6.7 %part_product.3.refs_6_ = f32[512,896]{1,0:T(8,128)} custom-call(s32[7]{0:T(128)} %stack.81.place_ref, bf16[512,4096]{1,0:T(8,128)(2,1)} %all-gather.3.cloned.1.call-done.refs_0_.refs_1_.gradient_ref, bf16[384,896]{1,0:T(8,128)(2,1)} %copy-done.16, bf16[384,896]{1,0:T(8,128)(2,1)} %copy-done.17, bf16[128,896]{1,0:T(8,128)(2,1)} %copy-done, ...), custom_call_target="tpu_custom_call" | custom-call | flops 1409286144 | bytes 6291456 | tf_op jit(solution)/shard_map/part_product/pallas_call | solution.py:378
  146.4 0.7 copy-done.22
  147.1 9.2 %hidden_side.1 = (f32[4,48,896]{2,1,0:T(8,128)}, f32[64,512]{1,0:T(8,128)}) custom-call(s32[4]{0:T(128)} %pad_add_fusion.place_ref, bf16[512,4096]{1,0:T(8,128)(2,1)} %all-gather.3.cloned.1.call-done.refs_0_.refs_1_.gradient_ref, bf16[192,896]{1,0:T(8,128)(2,1)} %copy-done.22, bf16[192,896]{1,0:T(8,128)(2,1)} %collective-permute-done.20.refs_1_, ...), custom_call_target="tpu_custom_call" | custom-call | tf_op jit(solution)/shard_map/hidden_side/pallas_call | solution.py:422
  156.3 11.2 %all_to_all.30 = f32[8,8,512]{2,1,0:T(8,128)S(1)} all-to-all(f32[8,8,512]{2,1,0:T(8,128)} %bitcast.45), channel_id=1, replica_groups=mesh['z'=16,'y'=4,'x'=4,'c'=2] {'x','c'}, dimensions={0} | all-to-all | bytes 262144 | tf_op jit(solution)/shard_map/all_to_all | solution.py:453
  168.2 3.4 %all-to-all-start.1 = ((f32[8,8,512]{2,1,0:T(8,128)}), f32[8,8,512]{2,1,0:T(8,128)S(1)}, u32[]{:S(2)}, u32[]{:S(2)}) async-start(f32[8,8,512]{2,1,0:T(8,128)} %broadcast_in_dim.9), calls=%async_computation.1 | async-start | bytes 262144 | tf_op jit(solution)/shard_map/all_to_all | solution.py:455
  172.2 5.4 %all-to-all-done.1 = f32[8,8,512]{2,1,0:T(8,128)S(1)} async-done(((f32[8,8,512]{2,1,0:T(8,128)}), f32[8,8,512]{2,1,0:T(8,128)S(1)}, u32[]{:S(2)}, u32[]{:S(2)}) %all-to-all-start.1) | async-done | bytes 131104 | tf_op jit(solution)/shard_map/all_to_all | solution.py:455
  178.3 2.9 %clip_side.1 = f32[72,8,128]{2,1,0:T(8,128)} custom-call(f32[1]{0:T(128)} %copy.36.clip_ref, f32[64,512]{1,0:T(8,128)} %bitcast.42, f32[4,48,896]{2,1,0:T(8,128)} %get-tuple-element.21.sums_ref, bf16[512,512]{1,0:T(8,128)(2,1)} %normed_ref.1, bf16[512,512]{1,0:T(8,128)(2,1)} %gradient_ref.1, f32[4,128,128]{2,1,0:T(8,128)} %get-tuple-element.22.normed_gram_ref, ...), custom_call_target="tpu_custom_call" | custom-call | tf_op jit(solution)/shard_map/clip_side/pallas_call | solution.py:462
  181.2 12.5 %all_to_all.31 = f32[4,144,128]{2,1,0:T(8,128)S(1)} all-to-all(f32[4,144,128]{2,1,0:T(8,128)} %bitcast.36), channel_id=1, replica_groups=mesh['z'=16,'y'=4,'x'=4,'c'=2] {'y'}, dimensions={0} | all-to-all | bytes 589824 | tf_op jit(solution)/shard_map/all_to_all | solution.py:480
  193.7 22.2 %all_to_all.32 = f32[16,9,128]{2,1,0:T(8,128)S(1)} all-to-all(f32[16,9,128]{2,1,0:T(8,128)S(1)} %reshape.39), channel_id=1, replica_groups=mesh['z'=16,'y'=4,'x'=4,'c'=2] {'z'}, dimensions={0} | all-to-all | bytes 147456 | tf_op jit(solution)/shard_map/all_to_all | solution.py:481
  216.0 17.0 %all_to_all.33 = f32[16,9,128]{2,1,0:T(8,128)S(1)} all-to-all(f32[16,9,128]{2,1,0:T(8,128)S(1)} %broadcast_in_dim.10), channel_id=1, replica_groups=mesh['z'=16,'y'=4,'x'=4,'c'=2] {'z'}, dimensions={0} | all-to-all | bytes 147456 | tf_op jit(solution)/shard_map/all_to_all | solution.py:482
  233.0 9.2 %all_to_all.34 = f32[4,144,128]{2,1,0:T(8,128)S(1)} all-to-all(f32[4,144,128]{2,1,0:T(8,128)S(1)} %broadcast_in_dim.11), channel_id=1, replica_groups=mesh['z'=16,'y'=4,'x'=4,'c'=2] {'y'}, dimensions={0} | all-to-all | bytes 589824 | tf_op jit(solution)/shard_map/all_to_all | solution.py:485
  243.0 0.7 fusion
  (89 shorter events, 6.8 us)
Async XLA Ops:
  7.2 72.6 %all-gather.3.cloned.1.call-start = ((), (), s32[]{:S(2)}) async-start(), calls=%async_computation.6 | async-start | bytes 4718592 | tf_op jit(solution)/shard_map/all_gather | solution.py:283
  7.9 125.2 %all-gather.5.cloned.1.call-start = ((), (), s32[]{:S(2)}) async-start(), calls=%async_computation.7 | async-start | bytes 4718592 | tf_op jit(solution)/shard_map/all_gather | solution.py:285
  8.6 7.6 %collective-permute-start = (bf16[64,896]{1,0:T(8,128)(2,1)}, bf16[64,896]{1,0:T(8,128)(2,1)S(1)}, u32[]{:S(2)}, u32[]{:S(2)}) collective-permute-start(bf16[64,896]{1,0:T(8,128)(2,1)} %bitcast.43), channel_id=1, source_target_pairs={{0,24},{8,0},{16,8},{24,16},{1,25},{9,1},{17,9},{25,17},{2,26},{10... | collective-permute-start | bytes 344072 | tf_op jit(solution)/shard_map/ppermute | solution.py:300
  17.2 67.3 %copy-start.6 = (bf16[128,896]{1,0:T(8,128)(2,1)}, bf16[128,896]{1,0:T(8,128)(2,1)S(1)}, u32[]{:S(2)}) copy-start(bf16[128,896]{1,0:T(8,128)(2,1)S(1)} %pad_maximum_fusion.2.refs_2_) | copy-start | bytes 688132
  17.2 11.4 %collective-permute-start.7 = (bf16[128,896]{1,0:T(8,128)(2,1)S(1)}, bf16[128,896]{1,0:T(8,128)(2,1)S(1)}, u32[]{:S(2)}, u32[]{:S(2)}) collective-permute-start(bf16[128,896]{1,0:T(8,128)(2,1)S(1)} %pad_maximum_fusion.2.refs_2_), channel_id=1, source_target_pairs={{0,480},{32,0},{64,32},{96,64},{128,96},{160,128},{192,160},{224,1... | collective-permute-start | bytes 688136 | tf_op jit(solution)/shard_map/ppermute | solution.py:306
  23.9 11.5 %collective-permute-start.1 = (bf16[128,896]{1,0:T(8,128)(2,1)S(1)}, bf16[128,896]{1,0:T(8,128)(2,1)S(1)}, u32[]{:S(2)}, u32[]{:S(2)}) collective-permute-start(bf16[128,896]{1,0:T(8,128)(2,1)S(1)} %pad_maximum_fusion.2.refs_2_), channel_id=1, source_target_pairs={{0,32},{32,64},{64,96},{96,128},{128,160},{160,192},{192,224},{224... | collective-permute-start | bytes 688136 | tf_op jit(solution)/shard_map/ppermute | solution.py:305
  28.6 55.9 %copy-start.7 = (bf16[128,896]{1,0:T(8,128)(2,1)}, bf16[128,896]{1,0:T(8,128)(2,1)S(1)}, u32[]{:S(2)}) copy-start(bf16[128,896]{1,0:T(8,128)(2,1)S(1)} %collective-permute-done.7.refs_4_) | copy-start | bytes 688132
  28.6 10.4 %collective-permute-start.8 = (bf16[128,896]{1,0:T(8,128)(2,1)S(1)}, bf16[128,896]{1,0:T(8,128)(2,1)S(1)}, u32[]{:S(2)}, u32[]{:S(2)}) collective-permute-start(bf16[128,896]{1,0:T(8,128)(2,1)S(1)} %collective-permute-done.7.refs_4_), channel_id=1, source_target_pairs={{0,480},{32,0},{64,32},{96,64},{128,96},{160,128},{192,160},{224,1... | collective-permute-start | bytes 688136 | tf_op jit(solution)/shard_map/ppermute | solution.py:306
  35.4 49.2 %copy-start.8 = (bf16[128,896]{1,0:T(8,128)(2,1)}, bf16[128,896]{1,0:T(8,128)(2,1)S(1)}, u32[]{:S(2)}) copy-start(bf16[128,896]{1,0:T(8,128)(2,1)S(1)} %collective-permute-done.1.refs_3_) | copy-start | bytes 688132
  35.4 9.1 %collective-permute-start.2 = (bf16[128,896]{1,0:T(8,128)(2,1)S(1)}, bf16[128,896]{1,0:T(8,128)(2,1)S(1)}, u32[]{:S(2)}, u32[]{:S(2)}) collective-permute-start(bf16[128,896]{1,0:T(8,128)(2,1)S(1)} %collective-permute-done.1.refs_3_), channel_id=1, source_target_pairs={{0,32},{32,64},{64,96},{96,128},{128,160},{160,192},{192,224},{224... | collective-permute-start | bytes 688136 | tf_op jit(solution)/shard_map/ppermute | solution.py:305
  39.0 45.5 %copy-start.11 = (bf16[128,896]{1,0:T(8,128)(2,1)}, bf16[128,896]{1,0:T(8,128)(2,1)S(1)}, u32[]{:S(2)}) copy-start(bf16[128,896]{1,0:T(8,128)(2,1)S(1)} %collective-permute-done.8.refs_6_) | copy-start | bytes 688132
  39.0 17.2 %collective-permute-start.9 = (bf16[128,896]{1,0:T(8,128)(2,1)S(1)}, bf16[128,896]{1,0:T(8,128)(2,1)S(1)}, u32[]{:S(2)}, u32[]{:S(2)}) collective-permute-start(bf16[128,896]{1,0:T(8,128)(2,1)S(1)} %collective-permute-done.8.refs_6_), channel_id=1, source_target_pairs={{0,480},{32,0},{64,32},{96,64},{128,96},{160,128},{192,160},{224,1... | collective-permute-start | bytes 688136 | tf_op jit(solution)/shard_map/ppermute | solution.py:306
  44.5 40.0 %copy-start.12 = (bf16[128,896]{1,0:T(8,128)(2,1)}, bf16[128,896]{1,0:T(8,128)(2,1)S(1)}, u32[]{:S(2)}) copy-start(bf16[128,896]{1,0:T(8,128)(2,1)S(1)} %collective-permute-done.2.refs_5_) | copy-start | bytes 688132
  44.5 9.1 %collective-permute-start.3 = (bf16[128,896]{1,0:T(8,128)(2,1)S(1)}, bf16[128,896]{1,0:T(8,128)(2,1)S(1)}, u32[]{:S(2)}, u32[]{:S(2)}) collective-permute-start(bf16[128,896]{1,0:T(8,128)(2,1)S(1)} %collective-permute-done.2.refs_5_), channel_id=1, source_target_pairs={{0,32},{32,64},{64,96},{96,128},{128,160},{160,192},{192,224},{224... | collective-permute-start | bytes 688136 | tf_op jit(solution)/shard_map/ppermute | solution.py:305
  53.6 30.9 %copy-start.14 = (bf16[128,896]{1,0:T(8,128)(2,1)}, bf16[128,896]{1,0:T(8,128)(2,1)S(1)}, u32[]{:S(2)}) copy-start(bf16[128,896]{1,0:T(8,128)(2,1)S(1)} %collective-permute-done.3.refs_7_) | copy-start | bytes 688132
  53.6 16.0 %collective-permute-start.4 = (bf16[128,896]{1,0:T(8,128)(2,1)S(1)}, bf16[128,896]{1,0:T(8,128)(2,1)S(1)}, u32[]{:S(2)}, u32[]{:S(2)}) collective-permute-start(bf16[128,896]{1,0:T(8,128)(2,1)S(1)} %collective-permute-done.3.refs_7_), channel_id=1, source_target_pairs={{0,32},{32,64},{64,96},{96,128},{128,160},{160,192},{192,224},{224... | collective-permute-start | bytes 688136 | tf_op jit(solution)/shard_map/ppermute | solution.py:305
  56.3 28.3 %copy-start.13 = (bf16[128,896]{1,0:T(8,128)(2,1)}, bf16[128,896]{1,0:T(8,128)(2,1)S(1)}, u32[]{:S(2)}) copy-start(bf16[128,896]{1,0:T(8,128)(2,1)S(1)} %collective-permute-done.9.refs_8_) | copy-start | bytes 688132
  57.0 35.9 %collective-permute-start.10 = (bf16[448,896]{1,0:T(8,128)(2,1)}, bf16[448,896]{1,0:T(8,128)(2,1)S(1)}, u32[]{:S(2)}, u32[]{:S(2)}) collective-permute-start(bf16[448,896]{1,0:T(8,128)(2,1)} %get-tuple-element.41), channel_id=1, source_target_pairs={{0,24},{8,0},{16,8},{24,16},{1,25},{9,1},{17,9},{25,17},{2,26},{10... | collective-permute-start | bytes 2408456 | tf_op jit(solution)/shard_map/ppermute | solution.py:317
  62.5 30.4 %collective-permute-start.11 = (bf16[448,896]{1,0:T(8,128)(2,1)}, bf16[448,896]{1,0:T(8,128)(2,1)}, u32[]{:S(2)}, u32[]{:S(2)}) collective-permute-start(bf16[448,896]{1,0:T(8,128)(2,1)} %get-tuple-element.40), channel_id=1, source_target_pairs={{0,8},{8,16},{16,24},{24,0},{1,9},{9,17},{17,25},{25,1},{2,10},{10... | collective-permute-start | bytes 2408456 | tf_op jit(solution)/shard_map/ppermute | solution.py:318
  64.4 8.7 %collective-permute-start.13 = (bf16[128,896]{1,0:T(8,128)(2,1)S(1)}, bf16[128,896]{1,0:T(8,128)(2,1)S(1)}, u32[]{:S(2)}, u32[]{:S(2)}) collective-permute-start(bf16[128,896]{1,0:T(8,128)(2,1)S(1)} %collective-permute-done.9.refs_8_), channel_id=1, source_target_pairs={{0,480},{32,0},{64,32},{96,64},{128,96},{160,128},{192,160},{224,1... | collective-permute-start | bytes 688136 | tf_op jit(solution)/shard_map/ppermute | solution.py:306
  69.6 15.0 %copy-start = (bf16[128,896]{1,0:T(8,128)(2,1)}, bf16[128,896]{1,0:T(8,128)(2,1)S(1)}, u32[]{:S(2)}) copy-start(bf16[128,896]{1,0:T(8,128)(2,1)S(1)} %collective-permute-done.4.refs_2_) | copy-start | bytes 688132
  69.6 9.4 %collective-permute-start.5 = (bf16[128,896]{1,0:T(8,128)(2,1)S(1)}, bf16[128,896]{1,0:T(8,128)(2,1)S(1)}, u32[]{:S(2)}, u32[]{:S(2)}) collective-permute-start(bf16[128,896]{1,0:T(8,128)(2,1)S(1)} %collective-permute-done.4.refs_2_), channel_id=1, source_target_pairs={{0,32},{32,64},{64,96},{96,128},{128,160},{160,192},{192,224},{224... | collective-permute-start | bytes 688136 | tf_op jit(solution)/shard_map/ppermute | solution.py:305
  73.1 11.5 %copy-start.1 = (bf16[128,896]{1,0:T(8,128)(2,1)}, bf16[128,896]{1,0:T(8,128)(2,1)S(1)}, u32[]{:S(2)}) copy-start(bf16[128,896]{1,0:T(8,128)(2,1)S(1)} %collective-permute-done.13.refs_3_) | copy-start | bytes 688132
  73.1 11.5 %collective-permute-start.14 = (bf16[128,896]{1,0:T(8,128)(2,1)S(1)}, bf16[128,896]{1,0:T(8,128)(2,1)S(1)}, u32[]{:S(2)}, u32[]{:S(2)}) collective-permute-start(bf16[128,896]{1,0:T(8,128)(2,1)S(1)} %collective-permute-done.13.refs_3_), channel_id=1, source_target_pairs={{0,480},{32,0},{64,32},{96,64},{128,96},{160,128},{192,160},{224,1... | collective-permute-start | bytes 688136 | tf_op jit(solution)/shard_map/ppermute | solution.py:306
  78.9 11.3 %copy-start.2 = (bf16[128,896]{1,0:T(8,128)(2,1)}, bf16[128,896]{1,0:T(8,128)(2,1)S(1)}, u32[]{:S(2)}) copy-start(bf16[128,896]{1,0:T(8,128)(2,1)S(1)} %collective-permute-done.5.refs_4_) | copy-start | bytes 688132
  84.6 15.8 %copy-start.3 = (bf16[128,896]{1,0:T(8,128)(2,1)}, bf16[128,896]{1,0:T(8,128)(2,1)S(1)}, u32[]{:S(2)}) copy-start(bf16[128,896]{1,0:T(8,128)(2,1)S(1)} %collective-permute-done.14.refs_5_) | copy-start | bytes 688132
  84.6 15.8 %collective-permute-start.15 = (bf16[128,896]{1,0:T(8,128)(2,1)S(1)}, bf16[128,896]{1,0:T(8,128)(2,1)S(1)}, u32[]{:S(2)}, u32[]{:S(2)}) collective-permute-start(bf16[128,896]{1,0:T(8,128)(2,1)S(1)} %collective-permute-done.14.refs_5_), channel_id=1, source_target_pairs={{0,480},{32,0},{64,32},{96,64},{128,96},{160,128},{192,160},{224,1... | collective-permute-start | bytes 688136 | tf_op jit(solution)/shard_map/ppermute | solution.py:306
  90.2 14.1 %collective-permute-start.6 = (bf16[128,896]{1,0:T(8,128)(2,1)S(1)}, bf16[128,896]{1,0:T(8,128)(2,1)S(1)}, u32[]{:S(2)}, u32[]{:S(2)}) collective-permute-start(bf16[128,896]{1,0:T(8,128)(2,1)S(1)} %collective-permute-done.5.refs_4_), channel_id=1, source_target_pairs={{0,32},{32,64},{64,96},{96,128},{128,160},{160,192},{192,224},{224... | collective-permute-start | bytes 688136 | tf_op jit(solution)/shard_map/ppermute | solution.py:305
  92.9 37.4 %copy-start.21 = (bf16[3,16,4096]{2,1,0:T(8,128)(2,1)S(1)}, bf16[3,16,4096]{2,1,0:T(8,128)(2,1)}, u32[]{:S(2)}) copy-start(bf16[3,16,4096]{2,1,0:T(8,128)(2,1)} %param.15) | copy-start | bytes 1179652
  92.9 39.5 %copy-start.25 = (bf16[16,512]{1,0:T(8,128)(2,1)S(1)}, bf16[16,512]{1,0:T(8,128)(2,1)}, u32[]{:S(2)}) copy-start(bf16[16,512]{1,0:T(8,128)(2,1)} %get-tuple-element.13.refs_12_) | copy-start | bytes 49156
  92.9 0.9 copy-start.15
  100.5 37.5 %copy-start.4 = (bf16[128,896]{1,0:T(8,128)(2,1)}, bf16[128,896]{1,0:T(8,128)(2,1)S(1)}, u32[]{:S(2)}) copy-start(bf16[128,896]{1,0:T(8,128)(2,1)S(1)} %collective-permute-done.15.refs_7_) | copy-start | bytes 688132
  100.5 14.3 %collective-permute-start.16 = (bf16[128,896]{1,0:T(8,128)(2,1)S(1)}, bf16[128,896]{1,0:T(8,128)(2,1)S(1)}, u32[]{:S(2)}, u32[]{:S(2)}) collective-permute-start(bf16[128,896]{1,0:T(8,128)(2,1)S(1)} %collective-permute-done.15.refs_7_), channel_id=1, source_target_pairs={{0,480},{32,0},{64,32},{96,64},{128,96},{160,128},{192,160},{224,1... | collective-permute-start | bytes 688136 | tf_op jit(solution)/shard_map/ppermute | solution.py:306
  104.4 33.5 %copy-start.5 = (bf16[128,896]{1,0:T(8,128)(2,1)}, bf16[128,896]{1,0:T(8,128)(2,1)S(1)}, u32[]{:S(2)}) copy-start(bf16[128,896]{1,0:T(8,128)(2,1)S(1)} %collective-permute-done.6.refs_6_) | copy-start | bytes 688132
  104.4 14.8 %collective-permute-start.12 = (bf16[128,896]{1,0:T(8,128)(2,1)S(1)}, bf16[128,896]{1,0:T(8,128)(2,1)S(1)}, u32[]{:S(2)}, u32[]{:S(2)}) collective-permute-start(bf16[128,896]{1,0:T(8,128)(2,1)S(1)} %collective-permute-done.6.refs_6_), channel_id=1, source_target_pairs={{0,32},{32,64},{64,96},{96,128},{128,160},{160,192},{192,224},{224... | collective-permute-start | bytes 688136 | tf_op jit(solution)/shard_map/ppermute | solution.py:305
  107.8 30.2 %collective-permute-start.21 = (bf16[384,896]{1,0:T(8,128)(2,1)}, bf16[384,896]{1,0:T(8,128)(2,1)S(1)}, u32[]{:S(2)}, u32[]{:S(2)}) collective-permute-start(bf16[384,896]{1,0:T(8,128)(2,1)} %get-tuple-element.25), channel_id=1, source_target_pairs={{0,24},{8,0},{16,8},{24,16},{1,25},{9,1},{17,9},{25,17},{2,26},{10... | collective-permute-start | bytes 2064392 | tf_op jit(solution)/shard_map/ppermute | solution.py:317
  112.8 25.1 %collective-permute-start.22 = (bf16[384,896]{1,0:T(8,128)(2,1)}, bf16[384,896]{1,0:T(8,128)(2,1)S(1)}, u32[]{:S(2)}, u32[]{:S(2)}) collective-permute-start(bf16[384,896]{1,0:T(8,128)(2,1)} %get-tuple-element.24), channel_id=1, source_target_pairs={{0,8},{8,16},{16,24},{24,0},{1,9},{9,17},{17,25},{25,1},{2,10},{10... | collective-permute-start | bytes 2064392 | tf_op jit(solution)/shard_map/ppermute | solution.py:318
  114.8 23.1 %copy-start.9 = (bf16[128,896]{1,0:T(8,128)(2,1)}, bf16[128,896]{1,0:T(8,128)(2,1)S(1)}, u32[]{:S(2)}) copy-start(bf16[128,896]{1,0:T(8,128)(2,1)S(1)} %collective-permute-done.16.refs_3_) | copy-start | bytes 688132
  114.8 6.7 %collective-permute-start.17 = (bf16[64,896]{1,0:T(8,128)(2,1)S(1)}, bf16[64,896]{1,0:T(8,128)(2,1)S(1)}, u32[]{:S(2)}, u32[]{:S(2)}) collective-permute-start(bf16[64,896]{1,0:T(8,128)(2,1)S(1)} %get-tuple-element.37), channel_id=1, source_target_pairs={{0,480},{32,0},{64,32},{96,64},{128,96},{160,128},{192,160},{224,1... | collective-permute-start | bytes 344072 | tf_op jit(solution)/shard_map/ppermute | solution.py:306
  119.2 18.7 %copy-start.10 = (bf16[128,896]{1,0:T(8,128)(2,1)}, bf16[128,896]{1,0:T(8,128)(2,1)S(1)}, u32[]{:S(2)}) copy-start(bf16[128,896]{1,0:T(8,128)(2,1)S(1)} %collective-permute-done.12.refs_2_) | copy-start | bytes 688132
  119.3 8.2 %collective-permute-start.19 = (bf16[64,896]{1,0:T(8,128)(2,1)S(1)}, bf16[64,896]{1,0:T(8,128)(2,1)S(1)}, u32[]{:S(2)}, u32[]{:S(2)}) collective-permute-start(bf16[64,896]{1,0:T(8,128)(2,1)S(1)} %get-tuple-element.38), channel_id=1, source_target_pairs={{0,32},{32,64},{64,96},{96,128},{128,160},{160,192},{192,224},{224... | collective-permute-start | bytes 344072 | tf_op jit(solution)/shard_map/ppermute | solution.py:305
  121.5 16.4 %copy-start.19 = (bf16[64,896]{1,0:T(8,128)(2,1)}, bf16[64,896]{1,0:T(8,128)(2,1)S(1)}, u32[]{:S(2)}) copy-start(bf16[64,896]{1,0:T(8,128)(2,1)S(1)} %collective-permute-done.17.refs_5_) | copy-start | bytes 344068
  122.3 24.1 %collective-permute-start.18 = (bf16[192,896]{1,0:T(8,128)(2,1)}, bf16[192,896]{1,0:T(8,128)(2,1)S(1)}, u32[]{:S(2)}, u32[]{:S(2)}) collective-permute-start(bf16[192,896]{1,0:T(8,128)(2,1)} %pad_maximum_fusion), channel_id=1, source_target_pairs={{0,24},{8,0},{16,8},{24,16},{1,25},{9,1},{17,9},{25,17},{2,26},{10... | collective-permute-start | bytes 1032200 | tf_op jit(solution)/shard_map/ppermute | solution.py:317
  127.5 10.5 %copy-start.20 = (bf16[64,896]{1,0:T(8,128)(2,1)}, bf16[64,896]{1,0:T(8,128)(2,1)S(1)}, u32[]{:S(2)}) copy-start(bf16[64,896]{1,0:T(8,128)(2,1)S(1)} %collective-permute-done.19.refs_4_) | copy-start | bytes 344068
  128.3 18.1 %collective-permute-start.20 = (bf16[192,896]{1,0:T(8,128)(2,1)}, bf16[192,896]{1,0:T(8,128)(2,1)}, u32[]{:S(2)}, u32[]{:S(2)}) collective-permute-start(bf16[192,896]{1,0:T(8,128)(2,1)} %pad_maximum_fusion.1), channel_id=1, source_target_pairs={{0,8},{8,16},{16,24},{24,0},{1,9},{9,17},{17,25},{25,1},{2,10},{10... | collective-permute-start | bytes 1032200 | tf_op jit(solution)/shard_map/ppermute | solution.py:318
  138.0 0.8 copy-start.16
  138.8 0.9 copy-start.17
  146.4 0.7 copy-start.22
  156.3 86.0 %copy-start.24 = (f32[3,16,512]{2,1,0:T(8,128)S(1)}, f32[3,16,512]{2,1,0:T(8,128)}, u32[]{:S(2)}) copy-start(f32[3,16,512]{2,1,0:T(8,128)} %param.18) | copy-start | bytes 294916
  156.3 86.6 %copy-start.23 = (f32[3,16,896]{2,1,0:T(8,128)S(1)}, f32[3,16,896]{2,1,0:T(8,128)}, u32[]{:S(2)}) copy-start(f32[3,16,896]{2,1,0:T(8,128)} %param.19) | copy-start | bytes 516100
  168.2 9.4 %all-to-all-start.1 = ((f32[8,8,512]{2,1,0:T(8,128)}), f32[8,8,512]{2,1,0:T(8,128)S(1)}, u32[]{:S(2)}, u32[]{:S(2)}) async-start(f32[8,8,512]{2,1,0:T(8,128)} %broadcast_in_dim.9), calls=%async_computation.1 | async-start | bytes 262144 | tf_op jit(solution)/shard_map/all_to_all | solution.py:455
  177.6 0.7 copy-start.18
Sparse Core Ops, SparseCore 0:
  10.1 43.8 all-gather.2
  56.2 39.7 all-gather.4

commit v8 on v6

--- a/solution.py
+++ b/solution.py
@@ -47,21 +47,26 @@
     return copies
 
 
-def fetch_blocks(place_ref, gradient_ref, block_refs, left, right, sems):
-    copies, row = [], 0
-    for i, block in enumerate(block_refs):
+def fetch_blocks(plan, z_ref, gradient_ref, block_refs, left, right, sems):
+    n_z, rows_z = plan["n_z"], plan["rows"]
+    fetched, row, at = [], 0, 0
+    for (offset, first), block in zip(plan["blocks"], block_refs, strict=True):
         rows = block.shape[0]
-        at = pl.ds(pl.multiple_of(place_ref[i] * 128, 128), rows)
+        start = lax.rem(z_ref[0] + (offset + n_z), n_z) * rows_z + first
+        columns = pl.ds(pl.multiple_of(start, 128), rows)
         span = pl.ds(row, rows)
-        copies += copy_rows(gradient_ref.at[:, at], left.at[:, span], sems, 4 * i, 2)
-        copies += copy_rows(block, right.at[span, :], sems, 4 * i + 2, 2)
+        fetched.append(
+            copy_rows(gradient_ref.at[:, columns], left.at[:, span], sems, at, 2)
+            + copy_rows(block, right.at[span, :], sems, at + 2, 2)
+        )
         row += rows
-    return copies
+        at += 4
+    return fetched
 
 
 def side_kernel(n_pairs, *refs):
     row_refs = refs[:n_pairs]
-    factors_ref, projected_ref, gram_ref, total = refs[n_pairs:]
+    factors_ref, projected_ref, turned_ref, gram_ref, total = refs[n_pairs:]
     step = pl.program_id(0)
     size = SEQUENCE_TOKENS
 
@@ -79,18 +84,17 @@
         for p in range(n_pairs):
             gram_ref[2 * p] = total[p, :size, :size]
             gram_ref[2 * p + 1] = total[p, size : 2 * size, size:]
-            projected_ref[:, 2 * size * p : 2 * size * (p + 1)] = total[p, 2 * size :].astype(BF16)
-
-
-def part_kernel(n_blocks, first, place_ref, gradient_ref, *refs):
+            span = slice(2 * size * p, 2 * size * (p + 1))
+            projected = total[p, 2 * size :]
+            projected_ref[:, span] = projected.astype(BF16)
+            turned_ref[span, :] = projected.T.astype(BF16)
+
+
+def part_kernel(plan, z_ref, gradient_ref, *refs):
+    n_blocks = len(plan["blocks"])
     block_refs = refs[:n_blocks]
-    refs = refs[n_blocks:]
-    if not first:
-        before_ref, refs = refs[0], refs[1:]
-    out_ref, total, left, right, sems, out_sems = refs
-    copies = fetch_blocks(place_ref, gradient_ref, block_refs, left, right, sems)
-    if not first:
-        copies += copy_rows(before_ref, total, sems, 4 * n_blocks, 4)
+    out_ref, total, left, right, sems, out_sems = refs[n_blocks:]
+    copies = sum(fetch_blocks(plan, z_ref, gradient_ref, block_refs, left, right, sems), [])
     for copy in copies:
         copy.start()
     for copy in copies:
@@ -100,8 +104,7 @@
     hidden = total.shape[1]
     for i, start in enumerate(range(0, hidden, 512)):
         cols = slice(start, min(start + 512, hidden))
-        product = jnp.dot(left[...], right[:, cols], preferred_element_type=F32)
-        total[:, cols] = product if first else total[:, cols] + product
+        total[:, cols] = jnp.dot(left[...], right[:, cols], preferred_element_type=F32)
         write = pltpu.make_async_copy(total.at[:, cols], out_ref.at[:, cols], out_sems.at[i])
         write.start()
         writes.append(write)
@@ -109,65 +112,82 @@
         write.wait()
 
 
-def hidden_kernel(n_blocks, place_ref, gradient_ref, *refs):
+def hidden_kernel(plan, z_ref, gradient_ref, *refs):
+    n_blocks = len(plan["blocks"])
     block_refs = refs[:n_blocks]
     (before_hbm, gate_hbm, up_hbm, factors_ref, in_ref, lora_ref, lora_t_ref) = refs[
         n_blocks : n_blocks + 7
     ]
-    (sums_hbm, mids_ref, total, before_ref, gate_ref, up_ref, sums_ref, left_rows, right_rows) = (
-        refs[n_blocks + 7 : -2]
-    )
-    sems, out_sems = refs[-2:]
+    sums_hbm, mids_ref, total, before_ref, gate_ref, up_ref, silu_ref, scaled_ref, sums_ref = refs[
+        n_blocks + 7 : -4
+    ]
+    left_rows, right_rows, sems, out_sems = refs[-4:]
     tokens, hidden = gate_ref.shape
     sequences = tokens // SEQUENCE_TOKENS
-    blocks = fetch_blocks(place_ref, gradient_ref, block_refs, left_rows, right_rows, sems)
-    copies, at = [], 4 * n_blocks
-    for source, target in ((before_hbm, before_ref), (gate_hbm, gate_ref), (up_hbm, up_ref)):
-        copies += copy_rows(source, target, sems, at, 4)
-        at += 4
-    for copy in blocks + copies:
+    fetched = fetch_blocks(plan, z_ref, gradient_ref, block_refs, left_rows, right_rows, sems)
+    at = 4 * n_blocks
+    activations = copy_rows(gate_hbm, gate_ref, sems, at, 4)
+    activations += copy_rows(up_hbm, up_ref, sems, at + 4, 4)
+    running = copy_rows(before_hbm, before_ref, sems, at + 8, 4)
+    for copy in activations + sum(fetched, []) + running:
         copy.start()
     mids_ref[...] = jnp.zeros_like(mids_ref)
-    for copy in blocks:
-        copy.wait()
-    total[...] = jnp.dot(left_rows[...], right_rows[...], preferred_element_type=F32)
-    for copy in copies:
-        copy.wait()
+
+    def adapters(j, e, rows, cols, left, right):
+        part = slice(j * RANK, (j + 1) * RANK)
+        sums_ref[e, part, cols] = SCALE * jnp.dot(left, right, preferred_element_type=F32)
+        mids_ref[part, rows] += contract(factors_ref[part, cols], right, 1, 1)
+
+    def each(i, start, width, body):
+        for e in range(sequences):
+            body(e, slice(e * SEQUENCE_TOKENS, (e + 1) * SEQUENCE_TOKENS), pl.ds(start, width))
+
+    def forward(e, rows, cols):
+        gate = gate_ref[rows, cols].astype(F32)
+        up = up_ref[rows, cols].astype(F32)
+        sigmoid = jax.nn.sigmoid(gate)
+        silu = gate * sigmoid
+        slope = sigmoid * (1.0 + gate * (1.0 - sigmoid))
+        silu_ref[rows, cols] = silu
+        scaled_ref[rows, cols] = up * slope
+        adapters(2, e, rows, cols, lora_t_ref[:, rows], (silu * up).astype(BF16))
+
+    def backward(e, rows, cols):
+        hidden_grad = (
+            total[rows, cols]
+            + before_ref[rows, cols]
+            + SCALE
+            * jnp.dot(lora_ref[rows, :], factors_ref[2 * RANK :, cols], preferred_element_type=F32)
+        )
+        gate_grad = (hidden_grad * scaled_ref[rows, cols]).astype(BF16)
+        adapters(0, e, rows, cols, in_ref[:RANK, rows], gate_grad)
+        up_grad = (hidden_grad * silu_ref[rows, cols]).astype(BF16)
+        adapters(1, e, rows, cols, in_ref[RANK:, rows], up_grad)
 
     def write(i, cols):
         return pltpu.make_async_copy(
             sums_ref.at[:, :, cols], sums_hbm.at[:, :, cols], out_sems.at[i]
         )
 
-    def tile(i, start, width):
-        cols = pl.ds(start, width)
-        factors = factors_ref[:, cols]
-        for e in range(sequences):
-            rows = slice(e * SEQUENCE_TOKENS, (e + 1) * SEQUENCE_TOKENS)
-            hidden_grad = (
-                total[rows, cols]
-                + before_ref[rows, cols]
-                + SCALE
-                * jnp.dot(lora_ref[rows, :], factors[2 * RANK :], preferred_element_type=F32)
-            )
-            gate = gate_ref[rows, cols].astype(F32)
-            up = up_ref[rows, cols].astype(F32)
-            sigmoid = jax.nn.sigmoid(gate)
-            silu = gate * sigmoid
-            slope = sigmoid * (1.0 + gate * (1.0 - sigmoid))
-            activation = (silu * up).astype(BF16)
-            gate_grad = (hidden_grad * up * slope).astype(BF16)
-            up_grad = (hidden_grad * silu).astype(BF16)
-            left = (in_ref[:RANK, rows], in_ref[RANK:, rows], lora_t_ref[:, rows])
-            for j, right in enumerate((gate_grad, up_grad, activation)):
-                part = slice(j * RANK, (j + 1) * RANK)
-                sums_ref[e, part, cols] = SCALE * jnp.dot(
-                    left[j], right, preferred_element_type=F32
-                )
-                mids_ref[part, rows] += contract(factors[part], right, 1, 1)
-        write(i, cols).start()
-
-    spans = column_tiles(hidden, 256, tile)
+    def last_tile(i, start, width):
+        each(i, start, width, backward)
+        write(i, pl.ds(start, width)).start()
+
+    for copy in activations:
+        copy.wait()
+    column_tiles(hidden, hidden, functools.partial(each, body=forward))
+    row = 0
+    for some in plan["chunks"]:
+        for copy in sum(fetched[some], []):
+            copy.wait()
+        rows = sum(block.shape[0] for block in block_refs[some])
+        span = slice(row, row + rows)
+        product = jnp.dot(left_rows[:, span], right_rows[span, :], preferred_element_type=F32)
+        total[...] = product if row == 0 else total[...] + product
+        row += rows
+    for copy in running:
+        copy.wait()
+    spans = column_tiles(hidden, hidden, last_tile)
     for e in range(sequences):
         square = sums_ref[e] * sums_ref[e]
         line = jnp.sum(jnp.sum(square, axis=0, keepdims=True), axis=1, keepdims=True)
@@ -267,7 +287,7 @@
     n_z = sizes["z"]
     n_tensor = sizes["x"] * sizes["c"]
     z_axes, tensor_axes = "z", ("x", "c")
-    z = lax.axis_index(z_axes)
+    spot = lax.axis_index(z_axes).reshape(1).astype(jnp.int32)
 
     gradient = lax.all_gather(output_gradient, tensor_axes, axis=1, tiled=True)
     block = lax.all_gather(frozen_down_weight.T, "y", axis=0, tiled=True)
@@ -275,29 +295,25 @@
 
     rows = block.shape[0]
     half = rows // 2
-    units = rows // 128
     vmem = pl.BlockSpec(memory_space=pltpu.VMEM)
     smem = pl.BlockSpec(memory_space=pltpu.SMEM)
     hbm = pl.BlockSpec(memory_space=pl.ANY)
     params = pltpu.CompilerParams(vmem_limit_bytes=60 * 2**20)
 
-    def place(offsets):
-        at = [((z + offset) % n_z) * units for offset in offsets]
-        return jnp.stack(at).astype(jnp.int32)
-
     low, high = {0: block}, {0: block}
 
     def step(k, low_from, high_from):
         low[k] = lax.ppermute(low_from, z_axes, ring(n_z, 1))
         high[k] = lax.ppermute(high_from, z_axes, ring(n_z, -1))
 
-    def side(values, factors, name):
+    def side(values, first, count, name):
         width = values.shape[1]
         chunk = 1024
         return pl.pallas_call(
             functools.partial(side_kernel, sequences // 2),
             out_shape=(
-                jax.ShapeDtypeStruct((factors.shape[0], tokens), BF16),
+                jax.ShapeDtypeStruct((count, tokens), BF16),
+                jax.ShapeDtypeStruct((tokens, count), BF16),
                 jax.ShapeDtypeStruct((sequences, SEQUENCE_TOKENS, SEQUENCE_TOKENS), F32),
             ),
             grid=(width // chunk,),
@@ -305,24 +321,25 @@
                 pl.BlockSpec((2 * SEQUENCE_TOKENS, chunk), functools.partial(lambda p, i: (p, i), p))
                 for p in range(sequences // 2)
             ]
-            + [pl.BlockSpec((factors.shape[0], chunk), lambda i: (0, i))],
+            + [pl.BlockSpec((count, chunk), lambda i: (first // count, i))],
             out_specs=(
-                pl.BlockSpec((factors.shape[0], tokens), lambda i: (0, 0)),
+                pl.BlockSpec((count, tokens), lambda i: (0, 0)),
+                pl.BlockSpec((tokens, count), lambda i: (0, 0)),
                 pl.BlockSpec((sequences, SEQUENCE_TOKENS, SEQUENCE_TOKENS), lambda i: (0, 0, 0)),
             ),
             scratch_shapes=[
                 pltpu.VMEM(
-                    (sequences // 2, 2 * SEQUENCE_TOKENS + factors.shape[0], 2 * SEQUENCE_TOKENS), F32
+                    (sequences // 2, 2 * SEQUENCE_TOKENS + count, 2 * SEQUENCE_TOKENS), F32
                 )
             ],
             compiler_params=params,
             cost_estimate=pl.CostEstimate(
-                flops=2 * tokens * width * (128 + factors.shape[0]),
+                flops=2 * tokens * width * (128 + count),
                 bytes_accessed=5 * 2**20,
                 transcendentals=0,
             ),
             name=name,
-        )(*[values] * (sequences // 2), factors)
+        )(*[values] * (sequences // 2), adapter_width_factors.reshape(3 * RANK, width))
 
     def scratch(n_rows, n_sems):
         return [
@@ -332,16 +349,19 @@
             pltpu.SemaphoreType.DMA((-(-hidden // 256),)),
         ]
 
-    def part(offsets, before=None):
-        blocks = [(low if offset < 0 else high)[abs(offset)] for offset in offsets]
+    def at_z(offset):
+        return (low if offset < 0 else high)[abs(offset)]
+
+    def part(offsets):
+        blocks = [at_z(offset) for offset in offsets]
+        plan = dict(n_z=n_z, rows=rows, blocks=[(offset, 0) for offset in offsets])
         n = len(blocks)
-        given = [] if before is None else [before]
         return pl.pallas_call(
-            functools.partial(part_kernel, n, before is None),
+            functools.partial(part_kernel, plan),
             out_shape=jax.ShapeDtypeStruct((tokens, hidden), F32),
-            in_specs=[smem] + [hbm] * (n + 1 + len(given)),
+            in_specs=[smem] + [hbm] * (n + 1),
             out_specs=hbm,
-            scratch_shapes=[pltpu.VMEM((tokens, hidden), F32)] + scratch(n * rows, 4 * n + 4),
+            scratch_shapes=[pltpu.VMEM((tokens, hidden), F32)] + scratch(n * rows, 4 * n),
             compiler_params=params,
             cost_estimate=pl.CostEstimate(
                 flops=2 * tokens * n * rows * hidden,
@@ -349,7 +369,7 @@
                 transcendentals=0,
             ),
             name="part_product",
-        )(place(offsets), gradient, *blocks, *given)
+        )(spot, gradient, *blocks)
 
     def after(value, other):
         return lax.optimization_barrier((value, other))[0]
@@ -360,27 +380,25 @@
     last = n_z // 2
     for k in range(1, last - 3):
         step(k, low[k - 1], high[k - 1])
-    total = part([0] + pairs(1, last - 5))
+    total = part([0] + pairs(1, last - 4))
     at = last - 4
     step(at + 1, after(low[at], total), after(high[at], total))
-    lora_t, gradient_gram = side(gradient, adapter_width_factors[2], "gradient_side")
+    lora_t, lora, gradient_gram = side(gradient, 2 * RANK, RANK, "gradient_side")
     at = last - 3
     step(at + 1, after(low[at], lora_t), after(high[at], lora_t))
-    total = part(pairs(last - 5, last - 2), total)
-    at = last - 2
-    step(at + 1, after(low[at], total), after(high[at], total))
-    at = last - 1
-    step(last, low[at][:half], high[at][half:])
-    in_t, normed_gram = side(
-        normed_all, adapter_width_factors[:2].reshape(2 * RANK, -1), "normed_side"
-    )
-    far = ((z + last) % n_z) * units
-    blocks = [side_of[k] for k in range(last - 2, last + 1) for side_of in (low, high)]
-    places = jnp.concatenate(
-        [place(pairs(last - 2, last)), jnp.stack([far, far + units // 2]).astype(jnp.int32)]
+    step(last - 1, low[last - 2], high[last - 2])
+    step(last, low[last - 1][:half], high[last - 1][half:])
+    in_t, _, normed_gram = side(normed_all, 0, 2 * RANK, "normed_side")
+    offsets = pairs(last - 4, last)
+    blocks = [at_z(offset) for offset in offsets] + [low[last], high[last]]
+    plan = dict(
+        n_z=n_z,
+        rows=rows,
+        blocks=[(offset, 0) for offset in offsets] + [(last, 0), (last, half)],
+        chunks=[slice(0, 4), slice(4, 8), slice(8, 10)],
     )
     sums, mids = pl.pallas_call(
-        functools.partial(hidden_kernel, len(blocks)),
+        functools.partial(hidden_kernel, plan),
         out_shape=(
             jax.ShapeDtypeStruct((sequences, 3 * RANK, hidden), F32),
             jax.ShapeDtypeStruct((8 * n_tensor, tokens), F32),
@@ -392,13 +410,15 @@
             pltpu.VMEM((tokens, hidden), F32),
             pltpu.VMEM((tokens, hidden), BF16),
             pltpu.VMEM((tokens, hidden), BF16),
+            pltpu.VMEM((tokens, hidden), F32),
+            pltpu.VMEM((tokens, hidden), F32),
             pltpu.VMEM((sequences, 3 * RANK, hidden), F32),
         ]
-        + scratch(5 * rows, 4 * len(blocks) + 12),
+        + scratch((len(offsets) + 1) * rows, 4 * len(blocks) + 12),
         compiler_params=params,
         name="hidden_side",
     )(
-        places,
+        spot,
         gradient,
         *blocks,
         total,
@@ -406,7 +426,7 @@
         upward_preactivation,
         adapter_hidden_factors.reshape(3 * RANK, hidden),
         in_t,
-        lora_t.T,
+        lora,
         lora_t,
     )
 

time: 242 us -> 235 us (0.971)
  Pallas kernels: 35.2 us -> 28.9 us
  local copies, waits for them, and re-layouts: 7.24 us -> 1.5 us
  waiting for transfers between devices: 31.4 us -> 35.8 us
    ppermute x8, waiting for transfers between devices: 12.7 us -> 24.2 us  [step(): high[k] = lax.ppermute(high_from, z_axes, ring(n_z, -1))]
    ppermute x8, waiting for transfers between devices: 11.9 us -> 4.81 us  [step(): low[k] = lax.ppermute(low_from, z_axes, ring(n_z, 1))]
    pallas_call x3 -> x2, Pallas kernels: 22.7 us -> 16 us  [the longest x1 9.97 us: per_device(): pl.pallas_call(functools.partial(hidden_kernel, plan), out_shape=(jax.Sha...]
  transfers between devices with their start and end apart: 19 -> 19, of which waited for: 9 -> 12; matrix products, arithmetic and copies ran while one was open for 2% -> 0% of each run, Pallas kernels for 9% -> 7%
where the time goes in v8:
time: 235 us; the launch traced here: 234 us
  blocking collectives  84.5 us (36%)
  starting transfers between devices  67.1 us (29%)
  waiting for transfers between devices  35.8 us (15%)
  Pallas kernels  28.9 us (12%)
  between operations  15.1 us (6%)
    ppermute x8, starting transfers between devices, step(): high[k] = lax.ppermute(high_from, z_axes, ring(n_z, -1))  48.3 us
    ppermute x8, waiting for transfers between devices, step(): high[k] = lax.ppermute(high_from, z_axes, ring(n_z, -1))  24.2 us
    all_to_all x1, blocking collectives, per_device(): lax.all_to_all(share.reshape(n_z, -1, 128), z_axes, 0, 0)  21.2 us
    all_to_all x1, blocking collectives, per_device(): lax.all_to_all(jnp.broadcast_to(share, (n_z,) + share.shape), z_axes, 0, 0)  17 us
    ppermute x8, starting transfers between devices, step(): low[k] = lax.ppermute(low_from, z_axes, ring(n_z, 1))  15.3 us
    all_gather x1, blocking collectives, per_device(): block = lax.all_gather(frozen_down_weight.T, 'y', axis=0, tiled=True)  13.4 us
    all_to_all x1, blocking collectives, per_device(): lax.all_to_all(out.reshape(n_y, -1, 128), 'y', 0, 0)  13.3 us
    all_to_all x1, blocking collectives, per_device(): lax.all_to_all(mids.reshape(n_tensor, 8, tokens), tensor_axes, 0, 0)  10.3 us
  transfers between devices with their start and end apart: 19, of which 12 were waited for; matrix products, arithmetic and copies ran while one was open for 0% of the time, Pallas kernels for 7%

profile of v8, /device:TPU:32, one launch (start us, length us, event | category | flops | bytes accessed | tf_op | source)
XLA Modules:
  0.0 234.2 jit_solution(748019765818486620)
XLA Ops:
  7.2 0.0 all-gather.3.cloned.1.call-start
  7.2 0.7 all-gather.3.cloned.1.call-update
  7.9 0.0 all-gather.5.cloned.1.call-start
  7.9 0.7 all-gather.5.cloned.1.call-update
  8.6 13.4 %all_gather.10.refs_0_ = bf16[256,896]{1,0:T(8,128)(2,1)S(1)} all-gather(bf16[64,896]{1,0:T(8,128)(2,1)} %bitcast.24), channel_id=1, replica_groups=mesh['z'=16,'y'=4,'x'=4,'c'=2] {'y'}, dimensions={0}, use_global_device_ids=true | all-gather | bytes 573440 | tf_op jit(solution)/shard_map/all_gather | solution.py:293
  22.0 6.9 %collective-permute-start.4 = (bf16[256,896]{1,0:T(8,128)(2,1)S(1)}, bf16[256,896]{1,0:T(8,128)(2,1)S(1)}, u32[]{:S(2)}, u32[]{:S(2)}) collective-permute-start(bf16[256,896]{1,0:T(8,128)(2,1)S(1)} %all_gather.10.refs_0_), channel_id=1, source_target_pairs={{0,480},{32,0},{64,32},{96,64},{128,96},{160,128},{192,160},{224,1... | collective-permute-start | bytes 1376264 | tf_op jit(solution)/shard_map/ppermute | solution.py:307
  28.9 1.9 collective-permute-start
  30.8 4.0 %collective-permute-done.4.refs_2_ = bf16[256,896]{1,0:T(8,128)(2,1)S(1)} collective-permute-done((bf16[256,896]{1,0:T(8,128)(2,1)S(1)}, bf16[256,896]{1,0:T(8,128)(2,1)S(1)}, u32[]{:S(2)}, u32[]{:S(2)}) %collective-permute-start.4) | collective-permute-done | bytes 458784 | tf_op jit(solution)/shard_map/ppermute | solution.py:307
  34.9 8.6 %collective-permute-start.5 = (bf16[256,896]{1,0:T(8,128)(2,1)S(1)}, bf16[256,896]{1,0:T(8,128)(2,1)S(1)}, u32[]{:S(2)}, u32[]{:S(2)}) collective-permute-start(bf16[256,896]{1,0:T(8,128)(2,1)S(1)} %collective-permute-done.4.refs_2_), channel_id=1, source_target_pairs={{0,480},{32,0},{64,32},{96,64},{128,96},{160,128},{192,160},{224,1... | collective-permute-start | bytes 1376264 | tf_op jit(solution)/shard_map/ppermute | solution.py:307
  43.5 0.5 collective-permute-done.refs_1_
  44.0 1.9 collective-permute-start.1
  45.9 4.7 %collective-permute-done.5.refs_4_ = bf16[256,896]{1,0:T(8,128)(2,1)S(1)} collective-permute-done((bf16[256,896]{1,0:T(8,128)(2,1)S(1)}, bf16[256,896]{1,0:T(8,128)(2,1)S(1)}, u32[]{:S(2)}, u32[]{:S(2)}) %collective-permute-start.5) | collective-permute-done | bytes 458784 | tf_op jit(solution)/shard_map/ppermute | solution.py:307
  50.7 5.7 %collective-permute-start.6 = (bf16[256,896]{1,0:T(8,128)(2,1)S(1)}, bf16[256,896]{1,0:T(8,128)(2,1)}, u32[]{:S(2)}, u32[]{:S(2)}) collective-permute-start(bf16[256,896]{1,0:T(8,128)(2,1)S(1)} %collective-permute-done.5.refs_4_), channel_id=1, source_target_pairs={{0,480},{32,0},{64,32},{96,64},{128,96},{160,128},{192,160},{224,1... | collective-permute-start | bytes 1376264 | tf_op jit(solution)/shard_map/ppermute | solution.py:307
  56.4 0.5 collective-permute-done.1.refs_3_
  56.9 1.9 collective-permute-start.2
  58.8 3.9 %collective-permute-done.6.refs_6_ = bf16[256,896]{1,0:T(8,128)(2,1)} collective-permute-done((bf16[256,896]{1,0:T(8,128)(2,1)S(1)}, bf16[256,896]{1,0:T(8,128)(2,1)}, u32[]{:S(2)}, u32[]{:S(2)}) %collective-permute-start.6) | collective-permute-done | bytes 458784 | tf_op jit(solution)/shard_map/ppermute | solution.py:307
  62.7 5.7 %collective-permute-start.7 = (bf16[256,896]{1,0:T(8,128)(2,1)}, bf16[256,896]{1,0:T(8,128)(2,1)S(1)}, u32[]{:S(2)}, u32[]{:S(2)}) collective-permute-start(bf16[256,896]{1,0:T(8,128)(2,1)} %collective-permute-done.6.refs_6_), channel_id=1, source_target_pairs={{0,480},{32,0},{64,32},{96,64},{128,96},{160,128},{192,160},{224,1... | collective-permute-start | bytes 1376264 | tf_op jit(solution)/shard_map/ppermute | solution.py:307
  68.4 0.6 collective-permute-done.2.refs_5_
  69.0 1.9 collective-permute-start.3
  70.9 0.0 all-gather.3.cloned.1.call-done.gradient_ref.refs_0_.refs_1_
  70.9 0.0 copy-done
  71.0 6.1 %part_product.1.refs_10_ = f32[512,896]{1,0:T(8,128)} custom-call(s32[1]{0:T(128)} %bitcast.z_ref, bf16[512,4096]{1,0:T(8,128)(2,1)} %all-gather.3.cloned.1.call-done.gradient_ref.refs_0_.refs_1_, bf16[256,896]{1,0:T(8,128)(2,1)} %copy-done, bf16[256,896]{1,0:T(8,128)(2,1)} %copy-done.11, bf16[256,896]{1,0:T(8,128)(2,1)} %copy-done.9, ...), custom_call_target="tpu_custom_call" | custom-call | flops 1644167168 | bytes 6291456 | tf_op jit(solution)/shard_map/part_product/pallas_call | solution.py:359
  77.0 0.0 collective-permute-done.7.refs_1_
  77.1 0.0 copy-start.4
  77.1 5.4 %collective-permute-start.9 = (bf16[256,896]{1,0:T(8,128)(2,1)S(1)}, bf16[256,896]{1,0:T(8,128)(2,1)S(1)}, u32[]{:S(2)}, u32[]{:S(2)}) collective-permute-start(bf16[256,896]{1,0:T(8,128)(2,1)S(1)} %collective-permute-done.7.refs_1_), channel_id=1, source_target_pairs={{0,480},{32,0},{64,32},{96,64},{128,96},{160,128},{192,160},{224,1... | collective-permute-start | bytes 1376264 | tf_op jit(solution)/shard_map/ppermute | solution.py:307
  82.5 0.0 collective-permute-done.3.refs_0_
  82.5 1.9 collective-permute-start.8
  84.5 4.9 %gradient_side.1 = (bf16[16,512]{1,0:T(8,128)(2,1)}, bf16[512,16]{1,0:T(8,128)(2,1)}, f32[4,128,128]{2,1,0:T(8,128)}) custom-call(bf16[512,4096]{1,0:T(8,128)(2,1)} %all-gather.3.cloned.1.call-done.gradient_ref.refs_0_.refs_1_, bf16[512,4096]{1,0:T(8,128)(2,1)} %all-gather.3.cloned.1.call-done.gradient_ref.refs_0_.refs_1_, bf16[48,4096]{1,0:T(8,128)(2,1)} %bitcast.16), custom_call_target="tpu_custom_call" | custom-call | flops 603979776 | bytes 5242880 | tf_op jit(solution)/shard_map/gradient_side/pallas_call | solution.py:312
  89.4 0.0 copy-done.5
  89.4 0.0 collective-permute-done.9.refs_3_
  89.4 0.0 copy-start.6
  89.4 5.1 %collective-permute-start.11 = (bf16[256,896]{1,0:T(8,128)(2,1)S(1)}, bf16[256,896]{1,0:T(8,128)(2,1)S(1)}, u32[]{:S(2)}, u32[]{:S(2)}) collective-permute-start(bf16[256,896]{1,0:T(8,128)(2,1)S(1)} %collective-permute-done.9.refs_3_), channel_id=1, source_target_pairs={{0,480},{32,0},{64,32},{96,64},{128,96},{160,128},{192,160},{224,1... | collective-permute-start | bytes 1376264 | tf_op jit(solution)/shard_map/ppermute | solution.py:307
  94.5 0.0 collective-permute-done.8.refs_2_
  94.6 0.0 copy-start.7
  94.6 1.9 collective-permute-start.10
  96.5 5.6 %collective-permute-done.11.refs_5_ = bf16[256,896]{1,0:T(8,128)(2,1)S(1)} collective-permute-done((bf16[256,896]{1,0:T(8,128)(2,1)S(1)}, bf16[256,896]{1,0:T(8,128)(2,1)S(1)}, u32[]{:S(2)}, u32[]{:S(2)}) %collective-permute-start.11) | collective-permute-done | bytes 458784 | tf_op jit(solution)/shard_map/ppermute | solution.py:307
  102.1 5.0 %collective-permute-start.13 = (bf16[256,896]{1,0:T(8,128)(2,1)S(1)}, bf16[256,896]{1,0:T(8,128)(2,1)S(1)}, u32[]{:S(2)}, u32[]{:S(2)}) collective-permute-start(bf16[256,896]{1,0:T(8,128)(2,1)S(1)} %collective-permute-done.11.refs_5_), channel_id=1, source_target_pairs={{0,480},{32,0},{64,32},{96,64},{128,96},{160,128},{192,160},{224,1... | collective-permute-start | bytes 1376264 | tf_op jit(solution)/shard_map/ppermute | solution.py:307
  107.1 0.4 collective-permute-done.10.refs_4_
  107.5 1.9 collective-permute-start.12
  109.4 5.9 %collective-permute-done.13.refs_7_ = bf16[256,896]{1,0:T(8,128)(2,1)S(1)} collective-permute-done((bf16[256,896]{1,0:T(8,128)(2,1)S(1)}, bf16[256,896]{1,0:T(8,128)(2,1)S(1)}, u32[]{:S(2)}, u32[]{:S(2)}) %collective-permute-start.13) | collective-permute-done | bytes 458784 | tf_op jit(solution)/shard_map/ppermute | solution.py:307
  115.3 5.9 %collective-permute-start.15 = (bf16[128,896]{1,0:T(8,128)(2,1)S(1)}, bf16[128,896]{1,0:T(8,128)(2,1)S(1)}, u32[]{:S(2)}, u32[]{:S(2)}) collective-permute-start(bf16[128,896]{1,0:T(8,128)(2,1)S(1)} %slice.21), channel_id=1, source_target_pairs={{0,480},{32,0},{64,32},{96,64},{128,96},{160,128},{192,160},{224,1... | collective-permute-start | bytes 688136 | tf_op jit(solution)/shard_map/ppermute | solution.py:307
  121.2 0.5 collective-permute-done.12.refs_6_
  121.7 1.9 collective-permute-start.14
  123.7 0.0 all-gather.5.cloned.1.call-done.refs_0_.refs_1_
  123.7 5.0 %normed_side.1 = (bf16[32,512]{1,0:T(8,128)(2,1)}, bf16[512,32]{1,0:T(8,128)(2,1)}, f32[4,128,128]{2,1,0:T(8,128)}) custom-call(bf16[512,4096]{1,0:T(8,128)(2,1)} %all-gather.5.cloned.1.call-done.refs_0_.refs_1_, bf16[512,4096]{1,0:T(8,128)(2,1)} %all-gather.5.cloned.1.call-done.refs_0_.refs_1_, bf16[48,4096]{1,0:T(8,128)(2,1)} %bitcast.17), custom_call_target="tpu_custom_call" | custom-call | flops 671088640 | bytes 5242880 | tf_op jit(solution)/shard_map/normed_side/pallas_call | solution.py:312
  128.7 0.0 copy-done.7
  128.7 0.0 collective-permute-done.15.refs_9_
  128.7 0.0 copy-start.14
  128.7 2.3 collective-permute-done.14.refs_8_
  131.1 10.0 %hidden_side.1 = (f32[4,48,896]{2,1,0:T(8,128)}, f32[64,512]{1,0:T(8,128)}) custom-call(s32[1]{0:T(128)} %bitcast.z_ref, bf16[512,4096]{1,0:T(8,128)(2,1)} %all-gather.3.cloned.1.call-done.gradient_ref.refs_0_.refs_1_, bf16[256,896]{1,0:T(8,128)(2,1)} %copy-done.5, bf16[256,896]{1,0:T(8,128)(2,1)} %copy-done.4, bf16[256,896]{1,0:T(8,128)(2,1)} %copy-done.7, ...), custom_call_target="tpu_custom_call" | custom-call | tf_op jit(solution)/shard_map/hidden_side/pallas_call | solution.py:400
  141.0 0.0 copy-start.16
  141.0 0.0 copy-start.15
  141.1 10.3 %all_to_all.30 = f32[8,8,512]{2,1,0:T(8,128)S(1)} all-to-all(f32[8,8,512]{2,1,0:T(8,128)} %bitcast.23), channel_id=1, replica_groups=mesh['z'=16,'y'=4,'x'=4,'c'=2] {'x','c'}, dimensions={0} | all-to-all | bytes 262144 | tf_op jit(solution)/shard_map/all_to_all | solution.py:433
  151.4 0.7 broadcast_in_dim.9
  152.1 3.4 %all-to-all-start.1 = ((f32[8,8,512]{2,1,0:T(8,128)}), f32[8,8,512]{2,1,0:T(8,128)S(1)}, u32[]{:S(2)}, u32[]{:S(2)}) async-start(f32[8,8,512]{2,1,0:T(8,128)} %broadcast_in_dim.9), calls=%async_computation.1 | async-start | bytes 262144 | tf_op jit(solution)/shard_map/all_to_all | solution.py:435
  156.1 5.4 %all-to-all-done.1 = f32[8,8,512]{2,1,0:T(8,128)S(1)} async-done(((f32[8,8,512]{2,1,0:T(8,128)}), f32[8,8,512]{2,1,0:T(8,128)S(1)}, u32[]{:S(2)}, u32[]{:S(2)}) %all-to-all-start.1) | async-done | bytes 131104 | tf_op jit(solution)/shard_map/all_to_all | solution.py:435
  161.5 0.7 copy-done.3
  162.1 2.9 %clip_side.1 = f32[72,8,128]{2,1,0:T(8,128)} custom-call(f32[1]{0:T(128)} %copy.12.clip_ref, f32[64,512]{1,0:T(8,128)} %bitcast.22, f32[4,48,896]{2,1,0:T(8,128)} %get-tuple-element.21.sums_ref, bf16[512,512]{1,0:T(8,128)(2,1)} %normed_ref.1, bf16[512,512]{1,0:T(8,128)(2,1)} %gradient_ref.1, f32[4,128,128]{2,1,0:T(8,128)} %get-tuple-element.22.normed_gram_ref, ...), custom_call_target="tpu_custom_call" | custom-call | tf_op jit(solution)/shard_map/clip_side/pallas_call | solution.py:442
  165.1 13.3 %all_to_all.31 = f32[4,144,128]{2,1,0:T(8,128)S(1)} all-to-all(f32[4,144,128]{2,1,0:T(8,128)} %bitcast.18), channel_id=1, replica_groups=mesh['z'=16,'y'=4,'x'=4,'c'=2] {'y'}, dimensions={0} | all-to-all | bytes 589824 | tf_op jit(solution)/shard_map/all_to_all | solution.py:461
  178.4 21.2 %all_to_all.32 = f32[16,9,128]{2,1,0:T(8,128)S(1)} all-to-all(f32[16,9,128]{2,1,0:T(8,128)S(1)} %reshape.44), channel_id=1, replica_groups=mesh['z'=16,'y'=4,'x'=4,'c'=2] {'z'}, dimensions={0} | all-to-all | bytes 147456 | tf_op jit(solution)/shard_map/all_to_all | solution.py:462
  199.7 17.0 %all_to_all.33 = f32[16,9,128]{2,1,0:T(8,128)S(1)} all-to-all(f32[16,9,128]{2,1,0:T(8,128)S(1)} %broadcast_in_dim.10), channel_id=1, replica_groups=mesh['z'=16,'y'=4,'x'=4,'c'=2] {'z'}, dimensions={0} | all-to-all | bytes 147456 | tf_op jit(solution)/shard_map/all_to_all | solution.py:463
  216.7 9.2 %all_to_all.34 = f32[4,144,128]{2,1,0:T(8,128)S(1)} all-to-all(f32[4,144,128]{2,1,0:T(8,128)S(1)} %broadcast_in_dim.11), channel_id=1, replica_groups=mesh['z'=16,'y'=4,'x'=4,'c'=2] {'y'}, dimensions={0} | all-to-all | bytes 589824 | tf_op jit(solution)/shard_map/all_to_all | solution.py:466
  226.0 0.7 fusion.1
  226.7 0.7 fusion
  (34 shorter events, 0.2 us)
Async XLA Ops:
  7.2 63.8 %all-gather.3.cloned.1.call-start = ((), (), s32[]{:S(2)}) async-start(), calls=%async_computation.6 | async-start | bytes 4718592 | tf_op jit(solution)/shard_map/all_gather | solution.py:292
  7.9 115.8 %all-gather.5.cloned.1.call-start = ((), (), s32[]{:S(2)}) async-start(), calls=%async_computation.7 | async-start | bytes 4718592 | tf_op jit(solution)/shard_map/all_gather | solution.py:294
  22.0 48.9 %copy-start = (bf16[256,896]{1,0:T(8,128)(2,1)}, bf16[256,896]{1,0:T(8,128)(2,1)S(1)}, u32[]{:S(2)}) copy-start(bf16[256,896]{1,0:T(8,128)(2,1)S(1)} %all_gather.10.refs_0_) | copy-start | bytes 1376260
  22.0 12.8 %collective-permute-start.4 = (bf16[256,896]{1,0:T(8,128)(2,1)S(1)}, bf16[256,896]{1,0:T(8,128)(2,1)S(1)}, u32[]{:S(2)}, u32[]{:S(2)}) collective-permute-start(bf16[256,896]{1,0:T(8,128)(2,1)S(1)} %all_gather.10.refs_0_), channel_id=1, source_target_pairs={{0,480},{32,0},{64,32},{96,64},{128,96},{160,128},{192,160},{224,1... | collective-permute-start | bytes 1376264 | tf_op jit(solution)/shard_map/ppermute | solution.py:307
  28.9 15.1 %collective-permute-start = (bf16[256,896]{1,0:T(8,128)(2,1)S(1)}, bf16[256,896]{1,0:T(8,128)(2,1)S(1)}, u32[]{:S(2)}, u32[]{:S(2)}) collective-permute-start(bf16[256,896]{1,0:T(8,128)(2,1)S(1)} %all_gather.10.refs_0_), channel_id=1, source_target_pairs={{0,32},{32,64},{64,96},{96,128},{128,160},{160,192},{192,224},{224... | collective-permute-start | bytes 1376264 | tf_op jit(solution)/shard_map/ppermute | solution.py:306
  34.9 36.1 %copy-start.9 = (bf16[256,896]{1,0:T(8,128)(2,1)}, bf16[256,896]{1,0:T(8,128)(2,1)S(1)}, u32[]{:S(2)}) copy-start(bf16[256,896]{1,0:T(8,128)(2,1)S(1)} %collective-permute-done.4.refs_2_) | copy-start | bytes 1376260
  34.9 15.8 %collective-permute-start.5 = (bf16[256,896]{1,0:T(8,128)(2,1)S(1)}, bf16[256,896]{1,0:T(8,128)(2,1)S(1)}, u32[]{:S(2)}, u32[]{:S(2)}) collective-permute-start(bf16[256,896]{1,0:T(8,128)(2,1)S(1)} %collective-permute-done.4.refs_2_), channel_id=1, source_target_pairs={{0,480},{32,0},{64,32},{96,64},{128,96},{160,128},{192,160},{224,1... | collective-permute-start | bytes 1376264 | tf_op jit(solution)/shard_map/ppermute | solution.py:307
  44.0 27.0 %copy-start.11 = (bf16[256,896]{1,0:T(8,128)(2,1)}, bf16[256,896]{1,0:T(8,128)(2,1)S(1)}, u32[]{:S(2)}) copy-start(bf16[256,896]{1,0:T(8,128)(2,1)S(1)} %collective-permute-done.refs_1_) | copy-start | bytes 1376260
  44.0 12.9 %collective-permute-start.1 = (bf16[256,896]{1,0:T(8,128)(2,1)S(1)}, bf16[256,896]{1,0:T(8,128)(2,1)S(1)}, u32[]{:S(2)}, u32[]{:S(2)}) collective-permute-start(bf16[256,896]{1,0:T(8,128)(2,1)S(1)} %collective-permute-done.refs_1_), channel_id=1, source_target_pairs={{0,32},{32,64},{64,96},{96,128},{128,160},{160,192},{192,224},{224... | collective-permute-start | bytes 1376264 | tf_op jit(solution)/shard_map/ppermute | solution.py:306
  50.7 20.3 %copy-start.12 = (bf16[256,896]{1,0:T(8,128)(2,1)}, bf16[256,896]{1,0:T(8,128)(2,1)S(1)}, u32[]{:S(2)}) copy-start(bf16[256,896]{1,0:T(8,128)(2,1)S(1)} %collective-permute-done.5.refs_4_) | copy-start | bytes 1376260
  50.7 12.0 %collective-permute-start.6 = (bf16[256,896]{1,0:T(8,128)(2,1)S(1)}, bf16[256,896]{1,0:T(8,128)(2,1)}, u32[]{:S(2)}, u32[]{:S(2)}) collective-permute-start(bf16[256,896]{1,0:T(8,128)(2,1)S(1)} %collective-permute-done.5.refs_4_), channel_id=1, source_target_pairs={{0,480},{32,0},{64,32},{96,64},{128,96},{160,128},{192,160},{224,1... | collective-permute-start | bytes 1376264 | tf_op jit(solution)/shard_map/ppermute | solution.py:307
  56.9 14.1 %copy-start.13 = (bf16[256,896]{1,0:T(8,128)(2,1)}, bf16[256,896]{1,0:T(8,128)(2,1)S(1)}, u32[]{:S(2)}) copy-start(bf16[256,896]{1,0:T(8,128)(2,1)S(1)} %collective-permute-done.1.refs_3_) | copy-start | bytes 1376260
  56.9 12.1 %collective-permute-start.2 = (bf16[256,896]{1,0:T(8,128)(2,1)S(1)}, bf16[256,896]{1,0:T(8,128)(2,1)}, u32[]{:S(2)}, u32[]{:S(2)}) collective-permute-start(bf16[256,896]{1,0:T(8,128)(2,1)S(1)} %collective-permute-done.1.refs_3_), channel_id=1, source_target_pairs={{0,32},{32,64},{64,96},{96,128},{128,160},{160,192},{192,224},{224... | collective-permute-start | bytes 1376264 | tf_op jit(solution)/shard_map/ppermute | solution.py:306
  62.7 14.4 %collective-permute-start.7 = (bf16[256,896]{1,0:T(8,128)(2,1)}, bf16[256,896]{1,0:T(8,128)(2,1)S(1)}, u32[]{:S(2)}, u32[]{:S(2)}) collective-permute-start(bf16[256,896]{1,0:T(8,128)(2,1)} %collective-permute-done.6.refs_6_), channel_id=1, source_target_pairs={{0,480},{32,0},{64,32},{96,64},{128,96},{160,128},{192,160},{224,1... | collective-permute-start | bytes 1376264 | tf_op jit(solution)/shard_map/ppermute | solution.py:307
  69.0 13.5 %collective-permute-start.3 = (bf16[256,896]{1,0:T(8,128)(2,1)}, bf16[256,896]{1,0:T(8,128)(2,1)S(1)}, u32[]{:S(2)}, u32[]{:S(2)}) collective-permute-start(bf16[256,896]{1,0:T(8,128)(2,1)} %collective-permute-done.2.refs_5_), channel_id=1, source_target_pairs={{0,32},{32,64},{64,96},{96,128},{128,160},{160,192},{192,224},{224... | collective-permute-start | bytes 1376264 | tf_op jit(solution)/shard_map/ppermute | solution.py:306
  77.1 12.4 %copy-start.4 = (bf16[256,896]{1,0:T(8,128)(2,1)}, bf16[256,896]{1,0:T(8,128)(2,1)S(1)}, u32[]{:S(2)}) copy-start(bf16[256,896]{1,0:T(8,128)(2,1)S(1)} %collective-permute-done.7.refs_1_) | copy-start | bytes 1376260
  77.1 12.4 %collective-permute-start.9 = (bf16[256,896]{1,0:T(8,128)(2,1)S(1)}, bf16[256,896]{1,0:T(8,128)(2,1)S(1)}, u32[]{:S(2)}, u32[]{:S(2)}) collective-permute-start(bf16[256,896]{1,0:T(8,128)(2,1)S(1)} %collective-permute-done.7.refs_1_), channel_id=1, source_target_pairs={{0,480},{32,0},{64,32},{96,64},{128,96},{160,128},{192,160},{224,1... | collective-permute-start | bytes 1376264 | tf_op jit(solution)/shard_map/ppermute | solution.py:307
  82.5 6.9 %copy-start.5 = (bf16[256,896]{1,0:T(8,128)(2,1)}, bf16[256,896]{1,0:T(8,128)(2,1)S(1)}, u32[]{:S(2)}) copy-start(bf16[256,896]{1,0:T(8,128)(2,1)S(1)} %collective-permute-done.3.refs_0_) | copy-start | bytes 1376260
  82.5 12.0 %collective-permute-start.8 = (bf16[256,896]{1,0:T(8,128)(2,1)S(1)}, bf16[256,896]{1,0:T(8,128)(2,1)S(1)}, u32[]{:S(2)}, u32[]{:S(2)}) collective-permute-start(bf16[256,896]{1,0:T(8,128)(2,1)S(1)} %collective-permute-done.3.refs_0_), channel_id=1, source_target_pairs={{0,32},{32,64},{64,96},{96,128},{128,160},{160,192},{192,224},{224... | collective-permute-start | bytes 1376264 | tf_op jit(solution)/shard_map/ppermute | solution.py:306
  89.4 39.2 %copy-start.6 = (bf16[256,896]{1,0:T(8,128)(2,1)}, bf16[256,896]{1,0:T(8,128)(2,1)S(1)}, u32[]{:S(2)}) copy-start(bf16[256,896]{1,0:T(8,128)(2,1)S(1)} %collective-permute-done.9.refs_3_) | copy-start | bytes 1376260
  89.4 12.7 %collective-permute-start.11 = (bf16[256,896]{1,0:T(8,128)(2,1)S(1)}, bf16[256,896]{1,0:T(8,128)(2,1)S(1)}, u32[]{:S(2)}, u32[]{:S(2)}) collective-permute-start(bf16[256,896]{1,0:T(8,128)(2,1)S(1)} %collective-permute-done.9.refs_3_), channel_id=1, source_target_pairs={{0,480},{32,0},{64,32},{96,64},{128,96},{160,128},{192,160},{224,1... | collective-permute-start | bytes 1376264 | tf_op jit(solution)/shard_map/ppermute | solution.py:307
  94.6 34.1 %copy-start.7 = (bf16[256,896]{1,0:T(8,128)(2,1)}, bf16[256,896]{1,0:T(8,128)(2,1)S(1)}, u32[]{:S(2)}) copy-start(bf16[256,896]{1,0:T(8,128)(2,1)S(1)} %collective-permute-done.8.refs_2_) | copy-start | bytes 1376260
  94.6 12.9 %collective-permute-start.10 = (bf16[256,896]{1,0:T(8,128)(2,1)S(1)}, bf16[256,896]{1,0:T(8,128)(2,1)S(1)}, u32[]{:S(2)}, u32[]{:S(2)}) collective-permute-start(bf16[256,896]{1,0:T(8,128)(2,1)S(1)} %collective-permute-done.8.refs_2_), channel_id=1, source_target_pairs={{0,32},{32,64},{64,96},{96,128},{128,160},{160,192},{192,224},{224... | collective-permute-start | bytes 1376264 | tf_op jit(solution)/shard_map/ppermute | solution.py:306
  102.1 26.6 %copy-start.8 = (bf16[256,896]{1,0:T(8,128)(2,1)}, bf16[256,896]{1,0:T(8,128)(2,1)S(1)}, u32[]{:S(2)}) copy-start(bf16[256,896]{1,0:T(8,128)(2,1)S(1)} %collective-permute-done.11.refs_5_) | copy-start | bytes 1376260
  102.1 13.2 %collective-permute-start.13 = (bf16[256,896]{1,0:T(8,128)(2,1)S(1)}, bf16[256,896]{1,0:T(8,128)(2,1)S(1)}, u32[]{:S(2)}, u32[]{:S(2)}) collective-permute-start(bf16[256,896]{1,0:T(8,128)(2,1)S(1)} %collective-permute-done.11.refs_5_), channel_id=1, source_target_pairs={{0,480},{32,0},{64,32},{96,64},{128,96},{160,128},{192,160},{224,1... | collective-permute-start | bytes 1376264 | tf_op jit(solution)/shard_map/ppermute | solution.py:307
  107.5 21.2 %copy-start.10 = (bf16[256,896]{1,0:T(8,128)(2,1)}, bf16[256,896]{1,0:T(8,128)(2,1)S(1)}, u32[]{:S(2)}) copy-start(bf16[256,896]{1,0:T(8,128)(2,1)S(1)} %collective-permute-done.10.refs_4_) | copy-start | bytes 1376260
  107.5 14.2 %collective-permute-start.12 = (bf16[256,896]{1,0:T(8,128)(2,1)S(1)}, bf16[256,896]{1,0:T(8,128)(2,1)S(1)}, u32[]{:S(2)}, u32[]{:S(2)}) collective-permute-start(bf16[256,896]{1,0:T(8,128)(2,1)S(1)} %collective-permute-done.10.refs_4_), channel_id=1, source_target_pairs={{0,32},{32,64},{64,96},{96,128},{128,160},{160,192},{192,224},{224... | collective-permute-start | bytes 1376264 | tf_op jit(solution)/shard_map/ppermute | solution.py:306
  115.3 13.4 %copy-start.1 = (bf16[256,896]{1,0:T(8,128)(2,1)}, bf16[256,896]{1,0:T(8,128)(2,1)S(1)}, u32[]{:S(2)}) copy-start(bf16[256,896]{1,0:T(8,128)(2,1)S(1)} %collective-permute-done.13.refs_7_) | copy-start | bytes 1376260
  115.3 13.4 %collective-permute-start.15 = (bf16[128,896]{1,0:T(8,128)(2,1)S(1)}, bf16[128,896]{1,0:T(8,128)(2,1)S(1)}, u32[]{:S(2)}, u32[]{:S(2)}) collective-permute-start(bf16[128,896]{1,0:T(8,128)(2,1)S(1)} %slice.21), channel_id=1, source_target_pairs={{0,480},{32,0},{64,32},{96,64},{128,96},{160,128},{192,160},{224,1... | collective-permute-start | bytes 688136 | tf_op jit(solution)/shard_map/ppermute | solution.py:307
  121.7 7.0 %copy-start.2 = (bf16[256,896]{1,0:T(8,128)(2,1)}, bf16[256,896]{1,0:T(8,128)(2,1)S(1)}, u32[]{:S(2)}) copy-start(bf16[256,896]{1,0:T(8,128)(2,1)S(1)} %collective-permute-done.12.refs_6_) | copy-start | bytes 1376260
  121.7 9.3 %collective-permute-start.14 = (bf16[128,896]{1,0:T(8,128)(2,1)S(1)}, bf16[128,896]{1,0:T(8,128)(2,1)}, u32[]{:S(2)}, u32[]{:S(2)}) collective-permute-start(bf16[128,896]{1,0:T(8,128)(2,1)S(1)} %slice.20), channel_id=1, source_target_pairs={{0,32},{32,64},{64,96},{96,128},{128,160},{160,192},{192,224},{224... | collective-permute-start | bytes 688136 | tf_op jit(solution)/shard_map/ppermute | solution.py:306
  128.7 2.3 %copy-start.14 = (bf16[128,896]{1,0:T(8,128)(2,1)}, bf16[128,896]{1,0:T(8,128)(2,1)S(1)}, u32[]{:S(2)}) copy-start(bf16[128,896]{1,0:T(8,128)(2,1)S(1)} %collective-permute-done.15.refs_9_) | copy-start | bytes 688132
  141.0 85.0 %copy-start.16 = (f32[3,16,512]{2,1,0:T(8,128)S(1)}, f32[3,16,512]{2,1,0:T(8,128)}, u32[]{:S(2)}) copy-start(f32[3,16,512]{2,1,0:T(8,128)} %param.18) | copy-start | bytes 294916
  141.0 85.6 %copy-start.15 = (f32[3,16,896]{2,1,0:T(8,128)S(1)}, f32[3,16,896]{2,1,0:T(8,128)}, u32[]{:S(2)}) copy-start(f32[3,16,896]{2,1,0:T(8,128)} %param.19) | copy-start | bytes 516100
  152.1 9.4 %all-to-all-start.1 = ((f32[8,8,512]{2,1,0:T(8,128)}), f32[8,8,512]{2,1,0:T(8,128)S(1)}, u32[]{:S(2)}, u32[]{:S(2)}) async-start(f32[8,8,512]{2,1,0:T(8,128)} %broadcast_in_dim.9), calls=%async_computation.1 | async-start | bytes 262144 | tf_op jit(solution)/shard_map/all_to_all | solution.py:435
  161.5 0.7 copy-start.3
Sparse Core Ops, SparseCore 0:
  10.1 43.8 all-gather.2
  56.2 39.7 all-gather.4

commit v9 on v8

--- a/solution.py
+++ b/solution.py
@@ -47,57 +47,96 @@
     return copies
 
 
-def fetch_blocks(plan, z_ref, gradient_ref, block_refs, left, right, sems):
-    n_z, rows_z = plan["n_z"], plan["rows"]
-    fetched, row, at = [], 0, 0
+def locate(spot_ref, n_x):
+    x, core = spot_ref[1], spot_ref[2]
+    other = 1 - core
+    near = lax.rem(x + jnp.where(core == 0, n_x - 1, 1), n_x) * 2
+    beyond = lax.rem(x + jnp.where(core == 0, 1, n_x - 1), n_x) * 2
+    across = lax.rem(x + 2, n_x) * 2
+    return [
+        (0, 0, 2 * x + core),
+        (1, 0, 2 * x + other),
+        (2, 0, near + core),
+        (2, 1, near + other),
+        (3, 0, across + core),
+        (4, 0, beyond + other),
+        (4, 1, beyond + core),
+        (5, 0, across + other),
+    ]
+
+
+def fetch_blocks(plan, spot_ref, piece_refs, block_refs, left, right, sems):
+    n_z, rows, tokens = plan["n_z"], plan["rows"], left.shape[0]
+    count = left.shape[1] // rows
+
+    def columns(array, piece, half, i):
+        return pltpu.make_async_copy(
+            piece_refs[array].at[pl.ds(2 * tokens * piece, tokens), pl.ds(half * rows, rows)],
+            left.at[:, pl.ds(pl.multiple_of(i * rows, rows), rows)],
+            sems.at[i],
+        )
+
+    halves = piece_refs[0].shape[1] // rows
+    for array, piece, rank in locate(spot_ref, plan["n_x"]):
+        for half in range(halves):
+            at = rank * halves + half
+            i = lax.rem(at - spot_ref[0] - plan["first"] + 2 * n_z, n_z)
+
+            @pl.when(i < count)
+            def _(array=array, piece=piece, half=half, i=i):
+                columns(array, piece, half, i).start()
+
+    waits = [[columns(0, 0, 0, i)] for i in range(count)]
+    sem = count
     for (offset, first), block in zip(plan["blocks"], block_refs, strict=True):
-        rows = block.shape[0]
-        start = lax.rem(z_ref[0] + (offset + n_z), n_z) * rows_z + first
-        columns = pl.ds(pl.multiple_of(start, 128), rows)
-        span = pl.ds(row, rows)
-        fetched.append(
-            copy_rows(gradient_ref.at[:, columns], left.at[:, span], sems, at, 2)
-            + copy_rows(block, right.at[span, :], sems, at + 2, 2)
-        )
-        row += rows
-        at += 4
-    return fetched
-
-
-def side_kernel(n_pairs, *refs):
-    row_refs = refs[:n_pairs]
-    factors_ref, projected_ref, turned_ref, gram_ref, total = refs[n_pairs:]
-    step = pl.program_id(0)
+        i = offset - plan["first"]
+        span = pl.ds(i * rows + first, block.shape[0])
+        copies = copy_rows(block, right.at[span, :], sems, sem, 2)
+        sem += 2
+        for copy in copies:
+            copy.start()
+        waits[i] += copies
+    return waits
+
+
+def side_kernel(n_x, first, count, which, spot_ref, *refs):
+    piece_refs = refs[:6]
+    factors_ref, projected_ref, turned_ref, gram_ref, total, rows_ref, sems = refs[6:]
     size = SEQUENCE_TOKENS
-
-    @pl.when(step == 0)
-    def _():
-        total[...] = jnp.zeros_like(total)
-
-    for p, rows_ref in enumerate(row_refs):
-        rows = rows_ref[...]
-        stacked = jnp.concatenate([rows, factors_ref[...]], axis=0)
-        total[p] += contract(stacked, rows, 1, 1)
-
-    @pl.when(step == pl.num_programs(0) - 1)
-    def _():
-        for p in range(n_pairs):
-            gram_ref[2 * p] = total[p, :size, :size]
-            gram_ref[2 * p + 1] = total[p, size : 2 * size, size:]
-            span = slice(2 * size * p, 2 * size * (p + 1))
-            projected = total[p, 2 * size :]
-            projected_ref[:, span] = projected.astype(BF16)
-            turned_ref[span, :] = projected.T.astype(BF16)
-
-
-def part_kernel(plan, z_ref, gradient_ref, *refs):
+    tokens, width = rows_ref.shape[1:]
+    places = locate(spot_ref, n_x)
+    copies = []
+    for i, (array, piece, _) in enumerate(places):
+        span = pl.ds((2 * piece + which) * tokens, tokens)
+        copies.append(
+            pltpu.make_async_copy(piece_refs[array].at[span, :], rows_ref.at[i], sems.at[i])
+        )
+    for copy in copies:
+        copy.start()
+    total[...] = jnp.zeros_like(total)
+    for i, (_, _, rank) in enumerate(places):
+        copies[i].wait()
+        columns = pl.ds(pl.multiple_of(rank * width, width), width)
+        factors = factors_ref[first : first + count, columns]
+        for p in range(total.shape[0]):
+            rows = rows_ref[i, 2 * size * p : 2 * size * (p + 1), :]
+            total[p] += contract(jnp.concatenate([rows, factors], axis=0), rows, 1, 1)
+    for p in range(total.shape[0]):
+        gram_ref[2 * p] = total[p, :size, :size]
+        gram_ref[2 * p + 1] = total[p, size : 2 * size, size:]
+        span = slice(2 * size * p, 2 * size * (p + 1))
+        projected = total[p, 2 * size :]
+        projected_ref[:, span] = projected.astype(BF16)
+        turned_ref[span, :] = projected.T.astype(BF16)
+
+
+def part_kernel(plan, spot_ref, *refs):
     n_blocks = len(plan["blocks"])
+    piece_refs, refs = refs[:6], refs[6:]
     block_refs = refs[:n_blocks]
     out_ref, total, left, right, sems, out_sems = refs[n_blocks:]
-    copies = sum(fetch_blocks(plan, z_ref, gradient_ref, block_refs, left, right, sems), [])
-    for copy in copies:
-        copy.start()
-    for copy in copies:
+    waits = fetch_blocks(plan, spot_ref, piece_refs, block_refs, left, right, sems)
+    for copy in sum(waits, []):
         copy.wait()
 
     writes = []
@@ -112,8 +151,9 @@
         write.wait()
 
 
-def hidden_kernel(plan, z_ref, gradient_ref, *refs):
+def hidden_kernel(plan, spot_ref, *refs):
     n_blocks = len(plan["blocks"])
+    piece_refs, refs = refs[:6], refs[6:]
     block_refs = refs[:n_blocks]
     (before_hbm, gate_hbm, up_hbm, factors_ref, in_ref, lora_ref, lora_t_ref) = refs[
         n_blocks : n_blocks + 7
@@ -124,12 +164,14 @@
     left_rows, right_rows, sems, out_sems = refs[-4:]
     tokens, hidden = gate_ref.shape
     sequences = tokens // SEQUENCE_TOKENS
-    fetched = fetch_blocks(plan, z_ref, gradient_ref, block_refs, left_rows, right_rows, sems)
-    at = 4 * n_blocks
+    at = sems.shape[0] - 12
     activations = copy_rows(gate_hbm, gate_ref, sems, at, 4)
     activations += copy_rows(up_hbm, up_ref, sems, at + 4, 4)
     running = copy_rows(before_hbm, before_ref, sems, at + 8, 4)
-    for copy in activations + sum(fetched, []) + running:
+    for copy in activations:
+        copy.start()
+    waits = fetch_blocks(plan, spot_ref, piece_refs, block_refs, left_rows, right_rows, sems)
+    for copy in running:
         copy.start()
     mids_ref[...] = jnp.zeros_like(mids_ref)
 
@@ -176,15 +218,12 @@
     for copy in activations:
         copy.wait()
     column_tiles(hidden, hidden, functools.partial(each, body=forward))
-    row = 0
-    for some in plan["chunks"]:
-        for copy in sum(fetched[some], []):
+    for start, end in plan["chunks"]:
+        for copy in sum(waits[start:end], []):
             copy.wait()
-        rows = sum(block.shape[0] for block in block_refs[some])
-        span = slice(row, row + rows)
+        span = slice(start * plan["rows"], end * plan["rows"])
         product = jnp.dot(left_rows[:, span], right_rows[span, :], preferred_element_type=F32)
-        total[...] = product if row == 0 else total[...] + product
-        row += rows
+        total[...] = product if start == 0 else total[...] + product
     for copy in running:
         copy.wait()
     spans = column_tiles(hidden, hidden, last_tile)
@@ -287,11 +326,20 @@
     n_z = sizes["z"]
     n_tensor = sizes["x"] * sizes["c"]
     z_axes, tensor_axes = "z", ("x", "c")
-    spot = lax.axis_index(z_axes).reshape(1).astype(jnp.int32)
-
-    gradient = lax.all_gather(output_gradient, tensor_axes, axis=1, tiled=True)
+    spot = jnp.stack([lax.axis_index(axis) for axis in ("z", "x", "c")]).astype(jnp.int32)
+
+    n_x = sizes["x"]
+    swap = [(0, 1), (1, 0)]
+    around = [(2 * i, 2 * ((i + 1) % n_x)) for i in range(n_x)]
+    around += [(2 * i + 1, 2 * ((i - 1) % n_x) + 1) for i in range(n_x)]
+    own = jnp.concatenate([output_gradient, normed], axis=0)
+    partner = lax.ppermute(own, "c", swap)
+    near = lax.ppermute(jnp.concatenate([own, partner], axis=0), tensor_axes, around)
+    across = lax.ppermute(near[: 2 * tokens], tensor_axes, around)
+    beyond = lax.ppermute(near, "c", swap)
+    across_partner = lax.ppermute(across, "c", swap)
+    pieces = (own, partner, near, across, beyond, across_partner)
     block = lax.all_gather(frozen_down_weight.T, "y", axis=0, tiled=True)
-    normed_all = lax.all_gather(normed, tensor_axes, axis=1, tiled=True)
 
     rows = block.shape[0]
     half = rows // 2
@@ -306,31 +354,23 @@
         low[k] = lax.ppermute(low_from, z_axes, ring(n_z, 1))
         high[k] = lax.ppermute(high_from, z_axes, ring(n_z, -1))
 
-    def side(values, first, count, name):
-        width = values.shape[1]
-        chunk = 1024
+    def side(which, first, count, name):
+        width = n_tensor * local_width
         return pl.pallas_call(
-            functools.partial(side_kernel, sequences // 2),
+            functools.partial(side_kernel, n_x, first, count, which),
             out_shape=(
                 jax.ShapeDtypeStruct((count, tokens), BF16),
                 jax.ShapeDtypeStruct((tokens, count), BF16),
                 jax.ShapeDtypeStruct((sequences, SEQUENCE_TOKENS, SEQUENCE_TOKENS), F32),
             ),
-            grid=(width // chunk,),
-            in_specs=[
-                pl.BlockSpec((2 * SEQUENCE_TOKENS, chunk), functools.partial(lambda p, i: (p, i), p))
-                for p in range(sequences // 2)
-            ]
-            + [pl.BlockSpec((count, chunk), lambda i: (first // count, i))],
-            out_specs=(
-                pl.BlockSpec((count, tokens), lambda i: (0, 0)),
-                pl.BlockSpec((tokens, count), lambda i: (0, 0)),
-                pl.BlockSpec((sequences, SEQUENCE_TOKENS, SEQUENCE_TOKENS), lambda i: (0, 0, 0)),
-            ),
+            in_specs=[smem] + [hbm] * len(pieces) + [vmem],
+            out_specs=(vmem, vmem, vmem),
             scratch_shapes=[
                 pltpu.VMEM(
                     (sequences // 2, 2 * SEQUENCE_TOKENS + count, 2 * SEQUENCE_TOKENS), F32
-                )
+                ),
+                pltpu.VMEM((n_tensor, tokens, local_width), BF16),
+                pltpu.SemaphoreType.DMA((n_tensor,)),
             ],
             compiler_params=params,
             cost_estimate=pl.CostEstimate(
@@ -339,7 +379,7 @@
                 transcendentals=0,
             ),
             name=name,
-        )(*[values] * (sequences // 2), adapter_width_factors.reshape(3 * RANK, width))
+        )(spot, *pieces, adapter_width_factors.reshape(3 * RANK, width))
 
     def scratch(n_rows, n_sems):
         return [
@@ -354,14 +394,20 @@
 
     def part(offsets):
         blocks = [at_z(offset) for offset in offsets]
-        plan = dict(n_z=n_z, rows=rows, blocks=[(offset, 0) for offset in offsets])
+        plan = dict(
+            n_z=n_z,
+            n_x=n_x,
+            rows=rows,
+            first=offsets[0],
+            blocks=[(offset, 0) for offset in offsets],
+        )
         n = len(blocks)
         return pl.pallas_call(
             functools.partial(part_kernel, plan),
             out_shape=jax.ShapeDtypeStruct((tokens, hidden), F32),
-            in_specs=[smem] + [hbm] * (n + 1),
+            in_specs=[smem] + [hbm] * (len(pieces) + n),
             out_specs=hbm,
-            scratch_shapes=[pltpu.VMEM((tokens, hidden), F32)] + scratch(n * rows, 4 * n),
+            scratch_shapes=[pltpu.VMEM((tokens, hidden), F32)] + scratch(n * rows, 3 * n),
             compiler_params=params,
             cost_estimate=pl.CostEstimate(
                 flops=2 * tokens * n * rows * hidden,
@@ -369,41 +415,41 @@
                 transcendentals=0,
             ),
             name="part_product",
-        )(spot, gradient, *blocks)
+        )(spot, *pieces, *blocks)
 
     def after(value, other):
         return lax.optimization_barrier((value, other))[0]
 
-    def pairs(first, end):
-        return [sign * k for k in range(first, end) for sign in (-1, 1)]
-
     last = n_z // 2
-    for k in range(1, last - 3):
+    for k in range(1, last - 1):
         step(k, low[k - 1], high[k - 1])
-    total = part([0] + pairs(1, last - 4))
-    at = last - 4
+    split = last - 4
+    total = part(list(range(1 - split, split)))
+    at = last - 2
     step(at + 1, after(low[at], total), after(high[at], total))
-    lora_t, lora, gradient_gram = side(gradient, 2 * RANK, RANK, "gradient_side")
-    at = last - 3
-    step(at + 1, after(low[at], lora_t), after(high[at], lora_t))
-    step(last - 1, low[last - 2], high[last - 2])
-    step(last, low[last - 1][:half], high[last - 1][half:])
-    in_t, _, normed_gram = side(normed_all, 0, 2 * RANK, "normed_side")
-    offsets = pairs(last - 4, last)
-    blocks = [at_z(offset) for offset in offsets] + [low[last], high[last]]
+    lora_t, lora, gradient_gram = side(0, 2 * RANK, RANK, "gradient_side")
+    at = last - 1
+    low_in, high_in = after(low[at], lora_t), after(high[at], lora_t)
+    step(last, low_in[:half], high_in[half:])
+    in_t, _, normed_gram = side(1, 0, 2 * RANK, "normed_side")
+    ahead, behind = list(range(split, last)), list(range(last + 1, n_z - split + 1))
+    blocks = [high[k] for k in ahead] + [low[last], high[last]] + [low[n_z - k] for k in behind]
     plan = dict(
         n_z=n_z,
+        n_x=n_x,
         rows=rows,
-        blocks=[(offset, 0) for offset in offsets] + [(last, 0), (last, half)],
-        chunks=[slice(0, 4), slice(4, 8), slice(8, 10)],
-    )
+        first=split,
+        blocks=[(k, 0) for k in ahead] + [(last, 0), (last, half)] + [(k, 0) for k in behind],
+        chunks=[(0, last - split), (last - split, n_z - 2 * split + 1)],
+    )
+    n_offsets = n_z - 2 * split + 1
     sums, mids = pl.pallas_call(
         functools.partial(hidden_kernel, plan),
         out_shape=(
             jax.ShapeDtypeStruct((sequences, 3 * RANK, hidden), F32),
             jax.ShapeDtypeStruct((8 * n_tensor, tokens), F32),
         ),
-        in_specs=[smem] + [hbm] * (len(blocks) + 4) + [vmem] * 4,
+        in_specs=[smem] + [hbm] * (len(pieces) + len(blocks) + 3) + [vmem] * 4,
         out_specs=(hbm, vmem),
         scratch_shapes=[
             pltpu.VMEM((tokens, hidden), F32),
@@ -414,12 +460,12 @@
             pltpu.VMEM((tokens, hidden), F32),
             pltpu.VMEM((sequences, 3 * RANK, hidden), F32),
         ]
-        + scratch((len(offsets) + 1) * rows, 4 * len(blocks) + 12),
+        + scratch(n_offsets * rows, n_offsets + 2 * len(blocks) + 12),
         compiler_params=params,
         name="hidden_side",
     )(
         spot,
-        gradient,
+        *pieces,
         *blocks,
         total,
         gate_preactivation,

time: 235 us -> 240 us (1.021)
  between operations: 15.1 us -> 1.8 us
  starting transfers between devices: 67.1 us -> 76 us
  local copies, waits for them, and re-layouts: 1.5 us -> 7.13 us
  blocking collectives: 84.5 us -> 88.2 us
    ppermute x0 -> x5, starting transfers between devices: none -> 11.2 us  [the longest x1 3.39 us: per_device(): lax.ppermute(jnp.concatenate([own, partner], axis=0), tensor_axes, around)]
    all_to_all x1, blocking collectives: 10.3 us -> 16.1 us  [per_device(): lax.all_to_all(mids.reshape(n_tensor, 8, tokens), tensor_axes, 0, 0)]
    unnamed x34 -> x47, local copies, waits for them, and re-layouts: 0.72 us -> 5.2 us
    ppermute x0 -> x5, waiting for transfers between devices: none -> 2.64 us  [the longest x1 2.63 us: per_device(): partner = lax.ppermute(own, 'c', swap)]
    all_to_all x1, blocking collectives: 13.3 us -> 10.7 us  [per_device(): lax.all_to_all(out.reshape(n_y, -1, 128), 'y', 0, 0)]
  transfers between devices with their start and end apart: 19 -> 22, of which waited for: 12 -> 12; matrix products, arithmetic and copies ran while one was open for 0% -> 0% of each run, Pallas kernels for 7% -> 7%
where the time goes in v9:
time: 240 us; the launch traced here: 239 us
  blocking collectives  88.2 us (37%)
  starting transfers between devices  76 us (32%)
  waiting for transfers between devices  34.5 us (14%)
  Pallas kernels  29.2 us (12%)
  local copies, waits for them, and re-layouts  7.13 us (3%)
    ppermute x8, starting transfers between devices, step(): high[k] = lax.ppermute(high_from, z_axes, ring(n_z, -1))  46.1 us
    ppermute x8, waiting for transfers between devices, step(): high[k] = lax.ppermute(high_from, z_axes, ring(n_z, -1))  22.1 us
    all_to_all x1, blocking collectives, per_device(): lax.all_to_all(share.reshape(n_z, -1, 128), z_axes, 0, 0)  21.4 us
    all_to_all x1, blocking collectives, per_device(): lax.all_to_all(jnp.broadcast_to(share, (n_z,) + share.shape), z_axes, 0, 0)  17 us
    all_to_all x1, blocking collectives, per_device(): lax.all_to_all(mids.reshape(n_tensor, 8, tokens), tensor_axes, 0, 0)  16.1 us
    ppermute x8, starting transfers between devices, step(): low[k] = lax.ppermute(low_from, z_axes, ring(n_z, 1))  15.3 us
    all_gather x1, blocking collectives, per_device(): block = lax.all_gather(frozen_down_weight.T, 'y', axis=0, tiled=True)  13.6 us
    all_to_all x1, blocking collectives, per_device(): lax.all_to_all(out.reshape(n_y, -1, 128), 'y', 0, 0)  10.7 us
  transfers between devices with their start and end apart: 22, of which 12 were waited for; matrix products, arithmetic and copies ran while one was open for 0% of the time, Pallas kernels for 7%

profile of v9, /device:TPU:32, one launch (start us, length us, event | category | flops | bytes accessed | tf_op | source)
XLA Modules:
  0.0 238.9 jit_solution(9076981312270380394)
XLA Ops:
  0.6 0.0 copy-start.4
  0.6 0.0 copy-start.5
  0.7 1.2 constant_dynamic-update-slice_fusion.1
  1.8 1.1 constant_dynamic-update-slice_fusion.refs_0_
  2.9 1.0 copy-done.2
  3.9 2.0 collective-permute-start
  5.9 2.6 %collective-permute-done.refs_1_ = bf16[1024,512]{1,0:T(8,128)(2,1)S(1)} collective-permute-done((bf16[1024,512]{1,0:T(8,128)(2,1)S(1)}, bf16[1024,512]{1,0:T(8,128)(2,1)S(1)}, u32[]{:S(2)}, u32[]{:S(2)}) %collective-permute-start) | collective-permute-done | bytes 1048608 | tf_op jit(solution)/shard_map/ppermute | solution.py:336
  8.6 0.1 pad_maximum_fusion
  8.7 0.8 copy-done.1
  9.5 3.4 %collective-permute-start.1 = (bf16[2048,512]{1,0:T(8,128)(2,1)S(1)}, bf16[2048,512]{1,0:T(8,128)(2,1)S(1)}, u32[]{:S(2)}, u32[]{:S(2)}) collective-permute-start(bf16[2048,512]{1,0:T(8,128)(2,1)S(1)} %pad_maximum_fusion), channel_id=1, source_target_pairs={{0,2},{2,4},{4,6},{6,0},{1,7},{3,1},{5,3},{7,5},{8,10},{10,12},{12... | collective-permute-start | bytes 6291464 | tf_op jit(solution)/shard_map/ppermute | solution.py:337
  12.9 13.6 %all_gather.3.refs_9_ = bf16[256,896]{1,0:T(8,128)(2,1)S(1)} all-gather(bf16[64,896]{1,0:T(8,128)(2,1)S(1)} %bitcast.26), channel_id=1, replica_groups=mesh['z'=16,'y'=4,'x'=4,'c'=2] {'y'}, dimensions={0}, use_global_device_ids=true | all-gather | bytes 573440 | tf_op jit(solution)/shard_map/all_gather | solution.py:342
  26.6 5.5 %collective-permute-start.5 = (bf16[256,896]{1,0:T(8,128)(2,1)S(1)}, bf16[256,896]{1,0:T(8,128)(2,1)S(1)}, u32[]{:S(2)}, u32[]{:S(2)}) collective-permute-start(bf16[256,896]{1,0:T(8,128)(2,1)S(1)} %all_gather.3.refs_9_), channel_id=1, source_target_pairs={{0,480},{32,0},{64,32},{96,64},{128,96},{160,128},{192,160},{224,1... | collective-permute-start | bytes 1376264 | tf_op jit(solution)/shard_map/ppermute | solution.py:355
  32.1 1.9 collective-permute-start.11
  34.0 6.5 %collective-permute-done.5.refs_10_ = bf16[256,896]{1,0:T(8,128)(2,1)S(1)} collective-permute-done((bf16[256,896]{1,0:T(8,128)(2,1)S(1)}, bf16[256,896]{1,0:T(8,128)(2,1)S(1)}, u32[]{:S(2)}, u32[]{:S(2)}) %collective-permute-start.5) | collective-permute-done | bytes 458784 | tf_op jit(solution)/shard_map/ppermute | solution.py:355
  40.5 8.8 %collective-permute-start.6 = (bf16[256,896]{1,0:T(8,128)(2,1)S(1)}, bf16[256,896]{1,0:T(8,128)(2,1)S(1)}, u32[]{:S(2)}, u32[]{:S(2)}) collective-permute-start(bf16[256,896]{1,0:T(8,128)(2,1)S(1)} %collective-permute-done.5.refs_10_), channel_id=1, source_target_pairs={{0,480},{32,0},{64,32},{96,64},{128,96},{160,128},{192,160},{224,1... | collective-permute-start | bytes 1376264 | tf_op jit(solution)/shard_map/ppermute | solution.py:355
  49.4 0.5 collective-permute-done.11.refs_8_
  49.8 1.9 collective-permute-start.12
  51.8 0.0 collective-permute-done.1.refs_2_
  51.8 0.1 slice.24
  51.9 1.9 collective-permute-start.2
  53.8 1.9 collective-permute-start.3
  55.7 2.1 collective-permute-done.6.refs_11_
  57.8 5.6 %collective-permute-start.7 = (bf16[256,896]{1,0:T(8,128)(2,1)S(1)}, bf16[256,896]{1,0:T(8,128)(2,1)S(1)}, u32[]{:S(2)}, u32[]{:S(2)}) collective-permute-start(bf16[256,896]{1,0:T(8,128)(2,1)S(1)} %collective-permute-done.6.refs_11_), channel_id=1, source_target_pairs={{0,480},{32,0},{64,32},{96,64},{128,96},{160,128},{192,160},{224,1... | collective-permute-start | bytes 1376264 | tf_op jit(solution)/shard_map/ppermute | solution.py:355
  63.4 0.5 collective-permute-done.12.refs_7_
  63.9 1.9 collective-permute-start.13
  65.8 5.5 %collective-permute-done.7.refs_12_ = bf16[256,896]{1,0:T(8,128)(2,1)S(1)} collective-permute-done((bf16[256,896]{1,0:T(8,128)(2,1)S(1)}, bf16[256,896]{1,0:T(8,128)(2,1)S(1)}, u32[]{:S(2)}, u32[]{:S(2)}) %collective-permute-start.7) | collective-permute-done | bytes 458784 | tf_op jit(solution)/shard_map/ppermute | solution.py:355
  71.3 5.2 %collective-permute-start.8 = (bf16[256,896]{1,0:T(8,128)(2,1)S(1)}, bf16[256,896]{1,0:T(8,128)(2,1)S(1)}, u32[]{:S(2)}, u32[]{:S(2)}) collective-permute-start(bf16[256,896]{1,0:T(8,128)(2,1)S(1)} %collective-permute-done.7.refs_12_), channel_id=1, source_target_pairs={{0,480},{32,0},{64,32},{96,64},{128,96},{160,128},{192,160},{224,1... | collective-permute-start | bytes 1376264 | tf_op jit(solution)/shard_map/ppermute | solution.py:355
  76.6 0.5 collective-permute-done.13.refs_6_
  77.1 1.9 collective-permute-start.15
  79.0 1.9 collective-permute-start.4
  80.9 2.2 collective-permute-done.8.refs_6_
  83.2 0.8 copy-done.10
  84.0 5.6 %collective-permute-start.9 = (bf16[256,896]{1,0:T(8,128)(2,1)S(1)}, bf16[256,896]{1,0:T(8,128)(2,1)}, u32[]{:S(2)}, u32[]{:S(2)}) collective-permute-start(bf16[256,896]{1,0:T(8,128)(2,1)S(1)} %collective-permute-done.8.refs_6_), channel_id=1, source_target_pairs={{0,480},{32,0},{64,32},{96,64},{128,96},{160,128},{192,160},{224,1... | collective-permute-start | bytes 1376264 | tf_op jit(solution)/shard_map/ppermute | solution.py:355
  89.6 0.0 collective-permute-done.15.refs_15_
  89.6 1.9 collective-permute-start.16
  91.5 5.8 %collective-permute-done.9.refs_7_ = bf16[256,896]{1,0:T(8,128)(2,1)} collective-permute-done((bf16[256,896]{1,0:T(8,128)(2,1)S(1)}, bf16[256,896]{1,0:T(8,128)(2,1)}, u32[]{:S(2)}, u32[]{:S(2)}) %collective-permute-start.9) | collective-permute-done | bytes 458784 | tf_op jit(solution)/shard_map/ppermute | solution.py:355
  97.3 5.1 %collective-permute-start.10 = (bf16[256,896]{1,0:T(8,128)(2,1)}, bf16[256,896]{1,0:T(8,128)(2,1)}, u32[]{:S(2)}, u32[]{:S(2)}) collective-permute-start(bf16[256,896]{1,0:T(8,128)(2,1)} %collective-permute-done.9.refs_7_), channel_id=1, source_target_pairs={{0,480},{32,0},{64,32},{96,64},{128,96},{160,128},{192,160},{224,1... | collective-permute-start | bytes 1376264 | tf_op jit(solution)/shard_map/ppermute | solution.py:355
  102.4 0.6 collective-permute-done.16.refs_14_
  103.0 1.9 collective-permute-start.17
  105.0 0.6 pad_add_fusion.spot_ref
  105.6 0.0 collective-permute-done.4.refs_5_
  105.6 0.0 collective-permute-done.3.refs_4_
  105.6 6.3 %part_product.1.refs_16_ = f32[512,896]{1,0:T(8,128)} custom-call(s32[3]{0:T(128)} %pad_add_fusion.spot_ref, bf16[1024,512]{1,0:T(8,128)(2,1)} %copy-done.2, bf16[1024,512]{1,0:T(8,128)(2,1)} %copy-done.1, bf16[2048,512]{1,0:T(8,128)(2,1)} %copy-done, bf16[1024,512]{1,0:T(8,128)(2,1)} %copy-done.3, bf16[2048,512]{1,0:T(8,128)(2,1)} %collective-permute-done.3.refs_4_, ...), custom_call_target="tpu_custom_call" | custom-call | flops 1644167168 | bytes 6291456 | tf_op jit(solution)/shard_map/part_product/pallas_call | solution.py:405
  112.0 5.1 %collective-permute-start.14 = (bf16[256,896]{1,0:T(8,128)(2,1)}, bf16[256,896]{1,0:T(8,128)(2,1)S(1)}, u32[]{:S(2)}, u32[]{:S(2)}) collective-permute-start(bf16[256,896]{1,0:T(8,128)(2,1)} %collective-permute-done.10.refs_8_), channel_id=1, source_target_pairs={{0,480},{32,0},{64,32},{96,64},{128,96},{160,128},{192,160},{224,1... | collective-permute-start | bytes 1376264 | tf_op jit(solution)/shard_map/ppermute | solution.py:355
  117.1 1.9 collective-permute-start.18
  119.1 4.9 %gradient_side.1 = (bf16[16,512]{1,0:T(8,128)(2,1)}, bf16[512,16]{1,0:T(8,128)(2,1)}, f32[4,128,128]{2,1,0:T(8,128)}) custom-call(s32[3]{0:T(128)} %pad_add_fusion.spot_ref, bf16[1024,512]{1,0:T(8,128)(2,1)} %copy-done.2, bf16[1024,512]{1,0:T(8,128)(2,1)} %copy-done.1, bf16[2048,512]{1,0:T(8,128)(2,1)} %copy-done, bf16[1024,512]{1,0:T(8,128)(2,1)} %copy-done.3, ...), custom_call_target="tpu_custom_call" | custom-call | flops 603979776 | bytes 5242880 | tf_op jit(solution)/shard_map/gradient_side/pallas_call | solution.py:359
  124.0 5.1 %collective-permute-start.20 = (bf16[128,896]{1,0:T(8,128)(2,1)S(1)}, bf16[128,896]{1,0:T(8,128)(2,1)S(1)}, u32[]{:S(2)}, u32[]{:S(2)}) collective-permute-start(bf16[128,896]{1,0:T(8,128)(2,1)S(1)} %slice.20), channel_id=1, source_target_pairs={{0,480},{32,0},{64,32},{96,64},{128,96},{160,128},{192,160},{224,1... | collective-permute-start | bytes 688136 | tf_op jit(solution)/shard_map/ppermute | solution.py:355
  129.2 1.9 collective-permute-start.19
  131.1 4.9 %normed_side.1 = (bf16[32,512]{1,0:T(8,128)(2,1)}, bf16[512,32]{1,0:T(8,128)(2,1)}, f32[4,128,128]{2,1,0:T(8,128)}) custom-call(s32[3]{0:T(128)} %pad_add_fusion.spot_ref, bf16[1024,512]{1,0:T(8,128)(2,1)} %copy-done.2, bf16[1024,512]{1,0:T(8,128)(2,1)} %copy-done.1, bf16[2048,512]{1,0:T(8,128)(2,1)} %copy-done, bf16[1024,512]{1,0:T(8,128)(2,1)} %copy-done.3, ...), custom_call_target="tpu_custom_call" | custom-call | flops 671088640 | bytes 5242880 | tf_op jit(solution)/shard_map/normed_side/pallas_call | solution.py:359
  136.1 2.2 collective-permute-done.19.refs_10_
  138.3 0.7 copy-done.19
  139.0 10.1 %hidden_side.1 = (f32[4,48,896]{2,1,0:T(8,128)}, f32[64,512]{1,0:T(8,128)}) custom-call(s32[3]{0:T(128)} %pad_add_fusion.spot_ref, bf16[1024,512]{1,0:T(8,128)(2,1)} %copy-done.2, bf16[1024,512]{1,0:T(8,128)(2,1)} %copy-done.1, bf16[2048,512]{1,0:T(8,128)(2,1)} %copy-done, bf16[1024,512]{1,0:T(8,128)(2,1)} %copy-done.3, ...), custom_call_target="tpu_custom_call" | custom-call | tf_op jit(solution)/shard_map/hidden_side/pallas_call | solution.py:446
  149.1 16.1 %all_to_all.30 = f32[8,8,512]{2,1,0:T(8,128)S(1)} all-to-all(f32[8,8,512]{2,1,0:T(8,128)} %bitcast.25), channel_id=1, replica_groups=mesh['z'=16,'y'=4,'x'=4,'c'=2] {'x','c'}, dimensions={0} | all-to-all | bytes 262144 | tf_op jit(solution)/shard_map/all_to_all | solution.py:479
  165.3 0.7 broadcast_in_dim.9
  165.9 3.4 %all-to-all-start.1 = ((f32[8,8,512]{2,1,0:T(8,128)}), f32[8,8,512]{2,1,0:T(8,128)S(1)}, u32[]{:S(2)}, u32[]{:S(2)}) async-start(f32[8,8,512]{2,1,0:T(8,128)} %broadcast_in_dim.9), calls=%async_computation.1 | async-start | bytes 262144 | tf_op jit(solution)/shard_map/all_to_all | solution.py:481
  170.0 5.4 %all-to-all-done.1 = f32[8,8,512]{2,1,0:T(8,128)S(1)} async-done(((f32[8,8,512]{2,1,0:T(8,128)}), f32[8,8,512]{2,1,0:T(8,128)S(1)}, u32[]{:S(2)}, u32[]{:S(2)}) %all-to-all-start.1) | async-done | bytes 131104 | tf_op jit(solution)/shard_map/all_to_all | solution.py:481
  175.4 0.7 copy-done.9
  176.0 2.9 %clip_side.1 = f32[72,8,128]{2,1,0:T(8,128)} custom-call(f32[1]{0:T(128)} %copy.13.clip_ref, f32[64,512]{1,0:T(8,128)} %bitcast.24, f32[4,48,896]{2,1,0:T(8,128)} %get-tuple-element.21.sums_ref, bf16[512,512]{1,0:T(8,128)(2,1)} %normed_ref.1, bf16[512,512]{1,0:T(8,128)(2,1)} %gradient_ref.1, f32[4,128,128]{2,1,0:T(8,128)} %get-tuple-element.22.normed_gram_ref, ...), custom_call_target="tpu_custom_call" | custom-call | tf_op jit(solution)/shard_map/clip_side/pallas_call | solution.py:488
  179.0 10.7 %all_to_all.31 = f32[4,144,128]{2,1,0:T(8,128)S(1)} all-to-all(f32[4,144,128]{2,1,0:T(8,128)} %bitcast.20), channel_id=1, replica_groups=mesh['z'=16,'y'=4,'x'=4,'c'=2] {'y'}, dimensions={0} | all-to-all | bytes 589824 | tf_op jit(solution)/shard_map/all_to_all | solution.py:507
  189.7 21.4 %all_to_all.32 = f32[16,9,128]{2,1,0:T(8,128)S(1)} all-to-all(f32[16,9,128]{2,1,0:T(8,128)S(1)} %reshape.40), channel_id=1, replica_groups=mesh['z'=16,'y'=4,'x'=4,'c'=2] {'z'}, dimensions={0} | all-to-all | bytes 147456 | tf_op jit(solution)/shard_map/all_to_all | solution.py:508
  211.2 17.0 %all_to_all.33 = f32[16,9,128]{2,1,0:T(8,128)S(1)} all-to-all(f32[16,9,128]{2,1,0:T(8,128)S(1)} %broadcast_in_dim.10), channel_id=1, replica_groups=mesh['z'=16,'y'=4,'x'=4,'c'=2] {'z'}, dimensions={0} | all-to-all | bytes 147456 | tf_op jit(solution)/shard_map/all_to_all | solution.py:509
  228.3 9.2 %all_to_all.34 = f32[4,144,128]{2,1,0:T(8,128)S(1)} all-to-all(f32[4,144,128]{2,1,0:T(8,128)S(1)} %broadcast_in_dim.11), channel_id=1, replica_groups=mesh['z'=16,'y'=4,'x'=4,'c'=2] {'y'}, dimensions={0} | all-to-all | bytes 589824 | tf_op jit(solution)/shard_map/all_to_all | solution.py:512
  237.5 0.7 fusion
  238.2 0.7 fusion.1
  (55 shorter events, 0.3 us)
Async XLA Ops:
  0.6 7.9 %copy-start.4 = (bf16[512,512]{1,0:T(8,128)(2,1)S(1)}, bf16[512,512]{1,0:T(8,128)(2,1)}, u32[]{:S(2)}) copy-start(bf16[512,512]{1,0:T(8,128)(2,1)} %gradient_ref.1) | copy-start | bytes 1572868
  0.6 7.9 %copy-start.5 = (bf16[512,512]{1,0:T(8,128)(2,1)S(1)}, bf16[512,512]{1,0:T(8,128)(2,1)}, u32[]{:S(2)}) copy-start(bf16[512,512]{1,0:T(8,128)(2,1)} %normed_ref.1) | copy-start | bytes 1572868
  2.9 1.0 copy-start.2
  3.9 9.1 %copy-start.21 = (bf16[896,64]{0,1:T(8,128)(2,1)S(1)}, bf16[896,64]{0,1:T(8,128)(2,1)}, u32[]{:S(2)}) copy-start(bf16[896,64]{0,1:T(8,128)(2,1)} %param.14) | copy-start | bytes 344068
  3.9 4.7 %collective-permute-start = (bf16[1024,512]{1,0:T(8,128)(2,1)S(1)}, bf16[1024,512]{1,0:T(8,128)(2,1)S(1)}, u32[]{:S(2)}, u32[]{:S(2)}) collective-permute-start(bf16[1024,512]{1,0:T(8,128)(2,1)S(1)} %constant_dynamic-update-slice_fusion.refs_0_), channel_id=1, source_target_pairs={{0,1},{1,0},{2,3},{3,2},{4,5},{5,4},{6,7},{7,6},{8,9},{9,8},{10,11... | collective-permute-start | bytes 3145736 | tf_op jit(solution)/shard_map/ppermute | solution.py:336
  8.6 1.0 copy-start.1
  9.5 42.2 %collective-permute-start.1 = (bf16[2048,512]{1,0:T(8,128)(2,1)S(1)}, bf16[2048,512]{1,0:T(8,128)(2,1)S(1)}, u32[]{:S(2)}, u32[]{:S(2)}) collective-permute-start(bf16[2048,512]{1,0:T(8,128)(2,1)S(1)} %pad_maximum_fusion), channel_id=1, source_target_pairs={{0,2},{2,4},{4,6},{6,0},{1,7},{3,1},{5,3},{7,5},{8,10},{10,12},{12... | collective-permute-start | bytes 6291464 | tf_op jit(solution)/shard_map/ppermute | solution.py:337
  26.6 23.3 %copy-start.6 = (bf16[256,896]{1,0:T(8,128)(2,1)}, bf16[256,896]{1,0:T(8,128)(2,1)S(1)}, u32[]{:S(2)}) copy-start(bf16[256,896]{1,0:T(8,128)(2,1)S(1)} %all_gather.3.refs_9_) | copy-start | bytes 1376260
  26.6 13.9 %collective-permute-start.5 = (bf16[256,896]{1,0:T(8,128)(2,1)S(1)}, bf16[256,896]{1,0:T(8,128)(2,1)S(1)}, u32[]{:S(2)}, u32[]{:S(2)}) collective-permute-start(bf16[256,896]{1,0:T(8,128)(2,1)S(1)} %all_gather.3.refs_9_), channel_id=1, source_target_pairs={{0,480},{32,0},{64,32},{96,64},{128,96},{160,128},{192,160},{224,1... | collective-permute-start | bytes 1376264 | tf_op jit(solution)/shard_map/ppermute | solution.py:355
  32.1 17.8 %collective-permute-start.11 = (bf16[256,896]{1,0:T(8,128)(2,1)S(1)}, bf16[256,896]{1,0:T(8,128)(2,1)S(1)}, u32[]{:S(2)}, u32[]{:S(2)}) collective-permute-start(bf16[256,896]{1,0:T(8,128)(2,1)S(1)} %all_gather.3.refs_9_), channel_id=1, source_target_pairs={{0,32},{32,64},{64,96},{96,128},{128,160},{160,192},{192,224},{224... | collective-permute-start | bytes 1376264 | tf_op jit(solution)/shard_map/ppermute | solution.py:354
  40.5 62.5 %copy-start.12 = (bf16[256,896]{1,0:T(8,128)(2,1)}, bf16[256,896]{1,0:T(8,128)(2,1)S(1)}, u32[]{:S(2)}) copy-start(bf16[256,896]{1,0:T(8,128)(2,1)S(1)} %collective-permute-done.5.refs_10_) | copy-start | bytes 1376260
  40.5 17.3 %collective-permute-start.6 = (bf16[256,896]{1,0:T(8,128)(2,1)S(1)}, bf16[256,896]{1,0:T(8,128)(2,1)S(1)}, u32[]{:S(2)}, u32[]{:S(2)}) collective-permute-start(bf16[256,896]{1,0:T(8,128)(2,1)S(1)} %collective-permute-done.5.refs_10_), channel_id=1, source_target_pairs={{0,480},{32,0},{64,32},{96,64},{128,96},{160,128},{192,160},{224,1... | collective-permute-start | bytes 1376264 | tf_op jit(solution)/shard_map/ppermute | solution.py:355
  49.8 55.1 %copy-start.13 = (bf16[256,896]{1,0:T(8,128)(2,1)}, bf16[256,896]{1,0:T(8,128)(2,1)S(1)}, u32[]{:S(2)}) copy-start(bf16[256,896]{1,0:T(8,128)(2,1)S(1)} %collective-permute-done.11.refs_8_) | copy-start | bytes 1376260
  49.8 14.1 %collective-permute-start.12 = (bf16[256,896]{1,0:T(8,128)(2,1)S(1)}, bf16[256,896]{1,0:T(8,128)(2,1)S(1)}, u32[]{:S(2)}, u32[]{:S(2)}) collective-permute-start(bf16[256,896]{1,0:T(8,128)(2,1)S(1)} %collective-permute-done.11.refs_8_), channel_id=1, source_target_pairs={{0,32},{32,64},{64,96},{96,128},{128,160},{160,192},{192,224},{224... | collective-permute-start | bytes 1376264 | tf_op jit(solution)/shard_map/ppermute | solution.py:354
  51.8 53.8 %copy-start = (bf16[2048,512]{1,0:T(8,128)(2,1)}, bf16[2048,512]{1,0:T(8,128)(2,1)S(1)}, u32[]{:S(2)}) copy-start(bf16[2048,512]{1,0:T(8,128)(2,1)S(1)} %collective-permute-done.1.refs_2_) | copy-start | bytes 6291460
  51.9 27.1 %collective-permute-start.2 = (bf16[1024,512]{1,0:T(8,128)(2,1)S(1)}, bf16[1024,512]{1,0:T(8,128)(2,1)S(1)}, u32[]{:S(2)}, u32[]{:S(2)}) collective-permute-start(bf16[1024,512]{1,0:T(8,128)(2,1)S(1)} %slice.24), channel_id=1, source_target_pairs={{0,2},{2,4},{4,6},{6,0},{1,7},{3,1},{5,3},{7,5},{8,10},{10,12},{12... | collective-permute-start | bytes 3145736 | tf_op jit(solution)/shard_map/ppermute | solution.py:338
  53.8 51.8 %collective-permute-start.3 = (bf16[2048,512]{1,0:T(8,128)(2,1)S(1)}, bf16[2048,512]{1,0:T(8,128)(2,1)}, u32[]{:S(2)}, u32[]{:S(2)}) collective-permute-start(bf16[2048,512]{1,0:T(8,128)(2,1)S(1)} %collective-permute-done.1.refs_2_), channel_id=1, source_target_pairs={{0,1},{1,0},{2,3},{3,2},{4,5},{5,4},{6,7},{7,6},{8,9},{9,8},{10,11... | collective-permute-start | bytes 6291464 | tf_op jit(solution)/shard_map/ppermute | solution.py:339
  57.8 47.1 %copy-start.14 = (bf16[256,896]{1,0:T(8,128)(2,1)}, bf16[256,896]{1,0:T(8,128)(2,1)S(1)}, u32[]{:S(2)}) copy-start(bf16[256,896]{1,0:T(8,128)(2,1)S(1)} %collective-permute-done.6.refs_11_) | copy-start | bytes 1376260
  57.8 13.5 %collective-permute-start.7 = (bf16[256,896]{1,0:T(8,128)(2,1)S(1)}, bf16[256,896]{1,0:T(8,128)(2,1)S(1)}, u32[]{:S(2)}, u32[]{:S(2)}) collective-permute-start(bf16[256,896]{1,0:T(8,128)(2,1)S(1)} %collective-permute-done.6.refs_11_), channel_id=1, source_target_pairs={{0,480},{32,0},{64,32},{96,64},{128,96},{160,128},{192,160},{224,1... | collective-permute-start | bytes 1376264 | tf_op jit(solution)/shard_map/ppermute | solution.py:355
  63.9 41.0 %copy-start.15 = (bf16[256,896]{1,0:T(8,128)(2,1)}, bf16[256,896]{1,0:T(8,128)(2,1)S(1)}, u32[]{:S(2)}) copy-start(bf16[256,896]{1,0:T(8,128)(2,1)S(1)} %collective-permute-done.12.refs_7_) | copy-start | bytes 1376260
  63.9 13.1 %collective-permute-start.13 = (bf16[256,896]{1,0:T(8,128)(2,1)S(1)}, bf16[256,896]{1,0:T(8,128)(2,1)S(1)}, u32[]{:S(2)}, u32[]{:S(2)}) collective-permute-start(bf16[256,896]{1,0:T(8,128)(2,1)S(1)} %collective-permute-done.12.refs_7_), channel_id=1, source_target_pairs={{0,32},{32,64},{64,96},{96,128},{128,160},{160,192},{192,224},{224... | collective-permute-start | bytes 1376264 | tf_op jit(solution)/shard_map/ppermute | solution.py:354
  71.3 33.7 %copy-start.16 = (bf16[256,896]{1,0:T(8,128)(2,1)}, bf16[256,896]{1,0:T(8,128)(2,1)S(1)}, u32[]{:S(2)}) copy-start(bf16[256,896]{1,0:T(8,128)(2,1)S(1)} %collective-permute-done.7.refs_12_) | copy-start | bytes 1376260
  71.3 11.8 %collective-permute-start.8 = (bf16[256,896]{1,0:T(8,128)(2,1)S(1)}, bf16[256,896]{1,0:T(8,128)(2,1)S(1)}, u32[]{:S(2)}, u32[]{:S(2)}) collective-permute-start(bf16[256,896]{1,0:T(8,128)(2,1)S(1)} %collective-permute-done.7.refs_12_), channel_id=1, source_target_pairs={{0,480},{32,0},{64,32},{96,64},{128,96},{160,128},{192,160},{224,1... | collective-permute-start | bytes 1376264 | tf_op jit(solution)/shard_map/ppermute | solution.py:355
  77.0 27.9 %copy-start.17 = (bf16[256,896]{1,0:T(8,128)(2,1)}, bf16[256,896]{1,0:T(8,128)(2,1)S(1)}, u32[]{:S(2)}) copy-start(bf16[256,896]{1,0:T(8,128)(2,1)S(1)} %collective-permute-done.13.refs_6_) | copy-start | bytes 1376260
  77.1 12.5 %collective-permute-start.15 = (bf16[256,896]{1,0:T(8,128)(2,1)S(1)}, bf16[256,896]{1,0:T(8,128)(2,1)S(1)}, u32[]{:S(2)}, u32[]{:S(2)}) collective-permute-start(bf16[256,896]{1,0:T(8,128)(2,1)S(1)} %collective-permute-done.13.refs_6_), channel_id=1, source_target_pairs={{0,32},{32,64},{64,96},{96,128},{128,160},{160,192},{192,224},{224... | collective-permute-start | bytes 1376264 | tf_op jit(solution)/shard_map/ppermute | solution.py:354
  79.0 26.6 %copy-start.3 = (bf16[1024,512]{1,0:T(8,128)(2,1)}, bf16[1024,512]{1,0:T(8,128)(2,1)S(1)}, u32[]{:S(2)}) copy-start(bf16[1024,512]{1,0:T(8,128)(2,1)S(1)} %collective-permute-done.2.refs_3_) | copy-start | bytes 3145732
  79.0 26.6 %collective-permute-start.4 = (bf16[1024,512]{1,0:T(8,128)(2,1)S(1)}, bf16[1024,512]{1,0:T(8,128)(2,1)}, u32[]{:S(2)}, u32[]{:S(2)}) collective-permute-start(bf16[1024,512]{1,0:T(8,128)(2,1)S(1)} %collective-permute-done.2.refs_3_), channel_id=1, source_target_pairs={{0,1},{1,0},{2,3},{3,2},{4,5},{5,4},{6,7},{7,6},{8,9},{9,8},{10,11... | collective-permute-start | bytes 3145736 | tf_op jit(solution)/shard_map/ppermute | solution.py:340
  83.2 0.8 copy-start.10
  84.0 13.3 %collective-permute-start.9 = (bf16[256,896]{1,0:T(8,128)(2,1)S(1)}, bf16[256,896]{1,0:T(8,128)(2,1)}, u32[]{:S(2)}, u32[]{:S(2)}) collective-permute-start(bf16[256,896]{1,0:T(8,128)(2,1)S(1)} %collective-permute-done.8.refs_6_), channel_id=1, source_target_pairs={{0,480},{32,0},{64,32},{96,64},{128,96},{160,128},{192,160},{224,1... | collective-permute-start | bytes 1376264 | tf_op jit(solution)/shard_map/ppermute | solution.py:355
  89.6 7.7 %copy-start.11 = (bf16[256,896]{1,0:T(8,128)(2,1)}, bf16[256,896]{1,0:T(8,128)(2,1)S(1)}, u32[]{:S(2)}) copy-start(bf16[256,896]{1,0:T(8,128)(2,1)S(1)} %collective-permute-done.15.refs_15_) | copy-start | bytes 1376260
  89.6 13.4 %collective-permute-start.16 = (bf16[256,896]{1,0:T(8,128)(2,1)S(1)}, bf16[256,896]{1,0:T(8,128)(2,1)}, u32[]{:S(2)}, u32[]{:S(2)}) collective-permute-start(bf16[256,896]{1,0:T(8,128)(2,1)S(1)} %collective-permute-done.15.refs_15_), channel_id=1, source_target_pairs={{0,32},{32,64},{64,96},{96,128},{128,160},{160,192},{192,224},{224... | collective-permute-start | bytes 1376264 | tf_op jit(solution)/shard_map/ppermute | solution.py:354
  97.3 14.7 %collective-permute-start.10 = (bf16[256,896]{1,0:T(8,128)(2,1)}, bf16[256,896]{1,0:T(8,128)(2,1)}, u32[]{:S(2)}, u32[]{:S(2)}) collective-permute-start(bf16[256,896]{1,0:T(8,128)(2,1)} %collective-permute-done.9.refs_7_), channel_id=1, source_target_pairs={{0,480},{32,0},{64,32},{96,64},{128,96},{160,128},{192,160},{224,1... | collective-permute-start | bytes 1376264 | tf_op jit(solution)/shard_map/ppermute | solution.py:355
  103.0 14.1 %collective-permute-start.17 = (bf16[256,896]{1,0:T(8,128)(2,1)}, bf16[256,896]{1,0:T(8,128)(2,1)}, u32[]{:S(2)}, u32[]{:S(2)}) collective-permute-start(bf16[256,896]{1,0:T(8,128)(2,1)} %collective-permute-done.16.refs_14_), channel_id=1, source_target_pairs={{0,32},{32,64},{64,96},{96,128},{128,160},{160,192},{192,224},{224... | collective-permute-start | bytes 1376264 | tf_op jit(solution)/shard_map/ppermute | solution.py:354
  112.0 12.0 %collective-permute-start.14 = (bf16[256,896]{1,0:T(8,128)(2,1)}, bf16[256,896]{1,0:T(8,128)(2,1)S(1)}, u32[]{:S(2)}, u32[]{:S(2)}) collective-permute-start(bf16[256,896]{1,0:T(8,128)(2,1)} %collective-permute-done.10.refs_8_), channel_id=1, source_target_pairs={{0,480},{32,0},{64,32},{96,64},{128,96},{160,128},{192,160},{224,1... | collective-permute-start | bytes 1376264 | tf_op jit(solution)/shard_map/ppermute | solution.py:355
  117.1 12.0 %collective-permute-start.18 = (bf16[256,896]{1,0:T(8,128)(2,1)}, bf16[256,896]{1,0:T(8,128)(2,1)S(1)}, u32[]{:S(2)}, u32[]{:S(2)}) collective-permute-start(bf16[256,896]{1,0:T(8,128)(2,1)} %collective-permute-done.17.refs_13_), channel_id=1, source_target_pairs={{0,32},{32,64},{64,96},{96,128},{128,160},{160,192},{192,224},{224... | collective-permute-start | bytes 1376264 | tf_op jit(solution)/shard_map/ppermute | solution.py:354
  124.0 12.1 %copy-start.7 = (bf16[256,896]{1,0:T(8,128)(2,1)}, bf16[256,896]{1,0:T(8,128)(2,1)S(1)}, u32[]{:S(2)}) copy-start(bf16[256,896]{1,0:T(8,128)(2,1)S(1)} %collective-permute-done.14.refs_9_) | copy-start | bytes 1376260
  124.0 12.1 %collective-permute-start.20 = (bf16[128,896]{1,0:T(8,128)(2,1)S(1)}, bf16[128,896]{1,0:T(8,128)(2,1)S(1)}, u32[]{:S(2)}, u32[]{:S(2)}) collective-permute-start(bf16[128,896]{1,0:T(8,128)(2,1)S(1)} %slice.20), channel_id=1, source_target_pairs={{0,480},{32,0},{64,32},{96,64},{128,96},{160,128},{192,160},{224,1... | collective-permute-start | bytes 688136 | tf_op jit(solution)/shard_map/ppermute | solution.py:355
  129.2 6.9 %copy-start.8 = (bf16[256,896]{1,0:T(8,128)(2,1)}, bf16[256,896]{1,0:T(8,128)(2,1)S(1)}, u32[]{:S(2)}) copy-start(bf16[256,896]{1,0:T(8,128)(2,1)S(1)} %collective-permute-done.18.refs_12_) | copy-start | bytes 1376260
  129.2 9.1 %collective-permute-start.19 = (bf16[128,896]{1,0:T(8,128)(2,1)S(1)}, bf16[128,896]{1,0:T(8,128)(2,1)S(1)}, u32[]{:S(2)}, u32[]{:S(2)}) collective-permute-start(bf16[128,896]{1,0:T(8,128)(2,1)S(1)} %slice.19), channel_id=1, source_target_pairs={{0,32},{32,64},{64,96},{96,128},{128,160},{160,192},{192,224},{224... | collective-permute-start | bytes 688136 | tf_op jit(solution)/shard_map/ppermute | solution.py:354
  136.1 2.2 copy-start.18
  138.3 0.7 copy-start.19
  165.9 9.4 %all-to-all-start.1 = ((f32[8,8,512]{2,1,0:T(8,128)}), f32[8,8,512]{2,1,0:T(8,128)S(1)}, u32[]{:S(2)}, u32[]{:S(2)}) async-start(f32[8,8,512]{2,1,0:T(8,128)} %broadcast_in_dim.9), calls=%async_computation.1 | async-start | bytes 262144 | tf_op jit(solution)/shard_map/all_to_all | solution.py:481
  175.4 0.7 copy-start.9
  179.0 58.6 %copy-start.20 = (f32[3,16,896]{2,1,0:T(8,128)S(1)}, f32[3,16,896]{2,1,0:T(8,128)}, u32[]{:S(2)}) copy-start(f32[3,16,896]{2,1,0:T(8,128)} %param.19) | copy-start | bytes 516100
  179.0 59.3 %copy-start.22 = (f32[3,16,512]{2,1,0:T(8,128)S(1)}, f32[3,16,512]{2,1,0:T(8,128)}, u32[]{:S(2)}) copy-start(f32[3,16,512]{2,1,0:T(8,128)} %param.18) | copy-start | bytes 294916

commit v10 on v9

--- a/solution.py
+++ b/solution.py
@@ -88,14 +88,21 @@
 
     waits = [[columns(0, 0, 0, i)] for i in range(count)]
     sem = count
+    column = plan["column"]
+    piece = rows // len(column)
     for (offset, first), block in zip(plan["blocks"], block_refs, strict=True):
         i = offset - plan["first"]
-        span = pl.ds(i * rows + first, block.shape[0])
-        copies = copy_rows(block, right.at[span, :], sems, sem, 2)
-        sem += 2
-        for copy in copies:
+        for row in range(0, block.shape[0], piece):
+            turn = spot_ref[3] + column[(first + row) // piece] + len(column)
+            to = i * rows + lax.rem(turn, len(column)) * piece
+            copy = pltpu.make_async_copy(
+                block.at[pl.ds(row, piece), :],
+                right.at[pl.ds(pl.multiple_of(to, piece), piece), :],
+                sems.at[sem],
+            )
+            sem += 1
             copy.start()
-        waits[i] += copies
+            waits[i].append(copy)
     return waits
 
 
@@ -303,6 +310,10 @@
         out_ref[t] = value
 
 
+def after(value, *others):
+    return lax.optimization_barrier((value, *others))[0]
+
+
 def ring(size, by):
     return [(i, (i + by) % size) for i in range(size)]
 
@@ -326,20 +337,19 @@
     n_z = sizes["z"]
     n_tensor = sizes["x"] * sizes["c"]
     z_axes, tensor_axes = "z", ("x", "c")
-    spot = jnp.stack([lax.axis_index(axis) for axis in ("z", "x", "c")]).astype(jnp.int32)
-
+    spot = jnp.stack([lax.axis_index(axis) for axis in ("z", "x", "c", "y")]).astype(jnp.int32)
+
+    shard = frozen_down_weight.T
+    n_y = sizes["y"]
+    column = [0, -1, 1, 2]
+    others = [lax.ppermute(shard, "y", ring(n_y, -by)) for by in column[1:]]
+    block = jnp.concatenate([shard, *others], axis=0)
     n_x = sizes["x"]
     swap = [(0, 1), (1, 0)]
     around = [(2 * i, 2 * ((i + 1) % n_x)) for i in range(n_x)]
     around += [(2 * i + 1, 2 * ((i - 1) % n_x) + 1) for i in range(n_x)]
-    own = jnp.concatenate([output_gradient, normed], axis=0)
+    own = jnp.concatenate([after(output_gradient, *others), normed], axis=0)
     partner = lax.ppermute(own, "c", swap)
-    near = lax.ppermute(jnp.concatenate([own, partner], axis=0), tensor_axes, around)
-    across = lax.ppermute(near[: 2 * tokens], tensor_axes, around)
-    beyond = lax.ppermute(near, "c", swap)
-    across_partner = lax.ppermute(across, "c", swap)
-    pieces = (own, partner, near, across, beyond, across_partner)
-    block = lax.all_gather(frozen_down_weight.T, "y", axis=0, tiled=True)
 
     rows = block.shape[0]
     half = rows // 2
@@ -397,6 +407,7 @@
         plan = dict(
             n_z=n_z,
             n_x=n_x,
+            column=column,
             rows=rows,
             first=offsets[0],
             blocks=[(offset, 0) for offset in offsets],
@@ -407,7 +418,7 @@
             out_shape=jax.ShapeDtypeStruct((tokens, hidden), F32),
             in_specs=[smem] + [hbm] * (len(pieces) + n),
             out_specs=hbm,
-            scratch_shapes=[pltpu.VMEM((tokens, hidden), F32)] + scratch(n * rows, 3 * n),
+            scratch_shapes=[pltpu.VMEM((tokens, hidden), F32)] + scratch(n * rows, (1 + n_y) * n),
             compiler_params=params,
             cost_estimate=pl.CostEstimate(
                 flops=2 * tokens * n * rows * hidden,
@@ -417,11 +428,15 @@
             name="part_product",
         )(spot, *pieces, *blocks)
 
-    def after(value, other):
-        return lax.optimization_barrier((value, other))[0]
-
     last = n_z // 2
-    for k in range(1, last - 1):
+    step(1, block, block)
+    pair = jnp.concatenate([own, partner], axis=0)
+    near = lax.ppermute(after(pair, low[1], high[1]), tensor_axes, around)
+    across = lax.ppermute(near[: 2 * tokens], tensor_axes, around)
+    beyond = lax.ppermute(near, "c", swap)
+    across_partner = lax.ppermute(across, "c", swap)
+    pieces = (own, partner, near, across, beyond, across_partner)
+    for k in range(2, last - 1):
         step(k, low[k - 1], high[k - 1])
     split = last - 4
     total = part(list(range(1 - split, split)))
@@ -437,6 +452,7 @@
     plan = dict(
         n_z=n_z,
         n_x=n_x,
+        column=column,
         rows=rows,
         first=split,
         blocks=[(k, 0) for k in ahead] + [(last, 0), (last, half)] + [(k, 0) for k in behind],
@@ -460,7 +476,7 @@
             pltpu.VMEM((tokens, hidden), F32),
             pltpu.VMEM((sequences, 3 * RANK, hidden), F32),
         ]
-        + scratch(n_offsets * rows, n_offsets + 2 * len(blocks) + 12),
+        + scratch(n_offsets * rows, (1 + n_y) * n_offsets + 12),
         compiler_params=params,
         name="hidden_side",
     )(
@@ -503,7 +519,6 @@
         gradient_gram,
     )
 
-    n_y = sizes["y"]
     share = jnp.sum(lax.all_to_all(out.reshape(n_y, -1, 128), "y", 0, 0), axis=0)
     share = jnp.sum(lax.all_to_all(share.reshape(n_z, -1, 128), z_axes, 0, 0), axis=0)
     share = lax.all_to_all(

time: 240 us -> 263 us (1.096)
  waiting for transfers between devices: 34.5 us -> 60.9 us
  blocking collectives: 88.2 us -> 73 us
  starting transfers between devices: 76 us -> 88.1 us
    ppermute x1 -> x4, waiting for transfers between devices: 0.01 us -> 22.3 us  [the longest x1 17.8 us: per_device(): near = lax.ppermute(after(pair, low[1], high[1]), tensor_axes, around)]
    all_gather x1 -> x0, blocking collectives: 13.6 us -> none  [per_device(): block = lax.all_gather(frozen_down_weight.T, 'y', axis=0, tiled=True)]
    ppermute x1 -> x4, starting transfers between devices: 3.39 us -> 13.3 us  [the longest x3 11.1 us: per_device(): others = [lax.ppermute(shard, 'y', ring(n_y, -by)) for by in column[1:]]]
    ppermute x8, waiting for transfers between devices: 4.29 us -> 12.7 us  [step(): low[k] = lax.ppermute(low_from, z_axes, ring(n_z, 1))]
    all_to_all x1, blocking collectives: 16.1 us -> 11.8 us  [per_device(): lax.all_to_all(mids.reshape(n_tensor, 8, tokens), tensor_axes, 0, 0)]
    all_to_all x1, blocking collectives: 21.4 us -> 24.2 us  [per_device(): lax.all_to_all(share.reshape(n_z, -1, 128), z_axes, 0, 0)]
  transfers between devices with their start and end apart: 22 -> 25, of which waited for: 12 -> 13; matrix products, arithmetic and copies ran while one was open for 0% -> 0% of each run, Pallas kernels for 7% -> 6%
where the time goes in v10:
time: 263 us; the launch traced here: 262 us
  starting transfers between devices  88.1 us (33%)
  blocking collectives  73 us (28%)
  waiting for transfers between devices  60.9 us (23%)
  Pallas kernels  29.4 us (11%)
  local copies, waits for them, and re-layouts  6.25 us (2%)
    ppermute x8, starting transfers between devices, step(): high[k] = lax.ppermute(high_from, z_axes, ring(n_z, -1))  46.5 us
    all_to_all x1, blocking collectives, per_device(): lax.all_to_all(share.reshape(n_z, -1, 128), z_axes, 0, 0)  24.2 us
    ppermute x8, waiting for transfers between devices, step(): high[k] = lax.ppermute(high_from, z_axes, ring(n_z, -1))  20.5 us
    ppermute x1, waiting for transfers between devices, per_device(): near = lax.ppermute(after(pair, low[1], high[1]), tensor_axes, around)  17.8 us
    ppermute x8, starting transfers between devices, step(): low[k] = lax.ppermute(low_from, z_axes, ring(n_z, 1))  17.2 us
    all_to_all x1, blocking collectives, per_device(): lax.all_to_all(jnp.broadcast_to(share, (n_z,) + share.shape), z_axes, 0, 0)  17.1 us
    ppermute x8, waiting for transfers between devices, step(): low[k] = lax.ppermute(low_from, z_axes, ring(n_z, 1))  12.7 us
    all_to_all x1, blocking collectives, per_device(): lax.all_to_all(mids.reshape(n_tensor, 8, tokens), tensor_axes, 0, 0)  11.8 us
  transfers between devices with their start and end apart: 25, of which 13 were waited for; matrix products, arithmetic and copies ran while one was open for 0% of the time, Pallas kernels for 6%

profile of v10, /device:TPU:32, one launch (start us, length us, event | category | flops | bytes accessed | tf_op | source)
XLA Modules:
  0.0 261.7 jit_solution(15098884681395206103)
XLA Ops:
  0.6 0.0 copy-start.4
  0.7 0.0 copy-start.5
  0.7 3.6 %collective-permute-start = (bf16[64,896]{1,0:T(8,128)(2,1)}, bf16[64,896]{1,0:T(8,128)(2,1)S(1)}, u32[]{:S(2)}, u32[]{:S(2)}) collective-permute-start(bf16[64,896]{1,0:T(8,128)(2,1)} %bitcast.27), channel_id=1, source_target_pairs={{0,8},{8,16},{16,24},{24,0},{1,9},{9,17},{17,25},{25,1},{2,10},{10... | collective-permute-start | bytes 344072 | tf_op jit(solution)/shard_map/ppermute | solution.py:345
  4.3 3.6 %collective-permute-start.1 = (bf16[64,896]{1,0:T(8,128)(2,1)}, bf16[64,896]{1,0:T(8,128)(2,1)S(1)}, u32[]{:S(2)}, u32[]{:S(2)}) collective-permute-start(bf16[64,896]{1,0:T(8,128)(2,1)} %bitcast.28), channel_id=1, source_target_pairs={{0,24},{8,0},{16,8},{24,16},{1,25},{9,1},{17,9},{25,17},{2,26},{10... | collective-permute-start | bytes 344072 | tf_op jit(solution)/shard_map/ppermute | solution.py:345
  7.9 3.9 %collective-permute-start.2 = (bf16[64,896]{1,0:T(8,128)(2,1)}, bf16[64,896]{1,0:T(8,128)(2,1)S(1)}, u32[]{:S(2)}, u32[]{:S(2)}) collective-permute-start(bf16[64,896]{1,0:T(8,128)(2,1)} %bitcast.29), channel_id=1, source_target_pairs={{0,16},{8,24},{16,0},{24,8},{1,17},{9,25},{17,1},{25,9},{2,18},{10... | collective-permute-start | bytes 344072 | tf_op jit(solution)/shard_map/ppermute | solution.py:345
  11.8 0.0 collective-permute-done
  11.8 4.5 %collective-permute-done.2 = bf16[64,896]{1,0:T(8,128)(2,1)S(1)} collective-permute-done((bf16[64,896]{1,0:T(8,128)(2,1)}, bf16[64,896]{1,0:T(8,128)(2,1)S(1)}, u32[]{:S(2)}, u32[]{:S(2)}) %collective-permute-start.2) | collective-permute-done | bytes 114720 | tf_op jit(solution)/shard_map/ppermute | solution.py:345
  16.3 1.1 constant_dynamic-update-slice_fusion.1
  17.3 1.1 constant_dynamic-update-slice_fusion.refs_0_
  18.4 1.9 collective-permute-start.3
  20.4 3.8 %collective-permute-start.4 = (bf16[256,896]{1,0:T(8,128)(2,1)S(1)}, bf16[256,896]{1,0:T(8,128)(2,1)S(1)}, u32[]{:S(2)}, u32[]{:S(2)}) collective-permute-start(bf16[256,896]{1,0:T(8,128)(2,1)S(1)} %pad_maximum_fusion.1.refs_9_), channel_id=1, source_target_pairs={{0,32},{32,64},{64,96},{96,128},{128,160},{160,192},{192,224},{224... | collective-permute-start | bytes 1376264 | tf_op jit(solution)/shard_map/ppermute | solution.py:364
  24.3 5.5 %collective-permute-start.5 = (bf16[256,896]{1,0:T(8,128)(2,1)S(1)}, bf16[256,896]{1,0:T(8,128)(2,1)S(1)}, u32[]{:S(2)}, u32[]{:S(2)}) collective-permute-start(bf16[256,896]{1,0:T(8,128)(2,1)S(1)} %pad_maximum_fusion.1.refs_9_), channel_id=1, source_target_pairs={{0,480},{32,0},{64,32},{96,64},{128,96},{160,128},{192,160},{224,1... | collective-permute-start | bytes 1376264 | tf_op jit(solution)/shard_map/ppermute | solution.py:365
  29.8 0.0 collective-permute-done.3.refs_1_
  29.8 0.1 pad_maximum_fusion
  30.0 9.0 %collective-permute-done.4.refs_8_ = bf16[256,896]{1,0:T(8,128)(2,1)S(1)} collective-permute-done((bf16[256,896]{1,0:T(8,128)(2,1)S(1)}, bf16[256,896]{1,0:T(8,128)(2,1)S(1)}, u32[]{:S(2)}, u32[]{:S(2)}) %collective-permute-start.4) | collective-permute-done | bytes 458784 | tf_op jit(solution)/shard_map/ppermute | solution.py:364
  39.0 1.2 collective-permute-done.5.refs_10_
  40.2 2.2 collective-permute-start.6
  42.4 7.2 %collective-permute-start.10 = (bf16[256,896]{1,0:T(8,128)(2,1)S(1)}, bf16[256,896]{1,0:T(8,128)(2,1)S(1)}, u32[]{:S(2)}, u32[]{:S(2)}) collective-permute-start(bf16[256,896]{1,0:T(8,128)(2,1)S(1)} %collective-permute-done.5.refs_10_), channel_id=1, source_target_pairs={{0,480},{32,0},{64,32},{96,64},{128,96},{160,128},{192,160},{224,1... | collective-permute-start | bytes 1376264 | tf_op jit(solution)/shard_map/ppermute | solution.py:365
  49.6 1.9 collective-permute-start.15
  51.5 17.8 %collective-permute-done.6.refs_2_ = bf16[2048,512]{1,0:T(8,128)(2,1)S(1)} collective-permute-done((bf16[2048,512]{1,0:T(8,128)(2,1)S(1)}, bf16[2048,512]{1,0:T(8,128)(2,1)S(1)}, u32[]{:S(2)}, u32[]{:S(2)}) %collective-permute-start.6) | collective-permute-done | bytes 2097184 | tf_op jit(solution)/shard_map/ppermute | solution.py:434
  69.3 0.1 slice.24
  69.4 1.9 collective-permute-start.7
  71.3 1.9 collective-permute-start.8
  73.3 7.0 %collective-permute-start.11 = (bf16[256,896]{1,0:T(8,128)(2,1)S(1)}, bf16[256,896]{1,0:T(8,128)(2,1)S(1)}, u32[]{:S(2)}, u32[]{:S(2)}) collective-permute-start(bf16[256,896]{1,0:T(8,128)(2,1)S(1)} %collective-permute-done.10.refs_11_), channel_id=1, source_target_pairs={{0,480},{32,0},{64,32},{96,64},{128,96},{160,128},{192,160},{224,1... | collective-permute-start | bytes 1376264 | tf_op jit(solution)/shard_map/ppermute | solution.py:365
  80.4 1.9 collective-permute-start.16
  82.3 8.0 %collective-permute-done.11.refs_12_ = bf16[256,896]{1,0:T(8,128)(2,1)S(1)} collective-permute-done((bf16[256,896]{1,0:T(8,128)(2,1)S(1)}, bf16[256,896]{1,0:T(8,128)(2,1)S(1)}, u32[]{:S(2)}, u32[]{:S(2)}) %collective-permute-start.11) | collective-permute-done | bytes 458784 | tf_op jit(solution)/shard_map/ppermute | solution.py:365
  90.3 5.6 %collective-permute-start.12 = (bf16[256,896]{1,0:T(8,128)(2,1)S(1)}, bf16[256,896]{1,0:T(8,128)(2,1)S(1)}, u32[]{:S(2)}, u32[]{:S(2)}) collective-permute-start(bf16[256,896]{1,0:T(8,128)(2,1)S(1)} %collective-permute-done.11.refs_12_), channel_id=1, source_target_pairs={{0,480},{32,0},{64,32},{96,64},{128,96},{160,128},{192,160},{224,1... | collective-permute-start | bytes 1376264 | tf_op jit(solution)/shard_map/ppermute | solution.py:365
  95.9 0.5 collective-permute-done.16.refs_6_
  96.4 1.9 collective-permute-start.18
  98.3 1.9 collective-permute-start.9
  100.2 4.7 %collective-permute-done.12.refs_6_ = bf16[256,896]{1,0:T(8,128)(2,1)S(1)} collective-permute-done((bf16[256,896]{1,0:T(8,128)(2,1)S(1)}, bf16[256,896]{1,0:T(8,128)(2,1)S(1)}, u32[]{:S(2)}, u32[]{:S(2)}) %collective-permute-start.12) | collective-permute-done | bytes 458784 | tf_op jit(solution)/shard_map/ppermute | solution.py:365
  105.0 0.8 copy-done.10
  105.8 5.6 %collective-permute-start.13 = (bf16[256,896]{1,0:T(8,128)(2,1)S(1)}, bf16[256,896]{1,0:T(8,128)(2,1)}, u32[]{:S(2)}, u32[]{:S(2)}) collective-permute-start(bf16[256,896]{1,0:T(8,128)(2,1)S(1)} %collective-permute-done.12.refs_6_), channel_id=1, source_target_pairs={{0,480},{32,0},{64,32},{96,64},{128,96},{160,128},{192,160},{224,1... | collective-permute-start | bytes 1376264 | tf_op jit(solution)/shard_map/ppermute | solution.py:365
  111.4 1.9 collective-permute-start.19
  113.3 6.2 %collective-permute-done.13.refs_7_ = bf16[256,896]{1,0:T(8,128)(2,1)} collective-permute-done((bf16[256,896]{1,0:T(8,128)(2,1)S(1)}, bf16[256,896]{1,0:T(8,128)(2,1)}, u32[]{:S(2)}, u32[]{:S(2)}) %collective-permute-start.13) | collective-permute-done | bytes 458784 | tf_op jit(solution)/shard_map/ppermute | solution.py:365
  119.5 5.6 %collective-permute-start.14 = (bf16[256,896]{1,0:T(8,128)(2,1)}, bf16[256,896]{1,0:T(8,128)(2,1)}, u32[]{:S(2)}, u32[]{:S(2)}) collective-permute-start(bf16[256,896]{1,0:T(8,128)(2,1)} %collective-permute-done.13.refs_7_), channel_id=1, source_target_pairs={{0,480},{32,0},{64,32},{96,64},{128,96},{160,128},{192,160},{224,1... | collective-permute-start | bytes 1376264 | tf_op jit(solution)/shard_map/ppermute | solution.py:365
  125.1 0.6 collective-permute-done.19.refs_14_
  125.7 1.9 collective-permute-start.20
  127.7 0.6 pad_add_fusion.spot_ref
  128.3 1.0 copy-done.3
  129.3 6.4 %part_product.1.refs_16_ = f32[512,896]{1,0:T(8,128)} custom-call(s32[4]{0:T(128)} %pad_add_fusion.spot_ref, bf16[1024,512]{1,0:T(8,128)(2,1)} %copy-done.2, bf16[1024,512]{1,0:T(8,128)(2,1)} %copy-done.1, bf16[2048,512]{1,0:T(8,128)(2,1)} %copy-done, bf16[1024,512]{1,0:T(8,128)(2,1)} %collective-permute-done.7.refs_3_, ...), custom_call_target="tpu_custom_call" | custom-call | flops 1644167168 | bytes 6291456 | tf_op jit(solution)/shard_map/part_product/pallas_call | solution.py:416
  135.8 5.1 %collective-permute-start.17 = (bf16[256,896]{1,0:T(8,128)(2,1)}, bf16[256,896]{1,0:T(8,128)(2,1)S(1)}, u32[]{:S(2)}, u32[]{:S(2)}) collective-permute-start(bf16[256,896]{1,0:T(8,128)(2,1)} %collective-permute-done.14.refs_8_), channel_id=1, source_target_pairs={{0,480},{32,0},{64,32},{96,64},{128,96},{160,128},{192,160},{224,1... | collective-permute-start | bytes 1376264 | tf_op jit(solution)/shard_map/ppermute | solution.py:365
  140.9 1.9 collective-permute-start.21
  142.8 4.9 %gradient_side.1 = (bf16[16,512]{1,0:T(8,128)(2,1)}, bf16[512,16]{1,0:T(8,128)(2,1)}, f32[4,128,128]{2,1,0:T(8,128)}) custom-call(s32[4]{0:T(128)} %pad_add_fusion.spot_ref, bf16[1024,512]{1,0:T(8,128)(2,1)} %copy-done.2, bf16[1024,512]{1,0:T(8,128)(2,1)} %copy-done.1, bf16[2048,512]{1,0:T(8,128)(2,1)} %copy-done, ...), custom_call_target="tpu_custom_call" | custom-call | flops 603979776 | bytes 5242880 | tf_op jit(solution)/shard_map/gradient_side/pallas_call | solution.py:369
  147.7 0.4 collective-permute-done.17.refs_9_
  148.2 4.9 %collective-permute-start.23 = (bf16[128,896]{1,0:T(8,128)(2,1)S(1)}, bf16[128,896]{1,0:T(8,128)(2,1)S(1)}, u32[]{:S(2)}, u32[]{:S(2)}) collective-permute-start(bf16[128,896]{1,0:T(8,128)(2,1)S(1)} %slice.20), channel_id=1, source_target_pairs={{0,480},{32,0},{64,32},{96,64},{128,96},{160,128},{192,160},{224,1... | collective-permute-start | bytes 688136 | tf_op jit(solution)/shard_map/ppermute | solution.py:365
  153.1 0.3 collective-permute-done.21.refs_12_
  153.4 1.9 collective-permute-start.22
  155.4 5.0 %normed_side.1 = (bf16[32,512]{1,0:T(8,128)(2,1)}, bf16[512,32]{1,0:T(8,128)(2,1)}, f32[4,128,128]{2,1,0:T(8,128)}) custom-call(s32[4]{0:T(128)} %pad_add_fusion.spot_ref, bf16[1024,512]{1,0:T(8,128)(2,1)} %copy-done.2, bf16[1024,512]{1,0:T(8,128)(2,1)} %copy-done.1, bf16[2048,512]{1,0:T(8,128)(2,1)} %copy-done, ...), custom_call_target="tpu_custom_call" | custom-call | flops 671088640 | bytes 5242880 | tf_op jit(solution)/shard_map/normed_side/pallas_call | solution.py:369
  160.4 2.2 collective-permute-done.22.refs_10_
  162.6 0.7 copy-done.19
  163.3 10.2 %hidden_side.1 = (f32[4,48,896]{2,1,0:T(8,128)}, f32[64,512]{1,0:T(8,128)}) custom-call(s32[4]{0:T(128)} %pad_add_fusion.spot_ref, bf16[1024,512]{1,0:T(8,128)(2,1)} %copy-done.2, bf16[1024,512]{1,0:T(8,128)(2,1)} %copy-done.1, bf16[2048,512]{1,0:T(8,128)(2,1)} %copy-done, bf16[1024,512]{1,0:T(8,128)(2,1)} %collective-permute-done.7.refs_3_, ...), custom_call_target="tpu_custom_call" | custom-call | tf_op jit(solution)/shard_map/hidden_side/pallas_call | solution.py:462
  173.5 11.8 %all_to_all.30 = f32[8,8,512]{2,1,0:T(8,128)S(1)} all-to-all(f32[8,8,512]{2,1,0:T(8,128)} %bitcast.26), channel_id=1, replica_groups=mesh['z'=16,'y'=4,'x'=4,'c'=2] {'x','c'}, dimensions={0} | all-to-all | bytes 262144 | tf_op jit(solution)/shard_map/all_to_all | solution.py:495
  185.4 0.7 broadcast_in_dim.9
  186.0 3.4 %all-to-all-start.1 = ((f32[8,8,512]{2,1,0:T(8,128)}), f32[8,8,512]{2,1,0:T(8,128)S(1)}, u32[]{:S(2)}, u32[]{:S(2)}) async-start(f32[8,8,512]{2,1,0:T(8,128)} %broadcast_in_dim.9), calls=%async_computation.1 | async-start | bytes 262144 | tf_op jit(solution)/shard_map/all_to_all | solution.py:497
  190.1 5.4 %all-to-all-done.1 = f32[8,8,512]{2,1,0:T(8,128)S(1)} async-done(((f32[8,8,512]{2,1,0:T(8,128)}), f32[8,8,512]{2,1,0:T(8,128)S(1)}, u32[]{:S(2)}, u32[]{:S(2)}) %all-to-all-start.1) | async-done | bytes 131104 | tf_op jit(solution)/shard_map/all_to_all | solution.py:497
  195.5 0.7 copy-done.9
  196.1 3.0 %clip_side.1 = f32[72,8,128]{2,1,0:T(8,128)} custom-call(f32[1]{0:T(128)} %copy.13.clip_ref, f32[64,512]{1,0:T(8,128)} %bitcast.25, f32[4,48,896]{2,1,0:T(8,128)} %get-tuple-element.25.sums_ref, bf16[512,512]{1,0:T(8,128)(2,1)} %normed_ref.1, bf16[512,512]{1,0:T(8,128)(2,1)} %gradient_ref.1, f32[4,128,128]{2,1,0:T(8,128)} %get-tuple-element.26.normed_gram_ref, ...), custom_call_target="tpu_custom_call" | custom-call | tf_op jit(solution)/shard_map/clip_side/pallas_call | solution.py:504
  199.1 10.7 %all_to_all.31 = f32[4,144,128]{2,1,0:T(8,128)S(1)} all-to-all(f32[4,144,128]{2,1,0:T(8,128)} %bitcast.21), channel_id=1, replica_groups=mesh['z'=16,'y'=4,'x'=4,'c'=2] {'y'}, dimensions={0} | all-to-all | bytes 589824 | tf_op jit(solution)/shard_map/all_to_all | solution.py:522
  209.8 24.2 %all_to_all.32 = f32[16,9,128]{2,1,0:T(8,128)S(1)} all-to-all(f32[16,9,128]{2,1,0:T(8,128)S(1)} %reshape.40), channel_id=1, replica_groups=mesh['z'=16,'y'=4,'x'=4,'c'=2] {'z'}, dimensions={0} | all-to-all | bytes 147456 | tf_op jit(solution)/shard_map/all_to_all | solution.py:523
  234.0 17.1 %all_to_all.33 = f32[16,9,128]{2,1,0:T(8,128)S(1)} all-to-all(f32[16,9,128]{2,1,0:T(8,128)S(1)} %broadcast_in_dim.10), channel_id=1, replica_groups=mesh['z'=16,'y'=4,'x'=4,'c'=2] {'z'}, dimensions={0} | all-to-all | bytes 147456 | tf_op jit(solution)/shard_map/all_to_all | solution.py:524
  251.1 9.2 %all_to_all.34 = f32[4,144,128]{2,1,0:T(8,128)S(1)} all-to-all(f32[4,144,128]{2,1,0:T(8,128)S(1)} %broadcast_in_dim.11), channel_id=1, replica_groups=mesh['z'=16,'y'=4,'x'=4,'c'=2] {'y'}, dimensions={0} | all-to-all | bytes 589824 | tf_op jit(solution)/shard_map/all_to_all | solution.py:527
  260.4 0.7 fusion
  261.1 0.7 fusion.1
  (61 shorter events, 0.3 us)
Async XLA Ops:
  0.6 19.7 %copy-start.21 = (bf16[896,64]{0,1:T(8,128)(2,1)S(1)}, bf16[896,64]{0,1:T(8,128)(2,1)}, u32[]{:S(2)}) copy-start(bf16[896,64]{0,1:T(8,128)(2,1)} %param.14) | copy-start | bytes 344068
  0.6 29.1 %copy-start.4 = (bf16[512,512]{1,0:T(8,128)(2,1)S(1)}, bf16[512,512]{1,0:T(8,128)(2,1)}, u32[]{:S(2)}) copy-start(bf16[512,512]{1,0:T(8,128)(2,1)} %gradient_ref.1) | copy-start | bytes 1572868
  0.7 29.1 %copy-start.5 = (bf16[512,512]{1,0:T(8,128)(2,1)S(1)}, bf16[512,512]{1,0:T(8,128)(2,1)}, u32[]{:S(2)}) copy-start(bf16[512,512]{1,0:T(8,128)(2,1)} %normed_ref.1) | copy-start | bytes 1572868
  0.7 11.1 %collective-permute-start = (bf16[64,896]{1,0:T(8,128)(2,1)}, bf16[64,896]{1,0:T(8,128)(2,1)S(1)}, u32[]{:S(2)}, u32[]{:S(2)}) collective-permute-start(bf16[64,896]{1,0:T(8,128)(2,1)} %bitcast.27), channel_id=1, source_target_pairs={{0,8},{8,16},{16,24},{24,0},{1,9},{9,17},{17,25},{25,1},{2,10},{10... | collective-permute-start | bytes 344072 | tf_op jit(solution)/shard_map/ppermute | solution.py:345
  4.3 7.5 %collective-permute-start.1 = (bf16[64,896]{1,0:T(8,128)(2,1)}, bf16[64,896]{1,0:T(8,128)(2,1)S(1)}, u32[]{:S(2)}, u32[]{:S(2)}) collective-permute-start(bf16[64,896]{1,0:T(8,128)(2,1)} %bitcast.28), channel_id=1, source_target_pairs={{0,24},{8,0},{16,8},{24,16},{1,25},{9,1},{17,9},{25,17},{2,26},{10... | collective-permute-start | bytes 344072 | tf_op jit(solution)/shard_map/ppermute | solution.py:345
  7.9 8.4 %collective-permute-start.2 = (bf16[64,896]{1,0:T(8,128)(2,1)}, bf16[64,896]{1,0:T(8,128)(2,1)S(1)}, u32[]{:S(2)}, u32[]{:S(2)}) collective-permute-start(bf16[64,896]{1,0:T(8,128)(2,1)} %bitcast.29), channel_id=1, source_target_pairs={{0,16},{8,24},{16,0},{24,8},{1,17},{9,25},{17,1},{25,9},{2,18},{10... | collective-permute-start | bytes 344072 | tf_op jit(solution)/shard_map/ppermute | solution.py:345
  18.4 5.8 %copy-start.2 = (bf16[1024,512]{1,0:T(8,128)(2,1)}, bf16[1024,512]{1,0:T(8,128)(2,1)S(1)}, u32[]{:S(2)}) copy-start(bf16[1024,512]{1,0:T(8,128)(2,1)S(1)} %constant_dynamic-update-slice_fusion.refs_0_) | copy-start | bytes 3145732
  18.4 11.3 %collective-permute-start.3 = (bf16[1024,512]{1,0:T(8,128)(2,1)S(1)}, bf16[1024,512]{1,0:T(8,128)(2,1)S(1)}, u32[]{:S(2)}, u32[]{:S(2)}) collective-permute-start(bf16[1024,512]{1,0:T(8,128)(2,1)S(1)} %constant_dynamic-update-slice_fusion.refs_0_), channel_id=1, source_target_pairs={{0,1},{1,0},{2,3},{3,2},{4,5},{5,4},{6,7},{7,6},{8,9},{9,8},{10,11... | collective-permute-start | bytes 3145736 | tf_op jit(solution)/shard_map/ppermute | solution.py:352
  20.4 49.0 %copy-start.6 = (bf16[256,896]{1,0:T(8,128)(2,1)}, bf16[256,896]{1,0:T(8,128)(2,1)S(1)}, u32[]{:S(2)}) copy-start(bf16[256,896]{1,0:T(8,128)(2,1)S(1)} %pad_maximum_fusion.1.refs_9_) | copy-start | bytes 1376260
  20.4 18.6 %collective-permute-start.4 = (bf16[256,896]{1,0:T(8,128)(2,1)S(1)}, bf16[256,896]{1,0:T(8,128)(2,1)S(1)}, u32[]{:S(2)}, u32[]{:S(2)}) collective-permute-start(bf16[256,896]{1,0:T(8,128)(2,1)S(1)} %pad_maximum_fusion.1.refs_9_), channel_id=1, source_target_pairs={{0,32},{32,64},{64,96},{96,128},{128,160},{160,192},{192,224},{224... | collective-permute-start | bytes 1376264 | tf_op jit(solution)/shard_map/ppermute | solution.py:364
  24.3 15.9 %collective-permute-start.5 = (bf16[256,896]{1,0:T(8,128)(2,1)S(1)}, bf16[256,896]{1,0:T(8,128)(2,1)S(1)}, u32[]{:S(2)}, u32[]{:S(2)}) collective-permute-start(bf16[256,896]{1,0:T(8,128)(2,1)S(1)} %pad_maximum_fusion.1.refs_9_), channel_id=1, source_target_pairs={{0,480},{32,0},{64,32},{96,64},{128,96},{160,128},{192,160},{224,1... | collective-permute-start | bytes 1376264 | tf_op jit(solution)/shard_map/ppermute | solution.py:365
  29.8 39.6 %copy-start.1 = (bf16[1024,512]{1,0:T(8,128)(2,1)}, bf16[1024,512]{1,0:T(8,128)(2,1)S(1)}, u32[]{:S(2)}) copy-start(bf16[1024,512]{1,0:T(8,128)(2,1)S(1)} %collective-permute-done.3.refs_1_) | copy-start | bytes 3145732
  39.0 86.7 %copy-start.12 = (bf16[256,896]{1,0:T(8,128)(2,1)}, bf16[256,896]{1,0:T(8,128)(2,1)S(1)}, u32[]{:S(2)}) copy-start(bf16[256,896]{1,0:T(8,128)(2,1)S(1)} %collective-permute-done.4.refs_8_) | copy-start | bytes 1376260
  40.2 87.5 %copy-start.13 = (bf16[256,896]{1,0:T(8,128)(2,1)}, bf16[256,896]{1,0:T(8,128)(2,1)S(1)}, u32[]{:S(2)}) copy-start(bf16[256,896]{1,0:T(8,128)(2,1)S(1)} %collective-permute-done.5.refs_10_) | copy-start | bytes 1376260
  40.2 29.1 %collective-permute-start.6 = (bf16[2048,512]{1,0:T(8,128)(2,1)S(1)}, bf16[2048,512]{1,0:T(8,128)(2,1)S(1)}, u32[]{:S(2)}, u32[]{:S(2)}) collective-permute-start(bf16[2048,512]{1,0:T(8,128)(2,1)S(1)} %pad_maximum_fusion), channel_id=1, source_target_pairs={{0,2},{2,4},{4,6},{6,0},{1,7},{3,1},{5,3},{7,5},{8,10},{10,12},{12... | collective-permute-start | bytes 6291464 | tf_op jit(solution)/shard_map/ppermute | solution.py:434
  42.4 30.9 %collective-permute-start.10 = (bf16[256,896]{1,0:T(8,128)(2,1)S(1)}, bf16[256,896]{1,0:T(8,128)(2,1)S(1)}, u32[]{:S(2)}, u32[]{:S(2)}) collective-permute-start(bf16[256,896]{1,0:T(8,128)(2,1)S(1)} %collective-permute-done.5.refs_10_), channel_id=1, source_target_pairs={{0,480},{32,0},{64,32},{96,64},{128,96},{160,128},{192,160},{224,1... | collective-permute-start | bytes 1376264 | tf_op jit(solution)/shard_map/ppermute | solution.py:365
  49.6 30.7 %collective-permute-start.15 = (bf16[256,896]{1,0:T(8,128)(2,1)S(1)}, bf16[256,896]{1,0:T(8,128)(2,1)S(1)}, u32[]{:S(2)}, u32[]{:S(2)}) collective-permute-start(bf16[256,896]{1,0:T(8,128)(2,1)S(1)} %collective-permute-done.4.refs_8_), channel_id=1, source_target_pairs={{0,32},{32,64},{64,96},{96,128},{128,160},{160,192},{192,224},{224... | collective-permute-start | bytes 1376264 | tf_op jit(solution)/shard_map/ppermute | solution.py:364
  69.3 59.0 %copy-start = (bf16[2048,512]{1,0:T(8,128)(2,1)}, bf16[2048,512]{1,0:T(8,128)(2,1)S(1)}, u32[]{:S(2)}) copy-start(bf16[2048,512]{1,0:T(8,128)(2,1)S(1)} %collective-permute-done.6.refs_2_) | copy-start | bytes 6291460
  69.4 28.9 %collective-permute-start.7 = (bf16[1024,512]{1,0:T(8,128)(2,1)S(1)}, bf16[1024,512]{1,0:T(8,128)(2,1)}, u32[]{:S(2)}, u32[]{:S(2)}) collective-permute-start(bf16[1024,512]{1,0:T(8,128)(2,1)S(1)} %slice.24), channel_id=1, source_target_pairs={{0,2},{2,4},{4,6},{6,0},{1,7},{3,1},{5,3},{7,5},{8,10},{10,12},{12... | collective-permute-start | bytes 3145736 | tf_op jit(solution)/shard_map/ppermute | solution.py:435
  71.3 57.0 %collective-permute-start.8 = (bf16[2048,512]{1,0:T(8,128)(2,1)S(1)}, bf16[2048,512]{1,0:T(8,128)(2,1)}, u32[]{:S(2)}, u32[]{:S(2)}) collective-permute-start(bf16[2048,512]{1,0:T(8,128)(2,1)S(1)} %collective-permute-done.6.refs_2_), channel_id=1, source_target_pairs={{0,1},{1,0},{2,3},{3,2},{4,5},{5,4},{6,7},{7,6},{8,9},{9,8},{10,11... | collective-permute-start | bytes 6291464 | tf_op jit(solution)/shard_map/ppermute | solution.py:436
  73.3 54.4 %copy-start.14 = (bf16[256,896]{1,0:T(8,128)(2,1)}, bf16[256,896]{1,0:T(8,128)(2,1)S(1)}, u32[]{:S(2)}) copy-start(bf16[256,896]{1,0:T(8,128)(2,1)S(1)} %collective-permute-done.10.refs_11_) | copy-start | bytes 1376260
  73.3 17.0 %collective-permute-start.11 = (bf16[256,896]{1,0:T(8,128)(2,1)S(1)}, bf16[256,896]{1,0:T(8,128)(2,1)S(1)}, u32[]{:S(2)}, u32[]{:S(2)}) collective-permute-start(bf16[256,896]{1,0:T(8,128)(2,1)S(1)} %collective-permute-done.10.refs_11_), channel_id=1, source_target_pairs={{0,480},{32,0},{64,32},{96,64},{128,96},{160,128},{192,160},{224,1... | collective-permute-start | bytes 1376264 | tf_op jit(solution)/shard_map/ppermute | solution.py:365
  80.4 47.3 %copy-start.15 = (bf16[256,896]{1,0:T(8,128)(2,1)}, bf16[256,896]{1,0:T(8,128)(2,1)S(1)}, u32[]{:S(2)}) copy-start(bf16[256,896]{1,0:T(8,128)(2,1)S(1)} %collective-permute-done.15.refs_7_) | copy-start | bytes 1376260
  80.4 16.0 %collective-permute-start.16 = (bf16[256,896]{1,0:T(8,128)(2,1)S(1)}, bf16[256,896]{1,0:T(8,128)(2,1)S(1)}, u32[]{:S(2)}, u32[]{:S(2)}) collective-permute-start(bf16[256,896]{1,0:T(8,128)(2,1)S(1)} %collective-permute-done.15.refs_7_), channel_id=1, source_target_pairs={{0,32},{32,64},{64,96},{96,128},{128,160},{160,192},{192,224},{224... | collective-permute-start | bytes 1376264 | tf_op jit(solution)/shard_map/ppermute | solution.py:364
  90.3 37.4 %copy-start.16 = (bf16[256,896]{1,0:T(8,128)(2,1)}, bf16[256,896]{1,0:T(8,128)(2,1)S(1)}, u32[]{:S(2)}) copy-start(bf16[256,896]{1,0:T(8,128)(2,1)S(1)} %collective-permute-done.11.refs_12_) | copy-start | bytes 1376260
  90.3 14.7 %collective-permute-start.12 = (bf16[256,896]{1,0:T(8,128)(2,1)S(1)}, bf16[256,896]{1,0:T(8,128)(2,1)S(1)}, u32[]{:S(2)}, u32[]{:S(2)}) collective-permute-start(bf16[256,896]{1,0:T(8,128)(2,1)S(1)} %collective-permute-done.11.refs_12_), channel_id=1, source_target_pairs={{0,480},{32,0},{64,32},{96,64},{128,96},{160,128},{192,160},{224,1... | collective-permute-start | bytes 1376264 | tf_op jit(solution)/shard_map/ppermute | solution.py:365
  96.4 31.3 %copy-start.17 = (bf16[256,896]{1,0:T(8,128)(2,1)}, bf16[256,896]{1,0:T(8,128)(2,1)S(1)}, u32[]{:S(2)}) copy-start(bf16[256,896]{1,0:T(8,128)(2,1)S(1)} %collective-permute-done.16.refs_6_) | copy-start | bytes 1376260
  96.4 15.0 %collective-permute-start.18 = (bf16[256,896]{1,0:T(8,128)(2,1)S(1)}, bf16[256,896]{1,0:T(8,128)(2,1)S(1)}, u32[]{:S(2)}, u32[]{:S(2)}) collective-permute-start(bf16[256,896]{1,0:T(8,128)(2,1)S(1)} %collective-permute-done.16.refs_6_), channel_id=1, source_target_pairs={{0,32},{32,64},{64,96},{96,128},{128,160},{160,192},{192,224},{224... | collective-permute-start | bytes 1376264 | tf_op jit(solution)/shard_map/ppermute | solution.py:364
  98.3 30.0 %collective-permute-start.9 = (bf16[1024,512]{1,0:T(8,128)(2,1)}, bf16[1024,512]{1,0:T(8,128)(2,1)S(1)}, u32[]{:S(2)}, u32[]{:S(2)}) collective-permute-start(bf16[1024,512]{1,0:T(8,128)(2,1)} %collective-permute-done.7.refs_3_), channel_id=1, source_target_pairs={{0,1},{1,0},{2,3},{3,2},{4,5},{5,4},{6,7},{7,6},{8,9},{9,8},{10,11... | collective-permute-start | bytes 3145736 | tf_op jit(solution)/shard_map/ppermute | solution.py:437
  105.0 0.8 copy-start.10
  105.8 13.8 %collective-permute-start.13 = (bf16[256,896]{1,0:T(8,128)(2,1)S(1)}, bf16[256,896]{1,0:T(8,128)(2,1)}, u32[]{:S(2)}, u32[]{:S(2)}) collective-permute-start(bf16[256,896]{1,0:T(8,128)(2,1)S(1)} %collective-permute-done.12.refs_6_), channel_id=1, source_target_pairs={{0,480},{32,0},{64,32},{96,64},{128,96},{160,128},{192,160},{224,1... | collective-permute-start | bytes 1376264 | tf_op jit(solution)/shard_map/ppermute | solution.py:365
  111.4 8.2 %copy-start.11 = (bf16[256,896]{1,0:T(8,128)(2,1)}, bf16[256,896]{1,0:T(8,128)(2,1)S(1)}, u32[]{:S(2)}) copy-start(bf16[256,896]{1,0:T(8,128)(2,1)S(1)} %collective-permute-done.18.refs_15_) | copy-start | bytes 1376260
  111.4 14.3 %collective-permute-start.19 = (bf16[256,896]{1,0:T(8,128)(2,1)S(1)}, bf16[256,896]{1,0:T(8,128)(2,1)}, u32[]{:S(2)}, u32[]{:S(2)}) collective-permute-start(bf16[256,896]{1,0:T(8,128)(2,1)S(1)} %collective-permute-done.18.refs_15_), channel_id=1, source_target_pairs={{0,32},{32,64},{64,96},{96,128},{128,160},{160,192},{192,224},{224... | collective-permute-start | bytes 1376264 | tf_op jit(solution)/shard_map/ppermute | solution.py:364
  119.5 16.2 %collective-permute-start.14 = (bf16[256,896]{1,0:T(8,128)(2,1)}, bf16[256,896]{1,0:T(8,128)(2,1)}, u32[]{:S(2)}, u32[]{:S(2)}) collective-permute-start(bf16[256,896]{1,0:T(8,128)(2,1)} %collective-permute-done.13.refs_7_), channel_id=1, source_target_pairs={{0,480},{32,0},{64,32},{96,64},{128,96},{160,128},{192,160},{224,1... | collective-permute-start | bytes 1376264 | tf_op jit(solution)/shard_map/ppermute | solution.py:365
  125.7 15.2 %collective-permute-start.20 = (bf16[256,896]{1,0:T(8,128)(2,1)}, bf16[256,896]{1,0:T(8,128)(2,1)}, u32[]{:S(2)}, u32[]{:S(2)}) collective-permute-start(bf16[256,896]{1,0:T(8,128)(2,1)} %collective-permute-done.19.refs_14_), channel_id=1, source_target_pairs={{0,32},{32,64},{64,96},{96,128},{128,160},{160,192},{192,224},{224... | collective-permute-start | bytes 1376264 | tf_op jit(solution)/shard_map/ppermute | solution.py:364
  128.3 1.0 copy-start.3
  135.8 12.4 %collective-permute-start.17 = (bf16[256,896]{1,0:T(8,128)(2,1)}, bf16[256,896]{1,0:T(8,128)(2,1)S(1)}, u32[]{:S(2)}, u32[]{:S(2)}) collective-permute-start(bf16[256,896]{1,0:T(8,128)(2,1)} %collective-permute-done.14.refs_8_), channel_id=1, source_target_pairs={{0,480},{32,0},{64,32},{96,64},{128,96},{160,128},{192,160},{224,1... | collective-permute-start | bytes 1376264 | tf_op jit(solution)/shard_map/ppermute | solution.py:365
  140.9 12.5 %collective-permute-start.21 = (bf16[256,896]{1,0:T(8,128)(2,1)}, bf16[256,896]{1,0:T(8,128)(2,1)S(1)}, u32[]{:S(2)}, u32[]{:S(2)}) collective-permute-start(bf16[256,896]{1,0:T(8,128)(2,1)} %collective-permute-done.20.refs_13_), channel_id=1, source_target_pairs={{0,32},{32,64},{64,96},{96,128},{128,160},{160,192},{192,224},{224... | collective-permute-start | bytes 1376264 | tf_op jit(solution)/shard_map/ppermute | solution.py:364
  148.2 12.2 %copy-start.7 = (bf16[256,896]{1,0:T(8,128)(2,1)}, bf16[256,896]{1,0:T(8,128)(2,1)S(1)}, u32[]{:S(2)}) copy-start(bf16[256,896]{1,0:T(8,128)(2,1)S(1)} %collective-permute-done.17.refs_9_) | copy-start | bytes 1376260
  148.2 12.1 %collective-permute-start.23 = (bf16[128,896]{1,0:T(8,128)(2,1)S(1)}, bf16[128,896]{1,0:T(8,128)(2,1)S(1)}, u32[]{:S(2)}, u32[]{:S(2)}) collective-permute-start(bf16[128,896]{1,0:T(8,128)(2,1)S(1)} %slice.20), channel_id=1, source_target_pairs={{0,480},{32,0},{64,32},{96,64},{128,96},{160,128},{192,160},{224,1... | collective-permute-start | bytes 688136 | tf_op jit(solution)/shard_map/ppermute | solution.py:365
  153.4 6.9 %copy-start.8 = (bf16[256,896]{1,0:T(8,128)(2,1)}, bf16[256,896]{1,0:T(8,128)(2,1)S(1)}, u32[]{:S(2)}) copy-start(bf16[256,896]{1,0:T(8,128)(2,1)S(1)} %collective-permute-done.21.refs_12_) | copy-start | bytes 1376260
  153.4 9.2 %collective-permute-start.22 = (bf16[128,896]{1,0:T(8,128)(2,1)S(1)}, bf16[128,896]{1,0:T(8,128)(2,1)S(1)}, u32[]{:S(2)}, u32[]{:S(2)}) collective-permute-start(bf16[128,896]{1,0:T(8,128)(2,1)S(1)} %slice.19), channel_id=1, source_target_pairs={{0,32},{32,64},{64,96},{96,128},{128,160},{160,192},{192,224},{224... | collective-permute-start | bytes 688136 | tf_op jit(solution)/shard_map/ppermute | solution.py:364
  160.4 2.2 copy-start.18
  162.6 0.7 copy-start.19
  186.0 9.4 %all-to-all-start.1 = ((f32[8,8,512]{2,1,0:T(8,128)}), f32[8,8,512]{2,1,0:T(8,128)S(1)}, u32[]{:S(2)}, u32[]{:S(2)}) async-start(f32[8,8,512]{2,1,0:T(8,128)} %broadcast_in_dim.9), calls=%async_computation.1 | async-start | bytes 262144 | tf_op jit(solution)/shard_map/all_to_all | solution.py:497
  195.5 0.7 copy-start.9
  199.1 61.3 %copy-start.20 = (f32[3,16,896]{2,1,0:T(8,128)S(1)}, f32[3,16,896]{2,1,0:T(8,128)}, u32[]{:S(2)}) copy-start(f32[3,16,896]{2,1,0:T(8,128)} %param.19) | copy-start | bytes 516100
  199.1 62.0 %copy-start.22 = (f32[3,16,512]{2,1,0:T(8,128)S(1)}, f32[3,16,512]{2,1,0:T(8,128)}, u32[]{:S(2)}) copy-start(f32[3,16,512]{2,1,0:T(8,128)} %param.18) | copy-start | bytes 294916

commit v11 on v8

--- a/solution.py
+++ b/solution.py
@@ -90,11 +90,15 @@
             turned_ref[span, :] = projected.T.astype(BF16)
 
 
-def part_kernel(plan, z_ref, gradient_ref, *refs):
+def part_kernel(plan, first, z_ref, gradient_ref, *refs):
     n_blocks = len(plan["blocks"])
-    block_refs = refs[:n_blocks]
-    out_ref, total, left, right, sems, out_sems = refs[n_blocks:]
+    block_refs, refs = refs[:n_blocks], refs[n_blocks:]
+    if not first:
+        before_ref, refs = refs[0], refs[1:]
+    out_ref, total, left, right, sems, out_sems = refs
     copies = sum(fetch_blocks(plan, z_ref, gradient_ref, block_refs, left, right, sems), [])
+    if not first:
+        copies += copy_rows(before_ref, total, sems, 4 * n_blocks, 4)
     for copy in copies:
         copy.start()
     for copy in copies:
@@ -104,7 +108,8 @@
     hidden = total.shape[1]
     for i, start in enumerate(range(0, hidden, 512)):
         cols = slice(start, min(start + 512, hidden))
-        total[:, cols] = jnp.dot(left[...], right[:, cols], preferred_element_type=F32)
+        product = jnp.dot(left[...], right[:, cols], preferred_element_type=F32)
+        total[:, cols] = product if first else total[:, cols] + product
         write = pltpu.make_async_copy(total.at[:, cols], out_ref.at[:, cols], out_sems.at[i])
         write.start()
         writes.append(write)
@@ -352,16 +357,17 @@
     def at_z(offset):
         return (low if offset < 0 else high)[abs(offset)]
 
-    def part(offsets):
+    def part(offsets, before=None):
         blocks = [at_z(offset) for offset in offsets]
         plan = dict(n_z=n_z, rows=rows, blocks=[(offset, 0) for offset in offsets])
         n = len(blocks)
+        given = [] if before is None else [before]
         return pl.pallas_call(
-            functools.partial(part_kernel, plan),
+            functools.partial(part_kernel, plan, before is None),
             out_shape=jax.ShapeDtypeStruct((tokens, hidden), F32),
-            in_specs=[smem] + [hbm] * (n + 1),
+            in_specs=[smem] + [hbm] * (n + 1 + len(given)),
             out_specs=hbm,
-            scratch_shapes=[pltpu.VMEM((tokens, hidden), F32)] + scratch(n * rows, 4 * n),
+            scratch_shapes=[pltpu.VMEM((tokens, hidden), F32)] + scratch(n * rows, 4 * n + 4),
             compiler_params=params,
             cost_estimate=pl.CostEstimate(
                 flops=2 * tokens * n * rows * hidden,
@@ -369,10 +375,10 @@
                 transcendentals=0,
             ),
             name="part_product",
-        )(spot, gradient, *blocks)
-
-    def after(value, other):
-        return lax.optimization_barrier((value, other))[0]
+        )(spot, gradient, *blocks, *given)
+
+    def after(value, *others):
+        return lax.optimization_barrier((value, *others))[0]
 
     def pairs(first, end):
         return [sign * k for k in range(first, end) for sign in (-1, 1)]
@@ -387,15 +393,18 @@
     at = last - 3
     step(at + 1, after(low[at], lora_t), after(high[at], lora_t))
     step(last - 1, low[last - 2], high[last - 2])
-    step(last, low[last - 1][:half], high[last - 1][half:])
     in_t, _, normed_gram = side(normed_all, 0, 2 * RANK, "normed_side")
-    offsets = pairs(last - 4, last)
+    at = last - 1
+    low_in, high_in = after(low[at], in_t), after(high[at], in_t)
+    step(last, low_in[:half], high_in[half:])
+    total = part(pairs(last - 4, last - 1), after(total, low_in, high_in))
+    offsets = pairs(last - 1, last)
     blocks = [at_z(offset) for offset in offsets] + [low[last], high[last]]
     plan = dict(
         n_z=n_z,
         rows=rows,
         blocks=[(offset, 0) for offset in offsets] + [(last, 0), (last, half)],
-        chunks=[slice(0, 4), slice(4, 8), slice(8, 10)],
+        chunks=[slice(0, 4)],
     )
     sums, mids = pl.pallas_call(
         functools.partial(hidden_kernel, plan),

time: 235 us -> 235 us (level)
  waiting for transfers between devices: 35.8 us -> 29.1 us
  Pallas kernels: 28.9 us -> 32.6 us
    pallas_call x1 -> x2, Pallas kernels: 6.05 us -> 12 us  [part(): pl.pallas_call(functools.partial(part_kernel, plan, before is None), out_...]
    ppermute x8, waiting for transfers between devices: 24.2 us -> 18.6 us  [step(): high[k] = lax.ppermute(high_from, z_axes, ring(n_z, -1))]
  transfers between devices with their start and end apart: 19 -> 19, of which waited for: 12 -> 12; matrix products, arithmetic and copies ran while one was open for 0% -> 0% of each run, Pallas kernels for 7% -> 9%
where the time goes in v11:
time: 235 us; the launch traced here: 234 us
  blocking collectives  86 us (37%)
  starting transfers between devices  67.5 us (29%)
  Pallas kernels  32.6 us (14%)
  waiting for transfers between devices  29.1 us (12%)
  between operations  15.1 us (6%)
    ppermute x8, starting transfers between devices, step(): high[k] = lax.ppermute(high_from, z_axes, ring(n_z, -1))  48.8 us
    all_to_all x1, blocking collectives, per_device(): lax.all_to_all(share.reshape(n_z, -1, 128), z_axes, 0, 0)  21.3 us
    ppermute x8, waiting for transfers between devices, step(): high[k] = lax.ppermute(high_from, z_axes, ring(n_z, -1))  18.6 us
    all_to_all x1, blocking collectives, per_device(): lax.all_to_all(jnp.broadcast_to(share, (n_z,) + share.shape), z_axes, 0, 0)  17 us
    ppermute x8, starting transfers between devices, step(): low[k] = lax.ppermute(low_from, z_axes, ring(n_z, 1))  15.3 us
    all_to_all x1, blocking collectives, per_device(): lax.all_to_all(out.reshape(n_y, -1, 128), 'y', 0, 0)  14.3 us
    all_gather x1, blocking collectives, per_device(): block = lax.all_gather(frozen_down_weight.T, 'y', axis=0, tiled=True)  13.4 us
    pallas_call x2, Pallas kernels, part(): pl.pallas_call(functools.partial(part_kernel, plan, before is None), out_...  12 us
  transfers between devices with their start and end apart: 19, of which 12 were waited for; matrix products, arithmetic and copies ran while one was open for 0% of the time, Pallas kernels for 9%

profile of v11, /device:TPU:32, one launch (start us, length us, event | category | flops | bytes accessed | tf_op | source)
XLA Modules:
  0.0 233.9 jit_solution(16582957252539598195)
XLA Ops:
  7.2 0.0 all-gather.3.cloned.1.call-start
  7.2 0.7 all-gather.3.cloned.1.call-update
  7.9 0.0 all-gather.5.cloned.1.call-start
  7.9 0.7 all-gather.5.cloned.1.call-update
  8.6 13.4 %all_gather.10.refs_0_ = bf16[256,896]{1,0:T(8,128)(2,1)S(1)} all-gather(bf16[64,896]{1,0:T(8,128)(2,1)} %bitcast.24), channel_id=1, replica_groups=mesh['z'=16,'y'=4,'x'=4,'c'=2] {'y'}, dimensions={0}, use_global_device_ids=true | all-gather | bytes 573440 | tf_op jit(solution)/shard_map/all_gather | solution.py:298
  22.0 6.9 %collective-permute-start.4 = (bf16[256,896]{1,0:T(8,128)(2,1)S(1)}, bf16[256,896]{1,0:T(8,128)(2,1)S(1)}, u32[]{:S(2)}, u32[]{:S(2)}) collective-permute-start(bf16[256,896]{1,0:T(8,128)(2,1)S(1)} %all_gather.10.refs_0_), channel_id=1, source_target_pairs={{0,480},{32,0},{64,32},{96,64},{128,96},{160,128},{192,160},{224,1... | collective-permute-start | bytes 1376264 | tf_op jit(solution)/shard_map/ppermute | solution.py:312
  28.9 1.9 collective-permute-start
  30.8 4.0 %collective-permute-done.4.refs_2_ = bf16[256,896]{1,0:T(8,128)(2,1)S(1)} collective-permute-done((bf16[256,896]{1,0:T(8,128)(2,1)S(1)}, bf16[256,896]{1,0:T(8,128)(2,1)S(1)}, u32[]{:S(2)}, u32[]{:S(2)}) %collective-permute-start.4) | collective-permute-done | bytes 458784 | tf_op jit(solution)/shard_map/ppermute | solution.py:312
  34.9 8.6 %collective-permute-start.5 = (bf16[256,896]{1,0:T(8,128)(2,1)S(1)}, bf16[256,896]{1,0:T(8,128)(2,1)S(1)}, u32[]{:S(2)}, u32[]{:S(2)}) collective-permute-start(bf16[256,896]{1,0:T(8,128)(2,1)S(1)} %collective-permute-done.4.refs_2_), channel_id=1, source_target_pairs={{0,480},{32,0},{64,32},{96,64},{128,96},{160,128},{192,160},{224,1... | collective-permute-start | bytes 1376264 | tf_op jit(solution)/shard_map/ppermute | solution.py:312
  43.5 0.5 collective-permute-done.refs_1_
  44.0 1.9 collective-permute-start.1
  45.9 4.7 %collective-permute-done.5.refs_4_ = bf16[256,896]{1,0:T(8,128)(2,1)S(1)} collective-permute-done((bf16[256,896]{1,0:T(8,128)(2,1)S(1)}, bf16[256,896]{1,0:T(8,128)(2,1)S(1)}, u32[]{:S(2)}, u32[]{:S(2)}) %collective-permute-start.5) | collective-permute-done | bytes 458784 | tf_op jit(solution)/shard_map/ppermute | solution.py:312
  50.7 5.7 %collective-permute-start.6 = (bf16[256,896]{1,0:T(8,128)(2,1)S(1)}, bf16[256,896]{1,0:T(8,128)(2,1)S(1)}, u32[]{:S(2)}, u32[]{:S(2)}) collective-permute-start(bf16[256,896]{1,0:T(8,128)(2,1)S(1)} %collective-permute-done.5.refs_4_), channel_id=1, source_target_pairs={{0,480},{32,0},{64,32},{96,64},{128,96},{160,128},{192,160},{224,1... | collective-permute-start | bytes 1376264 | tf_op jit(solution)/shard_map/ppermute | solution.py:312
  56.4 0.5 collective-permute-done.1.refs_3_
  56.9 1.9 collective-permute-start.2
  58.8 3.9 %collective-permute-done.6.refs_6_ = bf16[256,896]{1,0:T(8,128)(2,1)S(1)} collective-permute-done((bf16[256,896]{1,0:T(8,128)(2,1)S(1)}, bf16[256,896]{1,0:T(8,128)(2,1)S(1)}, u32[]{:S(2)}, u32[]{:S(2)}) %collective-permute-start.6) | collective-permute-done | bytes 458784 | tf_op jit(solution)/shard_map/ppermute | solution.py:312
  62.7 5.7 %collective-permute-start.10 = (bf16[256,896]{1,0:T(8,128)(2,1)S(1)}, bf16[256,896]{1,0:T(8,128)(2,1)}, u32[]{:S(2)}, u32[]{:S(2)}) collective-permute-start(bf16[256,896]{1,0:T(8,128)(2,1)S(1)} %collective-permute-done.6.refs_6_), channel_id=1, source_target_pairs={{0,480},{32,0},{64,32},{96,64},{128,96},{160,128},{192,160},{224,1... | collective-permute-start | bytes 1376264 | tf_op jit(solution)/shard_map/ppermute | solution.py:312
  68.4 0.5 collective-permute-done.2.refs_5_
  68.9 1.9 collective-permute-start.3
  70.8 0.0 all-gather.3.cloned.1.call-done.gradient_ref.refs_0_.refs_1_
  70.9 6.1 %part_product.2.refs_6_ = f32[512,896]{1,0:T(8,128)} custom-call(s32[1]{0:T(128)} %bitcast.z_ref, bf16[512,4096]{1,0:T(8,128)(2,1)} %all-gather.3.cloned.1.call-done.gradient_ref.refs_0_.refs_1_, bf16[256,896]{1,0:T(8,128)(2,1)} %copy-done, bf16[256,896]{1,0:T(8,128)(2,1)} %copy-done.5, bf16[256,896]{1,0:T(8,128)(2,1)} %copy-done.4, ...), custom_call_target="tpu_custom_call" | custom-call | flops 1644167168 | bytes 6291456 | tf_op jit(solution)/shard_map/part_product/pallas_call | solution.py:365
  77.0 0.0 collective-permute-done.10.refs_1_
  77.0 5.5 %collective-permute-start.11 = (bf16[256,896]{1,0:T(8,128)(2,1)}, bf16[256,896]{1,0:T(8,128)(2,1)S(1)}, u32[]{:S(2)}, u32[]{:S(2)}) collective-permute-start(bf16[256,896]{1,0:T(8,128)(2,1)} %collective-permute-done.10.refs_1_), channel_id=1, source_target_pairs={{0,480},{32,0},{64,32},{96,64},{128,96},{160,128},{192,160},{224,1... | collective-permute-start | bytes 1376264 | tf_op jit(solution)/shard_map/ppermute | solution.py:312
  82.5 0.0 collective-permute-done.3.refs_0_
  82.5 1.9 collective-permute-start.7
  84.4 4.9 %gradient_side.1 = (bf16[16,512]{1,0:T(8,128)(2,1)}, bf16[512,16]{1,0:T(8,128)(2,1)}, f32[4,128,128]{2,1,0:T(8,128)}) custom-call(bf16[512,4096]{1,0:T(8,128)(2,1)} %all-gather.3.cloned.1.call-done.gradient_ref.refs_0_.refs_1_, bf16[512,4096]{1,0:T(8,128)(2,1)} %all-gather.3.cloned.1.call-done.gradient_ref.refs_0_.refs_1_, bf16[48,4096]{1,0:T(8,128)(2,1)} %bitcast.16), custom_call_target="tpu_custom_call" | custom-call | flops 603979776 | bytes 5242880 | tf_op jit(solution)/shard_map/gradient_side/pallas_call | solution.py:317
  89.3 0.0 collective-permute-done.11.refs_3_
  89.4 5.1 %collective-permute-start.12 = (bf16[256,896]{1,0:T(8,128)(2,1)S(1)}, bf16[256,896]{1,0:T(8,128)(2,1)S(1)}, u32[]{:S(2)}, u32[]{:S(2)}) collective-permute-start(bf16[256,896]{1,0:T(8,128)(2,1)S(1)} %collective-permute-done.11.refs_3_), channel_id=1, source_target_pairs={{0,480},{32,0},{64,32},{96,64},{128,96},{160,128},{192,160},{224,1... | collective-permute-start | bytes 1376264 | tf_op jit(solution)/shard_map/ppermute | solution.py:312
  94.5 0.0 collective-permute-done.7.refs_2_
  94.5 0.0 copy-start.11
  94.5 1.9 collective-permute-start.8
  96.4 5.5 %collective-permute-done.12.refs_5_ = bf16[256,896]{1,0:T(8,128)(2,1)S(1)} collective-permute-done((bf16[256,896]{1,0:T(8,128)(2,1)S(1)}, bf16[256,896]{1,0:T(8,128)(2,1)S(1)}, u32[]{:S(2)}, u32[]{:S(2)}) %collective-permute-start.12) | collective-permute-done | bytes 458784 | tf_op jit(solution)/shard_map/ppermute | solution.py:312
  102.0 5.0 %collective-permute-start.13 = (bf16[256,896]{1,0:T(8,128)(2,1)S(1)}, bf16[256,896]{1,0:T(8,128)(2,1)S(1)}, u32[]{:S(2)}, u32[]{:S(2)}) collective-permute-start(bf16[256,896]{1,0:T(8,128)(2,1)S(1)} %collective-permute-done.12.refs_5_), channel_id=1, source_target_pairs={{0,480},{32,0},{64,32},{96,64},{128,96},{160,128},{192,160},{224,1... | collective-permute-start | bytes 1376264 | tf_op jit(solution)/shard_map/ppermute | solution.py:312
  106.9 0.3 collective-permute-done.8.refs_4_
  107.2 1.9 collective-permute-start.9
  109.2 0.0 all-gather.5.cloned.1.call-done.refs_0_.refs_1_
  109.2 5.0 %normed_side.1 = (bf16[32,512]{1,0:T(8,128)(2,1)}, bf16[512,32]{1,0:T(8,128)(2,1)}, f32[4,128,128]{2,1,0:T(8,128)}) custom-call(bf16[512,4096]{1,0:T(8,128)(2,1)} %all-gather.5.cloned.1.call-done.refs_0_.refs_1_, bf16[512,4096]{1,0:T(8,128)(2,1)} %all-gather.5.cloned.1.call-done.refs_0_.refs_1_, bf16[48,4096]{1,0:T(8,128)(2,1)} %bitcast.17), custom_call_target="tpu_custom_call" | custom-call | flops 671088640 | bytes 5242880 | tf_op jit(solution)/shard_map/normed_side/pallas_call | solution.py:317
  114.2 0.0 copy-done.12
  114.2 0.4 collective-permute-done.13.refs_1_
  114.6 6.3 %collective-permute-start.15 = (bf16[128,896]{1,0:T(8,128)(2,1)S(1)}, bf16[128,896]{1,0:T(8,128)(2,1)S(1)}, u32[]{:S(2)}, u32[]{:S(2)}) collective-permute-start(bf16[128,896]{1,0:T(8,128)(2,1)S(1)} %slice.16), channel_id=1, source_target_pairs={{0,480},{32,0},{64,32},{96,64},{128,96},{160,128},{192,160},{224,1... | collective-permute-start | bytes 688136 | tf_op jit(solution)/shard_map/ppermute | solution.py:312
  120.9 0.3 collective-permute-done.9.refs_0_
  121.3 1.9 collective-permute-start.14
  123.2 5.9 %part_product.3.refs_4_ = f32[512,896]{1,0:T(8,128)} custom-call(s32[1]{0:T(128)} %bitcast.z_ref, bf16[512,4096]{1,0:T(8,128)(2,1)} %all-gather.3.cloned.1.call-done.gradient_ref.refs_0_.refs_1_, bf16[256,896]{1,0:T(8,128)(2,1)} %collective-permute-done.3.refs_0_, bf16[256,896]{1,0:T(8,128)(2,1)} %collective-permute-done.10.refs_1_, ...), custom_call_target="tpu_custom_call" | custom-call | flops 1409286144 | bytes 6291456 | tf_op jit(solution)/shard_map/part_product/pallas_call | solution.py:365
  129.1 0.0 copy-done.1
  129.2 0.0 copy-done.2
  129.2 0.0 collective-permute-done.15.refs_3_
  129.2 1.5 collective-permute-done.14.refs_2_
  130.7 0.7 copy-done.15
  131.4 7.8 %hidden_side.1 = (f32[4,48,896]{2,1,0:T(8,128)}, f32[64,512]{1,0:T(8,128)}) custom-call(s32[1]{0:T(128)} %bitcast.z_ref, bf16[512,4096]{1,0:T(8,128)(2,1)} %all-gather.3.cloned.1.call-done.gradient_ref.refs_0_.refs_1_, bf16[256,896]{1,0:T(8,128)(2,1)} %copy-done.2, bf16[256,896]{1,0:T(8,128)(2,1)} %copy-done.1, bf16[128,896]{1,0:T(8,128)(2,1)} %copy-done.15, ...), custom_call_target="tpu_custom_call" | custom-call | tf_op jit(solution)/shard_map/hidden_side/pallas_call | solution.py:409
  139.2 0.0 copy-start.17
  139.2 0.0 copy-start.16
  139.3 10.8 %all_to_all.30 = f32[8,8,512]{2,1,0:T(8,128)S(1)} all-to-all(f32[8,8,512]{2,1,0:T(8,128)} %bitcast.23), channel_id=1, replica_groups=mesh['z'=16,'y'=4,'x'=4,'c'=2] {'x','c'}, dimensions={0} | all-to-all | bytes 262144 | tf_op jit(solution)/shard_map/all_to_all | solution.py:442
  150.0 0.7 broadcast_in_dim.9
  150.7 3.4 %all-to-all-start.1 = ((f32[8,8,512]{2,1,0:T(8,128)}), f32[8,8,512]{2,1,0:T(8,128)S(1)}, u32[]{:S(2)}, u32[]{:S(2)}) async-start(f32[8,8,512]{2,1,0:T(8,128)} %broadcast_in_dim.9), calls=%async_computation.1 | async-start | bytes 262144 | tf_op jit(solution)/shard_map/all_to_all | solution.py:444
  154.7 5.4 %all-to-all-done.1 = f32[8,8,512]{2,1,0:T(8,128)S(1)} async-done(((f32[8,8,512]{2,1,0:T(8,128)}), f32[8,8,512]{2,1,0:T(8,128)S(1)}, u32[]{:S(2)}, u32[]{:S(2)}) %all-to-all-start.1) | async-done | bytes 131104 | tf_op jit(solution)/shard_map/all_to_all | solution.py:444
  160.2 0.7 copy-done.3
  160.8 3.0 %clip_side.1 = f32[72,8,128]{2,1,0:T(8,128)} custom-call(f32[1]{0:T(128)} %copy.12.clip_ref, f32[64,512]{1,0:T(8,128)} %bitcast.22, f32[4,48,896]{2,1,0:T(8,128)} %get-tuple-element.27.sums_ref, bf16[512,512]{1,0:T(8,128)(2,1)} %normed_ref.1, bf16[512,512]{1,0:T(8,128)(2,1)} %gradient_ref.1, f32[4,128,128]{2,1,0:T(8,128)} %get-tuple-element.28.normed_gram_ref, ...), custom_call_target="tpu_custom_call" | custom-call | tf_op jit(solution)/shard_map/clip_side/pallas_call | solution.py:451
  163.8 14.3 %all_to_all.31 = f32[4,144,128]{2,1,0:T(8,128)S(1)} all-to-all(f32[4,144,128]{2,1,0:T(8,128)} %bitcast.18), channel_id=1, replica_groups=mesh['z'=16,'y'=4,'x'=4,'c'=2] {'y'}, dimensions={0} | all-to-all | bytes 589824 | tf_op jit(solution)/shard_map/all_to_all | solution.py:470
  178.1 21.3 %all_to_all.32 = f32[16,9,128]{2,1,0:T(8,128)S(1)} all-to-all(f32[16,9,128]{2,1,0:T(8,128)S(1)} %reshape.44), channel_id=1, replica_groups=mesh['z'=16,'y'=4,'x'=4,'c'=2] {'z'}, dimensions={0} | all-to-all | bytes 147456 | tf_op jit(solution)/shard_map/all_to_all | solution.py:471
  199.4 17.0 %all_to_all.33 = f32[16,9,128]{2,1,0:T(8,128)S(1)} all-to-all(f32[16,9,128]{2,1,0:T(8,128)S(1)} %broadcast_in_dim.10), channel_id=1, replica_groups=mesh['z'=16,'y'=4,'x'=4,'c'=2] {'z'}, dimensions={0} | all-to-all | bytes 147456 | tf_op jit(solution)/shard_map/all_to_all | solution.py:472
  216.5 9.2 %all_to_all.34 = f32[4,144,128]{2,1,0:T(8,128)S(1)} all-to-all(f32[4,144,128]{2,1,0:T(8,128)S(1)} %broadcast_in_dim.11), channel_id=1, replica_groups=mesh['z'=16,'y'=4,'x'=4,'c'=2] {'y'}, dimensions={0} | all-to-all | bytes 589824 | tf_op jit(solution)/shard_map/all_to_all | solution.py:475
  225.7 0.7 fusion.1
  226.4 0.0 copy-done.16
  226.4 0.7 fusion
  (37 shorter events, 0.2 us)
Async XLA Ops:
  7.2 63.7 %all-gather.3.cloned.1.call-start = ((), (), s32[]{:S(2)}) async-start(), calls=%async_computation.6 | async-start | bytes 4718592 | tf_op jit(solution)/shard_map/all_gather | solution.py:297
  7.9 101.3 %all-gather.5.cloned.1.call-start = ((), (), s32[]{:S(2)}) async-start(), calls=%async_computation.7 | async-start | bytes 4718592 | tf_op jit(solution)/shard_map/all_gather | solution.py:299
  22.0 48.8 %copy-start = (bf16[256,896]{1,0:T(8,128)(2,1)}, bf16[256,896]{1,0:T(8,128)(2,1)S(1)}, u32[]{:S(2)}) copy-start(bf16[256,896]{1,0:T(8,128)(2,1)S(1)} %all_gather.10.refs_0_) | copy-start | bytes 1376260
  22.0 12.8 %collective-permute-start.4 = (bf16[256,896]{1,0:T(8,128)(2,1)S(1)}, bf16[256,896]{1,0:T(8,128)(2,1)S(1)}, u32[]{:S(2)}, u32[]{:S(2)}) collective-permute-start(bf16[256,896]{1,0:T(8,128)(2,1)S(1)} %all_gather.10.refs_0_), channel_id=1, source_target_pairs={{0,480},{32,0},{64,32},{96,64},{128,96},{160,128},{192,160},{224,1... | collective-permute-start | bytes 1376264 | tf_op jit(solution)/shard_map/ppermute | solution.py:312
  28.9 15.1 %collective-permute-start = (bf16[256,896]{1,0:T(8,128)(2,1)S(1)}, bf16[256,896]{1,0:T(8,128)(2,1)S(1)}, u32[]{:S(2)}, u32[]{:S(2)}) collective-permute-start(bf16[256,896]{1,0:T(8,128)(2,1)S(1)} %all_gather.10.refs_0_), channel_id=1, source_target_pairs={{0,32},{32,64},{64,96},{96,128},{128,160},{160,192},{192,224},{224... | collective-permute-start | bytes 1376264 | tf_op jit(solution)/shard_map/ppermute | solution.py:311
  34.9 36.0 %copy-start.4 = (bf16[256,896]{1,0:T(8,128)(2,1)}, bf16[256,896]{1,0:T(8,128)(2,1)S(1)}, u32[]{:S(2)}) copy-start(bf16[256,896]{1,0:T(8,128)(2,1)S(1)} %collective-permute-done.4.refs_2_) | copy-start | bytes 1376260
  34.9 15.8 %collective-permute-start.5 = (bf16[256,896]{1,0:T(8,128)(2,1)S(1)}, bf16[256,896]{1,0:T(8,128)(2,1)S(1)}, u32[]{:S(2)}, u32[]{:S(2)}) collective-permute-start(bf16[256,896]{1,0:T(8,128)(2,1)S(1)} %collective-permute-done.4.refs_2_), channel_id=1, source_target_pairs={{0,480},{32,0},{64,32},{96,64},{128,96},{160,128},{192,160},{224,1... | collective-permute-start | bytes 1376264 | tf_op jit(solution)/shard_map/ppermute | solution.py:312
  44.0 26.9 %copy-start.5 = (bf16[256,896]{1,0:T(8,128)(2,1)}, bf16[256,896]{1,0:T(8,128)(2,1)S(1)}, u32[]{:S(2)}) copy-start(bf16[256,896]{1,0:T(8,128)(2,1)S(1)} %collective-permute-done.refs_1_) | copy-start | bytes 1376260
  44.0 12.9 %collective-permute-start.1 = (bf16[256,896]{1,0:T(8,128)(2,1)S(1)}, bf16[256,896]{1,0:T(8,128)(2,1)S(1)}, u32[]{:S(2)}, u32[]{:S(2)}) collective-permute-start(bf16[256,896]{1,0:T(8,128)(2,1)S(1)} %collective-permute-done.refs_1_), channel_id=1, source_target_pairs={{0,32},{32,64},{64,96},{96,128},{128,160},{160,192},{192,224},{224... | collective-permute-start | bytes 1376264 | tf_op jit(solution)/shard_map/ppermute | solution.py:311
  50.7 20.2 %copy-start.6 = (bf16[256,896]{1,0:T(8,128)(2,1)}, bf16[256,896]{1,0:T(8,128)(2,1)S(1)}, u32[]{:S(2)}) copy-start(bf16[256,896]{1,0:T(8,128)(2,1)S(1)} %collective-permute-done.5.refs_4_) | copy-start | bytes 1376260
  50.7 12.0 %collective-permute-start.6 = (bf16[256,896]{1,0:T(8,128)(2,1)S(1)}, bf16[256,896]{1,0:T(8,128)(2,1)S(1)}, u32[]{:S(2)}, u32[]{:S(2)}) collective-permute-start(bf16[256,896]{1,0:T(8,128)(2,1)S(1)} %collective-permute-done.5.refs_4_), channel_id=1, source_target_pairs={{0,480},{32,0},{64,32},{96,64},{128,96},{160,128},{192,160},{224,1... | collective-permute-start | bytes 1376264 | tf_op jit(solution)/shard_map/ppermute | solution.py:312
  56.9 14.0 %copy-start.7 = (bf16[256,896]{1,0:T(8,128)(2,1)}, bf16[256,896]{1,0:T(8,128)(2,1)S(1)}, u32[]{:S(2)}) copy-start(bf16[256,896]{1,0:T(8,128)(2,1)S(1)} %collective-permute-done.1.refs_3_) | copy-start | bytes 1376260
  56.9 12.0 %collective-permute-start.2 = (bf16[256,896]{1,0:T(8,128)(2,1)S(1)}, bf16[256,896]{1,0:T(8,128)(2,1)S(1)}, u32[]{:S(2)}, u32[]{:S(2)}) collective-permute-start(bf16[256,896]{1,0:T(8,128)(2,1)S(1)} %collective-permute-done.1.refs_3_), channel_id=1, source_target_pairs={{0,32},{32,64},{64,96},{96,128},{128,160},{160,192},{192,224},{224... | collective-permute-start | bytes 1376264 | tf_op jit(solution)/shard_map/ppermute | solution.py:311
  62.7 8.2 %copy-start.9 = (bf16[256,896]{1,0:T(8,128)(2,1)}, bf16[256,896]{1,0:T(8,128)(2,1)S(1)}, u32[]{:S(2)}) copy-start(bf16[256,896]{1,0:T(8,128)(2,1)S(1)} %collective-permute-done.6.refs_6_) | copy-start | bytes 1376260
  62.7 14.3 %collective-permute-start.10 = (bf16[256,896]{1,0:T(8,128)(2,1)S(1)}, bf16[256,896]{1,0:T(8,128)(2,1)}, u32[]{:S(2)}, u32[]{:S(2)}) collective-permute-start(bf16[256,896]{1,0:T(8,128)(2,1)S(1)} %collective-permute-done.6.refs_6_), channel_id=1, source_target_pairs={{0,480},{32,0},{64,32},{96,64},{128,96},{160,128},{192,160},{224,1... | collective-permute-start | bytes 1376264 | tf_op jit(solution)/shard_map/ppermute | solution.py:312
  68.9 2.0 copy-start.8
  68.9 13.6 %collective-permute-start.3 = (bf16[256,896]{1,0:T(8,128)(2,1)S(1)}, bf16[256,896]{1,0:T(8,128)(2,1)}, u32[]{:S(2)}, u32[]{:S(2)}) collective-permute-start(bf16[256,896]{1,0:T(8,128)(2,1)S(1)} %collective-permute-done.2.refs_5_), channel_id=1, source_target_pairs={{0,32},{32,64},{64,96},{96,128},{128,160},{160,192},{192,224},{224... | collective-permute-start | bytes 1376264 | tf_op jit(solution)/shard_map/ppermute | solution.py:311
  77.0 12.4 %collective-permute-start.11 = (bf16[256,896]{1,0:T(8,128)(2,1)}, bf16[256,896]{1,0:T(8,128)(2,1)S(1)}, u32[]{:S(2)}, u32[]{:S(2)}) collective-permute-start(bf16[256,896]{1,0:T(8,128)(2,1)} %collective-permute-done.10.refs_1_), channel_id=1, source_target_pairs={{0,480},{32,0},{64,32},{96,64},{128,96},{160,128},{192,160},{224,1... | collective-permute-start | bytes 1376264 | tf_op jit(solution)/shard_map/ppermute | solution.py:312
  82.5 12.0 %collective-permute-start.7 = (bf16[256,896]{1,0:T(8,128)(2,1)}, bf16[256,896]{1,0:T(8,128)(2,1)S(1)}, u32[]{:S(2)}, u32[]{:S(2)}) collective-permute-start(bf16[256,896]{1,0:T(8,128)(2,1)} %collective-permute-done.3.refs_0_), channel_id=1, source_target_pairs={{0,32},{32,64},{64,96},{96,128},{128,160},{160,192},{192,224},{224... | collective-permute-start | bytes 1376264 | tf_op jit(solution)/shard_map/ppermute | solution.py:311
  89.4 24.8 %copy-start.10 = (bf16[256,896]{1,0:T(8,128)(2,1)}, bf16[256,896]{1,0:T(8,128)(2,1)S(1)}, u32[]{:S(2)}) copy-start(bf16[256,896]{1,0:T(8,128)(2,1)S(1)} %collective-permute-done.11.refs_3_) | copy-start | bytes 1376260
  89.4 12.6 %collective-permute-start.12 = (bf16[256,896]{1,0:T(8,128)(2,1)S(1)}, bf16[256,896]{1,0:T(8,128)(2,1)S(1)}, u32[]{:S(2)}, u32[]{:S(2)}) collective-permute-start(bf16[256,896]{1,0:T(8,128)(2,1)S(1)} %collective-permute-done.11.refs_3_), channel_id=1, source_target_pairs={{0,480},{32,0},{64,32},{96,64},{128,96},{160,128},{192,160},{224,1... | collective-permute-start | bytes 1376264 | tf_op jit(solution)/shard_map/ppermute | solution.py:312
  94.5 19.7 %copy-start.11 = (bf16[256,896]{1,0:T(8,128)(2,1)}, bf16[256,896]{1,0:T(8,128)(2,1)S(1)}, u32[]{:S(2)}) copy-start(bf16[256,896]{1,0:T(8,128)(2,1)S(1)} %collective-permute-done.7.refs_2_) | copy-start | bytes 1376260
  94.5 12.7 %collective-permute-start.8 = (bf16[256,896]{1,0:T(8,128)(2,1)S(1)}, bf16[256,896]{1,0:T(8,128)(2,1)S(1)}, u32[]{:S(2)}, u32[]{:S(2)}) collective-permute-start(bf16[256,896]{1,0:T(8,128)(2,1)S(1)} %collective-permute-done.7.refs_2_), channel_id=1, source_target_pairs={{0,32},{32,64},{64,96},{96,128},{128,160},{160,192},{192,224},{224... | collective-permute-start | bytes 1376264 | tf_op jit(solution)/shard_map/ppermute | solution.py:311
  102.0 12.2 %copy-start.12 = (bf16[256,896]{1,0:T(8,128)(2,1)}, bf16[256,896]{1,0:T(8,128)(2,1)S(1)}, u32[]{:S(2)}) copy-start(bf16[256,896]{1,0:T(8,128)(2,1)S(1)} %collective-permute-done.12.refs_5_) | copy-start | bytes 1376260
  102.0 12.6 %collective-permute-start.13 = (bf16[256,896]{1,0:T(8,128)(2,1)S(1)}, bf16[256,896]{1,0:T(8,128)(2,1)S(1)}, u32[]{:S(2)}, u32[]{:S(2)}) collective-permute-start(bf16[256,896]{1,0:T(8,128)(2,1)S(1)} %collective-permute-done.12.refs_5_), channel_id=1, source_target_pairs={{0,480},{32,0},{64,32},{96,64},{128,96},{160,128},{192,160},{224,1... | collective-permute-start | bytes 1376264 | tf_op jit(solution)/shard_map/ppermute | solution.py:312
  107.2 6.9 %copy-start.13 = (bf16[256,896]{1,0:T(8,128)(2,1)}, bf16[256,896]{1,0:T(8,128)(2,1)S(1)}, u32[]{:S(2)}) copy-start(bf16[256,896]{1,0:T(8,128)(2,1)S(1)} %collective-permute-done.8.refs_4_) | copy-start | bytes 1376260
  107.2 14.0 %collective-permute-start.9 = (bf16[256,896]{1,0:T(8,128)(2,1)S(1)}, bf16[256,896]{1,0:T(8,128)(2,1)S(1)}, u32[]{:S(2)}, u32[]{:S(2)}) collective-permute-start(bf16[256,896]{1,0:T(8,128)(2,1)S(1)} %collective-permute-done.8.refs_4_), channel_id=1, source_target_pairs={{0,32},{32,64},{64,96},{96,128},{128,160},{160,192},{192,224},{224... | collective-permute-start | bytes 1376264 | tf_op jit(solution)/shard_map/ppermute | solution.py:311
  114.5 14.6 %copy-start.1 = (bf16[256,896]{1,0:T(8,128)(2,1)}, bf16[256,896]{1,0:T(8,128)(2,1)S(1)}, u32[]{:S(2)}) copy-start(bf16[256,896]{1,0:T(8,128)(2,1)S(1)} %collective-permute-done.13.refs_1_) | copy-start | bytes 1376260
  114.6 14.6 %collective-permute-start.15 = (bf16[128,896]{1,0:T(8,128)(2,1)S(1)}, bf16[128,896]{1,0:T(8,128)(2,1)S(1)}, u32[]{:S(2)}, u32[]{:S(2)}) collective-permute-start(bf16[128,896]{1,0:T(8,128)(2,1)S(1)} %slice.16), channel_id=1, source_target_pairs={{0,480},{32,0},{64,32},{96,64},{128,96},{160,128},{192,160},{224,1... | collective-permute-start | bytes 688136 | tf_op jit(solution)/shard_map/ppermute | solution.py:312
  121.3 7.9 %copy-start.2 = (bf16[256,896]{1,0:T(8,128)(2,1)}, bf16[256,896]{1,0:T(8,128)(2,1)S(1)}, u32[]{:S(2)}) copy-start(bf16[256,896]{1,0:T(8,128)(2,1)S(1)} %collective-permute-done.9.refs_0_) | copy-start | bytes 1376260
  121.3 9.4 %collective-permute-start.14 = (bf16[128,896]{1,0:T(8,128)(2,1)S(1)}, bf16[128,896]{1,0:T(8,128)(2,1)S(1)}, u32[]{:S(2)}, u32[]{:S(2)}) collective-permute-start(bf16[128,896]{1,0:T(8,128)(2,1)S(1)} %slice.15), channel_id=1, source_target_pairs={{0,32},{32,64},{64,96},{96,128},{128,160},{160,192},{192,224},{224... | collective-permute-start | bytes 688136 | tf_op jit(solution)/shard_map/ppermute | solution.py:311
  129.2 1.5 copy-start.14
  130.7 0.7 copy-start.15
  139.2 86.5 %copy-start.17 = (f32[3,16,512]{2,1,0:T(8,128)S(1)}, f32[3,16,512]{2,1,0:T(8,128)}, u32[]{:S(2)}) copy-start(f32[3,16,512]{2,1,0:T(8,128)} %param.18) | copy-start | bytes 294916
  139.2 87.2 %copy-start.16 = (f32[3,16,896]{2,1,0:T(8,128)S(1)}, f32[3,16,896]{2,1,0:T(8,128)}, u32[]{:S(2)}) copy-start(f32[3,16,896]{2,1,0:T(8,128)} %param.19) | copy-start | bytes 516100
  150.7 9.4 %all-to-all-start.1 = ((f32[8,8,512]{2,1,0:T(8,128)}), f32[8,8,512]{2,1,0:T(8,128)S(1)}, u32[]{:S(2)}, u32[]{:S(2)}) async-start(f32[8,8,512]{2,1,0:T(8,128)} %broadcast_in_dim.9), calls=%async_computation.1 | async-start | bytes 262144 | tf_op jit(solution)/shard_map/all_to_all | solution.py:444
  160.1 0.7 copy-start.3
Sparse Core Ops, SparseCore 0:
  10.1 43.8 all-gather.2
  56.2 39.7 all-gather.4

commit v12 on v11

--- a/solution.py
+++ b/solution.py
@@ -217,19 +217,43 @@
 
 def clip_kernel(
     clip_ref,
+    mids_hbm,
+    normed_gram_hbm,
+    gradient_gram_hbm,
+    normed_hbm,
+    gradient_hbm,
+    sums_hbm,
+    out_ref,
     mids_ref,
-    sums_ref,
+    normed_gram_ref,
+    gradient_gram_ref,
     normed_ref,
     gradient_ref,
-    normed_gram_ref,
-    gradient_gram_ref,
-    out_ref,
+    sums_ref,
     wide,
+    sems,
 ):
+    copies = [
+        pltpu.make_async_copy(source, target, sems.at[i])
+        for i, (source, target) in enumerate(
+            (
+                (mids_hbm, mids_ref),
+                (normed_gram_hbm, normed_gram_ref),
+                (gradient_gram_hbm, gradient_gram_ref),
+                (normed_hbm, normed_ref),
+                (gradient_hbm, gradient_ref),
+                (sums_hbm, sums_ref),
+            )
+        )
+    ]
+    for copy in copies:
+        copy.start()
     sequences, _, hidden = sums_ref.shape
     local = wide.shape[1]
     bound = clip_ref[0]
     weights = []
+    for copy in copies[:3]:
+        copy.wait()
     for e in range(sequences):
         rows = slice(e * SEQUENCE_TOKENS, (e + 1) * SEQUENCE_TOKENS)
         mids = mids_ref[: 3 * RANK, rows].astype(BF16)
@@ -238,8 +262,12 @@
         )
         square = SCALE * SCALE * jnp.maximum(square, 0.0)
         square = square + mids_ref[3 * RANK + e : 3 * RANK + e + 1, 0:1]
-        weight = bound / jnp.maximum(jnp.sqrt(square), bound)
-        weights.append(weight)
+        weights.append(bound / jnp.maximum(jnp.sqrt(square), bound))
+    for copy in copies[3:5]:
+        copy.wait()
+    for e, weight in enumerate(weights):
+        rows = slice(e * SEQUENCE_TOKENS, (e + 1) * SEQUENCE_TOKENS)
+        mids = mids_ref[: 3 * RANK, rows].astype(BF16)
         first = weight * (
             SCALE * jnp.dot(mids[: 2 * RANK], normed_ref[rows, :], preferred_element_type=F32)
         )
@@ -252,6 +280,7 @@
         else:
             wide[: 2 * RANK] += first
             wide[2 * RANK :] += second
+    copies[5].wait()
     lanes = (local + hidden) // 128
     for t in range(out_ref.shape[0]):
         r, c = divmod(t, lanes)
@@ -267,6 +296,27 @@
             for e in range(1, sequences):
                 value = value + weights[e] * sums_ref[e, rows, at : at + 128]
         out_ref[t] = value
+
+
+def share_kernel(shares_ref, out_ref):
+    total = shares_ref[0]
+    for i in range(1, shares_ref.shape[0]):
+        total = total + shares_ref[i]
+    for i in range(out_ref.shape[0]):
+        out_ref[i] = total
+
+
+def output_kernel(bound_ref, tiles_ref, wide_noise_ref, hidden_noise_ref, wide_ref, hidden_ref):
+    count = bound_ref[1]
+    lanes = wide_ref.shape[1] // 128
+    every = lanes + hidden_ref.shape[1] // 128
+    for t in range(every * wide_ref.shape[0] // 8):
+        r, c = divmod(t, every)
+        out, noise, c = (
+            (wide_ref, wide_noise_ref, c) if c < lanes else (hidden_ref, hidden_noise_ref, c - lanes)
+        )
+        at = (slice(8 * r, 8 * r + 8), slice(128 * c, 128 * c + 128))
+        out[at] = (tiles_ref[t] + bound_ref[0] * noise[at]) / count
 
 
 def ring(size, by):
@@ -439,11 +489,15 @@
         lora_t,
     )
 
-    pieces = lax.all_to_all(mids.reshape(n_tensor, 8, tokens), tensor_axes, 0, 0)
-    piece = jnp.sum(pieces, axis=0)
-    mids = lax.all_to_all(
-        jnp.broadcast_to(piece, (n_tensor,) + piece.shape), tensor_axes, 0, 0
-    ).reshape(8 * n_tensor, tokens)
+    shares = lax.all_to_all(mids.reshape(n_tensor, 8, tokens), tensor_axes, 0, 0)
+    shares = pl.pallas_call(
+        share_kernel,
+        out_shape=jax.ShapeDtypeStruct(shares.shape, F32),
+        in_specs=[vmem],
+        out_specs=vmem,
+        name="share_sum",
+    )(shares)
+    mids = lax.all_to_all(shares, tensor_axes, 0, 0).reshape(8 * n_tensor, tokens)
 
     lanes = (local_width + hidden) // 128
     tiles = 6 * lanes
@@ -451,19 +505,28 @@
     out = pl.pallas_call(
         clip_kernel,
         out_shape=jax.ShapeDtypeStruct((padded, 8, 128), F32),
-        in_specs=[smem] + [vmem] * 6,
+        in_specs=[smem] + [hbm] * 6,
         out_specs=vmem,
-        scratch_shapes=[pltpu.VMEM((3 * RANK, local_width), F32)],
+        scratch_shapes=[
+            pltpu.VMEM((8 * n_tensor, tokens), F32),
+            pltpu.VMEM((sequences, SEQUENCE_TOKENS, SEQUENCE_TOKENS), F32),
+            pltpu.VMEM((sequences, SEQUENCE_TOKENS, SEQUENCE_TOKENS), F32),
+            pltpu.VMEM((tokens, local_width), BF16),
+            pltpu.VMEM((tokens, local_width), BF16),
+            pltpu.VMEM((sequences, 3 * RANK, hidden), F32),
+            pltpu.VMEM((3 * RANK, local_width), F32),
+            pltpu.SemaphoreType.DMA((6,)),
+        ],
         compiler_params=params,
         name="clip_side",
     )(
         clipping_limit,
         mids,
-        sums,
+        normed_gram,
+        gradient_gram,
         normed,
         output_gradient,
-        normed_gram,
-        gradient_gram,
+        sums,
     )
 
     n_y = sizes["y"]
@@ -473,19 +536,25 @@
         jnp.broadcast_to(share, (n_z,) + share.shape), z_axes, 0, 0
     ).reshape(-1, 128)
     whole = lax.all_to_all(jnp.broadcast_to(share, (n_y,) + share.shape), "y", 0, 0)
-    total = (
-        whole.reshape(padded, 8, 128)[:tiles]
-        .reshape(6, lanes, 8, 128)
-        .transpose(0, 2, 1, 3)
-        .reshape(3, RANK, lanes * 128)
-    )
-    count = sequences * n_z * sizes["y"]
-    bound = clipping_limit[0]
-    wide = total[:, :, :local_width]
-    inner = total[:, :, local_width : local_width + hidden]
+    count = sequences * n_z * n_y
+    wide, inner = pl.pallas_call(
+        output_kernel,
+        out_shape=(
+            jax.ShapeDtypeStruct((3 * RANK, local_width), F32),
+            jax.ShapeDtypeStruct((3 * RANK, hidden), F32),
+        ),
+        in_specs=[smem] + [vmem] * 3,
+        out_specs=(vmem, vmem),
+        name="outputs",
+    )(
+        jnp.concatenate([clipping_limit, jnp.full((1,), count, F32)]),
+        whole.reshape(padded, 8, 128),
+        width_noise_draw.reshape(3 * RANK, local_width),
+        hidden_noise_draw.reshape(3 * RANK, hidden),
+    )
     return (
-        (wide + bound * width_noise_draw) / count,
-        (inner + bound * hidden_noise_draw) / count,
+        wide.reshape(3, RANK, local_width),
+        inner.reshape(3, RANK, hidden),
     )
 
 

time: 235 us -> 239 us (1.017)
  blocking collectives: 86 us -> 76.8 us
  waiting for transfers between devices: 29.1 us -> 35.2 us
  starting transfers between devices: 67.5 us -> 71 us
  Pallas kernels: 32.6 us -> 35.7 us
    all_to_all x1 -> x0, blocking collectives: 9.25 us -> none  [per_device(): lax.all_to_all(jnp.broadcast_to(share, (n_y,) + share.shape), 'y', 0, 0)]
    all_to_all x1 -> x2, waiting for transfers between devices: 5.41 us -> 11.6 us  [the longest x1 6.17 us: per_device(): lax.all_to_all(jnp.broadcast_to(share, (n_y,) + share.shape), 'y', 0, 0)]
    all_to_all x1 -> x2, starting transfers between devices: 3.37 us -> 6.82 us  [the longest x1 3.45 us: per_device(): lax.all_to_all(jnp.broadcast_to(share, (n_y,) + share.shape), 'y', 0, 0)]
    pallas_call x0 -> x2, Pallas kernels: none -> 3.37 us  [the longest x1 1.8 us: per_device(): pl.pallas_call(output_kernel, out_shape=(jax.ShapeDtypeStruct((3 * RANK,...]
  transfers between devices with their start and end apart: 19 -> 20, of which waited for: 12 -> 13; matrix products, arithmetic and copies ran while one was open for 0% -> 0% of each run, Pallas kernels for 9% -> 9%
where the time goes in v12:
time: 239 us; the launch traced here: 237 us
  blocking collectives  76.8 us (32%)
  starting transfers between devices  71 us (30%)
  Pallas kernels  35.7 us (15%)
  waiting for transfers between devices  35.2 us (15%)
  between operations  15.1 us (6%)
  local copies, waits for them, and re-layouts  2.94 us (1%)
    ppermute x8, starting transfers between devices, step(): high[k] = lax.ppermute(high_from, z_axes, ring(n_z, -1))  48.8 us
    all_to_all x1, blocking collectives, per_device(): lax.all_to_all(share.reshape(n_z, -1, 128), z_axes, 0, 0)  21.3 us
    ppermute x8, waiting for transfers between devices, step(): high[k] = lax.ppermute(high_from, z_axes, ring(n_z, -1))  18.7 us
    all_to_all x1, blocking collectives, per_device(): lax.all_to_all(jnp.broadcast_to(share, (n_z,) + share.shape), z_axes, 0, 0)  17 us
    ppermute x8, starting transfers between devices, step(): low[k] = lax.ppermute(low_from, z_axes, ring(n_z, 1))  15.3 us
    all_to_all x1, blocking collectives, per_device(): lax.all_to_all(out.reshape(n_y, -1, 128), 'y', 0, 0)  14.3 us
    all_gather x1, blocking collectives, per_device(): block = lax.all_gather(frozen_down_weight.T, 'y', axis=0, tiled=True)  13.4 us
    pallas_call x2, Pallas kernels, part(): pl.pallas_call(functools.partial(part_kernel, plan, before is None), out_...  12 us
  transfers between devices with their start and end apart: 20, of which 13 were waited for; matrix products, arithmetic and copies ran while one was open for 0% of the time, Pallas kernels for 9%

profile of v12, /device:TPU:32, one launch (start us, length us, event | category | flops | bytes accessed | tf_op | source)
XLA Modules:
  0.0 237.3 jit_solution(18250210686865099868)
XLA Ops:
  7.2 0.0 all-gather.3.cloned.1.call-start
  7.2 0.7 all-gather.3.cloned.1.call-update
  7.9 0.0 all-gather.5.cloned.1.call-start
  7.9 0.7 all-gather.5.cloned.1.call-update
  8.6 13.4 %all_gather.10.refs_0_ = bf16[256,896]{1,0:T(8,128)(2,1)S(1)} all-gather(bf16[64,896]{1,0:T(8,128)(2,1)} %bitcast.19), channel_id=1, replica_groups=mesh['z'=16,'y'=4,'x'=4,'c'=2] {'y'}, dimensions={0}, use_global_device_ids=true | all-gather | bytes 573440 | tf_op jit(solution)/shard_map/all_gather | solution.py:348
  22.0 6.9 %collective-permute-start.4 = (bf16[256,896]{1,0:T(8,128)(2,1)S(1)}, bf16[256,896]{1,0:T(8,128)(2,1)S(1)}, u32[]{:S(2)}, u32[]{:S(2)}) collective-permute-start(bf16[256,896]{1,0:T(8,128)(2,1)S(1)} %all_gather.10.refs_0_), channel_id=1, source_target_pairs={{0,480},{32,0},{64,32},{96,64},{128,96},{160,128},{192,160},{224,1... | collective-permute-start | bytes 1376264 | tf_op jit(solution)/shard_map/ppermute | solution.py:362
  28.9 1.9 collective-permute-start
  30.8 4.0 %collective-permute-done.4.refs_2_ = bf16[256,896]{1,0:T(8,128)(2,1)S(1)} collective-permute-done((bf16[256,896]{1,0:T(8,128)(2,1)S(1)}, bf16[256,896]{1,0:T(8,128)(2,1)S(1)}, u32[]{:S(2)}, u32[]{:S(2)}) %collective-permute-start.4) | collective-permute-done | bytes 458784 | tf_op jit(solution)/shard_map/ppermute | solution.py:362
  34.9 8.6 %collective-permute-start.5 = (bf16[256,896]{1,0:T(8,128)(2,1)S(1)}, bf16[256,896]{1,0:T(8,128)(2,1)S(1)}, u32[]{:S(2)}, u32[]{:S(2)}) collective-permute-start(bf16[256,896]{1,0:T(8,128)(2,1)S(1)} %collective-permute-done.4.refs_2_), channel_id=1, source_target_pairs={{0,480},{32,0},{64,32},{96,64},{128,96},{160,128},{192,160},{224,1... | collective-permute-start | bytes 1376264 | tf_op jit(solution)/shard_map/ppermute | solution.py:362
  43.5 0.5 collective-permute-done.refs_1_
  44.0 1.9 collective-permute-start.1
  45.9 4.7 %collective-permute-done.5.refs_4_ = bf16[256,896]{1,0:T(8,128)(2,1)S(1)} collective-permute-done((bf16[256,896]{1,0:T(8,128)(2,1)S(1)}, bf16[256,896]{1,0:T(8,128)(2,1)S(1)}, u32[]{:S(2)}, u32[]{:S(2)}) %collective-permute-start.5) | collective-permute-done | bytes 458784 | tf_op jit(solution)/shard_map/ppermute | solution.py:362
  50.7 5.7 %collective-permute-start.6 = (bf16[256,896]{1,0:T(8,128)(2,1)S(1)}, bf16[256,896]{1,0:T(8,128)(2,1)S(1)}, u32[]{:S(2)}, u32[]{:S(2)}) collective-permute-start(bf16[256,896]{1,0:T(8,128)(2,1)S(1)} %collective-permute-done.5.refs_4_), channel_id=1, source_target_pairs={{0,480},{32,0},{64,32},{96,64},{128,96},{160,128},{192,160},{224,1... | collective-permute-start | bytes 1376264 | tf_op jit(solution)/shard_map/ppermute | solution.py:362
  56.4 0.5 collective-permute-done.1.refs_3_
  56.9 1.9 collective-permute-start.2
  58.8 3.9 %collective-permute-done.6.refs_6_ = bf16[256,896]{1,0:T(8,128)(2,1)S(1)} collective-permute-done((bf16[256,896]{1,0:T(8,128)(2,1)S(1)}, bf16[256,896]{1,0:T(8,128)(2,1)S(1)}, u32[]{:S(2)}, u32[]{:S(2)}) %collective-permute-start.6) | collective-permute-done | bytes 458784 | tf_op jit(solution)/shard_map/ppermute | solution.py:362
  62.7 5.7 %collective-permute-start.10 = (bf16[256,896]{1,0:T(8,128)(2,1)S(1)}, bf16[256,896]{1,0:T(8,128)(2,1)}, u32[]{:S(2)}, u32[]{:S(2)}) collective-permute-start(bf16[256,896]{1,0:T(8,128)(2,1)S(1)} %collective-permute-done.6.refs_6_), channel_id=1, source_target_pairs={{0,480},{32,0},{64,32},{96,64},{128,96},{160,128},{192,160},{224,1... | collective-permute-start | bytes 1376264 | tf_op jit(solution)/shard_map/ppermute | solution.py:362
  68.4 0.5 collective-permute-done.2.refs_5_
  68.9 1.9 collective-permute-start.3
  70.8 0.0 all-gather.3.cloned.1.call-done.gradient_ref.refs_0_.refs_1_
  70.8 0.0 copy-done
  70.8 0.0 copy-done.5
  70.9 6.1 %part_product.2.refs_6_ = f32[512,896]{1,0:T(8,128)} custom-call(s32[1]{0:T(128)} %bitcast.z_ref, bf16[512,4096]{1,0:T(8,128)(2,1)} %all-gather.3.cloned.1.call-done.gradient_ref.refs_0_.refs_1_, bf16[256,896]{1,0:T(8,128)(2,1)} %copy-done, bf16[256,896]{1,0:T(8,128)(2,1)} %copy-done.6, bf16[256,896]{1,0:T(8,128)(2,1)} %copy-done.5, ...), custom_call_target="tpu_custom_call" | custom-call | flops 1644167168 | bytes 6291456 | tf_op jit(solution)/shard_map/part_product/pallas_call | solution.py:415
  77.0 0.0 collective-permute-done.10.refs_1_
  77.0 5.5 %collective-permute-start.11 = (bf16[256,896]{1,0:T(8,128)(2,1)}, bf16[256,896]{1,0:T(8,128)(2,1)S(1)}, u32[]{:S(2)}, u32[]{:S(2)}) collective-permute-start(bf16[256,896]{1,0:T(8,128)(2,1)} %collective-permute-done.10.refs_1_), channel_id=1, source_target_pairs={{0,480},{32,0},{64,32},{96,64},{128,96},{160,128},{192,160},{224,1... | collective-permute-start | bytes 1376264 | tf_op jit(solution)/shard_map/ppermute | solution.py:362
  82.5 0.0 collective-permute-done.3.refs_0_
  82.5 1.9 collective-permute-start.7
  84.4 4.9 %gradient_side.1 = (bf16[16,512]{1,0:T(8,128)(2,1)}, bf16[512,16]{1,0:T(8,128)(2,1)}, f32[4,128,128]{2,1,0:T(8,128)}) custom-call(bf16[512,4096]{1,0:T(8,128)(2,1)} %all-gather.3.cloned.1.call-done.gradient_ref.refs_0_.refs_1_, bf16[512,4096]{1,0:T(8,128)(2,1)} %all-gather.3.cloned.1.call-done.gradient_ref.refs_0_.refs_1_, bf16[48,4096]{1,0:T(8,128)(2,1)} %bitcast.12), custom_call_target="tpu_custom_call" | custom-call | flops 603979776 | bytes 5242880 | tf_op jit(solution)/shard_map/gradient_side/pallas_call | solution.py:367
  89.4 0.0 collective-permute-done.11.refs_3_
  89.4 5.1 %collective-permute-start.12 = (bf16[256,896]{1,0:T(8,128)(2,1)S(1)}, bf16[256,896]{1,0:T(8,128)(2,1)S(1)}, u32[]{:S(2)}, u32[]{:S(2)}) collective-permute-start(bf16[256,896]{1,0:T(8,128)(2,1)S(1)} %collective-permute-done.11.refs_3_), channel_id=1, source_target_pairs={{0,480},{32,0},{64,32},{96,64},{128,96},{160,128},{192,160},{224,1... | collective-permute-start | bytes 1376264 | tf_op jit(solution)/shard_map/ppermute | solution.py:362
  94.5 0.0 collective-permute-done.7.refs_2_
  94.5 0.0 copy-start.12
  94.5 1.9 collective-permute-start.8
  96.4 5.5 %collective-permute-done.12.refs_5_ = bf16[256,896]{1,0:T(8,128)(2,1)S(1)} collective-permute-done((bf16[256,896]{1,0:T(8,128)(2,1)S(1)}, bf16[256,896]{1,0:T(8,128)(2,1)S(1)}, u32[]{:S(2)}, u32[]{:S(2)}) %collective-permute-start.12) | collective-permute-done | bytes 458784 | tf_op jit(solution)/shard_map/ppermute | solution.py:362
  102.0 5.0 %collective-permute-start.13 = (bf16[256,896]{1,0:T(8,128)(2,1)S(1)}, bf16[256,896]{1,0:T(8,128)(2,1)S(1)}, u32[]{:S(2)}, u32[]{:S(2)}) collective-permute-start(bf16[256,896]{1,0:T(8,128)(2,1)S(1)} %collective-permute-done.12.refs_5_), channel_id=1, source_target_pairs={{0,480},{32,0},{64,32},{96,64},{128,96},{160,128},{192,160},{224,1... | collective-permute-start | bytes 1376264 | tf_op jit(solution)/shard_map/ppermute | solution.py:362
  107.0 0.3 collective-permute-done.8.refs_4_
  107.2 1.9 collective-permute-start.9
  109.1 0.0 all-gather.5.cloned.1.call-done.refs_0_.refs_1_
  109.2 5.0 %normed_side.1 = (bf16[32,512]{1,0:T(8,128)(2,1)}, bf16[512,32]{1,0:T(8,128)(2,1)}, f32[4,128,128]{2,1,0:T(8,128)}) custom-call(bf16[512,4096]{1,0:T(8,128)(2,1)} %all-gather.5.cloned.1.call-done.refs_0_.refs_1_, bf16[512,4096]{1,0:T(8,128)(2,1)} %all-gather.5.cloned.1.call-done.refs_0_.refs_1_, bf16[48,4096]{1,0:T(8,128)(2,1)} %bitcast.13), custom_call_target="tpu_custom_call" | custom-call | flops 671088640 | bytes 5242880 | tf_op jit(solution)/shard_map/normed_side/pallas_call | solution.py:367
  114.1 0.0 copy-done.14
  114.1 0.4 collective-permute-done.13.refs_1_
  114.6 6.3 %collective-permute-start.15 = (bf16[128,896]{1,0:T(8,128)(2,1)S(1)}, bf16[128,896]{1,0:T(8,128)(2,1)S(1)}, u32[]{:S(2)}, u32[]{:S(2)}) collective-permute-start(bf16[128,896]{1,0:T(8,128)(2,1)S(1)} %slice.7), channel_id=1, source_target_pairs={{0,480},{32,0},{64,32},{96,64},{128,96},{160,128},{192,160},{224,1... | collective-permute-start | bytes 688136 | tf_op jit(solution)/shard_map/ppermute | solution.py:362
  121.0 0.3 collective-permute-done.9.refs_0_
  121.2 1.9 collective-permute-start.14
  123.2 5.9 %part_product.3.refs_4_ = f32[512,896]{1,0:T(8,128)} custom-call(s32[1]{0:T(128)} %bitcast.z_ref, bf16[512,4096]{1,0:T(8,128)(2,1)} %all-gather.3.cloned.1.call-done.gradient_ref.refs_0_.refs_1_, bf16[256,896]{1,0:T(8,128)(2,1)} %collective-permute-done.3.refs_0_, bf16[256,896]{1,0:T(8,128)(2,1)} %collective-permute-done.10.refs_1_, ...), custom_call_target="tpu_custom_call" | custom-call | flops 1409286144 | bytes 6291456 | tf_op jit(solution)/shard_map/part_product/pallas_call | solution.py:415
  129.1 0.0 collective-permute-done.15.refs_3_
  129.2 1.5 collective-permute-done.14.refs_2_
  130.7 0.7 copy-done.16
  131.4 7.8 %hidden_side.1 = (f32[4,48,896]{2,1,0:T(8,128)}, f32[64,512]{1,0:T(8,128)}) custom-call(s32[1]{0:T(128)} %bitcast.z_ref, bf16[512,4096]{1,0:T(8,128)(2,1)} %all-gather.3.cloned.1.call-done.gradient_ref.refs_0_.refs_1_, bf16[256,896]{1,0:T(8,128)(2,1)} %copy-done.3, bf16[256,896]{1,0:T(8,128)(2,1)} %copy-done.2, bf16[128,896]{1,0:T(8,128)(2,1)} %copy-done.16, ...), custom_call_target="tpu_custom_call" | custom-call | tf_op jit(solution)/shard_map/hidden_side/pallas_call | solution.py:459
  139.2 10.8 %all_to_all.30.shares_ref = f32[8,8,512]{2,1,0:T(8,128)} all-to-all(f32[8,8,512]{2,1,0:T(8,128)} %bitcast.18), channel_id=1, replica_groups=mesh['z'=16,'y'=4,'x'=4,'c'=2] {'x','c'}, dimensions={0} | all-to-all | bytes 262144 | tf_op jit(solution)/shard_map/all_to_all | solution.py:492
  149.9 1.6 share_sum.1
  151.5 3.4 %all-to-all-start.1 = ((f32[8,8,512]{2,1,0:T(8,128)}), f32[8,8,512]{2,1,0:T(8,128)S(1)}, u32[]{:S(2)}, u32[]{:S(2)}) async-start(f32[8,8,512]{2,1,0:T(8,128)} %share_sum.1), calls=%async_computation.1 | async-start | bytes 262144 | tf_op jit(solution)/shard_map/all_to_all | solution.py:500
  155.6 5.4 %all-to-all-done.1 = f32[8,8,512]{2,1,0:T(8,128)S(1)} async-done(((f32[8,8,512]{2,1,0:T(8,128)}), f32[8,8,512]{2,1,0:T(8,128)S(1)}, u32[]{:S(2)}, u32[]{:S(2)}) %all-to-all-start.1) | async-done | bytes 131104 | tf_op jit(solution)/shard_map/all_to_all | solution.py:500
  161.0 0.7 copy-done.4
  161.6 2.6 %clip_side.1 = f32[72,8,128]{2,1,0:T(8,128)} custom-call(f32[1]{0:T(128)S(6)} %copy.12.clip_ref, f32[64,512]{1,0:T(8,128)} %bitcast.16, f32[4,128,128]{2,1,0:T(8,128)} %get-tuple-element.29.normed_gram_hbm, f32[4,128,128]{2,1,0:T(8,128)} %get-tuple-element.30.gradient_gram_hbm, bf16[512,512]{1,0:T(8,128)(2,1)} %normed_hbm.1, bf16[512,512]{1,0:T(8,128)(2,1)} %gradient_hbm.1, ...), custom_call_target="tpu_custom_call" | custom-call | tf_op jit(solution)/shard_map/clip_side/pallas_call | solution.py:505
  164.2 14.3 %all_to_all.31 = f32[4,144,128]{2,1,0:T(8,128)S(1)} all-to-all(f32[4,144,128]{2,1,0:T(8,128)} %bitcast.14), channel_id=1, replica_groups=mesh['z'=16,'y'=4,'x'=4,'c'=2] {'y'}, dimensions={0} | all-to-all | bytes 589824 | tf_op jit(solution)/shard_map/all_to_all | solution.py:533
  178.6 21.3 %all_to_all.32 = f32[16,9,128]{2,1,0:T(8,128)S(1)} all-to-all(f32[16,9,128]{2,1,0:T(8,128)S(1)} %reshape.50), channel_id=1, replica_groups=mesh['z'=16,'y'=4,'x'=4,'c'=2] {'z'}, dimensions={0} | all-to-all | bytes 147456 | tf_op jit(solution)/shard_map/all_to_all | solution.py:534
  199.9 17.0 %all_to_all.33 = f32[16,9,128]{2,1,0:T(8,128)S(1)} all-to-all(f32[16,9,128]{2,1,0:T(8,128)S(1)} %broadcast_in_dim.6), channel_id=1, replica_groups=mesh['z'=16,'y'=4,'x'=4,'c'=2] {'z'}, dimensions={0} | all-to-all | bytes 147456 | tf_op jit(solution)/shard_map/all_to_all | solution.py:535
  217.0 0.7 broadcast_in_dim.7
  217.7 3.5 %all-to-all-start.5 = ((f32[4,144,128]{2,1,0:T(8,128)}), f32[4,144,128]{2,1,0:T(8,128)S(1)}, u32[]{:S(2)}, u32[]{:S(2)}) async-start(f32[4,144,128]{2,1,0:T(8,128)} %broadcast_in_dim.7), calls=%async_computation.5 | async-start | bytes 589824 | tf_op jit(solution)/shard_map/all_to_all | solution.py:538
  221.1 0.7 pad_maximum_fusion.bound_ref
  221.8 6.2 %all-to-all-done.5 = f32[4,144,128]{2,1,0:T(8,128)S(1)} async-done(((f32[4,144,128]{2,1,0:T(8,128)}), f32[4,144,128]{2,1,0:T(8,128)S(1)}, u32[]{:S(2)}, u32[]{:S(2)}) %all-to-all-start.5) | async-done | bytes 294944 | tf_op jit(solution)/shard_map/all_to_all | solution.py:538
  228.0 0.7 copy-done.1
  228.7 1.8 outputs.1
  (34 shorter events, 0.2 us)
Async XLA Ops:
  7.2 63.7 %all-gather.3.cloned.1.call-start = ((), (), s32[]{:S(2)}) async-start(), calls=%async_computation.6 | async-start | bytes 4718592 | tf_op jit(solution)/shard_map/all_gather | solution.py:347
  7.9 101.3 %all-gather.5.cloned.1.call-start = ((), (), s32[]{:S(2)}) async-start(), calls=%async_computation.7 | async-start | bytes 4718592 | tf_op jit(solution)/shard_map/all_gather | solution.py:349
  22.0 48.8 %copy-start = (bf16[256,896]{1,0:T(8,128)(2,1)}, bf16[256,896]{1,0:T(8,128)(2,1)S(1)}, u32[]{:S(2)}) copy-start(bf16[256,896]{1,0:T(8,128)(2,1)S(1)} %all_gather.10.refs_0_) | copy-start | bytes 1376260
  22.0 12.8 %collective-permute-start.4 = (bf16[256,896]{1,0:T(8,128)(2,1)S(1)}, bf16[256,896]{1,0:T(8,128)(2,1)S(1)}, u32[]{:S(2)}, u32[]{:S(2)}) collective-permute-start(bf16[256,896]{1,0:T(8,128)(2,1)S(1)} %all_gather.10.refs_0_), channel_id=1, source_target_pairs={{0,480},{32,0},{64,32},{96,64},{128,96},{160,128},{192,160},{224,1... | collective-permute-start | bytes 1376264 | tf_op jit(solution)/shard_map/ppermute | solution.py:362
  28.9 15.1 %collective-permute-start = (bf16[256,896]{1,0:T(8,128)(2,1)S(1)}, bf16[256,896]{1,0:T(8,128)(2,1)S(1)}, u32[]{:S(2)}, u32[]{:S(2)}) collective-permute-start(bf16[256,896]{1,0:T(8,128)(2,1)S(1)} %all_gather.10.refs_0_), channel_id=1, source_target_pairs={{0,32},{32,64},{64,96},{96,128},{128,160},{160,192},{192,224},{224... | collective-permute-start | bytes 1376264 | tf_op jit(solution)/shard_map/ppermute | solution.py:361
  34.9 36.0 %copy-start.5 = (bf16[256,896]{1,0:T(8,128)(2,1)}, bf16[256,896]{1,0:T(8,128)(2,1)S(1)}, u32[]{:S(2)}) copy-start(bf16[256,896]{1,0:T(8,128)(2,1)S(1)} %collective-permute-done.4.refs_2_) | copy-start | bytes 1376260
  34.9 15.8 %collective-permute-start.5 = (bf16[256,896]{1,0:T(8,128)(2,1)S(1)}, bf16[256,896]{1,0:T(8,128)(2,1)S(1)}, u32[]{:S(2)}, u32[]{:S(2)}) collective-permute-start(bf16[256,896]{1,0:T(8,128)(2,1)S(1)} %collective-permute-done.4.refs_2_), channel_id=1, source_target_pairs={{0,480},{32,0},{64,32},{96,64},{128,96},{160,128},{192,160},{224,1... | collective-permute-start | bytes 1376264 | tf_op jit(solution)/shard_map/ppermute | solution.py:362
  44.0 26.9 %copy-start.6 = (bf16[256,896]{1,0:T(8,128)(2,1)}, bf16[256,896]{1,0:T(8,128)(2,1)S(1)}, u32[]{:S(2)}) copy-start(bf16[256,896]{1,0:T(8,128)(2,1)S(1)} %collective-permute-done.refs_1_) | copy-start | bytes 1376260
  44.0 12.9 %collective-permute-start.1 = (bf16[256,896]{1,0:T(8,128)(2,1)S(1)}, bf16[256,896]{1,0:T(8,128)(2,1)S(1)}, u32[]{:S(2)}, u32[]{:S(2)}) collective-permute-start(bf16[256,896]{1,0:T(8,128)(2,1)S(1)} %collective-permute-done.refs_1_), channel_id=1, source_target_pairs={{0,32},{32,64},{64,96},{96,128},{128,160},{160,192},{192,224},{224... | collective-permute-start | bytes 1376264 | tf_op jit(solution)/shard_map/ppermute | solution.py:361
  50.7 20.2 %copy-start.7 = (bf16[256,896]{1,0:T(8,128)(2,1)}, bf16[256,896]{1,0:T(8,128)(2,1)S(1)}, u32[]{:S(2)}) copy-start(bf16[256,896]{1,0:T(8,128)(2,1)S(1)} %collective-permute-done.5.refs_4_) | copy-start | bytes 1376260
  50.7 12.0 %collective-permute-start.6 = (bf16[256,896]{1,0:T(8,128)(2,1)S(1)}, bf16[256,896]{1,0:T(8,128)(2,1)S(1)}, u32[]{:S(2)}, u32[]{:S(2)}) collective-permute-start(bf16[256,896]{1,0:T(8,128)(2,1)S(1)} %collective-permute-done.5.refs_4_), channel_id=1, source_target_pairs={{0,480},{32,0},{64,32},{96,64},{128,96},{160,128},{192,160},{224,1... | collective-permute-start | bytes 1376264 | tf_op jit(solution)/shard_map/ppermute | solution.py:362
  56.9 14.0 %copy-start.8 = (bf16[256,896]{1,0:T(8,128)(2,1)}, bf16[256,896]{1,0:T(8,128)(2,1)S(1)}, u32[]{:S(2)}) copy-start(bf16[256,896]{1,0:T(8,128)(2,1)S(1)} %collective-permute-done.1.refs_3_) | copy-start | bytes 1376260
  56.9 12.0 %collective-permute-start.2 = (bf16[256,896]{1,0:T(8,128)(2,1)S(1)}, bf16[256,896]{1,0:T(8,128)(2,1)S(1)}, u32[]{:S(2)}, u32[]{:S(2)}) collective-permute-start(bf16[256,896]{1,0:T(8,128)(2,1)S(1)} %collective-permute-done.1.refs_3_), channel_id=1, source_target_pairs={{0,32},{32,64},{64,96},{96,128},{128,160},{160,192},{192,224},{224... | collective-permute-start | bytes 1376264 | tf_op jit(solution)/shard_map/ppermute | solution.py:361
  62.7 8.2 %copy-start.10 = (bf16[256,896]{1,0:T(8,128)(2,1)}, bf16[256,896]{1,0:T(8,128)(2,1)S(1)}, u32[]{:S(2)}) copy-start(bf16[256,896]{1,0:T(8,128)(2,1)S(1)} %collective-permute-done.6.refs_6_) | copy-start | bytes 1376260
  62.7 14.3 %collective-permute-start.10 = (bf16[256,896]{1,0:T(8,128)(2,1)S(1)}, bf16[256,896]{1,0:T(8,128)(2,1)}, u32[]{:S(2)}, u32[]{:S(2)}) collective-permute-start(bf16[256,896]{1,0:T(8,128)(2,1)S(1)} %collective-permute-done.6.refs_6_), channel_id=1, source_target_pairs={{0,480},{32,0},{64,32},{96,64},{128,96},{160,128},{192,160},{224,1... | collective-permute-start | bytes 1376264 | tf_op jit(solution)/shard_map/ppermute | solution.py:362
  68.9 2.0 copy-start.9
  68.9 13.6 %collective-permute-start.3 = (bf16[256,896]{1,0:T(8,128)(2,1)S(1)}, bf16[256,896]{1,0:T(8,128)(2,1)}, u32[]{:S(2)}, u32[]{:S(2)}) collective-permute-start(bf16[256,896]{1,0:T(8,128)(2,1)S(1)} %collective-permute-done.2.refs_5_), channel_id=1, source_target_pairs={{0,32},{32,64},{64,96},{96,128},{128,160},{160,192},{192,224},{224... | collective-permute-start | bytes 1376264 | tf_op jit(solution)/shard_map/ppermute | solution.py:361
  77.0 12.4 %collective-permute-start.11 = (bf16[256,896]{1,0:T(8,128)(2,1)}, bf16[256,896]{1,0:T(8,128)(2,1)S(1)}, u32[]{:S(2)}, u32[]{:S(2)}) collective-permute-start(bf16[256,896]{1,0:T(8,128)(2,1)} %collective-permute-done.10.refs_1_), channel_id=1, source_target_pairs={{0,480},{32,0},{64,32},{96,64},{128,96},{160,128},{192,160},{224,1... | collective-permute-start | bytes 1376264 | tf_op jit(solution)/shard_map/ppermute | solution.py:362
  82.5 12.0 %collective-permute-start.7 = (bf16[256,896]{1,0:T(8,128)(2,1)}, bf16[256,896]{1,0:T(8,128)(2,1)S(1)}, u32[]{:S(2)}, u32[]{:S(2)}) collective-permute-start(bf16[256,896]{1,0:T(8,128)(2,1)} %collective-permute-done.3.refs_0_), channel_id=1, source_target_pairs={{0,32},{32,64},{64,96},{96,128},{128,160},{160,192},{192,224},{224... | collective-permute-start | bytes 1376264 | tf_op jit(solution)/shard_map/ppermute | solution.py:361
  89.4 24.8 %copy-start.11 = (bf16[256,896]{1,0:T(8,128)(2,1)}, bf16[256,896]{1,0:T(8,128)(2,1)S(1)}, u32[]{:S(2)}) copy-start(bf16[256,896]{1,0:T(8,128)(2,1)S(1)} %collective-permute-done.11.refs_3_) | copy-start | bytes 1376260
  89.4 12.6 %collective-permute-start.12 = (bf16[256,896]{1,0:T(8,128)(2,1)S(1)}, bf16[256,896]{1,0:T(8,128)(2,1)S(1)}, u32[]{:S(2)}, u32[]{:S(2)}) collective-permute-start(bf16[256,896]{1,0:T(8,128)(2,1)S(1)} %collective-permute-done.11.refs_3_), channel_id=1, source_target_pairs={{0,480},{32,0},{64,32},{96,64},{128,96},{160,128},{192,160},{224,1... | collective-permute-start | bytes 1376264 | tf_op jit(solution)/shard_map/ppermute | solution.py:362
  94.5 19.6 %copy-start.12 = (bf16[256,896]{1,0:T(8,128)(2,1)}, bf16[256,896]{1,0:T(8,128)(2,1)S(1)}, u32[]{:S(2)}) copy-start(bf16[256,896]{1,0:T(8,128)(2,1)S(1)} %collective-permute-done.7.refs_2_) | copy-start | bytes 1376260
  94.5 12.7 %collective-permute-start.8 = (bf16[256,896]{1,0:T(8,128)(2,1)S(1)}, bf16[256,896]{1,0:T(8,128)(2,1)S(1)}, u32[]{:S(2)}, u32[]{:S(2)}) collective-permute-start(bf16[256,896]{1,0:T(8,128)(2,1)S(1)} %collective-permute-done.7.refs_2_), channel_id=1, source_target_pairs={{0,32},{32,64},{64,96},{96,128},{128,160},{160,192},{192,224},{224... | collective-permute-start | bytes 1376264 | tf_op jit(solution)/shard_map/ppermute | solution.py:361
  102.0 12.2 %copy-start.13 = (bf16[256,896]{1,0:T(8,128)(2,1)}, bf16[256,896]{1,0:T(8,128)(2,1)S(1)}, u32[]{:S(2)}) copy-start(bf16[256,896]{1,0:T(8,128)(2,1)S(1)} %collective-permute-done.12.refs_5_) | copy-start | bytes 1376260
  102.0 12.6 %collective-permute-start.13 = (bf16[256,896]{1,0:T(8,128)(2,1)S(1)}, bf16[256,896]{1,0:T(8,128)(2,1)S(1)}, u32[]{:S(2)}, u32[]{:S(2)}) collective-permute-start(bf16[256,896]{1,0:T(8,128)(2,1)S(1)} %collective-permute-done.12.refs_5_), channel_id=1, source_target_pairs={{0,480},{32,0},{64,32},{96,64},{128,96},{160,128},{192,160},{224,1... | collective-permute-start | bytes 1376264 | tf_op jit(solution)/shard_map/ppermute | solution.py:362
  107.2 6.9 %copy-start.14 = (bf16[256,896]{1,0:T(8,128)(2,1)}, bf16[256,896]{1,0:T(8,128)(2,1)S(1)}, u32[]{:S(2)}) copy-start(bf16[256,896]{1,0:T(8,128)(2,1)S(1)} %collective-permute-done.8.refs_4_) | copy-start | bytes 1376260
  107.2 14.0 %collective-permute-start.9 = (bf16[256,896]{1,0:T(8,128)(2,1)S(1)}, bf16[256,896]{1,0:T(8,128)(2,1)S(1)}, u32[]{:S(2)}, u32[]{:S(2)}) collective-permute-start(bf16[256,896]{1,0:T(8,128)(2,1)S(1)} %collective-permute-done.8.refs_4_), channel_id=1, source_target_pairs={{0,32},{32,64},{64,96},{96,128},{128,160},{160,192},{192,224},{224... | collective-permute-start | bytes 1376264 | tf_op jit(solution)/shard_map/ppermute | solution.py:361
  114.6 14.5 %copy-start.2 = (bf16[256,896]{1,0:T(8,128)(2,1)}, bf16[256,896]{1,0:T(8,128)(2,1)S(1)}, u32[]{:S(2)}) copy-start(bf16[256,896]{1,0:T(8,128)(2,1)S(1)} %collective-permute-done.13.refs_1_) | copy-start | bytes 1376260
  114.6 14.5 %collective-permute-start.15 = (bf16[128,896]{1,0:T(8,128)(2,1)S(1)}, bf16[128,896]{1,0:T(8,128)(2,1)S(1)}, u32[]{:S(2)}, u32[]{:S(2)}) collective-permute-start(bf16[128,896]{1,0:T(8,128)(2,1)S(1)} %slice.7), channel_id=1, source_target_pairs={{0,480},{32,0},{64,32},{96,64},{128,96},{160,128},{192,160},{224,1... | collective-permute-start | bytes 688136 | tf_op jit(solution)/shard_map/ppermute | solution.py:362
  121.2 7.9 %copy-start.3 = (bf16[256,896]{1,0:T(8,128)(2,1)}, bf16[256,896]{1,0:T(8,128)(2,1)S(1)}, u32[]{:S(2)}) copy-start(bf16[256,896]{1,0:T(8,128)(2,1)S(1)} %collective-permute-done.9.refs_0_) | copy-start | bytes 1376260
  121.2 9.4 %collective-permute-start.14 = (bf16[128,896]{1,0:T(8,128)(2,1)S(1)}, bf16[128,896]{1,0:T(8,128)(2,1)S(1)}, u32[]{:S(2)}, u32[]{:S(2)}) collective-permute-start(bf16[128,896]{1,0:T(8,128)(2,1)S(1)} %slice.6), channel_id=1, source_target_pairs={{0,32},{32,64},{64,96},{96,128},{128,160},{160,192},{192,224},{224... | collective-permute-start | bytes 688136 | tf_op jit(solution)/shard_map/ppermute | solution.py:361
  129.2 1.5 copy-start.15
  130.7 0.7 copy-start.16
  151.5 9.4 %all-to-all-start.1 = ((f32[8,8,512]{2,1,0:T(8,128)}), f32[8,8,512]{2,1,0:T(8,128)S(1)}, u32[]{:S(2)}, u32[]{:S(2)}) async-start(f32[8,8,512]{2,1,0:T(8,128)} %share_sum.1), calls=%async_computation.1 | async-start | bytes 262144 | tf_op jit(solution)/shard_map/all_to_all | solution.py:500
  161.0 0.7 copy-start.4
  217.7 10.3 %all-to-all-start.5 = ((f32[4,144,128]{2,1,0:T(8,128)}), f32[4,144,128]{2,1,0:T(8,128)S(1)}, u32[]{:S(2)}, u32[]{:S(2)}) async-start(f32[4,144,128]{2,1,0:T(8,128)} %broadcast_in_dim.7), calls=%async_computation.5 | async-start | bytes 589824 | tf_op jit(solution)/shard_map/all_to_all | solution.py:538
  228.0 0.7 copy-start.1
Sparse Core Ops, SparseCore 0:
  10.1 43.8 all-gather.2
  56.2 39.7 all-gather.4

commit v13 on v12

--- a/solution.py
+++ b/solution.py
@@ -95,20 +95,28 @@
     block_refs, refs = refs[:n_blocks], refs[n_blocks:]
     if not first:
         before_ref, refs = refs[0], refs[1:]
-    out_ref, total, left, right, sems, out_sems = refs
-    copies = sum(fetch_blocks(plan, z_ref, gradient_ref, block_refs, left, right, sems), [])
+    out_ref, total, front, left, right, sems, out_sems = refs
+    fetched = fetch_blocks(plan, z_ref, gradient_ref, block_refs, left, right, sems)
+    early = n_blocks // 2 + 1
+    head, tail = sum(fetched[:early], []), sum(fetched[early:], [])
     if not first:
-        copies += copy_rows(before_ref, total, sems, 4 * n_blocks, 4)
-    for copy in copies:
+        tail += copy_rows(before_ref, total, sems, 4 * n_blocks, 4)
+    for copy in head + tail:
         copy.start()
-    for copy in copies:
+    for copy in head:
+        copy.wait()
+    split = early * plan["rows"]
+    front[...] = jnp.dot(left[:, :split], right[:split, :], preferred_element_type=F32)
+    for copy in tail:
         copy.wait()
 
     writes = []
     hidden = total.shape[1]
     for i, start in enumerate(range(0, hidden, 512)):
         cols = slice(start, min(start + 512, hidden))
-        product = jnp.dot(left[...], right[:, cols], preferred_element_type=F32)
+        product = front[:, cols] + jnp.dot(
+            left[:, split:], right[split:, cols], preferred_element_type=F32
+        )
         total[:, cols] = product if first else total[:, cols] + product
         write = pltpu.make_async_copy(total.at[:, cols], out_ref.at[:, cols], out_sems.at[i])
         write.start()
@@ -298,27 +306,6 @@
         out_ref[t] = value
 
 
-def share_kernel(shares_ref, out_ref):
-    total = shares_ref[0]
-    for i in range(1, shares_ref.shape[0]):
-        total = total + shares_ref[i]
-    for i in range(out_ref.shape[0]):
-        out_ref[i] = total
-
-
-def output_kernel(bound_ref, tiles_ref, wide_noise_ref, hidden_noise_ref, wide_ref, hidden_ref):
-    count = bound_ref[1]
-    lanes = wide_ref.shape[1] // 128
-    every = lanes + hidden_ref.shape[1] // 128
-    for t in range(every * wide_ref.shape[0] // 8):
-        r, c = divmod(t, every)
-        out, noise, c = (
-            (wide_ref, wide_noise_ref, c) if c < lanes else (hidden_ref, hidden_noise_ref, c - lanes)
-        )
-        at = (slice(8 * r, 8 * r + 8), slice(128 * c, 128 * c + 128))
-        out[at] = (tiles_ref[t] + bound_ref[0] * noise[at]) / count
-
-
 def ring(size, by):
     return [(i, (i + by) % size) for i in range(size)]
 
@@ -363,7 +350,7 @@
 
     def side(values, first, count, name):
         width = values.shape[1]
-        chunk = 1024
+        chunk = 2048
         return pl.pallas_call(
             functools.partial(side_kernel, sequences // 2),
             out_shape=(
@@ -417,7 +404,8 @@
             out_shape=jax.ShapeDtypeStruct((tokens, hidden), F32),
             in_specs=[smem] + [hbm] * (n + 1 + len(given)),
             out_specs=hbm,
-            scratch_shapes=[pltpu.VMEM((tokens, hidden), F32)] + scratch(n * rows, 4 * n + 4),
+            scratch_shapes=[pltpu.VMEM((tokens, hidden), F32)] * 2
+            + scratch(n * rows, 4 * n + 4),
             compiler_params=params,
             cost_estimate=pl.CostEstimate(
                 flops=2 * tokens * n * rows * hidden,
@@ -489,15 +477,11 @@
         lora_t,
     )
 
-    shares = lax.all_to_all(mids.reshape(n_tensor, 8, tokens), tensor_axes, 0, 0)
-    shares = pl.pallas_call(
-        share_kernel,
-        out_shape=jax.ShapeDtypeStruct(shares.shape, F32),
-        in_specs=[vmem],
-        out_specs=vmem,
-        name="share_sum",
-    )(shares)
-    mids = lax.all_to_all(shares, tensor_axes, 0, 0).reshape(8 * n_tensor, tokens)
+    pieces = lax.all_to_all(mids.reshape(n_tensor, 8, tokens), tensor_axes, 0, 0)
+    piece = jnp.sum(pieces, axis=0)
+    mids = lax.all_to_all(
+        jnp.broadcast_to(piece, (n_tensor,) + piece.shape), tensor_axes, 0, 0
+    ).reshape(8 * n_tensor, tokens)
 
     lanes = (local_width + hidden) // 128
     tiles = 6 * lanes
@@ -536,25 +520,19 @@
         jnp.broadcast_to(share, (n_z,) + share.shape), z_axes, 0, 0
     ).reshape(-1, 128)
     whole = lax.all_to_all(jnp.broadcast_to(share, (n_y,) + share.shape), "y", 0, 0)
-    count = sequences * n_z * n_y
-    wide, inner = pl.pallas_call(
-        output_kernel,
-        out_shape=(
-            jax.ShapeDtypeStruct((3 * RANK, local_width), F32),
-            jax.ShapeDtypeStruct((3 * RANK, hidden), F32),
-        ),
-        in_specs=[smem] + [vmem] * 3,
-        out_specs=(vmem, vmem),
-        name="outputs",
-    )(
-        jnp.concatenate([clipping_limit, jnp.full((1,), count, F32)]),
-        whole.reshape(padded, 8, 128),
-        width_noise_draw.reshape(3 * RANK, local_width),
-        hidden_noise_draw.reshape(3 * RANK, hidden),
-    )
+    total = (
+        whole.reshape(padded, 8, 128)[:tiles]
+        .reshape(6, lanes, 8, 128)
+        .transpose(0, 2, 1, 3)
+        .reshape(3, RANK, lanes * 128)
+    )
+    count = sequences * n_z * sizes["y"]
+    bound = clipping_limit[0]
+    wide = total[:, :, :local_width]
+    inner = total[:, :, local_width : local_width + hidden]
     return (
-        wide.reshape(3, RANK, local_width),
-        inner.reshape(3, RANK, hidden),
+        (wide + bound * width_noise_draw) / count,
+        (inner + bound * hidden_noise_draw) / count,
     )
 
 

time: 239 us -> 235 us (0.983)
  blocking collectives: 76.8 us -> 86.6 us
  Pallas kernels: 35.7 us -> 29.1 us
  starting transfers between devices: 71 us -> 67.4 us
  waiting for transfers between devices: 35.2 us -> 31.7 us
    all_to_all x0 -> x1, blocking collectives: none -> 9.25 us  [per_device(): lax.all_to_all(jnp.broadcast_to(share, (n_y,) + share.shape), 'y', 0, 0)]
    all_to_all x2 -> x1, waiting for transfers between devices: 11.6 us -> 5.41 us  [per_device(): lax.all_to_all(jnp.broadcast_to(piece, (n_tensor,) + piece.shape), tensor...]
    all_to_all x2 -> x1, starting transfers between devices: 6.82 us -> 3.37 us  [per_device(): lax.all_to_all(jnp.broadcast_to(piece, (n_tensor,) + piece.shape), tensor...]
    pallas_call x2 -> x0, Pallas kernels: 3.37 us -> none  [the longest x1 1.8 us: per_device(): pl.pallas_call(output_kernel, out_shape=(jax.ShapeDtypeStruct((3 * RANK,...]
  transfers between devices with their start and end apart: 20 -> 19, of which waited for: 13 -> 14; matrix products, arithmetic and copies ran while one was open for 0% -> 0% of each run, Pallas kernels for 9% -> 8%
where the time goes in v13:
time: 235 us; the launch traced here: 234 us
  blocking collectives  86.6 us (37%)
  starting transfers between devices  67.4 us (29%)
  waiting for transfers between devices  31.7 us (13%)
  Pallas kernels  29.1 us (12%)
  between operations  15.1 us (6%)
    ppermute x8, starting transfers between devices, step(): high[k] = lax.ppermute(high_from, z_axes, ring(n_z, -1))  48.6 us
    all_to_all x1, blocking collectives, per_device(): lax.all_to_all(share.reshape(n_z, -1, 128), z_axes, 0, 0)  21.1 us
    ppermute x8, waiting for transfers between devices, step(): high[k] = lax.ppermute(high_from, z_axes, ring(n_z, -1))  19.2 us
    all_to_all x1, blocking collectives, per_device(): lax.all_to_all(jnp.broadcast_to(share, (n_z,) + share.shape), z_axes, 0, 0)  17 us
    ppermute x8, starting transfers between devices, step(): low[k] = lax.ppermute(low_from, z_axes, ring(n_z, 1))  15.3 us
    all_to_all x1, blocking collectives, per_device(): lax.all_to_all(out.reshape(n_y, -1, 128), 'y', 0, 0)  14.4 us
    all_gather x1, blocking collectives, per_device(): block = lax.all_gather(frozen_down_weight.T, 'y', axis=0, tiled=True)  13.4 us
    all_to_all x1, blocking collectives, per_device(): lax.all_to_all(mids.reshape(n_tensor, 8, tokens), tensor_axes, 0, 0)  11.5 us
  transfers between devices with their start and end apart: 19, of which 14 were waited for; matrix products, arithmetic and copies ran while one was open for 0% of the time, Pallas kernels for 8%

profile of v13, /device:TPU:32, one launch (start us, length us, event | category | flops | bytes accessed | tf_op | source)
XLA Modules:
  0.0 233.6 jit_solution(357351935551724367)
XLA Ops:
  7.2 0.0 all-gather.3.cloned.1.call-start
  7.2 0.7 all-gather.3.cloned.1.call-update
  7.9 0.0 all-gather.5.cloned.1.call-start
  7.9 0.7 all-gather.5.cloned.1.call-update
  8.6 13.4 %all_gather.10.refs_0_ = bf16[256,896]{1,0:T(8,128)(2,1)S(1)} all-gather(bf16[64,896]{1,0:T(8,128)(2,1)} %bitcast.24), channel_id=1, replica_groups=mesh['z'=16,'y'=4,'x'=4,'c'=2] {'y'}, dimensions={0}, use_global_device_ids=true | all-gather | bytes 573440 | tf_op jit(solution)/shard_map/all_gather | solution.py:335
  22.0 6.9 %collective-permute-start.4 = (bf16[256,896]{1,0:T(8,128)(2,1)S(1)}, bf16[256,896]{1,0:T(8,128)(2,1)S(1)}, u32[]{:S(2)}, u32[]{:S(2)}) collective-permute-start(bf16[256,896]{1,0:T(8,128)(2,1)S(1)} %all_gather.10.refs_0_), channel_id=1, source_target_pairs={{0,480},{32,0},{64,32},{96,64},{128,96},{160,128},{192,160},{224,1... | collective-permute-start | bytes 1376264 | tf_op jit(solution)/shard_map/ppermute | solution.py:349
  28.9 1.9 collective-permute-start
  30.8 4.0 %collective-permute-done.4.refs_2_ = bf16[256,896]{1,0:T(8,128)(2,1)S(1)} collective-permute-done((bf16[256,896]{1,0:T(8,128)(2,1)S(1)}, bf16[256,896]{1,0:T(8,128)(2,1)S(1)}, u32[]{:S(2)}, u32[]{:S(2)}) %collective-permute-start.4) | collective-permute-done | bytes 458784 | tf_op jit(solution)/shard_map/ppermute | solution.py:349
  34.9 8.6 %collective-permute-start.5 = (bf16[256,896]{1,0:T(8,128)(2,1)S(1)}, bf16[256,896]{1,0:T(8,128)(2,1)S(1)}, u32[]{:S(2)}, u32[]{:S(2)}) collective-permute-start(bf16[256,896]{1,0:T(8,128)(2,1)S(1)} %collective-permute-done.4.refs_2_), channel_id=1, source_target_pairs={{0,480},{32,0},{64,32},{96,64},{128,96},{160,128},{192,160},{224,1... | collective-permute-start | bytes 1376264 | tf_op jit(solution)/shard_map/ppermute | solution.py:349
  43.5 0.5 collective-permute-done.refs_1_
  44.0 1.9 collective-permute-start.1
  45.9 4.7 %collective-permute-done.5.refs_4_ = bf16[256,896]{1,0:T(8,128)(2,1)S(1)} collective-permute-done((bf16[256,896]{1,0:T(8,128)(2,1)S(1)}, bf16[256,896]{1,0:T(8,128)(2,1)S(1)}, u32[]{:S(2)}, u32[]{:S(2)}) %collective-permute-start.5) | collective-permute-done | bytes 458784 | tf_op jit(solution)/shard_map/ppermute | solution.py:349
  50.7 5.7 %collective-permute-start.6 = (bf16[256,896]{1,0:T(8,128)(2,1)S(1)}, bf16[256,896]{1,0:T(8,128)(2,1)S(1)}, u32[]{:S(2)}, u32[]{:S(2)}) collective-permute-start(bf16[256,896]{1,0:T(8,128)(2,1)S(1)} %collective-permute-done.5.refs_4_), channel_id=1, source_target_pairs={{0,480},{32,0},{64,32},{96,64},{128,96},{160,128},{192,160},{224,1... | collective-permute-start | bytes 1376264 | tf_op jit(solution)/shard_map/ppermute | solution.py:349
  56.4 0.5 collective-permute-done.1.refs_3_
  56.9 1.9 collective-permute-start.2
  58.8 3.9 %collective-permute-done.6.refs_6_ = bf16[256,896]{1,0:T(8,128)(2,1)S(1)} collective-permute-done((bf16[256,896]{1,0:T(8,128)(2,1)S(1)}, bf16[256,896]{1,0:T(8,128)(2,1)S(1)}, u32[]{:S(2)}, u32[]{:S(2)}) %collective-permute-start.6) | collective-permute-done | bytes 458784 | tf_op jit(solution)/shard_map/ppermute | solution.py:349
  62.7 5.7 %collective-permute-start.10 = (bf16[256,896]{1,0:T(8,128)(2,1)S(1)}, bf16[256,896]{1,0:T(8,128)(2,1)}, u32[]{:S(2)}, u32[]{:S(2)}) collective-permute-start(bf16[256,896]{1,0:T(8,128)(2,1)S(1)} %collective-permute-done.6.refs_6_), channel_id=1, source_target_pairs={{0,480},{32,0},{64,32},{96,64},{128,96},{160,128},{192,160},{224,1... | collective-permute-start | bytes 1376264 | tf_op jit(solution)/shard_map/ppermute | solution.py:349
  68.4 0.5 collective-permute-done.2.refs_5_
  68.9 1.9 collective-permute-start.3
  70.8 0.0 all-gather.3.cloned.1.call-done.gradient_ref.refs_0_.refs_1_
  70.8 0.0 copy-done
  70.8 0.0 copy-done.4
  70.9 5.3 %part_product.2.refs_6_ = f32[512,896]{1,0:T(8,128)} custom-call(s32[1]{0:T(128)} %bitcast.z_ref, bf16[512,4096]{1,0:T(8,128)(2,1)} %all-gather.3.cloned.1.call-done.gradient_ref.refs_0_.refs_1_, bf16[256,896]{1,0:T(8,128)(2,1)} %copy-done, bf16[256,896]{1,0:T(8,128)(2,1)} %copy-done.5, bf16[256,896]{1,0:T(8,128)(2,1)} %copy-done.4, ...), custom_call_target="tpu_custom_call" | custom-call | flops 1644167168 | bytes 6291456 | tf_op jit(solution)/shard_map/part_product/pallas_call | solution.py:402
  76.3 0.0 collective-permute-done.10.refs_1_
  76.3 5.3 %collective-permute-start.11 = (bf16[256,896]{1,0:T(8,128)(2,1)}, bf16[256,896]{1,0:T(8,128)(2,1)S(1)}, u32[]{:S(2)}, u32[]{:S(2)}) collective-permute-start(bf16[256,896]{1,0:T(8,128)(2,1)} %collective-permute-done.10.refs_1_), channel_id=1, source_target_pairs={{0,480},{32,0},{64,32},{96,64},{128,96},{160,128},{192,160},{224,1... | collective-permute-start | bytes 1376264 | tf_op jit(solution)/shard_map/ppermute | solution.py:349
  81.5 0.0 collective-permute-done.3.refs_0_
  81.6 1.9 collective-permute-start.7
  83.5 4.1 %gradient_side.1 = (bf16[16,512]{1,0:T(8,128)(2,1)}, bf16[512,16]{1,0:T(8,128)(2,1)}, f32[4,128,128]{2,1,0:T(8,128)}) custom-call(bf16[512,4096]{1,0:T(8,128)(2,1)} %all-gather.3.cloned.1.call-done.gradient_ref.refs_0_.refs_1_, bf16[512,4096]{1,0:T(8,128)(2,1)} %all-gather.3.cloned.1.call-done.gradient_ref.refs_0_.refs_1_, bf16[48,4096]{1,0:T(8,128)(2,1)} %bitcast.16), custom_call_target="tpu_custom_call" | custom-call | flops 603979776 | bytes 5242880 | tf_op jit(solution)/shard_map/gradient_side/pallas_call | solution.py:354
  87.6 0.6 collective-permute-done.11.refs_3_
  88.2 4.9 %collective-permute-start.12 = (bf16[256,896]{1,0:T(8,128)(2,1)S(1)}, bf16[256,896]{1,0:T(8,128)(2,1)S(1)}, u32[]{:S(2)}, u32[]{:S(2)}) collective-permute-start(bf16[256,896]{1,0:T(8,128)(2,1)S(1)} %collective-permute-done.11.refs_3_), channel_id=1, source_target_pairs={{0,480},{32,0},{64,32},{96,64},{128,96},{160,128},{192,160},{224,1... | collective-permute-start | bytes 1376264 | tf_op jit(solution)/shard_map/ppermute | solution.py:349
  93.1 0.4 collective-permute-done.7.refs_2_
  93.5 1.9 collective-permute-start.8
  95.4 4.7 %collective-permute-done.12.refs_5_ = bf16[256,896]{1,0:T(8,128)(2,1)S(1)} collective-permute-done((bf16[256,896]{1,0:T(8,128)(2,1)S(1)}, bf16[256,896]{1,0:T(8,128)(2,1)S(1)}, u32[]{:S(2)}, u32[]{:S(2)}) %collective-permute-start.12) | collective-permute-done | bytes 458784 | tf_op jit(solution)/shard_map/ppermute | solution.py:349
  100.1 5.7 %collective-permute-start.13 = (bf16[256,896]{1,0:T(8,128)(2,1)S(1)}, bf16[256,896]{1,0:T(8,128)(2,1)S(1)}, u32[]{:S(2)}, u32[]{:S(2)}) collective-permute-start(bf16[256,896]{1,0:T(8,128)(2,1)S(1)} %collective-permute-done.12.refs_5_), channel_id=1, source_target_pairs={{0,480},{32,0},{64,32},{96,64},{128,96},{160,128},{192,160},{224,1... | collective-permute-start | bytes 1376264 | tf_op jit(solution)/shard_map/ppermute | solution.py:349
  105.8 0.7 collective-permute-done.8.refs_4_
  106.6 1.9 collective-permute-start.9
  108.5 0.0 all-gather.5.cloned.1.call-done.refs_0_.refs_1_
  108.5 4.1 %normed_side.1 = (bf16[32,512]{1,0:T(8,128)(2,1)}, bf16[512,32]{1,0:T(8,128)(2,1)}, f32[4,128,128]{2,1,0:T(8,128)}) custom-call(bf16[512,4096]{1,0:T(8,128)(2,1)} %all-gather.5.cloned.1.call-done.refs_0_.refs_1_, bf16[512,4096]{1,0:T(8,128)(2,1)} %all-gather.5.cloned.1.call-done.refs_0_.refs_1_, bf16[48,4096]{1,0:T(8,128)(2,1)} %bitcast.17), custom_call_target="tpu_custom_call" | custom-call | flops 671088640 | bytes 5242880 | tf_op jit(solution)/shard_map/normed_side/pallas_call | solution.py:354
  112.6 0.0 copy-done.11
  112.6 1.1 collective-permute-done.13.refs_1_
  113.8 5.9 %collective-permute-start.15 = (bf16[128,896]{1,0:T(8,128)(2,1)S(1)}, bf16[128,896]{1,0:T(8,128)(2,1)S(1)}, u32[]{:S(2)}, u32[]{:S(2)}) collective-permute-start(bf16[128,896]{1,0:T(8,128)(2,1)S(1)} %slice.16), channel_id=1, source_target_pairs={{0,480},{32,0},{64,32},{96,64},{128,96},{160,128},{192,160},{224,1... | collective-permute-start | bytes 688136 | tf_op jit(solution)/shard_map/ppermute | solution.py:349
  119.7 1.0 collective-permute-done.9.refs_0_
  120.7 1.9 collective-permute-start.14
  122.6 5.1 %part_product.3.refs_4_ = f32[512,896]{1,0:T(8,128)} custom-call(s32[1]{0:T(128)} %bitcast.z_ref, bf16[512,4096]{1,0:T(8,128)(2,1)} %all-gather.3.cloned.1.call-done.gradient_ref.refs_0_.refs_1_, bf16[256,896]{1,0:T(8,128)(2,1)} %collective-permute-done.3.refs_0_, bf16[256,896]{1,0:T(8,128)(2,1)} %collective-permute-done.10.refs_1_, ...), custom_call_target="tpu_custom_call" | custom-call | flops 1409286144 | bytes 6291456 | tf_op jit(solution)/shard_map/part_product/pallas_call | solution.py:402
  127.8 0.0 collective-permute-done.15.refs_3_
  127.8 2.2 collective-permute-done.14.refs_2_
  130.0 0.0 copy-done.14
  130.0 0.7 copy-done.15
  130.8 7.8 %hidden_side.1 = (f32[4,48,896]{2,1,0:T(8,128)}, f32[64,512]{1,0:T(8,128)}) custom-call(s32[1]{0:T(128)} %bitcast.z_ref, bf16[512,4096]{1,0:T(8,128)(2,1)} %all-gather.3.cloned.1.call-done.gradient_ref.refs_0_.refs_1_, bf16[256,896]{1,0:T(8,128)(2,1)} %copy-done.2, bf16[256,896]{1,0:T(8,128)(2,1)} %copy-done.1, bf16[128,896]{1,0:T(8,128)(2,1)} %copy-done.15, ...), custom_call_target="tpu_custom_call" | custom-call | tf_op jit(solution)/shard_map/hidden_side/pallas_call | solution.py:447
  138.6 0.0 copy-start.17
  138.6 0.0 copy-start.16
  138.6 11.5 %all_to_all.30 = f32[8,8,512]{2,1,0:T(8,128)S(1)} all-to-all(f32[8,8,512]{2,1,0:T(8,128)} %bitcast.23), channel_id=1, replica_groups=mesh['z'=16,'y'=4,'x'=4,'c'=2] {'x','c'}, dimensions={0} | all-to-all | bytes 262144 | tf_op jit(solution)/shard_map/all_to_all | solution.py:480
  150.2 0.7 broadcast_in_dim.9
  150.8 3.4 %all-to-all-start.1 = ((f32[8,8,512]{2,1,0:T(8,128)}), f32[8,8,512]{2,1,0:T(8,128)S(1)}, u32[]{:S(2)}, u32[]{:S(2)}) async-start(f32[8,8,512]{2,1,0:T(8,128)} %broadcast_in_dim.9), calls=%async_computation.1 | async-start | bytes 262144 | tf_op jit(solution)/shard_map/all_to_all | solution.py:482
  154.8 5.4 %all-to-all-done.1 = f32[8,8,512]{2,1,0:T(8,128)S(1)} async-done(((f32[8,8,512]{2,1,0:T(8,128)}), f32[8,8,512]{2,1,0:T(8,128)S(1)}, u32[]{:S(2)}, u32[]{:S(2)}) %all-to-all-start.1) | async-done | bytes 131104 | tf_op jit(solution)/shard_map/all_to_all | solution.py:482
  160.3 0.7 copy-done.3
  160.9 2.6 %clip_side.1 = f32[72,8,128]{2,1,0:T(8,128)} custom-call(f32[1]{0:T(128)} %copy.12.clip_ref, f32[64,512]{1,0:T(8,128)} %bitcast.22, f32[4,128,128]{2,1,0:T(8,128)} %get-tuple-element.27.normed_gram_hbm, f32[4,128,128]{2,1,0:T(8,128)} %get-tuple-element.28.gradient_gram_hbm, bf16[512,512]{1,0:T(8,128)(2,1)} %normed_hbm.1, bf16[512,512]{1,0:T(8,128)(2,1)} %gradient_hbm.1, ...), custom_call_target="tpu_custom_call" | custom-call | tf_op jit(solution)/shard_map/clip_side/pallas_call | solution.py:489
  163.5 14.4 %all_to_all.31 = f32[4,144,128]{2,1,0:T(8,128)S(1)} all-to-all(f32[4,144,128]{2,1,0:T(8,128)} %bitcast.18), channel_id=1, replica_groups=mesh['z'=16,'y'=4,'x'=4,'c'=2] {'y'}, dimensions={0} | all-to-all | bytes 589824 | tf_op jit(solution)/shard_map/all_to_all | solution.py:517
  178.0 21.1 %all_to_all.32 = f32[16,9,128]{2,1,0:T(8,128)S(1)} all-to-all(f32[16,9,128]{2,1,0:T(8,128)S(1)} %reshape.44), channel_id=1, replica_groups=mesh['z'=16,'y'=4,'x'=4,'c'=2] {'z'}, dimensions={0} | all-to-all | bytes 147456 | tf_op jit(solution)/shard_map/all_to_all | solution.py:518
  199.1 17.0 %all_to_all.33 = f32[16,9,128]{2,1,0:T(8,128)S(1)} all-to-all(f32[16,9,128]{2,1,0:T(8,128)S(1)} %broadcast_in_dim.10), channel_id=1, replica_groups=mesh['z'=16,'y'=4,'x'=4,'c'=2] {'z'}, dimensions={0} | all-to-all | bytes 147456 | tf_op jit(solution)/shard_map/all_to_all | solution.py:519
  216.1 9.2 %all_to_all.34 = f32[4,144,128]{2,1,0:T(8,128)S(1)} all-to-all(f32[4,144,128]{2,1,0:T(8,128)S(1)} %broadcast_in_dim.11), channel_id=1, replica_groups=mesh['z'=16,'y'=4,'x'=4,'c'=2] {'y'}, dimensions={0} | all-to-all | bytes 589824 | tf_op jit(solution)/shard_map/all_to_all | solution.py:522
  225.4 0.0 copy-done.17
  225.4 0.7 fusion.1
  226.1 0.7 fusion
  (37 shorter events, 0.2 us)
Async XLA Ops:
  7.2 63.7 %all-gather.3.cloned.1.call-start = ((), (), s32[]{:S(2)}) async-start(), calls=%async_computation.6 | async-start | bytes 4718592 | tf_op jit(solution)/shard_map/all_gather | solution.py:334
  7.9 100.6 %all-gather.5.cloned.1.call-start = ((), (), s32[]{:S(2)}) async-start(), calls=%async_computation.7 | async-start | bytes 4718592 | tf_op jit(solution)/shard_map/all_gather | solution.py:336
  22.0 48.8 %copy-start = (bf16[256,896]{1,0:T(8,128)(2,1)}, bf16[256,896]{1,0:T(8,128)(2,1)S(1)}, u32[]{:S(2)}) copy-start(bf16[256,896]{1,0:T(8,128)(2,1)S(1)} %all_gather.10.refs_0_) | copy-start | bytes 1376260
  22.0 12.8 %collective-permute-start.4 = (bf16[256,896]{1,0:T(8,128)(2,1)S(1)}, bf16[256,896]{1,0:T(8,128)(2,1)S(1)}, u32[]{:S(2)}, u32[]{:S(2)}) collective-permute-start(bf16[256,896]{1,0:T(8,128)(2,1)S(1)} %all_gather.10.refs_0_), channel_id=1, source_target_pairs={{0,480},{32,0},{64,32},{96,64},{128,96},{160,128},{192,160},{224,1... | collective-permute-start | bytes 1376264 | tf_op jit(solution)/shard_map/ppermute | solution.py:349
  28.9 15.1 %collective-permute-start = (bf16[256,896]{1,0:T(8,128)(2,1)S(1)}, bf16[256,896]{1,0:T(8,128)(2,1)S(1)}, u32[]{:S(2)}, u32[]{:S(2)}) collective-permute-start(bf16[256,896]{1,0:T(8,128)(2,1)S(1)} %all_gather.10.refs_0_), channel_id=1, source_target_pairs={{0,32},{32,64},{64,96},{96,128},{128,160},{160,192},{192,224},{224... | collective-permute-start | bytes 1376264 | tf_op jit(solution)/shard_map/ppermute | solution.py:348
  34.9 36.0 %copy-start.4 = (bf16[256,896]{1,0:T(8,128)(2,1)}, bf16[256,896]{1,0:T(8,128)(2,1)S(1)}, u32[]{:S(2)}) copy-start(bf16[256,896]{1,0:T(8,128)(2,1)S(1)} %collective-permute-done.4.refs_2_) | copy-start | bytes 1376260
  34.9 15.8 %collective-permute-start.5 = (bf16[256,896]{1,0:T(8,128)(2,1)S(1)}, bf16[256,896]{1,0:T(8,128)(2,1)S(1)}, u32[]{:S(2)}, u32[]{:S(2)}) collective-permute-start(bf16[256,896]{1,0:T(8,128)(2,1)S(1)} %collective-permute-done.4.refs_2_), channel_id=1, source_target_pairs={{0,480},{32,0},{64,32},{96,64},{128,96},{160,128},{192,160},{224,1... | collective-permute-start | bytes 1376264 | tf_op jit(solution)/shard_map/ppermute | solution.py:349
  44.0 26.9 %copy-start.5 = (bf16[256,896]{1,0:T(8,128)(2,1)}, bf16[256,896]{1,0:T(8,128)(2,1)S(1)}, u32[]{:S(2)}) copy-start(bf16[256,896]{1,0:T(8,128)(2,1)S(1)} %collective-permute-done.refs_1_) | copy-start | bytes 1376260
  44.0 12.9 %collective-permute-start.1 = (bf16[256,896]{1,0:T(8,128)(2,1)S(1)}, bf16[256,896]{1,0:T(8,128)(2,1)S(1)}, u32[]{:S(2)}, u32[]{:S(2)}) collective-permute-start(bf16[256,896]{1,0:T(8,128)(2,1)S(1)} %collective-permute-done.refs_1_), channel_id=1, source_target_pairs={{0,32},{32,64},{64,96},{96,128},{128,160},{160,192},{192,224},{224... | collective-permute-start | bytes 1376264 | tf_op jit(solution)/shard_map/ppermute | solution.py:348
  50.7 20.2 %copy-start.6 = (bf16[256,896]{1,0:T(8,128)(2,1)}, bf16[256,896]{1,0:T(8,128)(2,1)S(1)}, u32[]{:S(2)}) copy-start(bf16[256,896]{1,0:T(8,128)(2,1)S(1)} %collective-permute-done.5.refs_4_) | copy-start | bytes 1376260
  50.7 12.0 %collective-permute-start.6 = (bf16[256,896]{1,0:T(8,128)(2,1)S(1)}, bf16[256,896]{1,0:T(8,128)(2,1)S(1)}, u32[]{:S(2)}, u32[]{:S(2)}) collective-permute-start(bf16[256,896]{1,0:T(8,128)(2,1)S(1)} %collective-permute-done.5.refs_4_), channel_id=1, source_target_pairs={{0,480},{32,0},{64,32},{96,64},{128,96},{160,128},{192,160},{224,1... | collective-permute-start | bytes 1376264 | tf_op jit(solution)/shard_map/ppermute | solution.py:349
  56.9 14.0 %copy-start.7 = (bf16[256,896]{1,0:T(8,128)(2,1)}, bf16[256,896]{1,0:T(8,128)(2,1)S(1)}, u32[]{:S(2)}) copy-start(bf16[256,896]{1,0:T(8,128)(2,1)S(1)} %collective-permute-done.1.refs_3_) | copy-start | bytes 1376260
  56.9 12.0 %collective-permute-start.2 = (bf16[256,896]{1,0:T(8,128)(2,1)S(1)}, bf16[256,896]{1,0:T(8,128)(2,1)S(1)}, u32[]{:S(2)}, u32[]{:S(2)}) collective-permute-start(bf16[256,896]{1,0:T(8,128)(2,1)S(1)} %collective-permute-done.1.refs_3_), channel_id=1, source_target_pairs={{0,32},{32,64},{64,96},{96,128},{128,160},{160,192},{192,224},{224... | collective-permute-start | bytes 1376264 | tf_op jit(solution)/shard_map/ppermute | solution.py:348
  62.7 8.2 %copy-start.9 = (bf16[256,896]{1,0:T(8,128)(2,1)}, bf16[256,896]{1,0:T(8,128)(2,1)S(1)}, u32[]{:S(2)}) copy-start(bf16[256,896]{1,0:T(8,128)(2,1)S(1)} %collective-permute-done.6.refs_6_) | copy-start | bytes 1376260
  62.7 13.6 %collective-permute-start.10 = (bf16[256,896]{1,0:T(8,128)(2,1)S(1)}, bf16[256,896]{1,0:T(8,128)(2,1)}, u32[]{:S(2)}, u32[]{:S(2)}) collective-permute-start(bf16[256,896]{1,0:T(8,128)(2,1)S(1)} %collective-permute-done.6.refs_6_), channel_id=1, source_target_pairs={{0,480},{32,0},{64,32},{96,64},{128,96},{160,128},{192,160},{224,1... | collective-permute-start | bytes 1376264 | tf_op jit(solution)/shard_map/ppermute | solution.py:349
  68.9 2.0 copy-start.8
  68.9 12.7 %collective-permute-start.3 = (bf16[256,896]{1,0:T(8,128)(2,1)S(1)}, bf16[256,896]{1,0:T(8,128)(2,1)}, u32[]{:S(2)}, u32[]{:S(2)}) collective-permute-start(bf16[256,896]{1,0:T(8,128)(2,1)S(1)} %collective-permute-done.2.refs_5_), channel_id=1, source_target_pairs={{0,32},{32,64},{64,96},{96,128},{128,160},{160,192},{192,224},{224... | collective-permute-start | bytes 1376264 | tf_op jit(solution)/shard_map/ppermute | solution.py:348
  76.3 11.9 %collective-permute-start.11 = (bf16[256,896]{1,0:T(8,128)(2,1)}, bf16[256,896]{1,0:T(8,128)(2,1)S(1)}, u32[]{:S(2)}, u32[]{:S(2)}) collective-permute-start(bf16[256,896]{1,0:T(8,128)(2,1)} %collective-permute-done.10.refs_1_), channel_id=1, source_target_pairs={{0,480},{32,0},{64,32},{96,64},{128,96},{160,128},{192,160},{224,1... | collective-permute-start | bytes 1376264 | tf_op jit(solution)/shard_map/ppermute | solution.py:349
  81.6 11.9 %collective-permute-start.7 = (bf16[256,896]{1,0:T(8,128)(2,1)}, bf16[256,896]{1,0:T(8,128)(2,1)S(1)}, u32[]{:S(2)}, u32[]{:S(2)}) collective-permute-start(bf16[256,896]{1,0:T(8,128)(2,1)} %collective-permute-done.3.refs_0_), channel_id=1, source_target_pairs={{0,32},{32,64},{64,96},{96,128},{128,160},{160,192},{192,224},{224... | collective-permute-start | bytes 1376264 | tf_op jit(solution)/shard_map/ppermute | solution.py:348
  88.2 24.4 %copy-start.10 = (bf16[256,896]{1,0:T(8,128)(2,1)}, bf16[256,896]{1,0:T(8,128)(2,1)S(1)}, u32[]{:S(2)}) copy-start(bf16[256,896]{1,0:T(8,128)(2,1)S(1)} %collective-permute-done.11.refs_3_) | copy-start | bytes 1376260
  88.2 12.0 %collective-permute-start.12 = (bf16[256,896]{1,0:T(8,128)(2,1)S(1)}, bf16[256,896]{1,0:T(8,128)(2,1)S(1)}, u32[]{:S(2)}, u32[]{:S(2)}) collective-permute-start(bf16[256,896]{1,0:T(8,128)(2,1)S(1)} %collective-permute-done.11.refs_3_), channel_id=1, source_target_pairs={{0,480},{32,0},{64,32},{96,64},{128,96},{160,128},{192,160},{224,1... | collective-permute-start | bytes 1376264 | tf_op jit(solution)/shard_map/ppermute | solution.py:349
  93.5 19.1 %copy-start.11 = (bf16[256,896]{1,0:T(8,128)(2,1)}, bf16[256,896]{1,0:T(8,128)(2,1)S(1)}, u32[]{:S(2)}) copy-start(bf16[256,896]{1,0:T(8,128)(2,1)S(1)} %collective-permute-done.7.refs_2_) | copy-start | bytes 1376260
  93.5 13.1 %collective-permute-start.8 = (bf16[256,896]{1,0:T(8,128)(2,1)S(1)}, bf16[256,896]{1,0:T(8,128)(2,1)S(1)}, u32[]{:S(2)}, u32[]{:S(2)}) collective-permute-start(bf16[256,896]{1,0:T(8,128)(2,1)S(1)} %collective-permute-done.7.refs_2_), channel_id=1, source_target_pairs={{0,32},{32,64},{64,96},{96,128},{128,160},{160,192},{192,224},{224... | collective-permute-start | bytes 1376264 | tf_op jit(solution)/shard_map/ppermute | solution.py:348
  100.1 12.5 %copy-start.12 = (bf16[256,896]{1,0:T(8,128)(2,1)}, bf16[256,896]{1,0:T(8,128)(2,1)S(1)}, u32[]{:S(2)}) copy-start(bf16[256,896]{1,0:T(8,128)(2,1)S(1)} %collective-permute-done.12.refs_5_) | copy-start | bytes 1376260
  100.1 13.6 %collective-permute-start.13 = (bf16[256,896]{1,0:T(8,128)(2,1)S(1)}, bf16[256,896]{1,0:T(8,128)(2,1)S(1)}, u32[]{:S(2)}, u32[]{:S(2)}) collective-permute-start(bf16[256,896]{1,0:T(8,128)(2,1)S(1)} %collective-permute-done.12.refs_5_), channel_id=1, source_target_pairs={{0,480},{32,0},{64,32},{96,64},{128,96},{160,128},{192,160},{224,1... | collective-permute-start | bytes 1376264 | tf_op jit(solution)/shard_map/ppermute | solution.py:349
  106.6 6.1 %copy-start.13 = (bf16[256,896]{1,0:T(8,128)(2,1)}, bf16[256,896]{1,0:T(8,128)(2,1)S(1)}, u32[]{:S(2)}) copy-start(bf16[256,896]{1,0:T(8,128)(2,1)S(1)} %collective-permute-done.8.refs_4_) | copy-start | bytes 1376260
  106.6 14.1 %collective-permute-start.9 = (bf16[256,896]{1,0:T(8,128)(2,1)S(1)}, bf16[256,896]{1,0:T(8,128)(2,1)S(1)}, u32[]{:S(2)}, u32[]{:S(2)}) collective-permute-start(bf16[256,896]{1,0:T(8,128)(2,1)S(1)} %collective-permute-done.8.refs_4_), channel_id=1, source_target_pairs={{0,32},{32,64},{64,96},{96,128},{128,160},{160,192},{192,224},{224... | collective-permute-start | bytes 1376264 | tf_op jit(solution)/shard_map/ppermute | solution.py:348
  113.8 14.0 %copy-start.1 = (bf16[256,896]{1,0:T(8,128)(2,1)}, bf16[256,896]{1,0:T(8,128)(2,1)S(1)}, u32[]{:S(2)}) copy-start(bf16[256,896]{1,0:T(8,128)(2,1)S(1)} %collective-permute-done.13.refs_1_) | copy-start | bytes 1376260
  113.8 14.0 %collective-permute-start.15 = (bf16[128,896]{1,0:T(8,128)(2,1)S(1)}, bf16[128,896]{1,0:T(8,128)(2,1)S(1)}, u32[]{:S(2)}, u32[]{:S(2)}) collective-permute-start(bf16[128,896]{1,0:T(8,128)(2,1)S(1)} %slice.16), channel_id=1, source_target_pairs={{0,480},{32,0},{64,32},{96,64},{128,96},{160,128},{192,160},{224,1... | collective-permute-start | bytes 688136 | tf_op jit(solution)/shard_map/ppermute | solution.py:349
  120.7 7.1 %copy-start.2 = (bf16[256,896]{1,0:T(8,128)(2,1)}, bf16[256,896]{1,0:T(8,128)(2,1)S(1)}, u32[]{:S(2)}) copy-start(bf16[256,896]{1,0:T(8,128)(2,1)S(1)} %collective-permute-done.9.refs_0_) | copy-start | bytes 1376260
  120.7 9.3 %collective-permute-start.14 = (bf16[128,896]{1,0:T(8,128)(2,1)S(1)}, bf16[128,896]{1,0:T(8,128)(2,1)S(1)}, u32[]{:S(2)}, u32[]{:S(2)}) collective-permute-start(bf16[128,896]{1,0:T(8,128)(2,1)S(1)} %slice.15), channel_id=1, source_target_pairs={{0,32},{32,64},{64,96},{96,128},{128,160},{160,192},{192,224},{224... | collective-permute-start | bytes 688136 | tf_op jit(solution)/shard_map/ppermute | solution.py:348
  127.8 2.2 copy-start.14
  130.0 0.7 copy-start.15
  138.6 86.8 %copy-start.17 = (f32[3,16,512]{2,1,0:T(8,128)S(1)}, f32[3,16,512]{2,1,0:T(8,128)}, u32[]{:S(2)}) copy-start(f32[3,16,512]{2,1,0:T(8,128)} %param.18) | copy-start | bytes 294916
  138.6 87.5 %copy-start.16 = (f32[3,16,896]{2,1,0:T(8,128)S(1)}, f32[3,16,896]{2,1,0:T(8,128)}, u32[]{:S(2)}) copy-start(f32[3,16,896]{2,1,0:T(8,128)} %param.19) | copy-start | bytes 516100
  150.8 9.4 %all-to-all-start.1 = ((f32[8,8,512]{2,1,0:T(8,128)}), f32[8,8,512]{2,1,0:T(8,128)S(1)}, u32[]{:S(2)}, u32[]{:S(2)}) async-start(f32[8,8,512]{2,1,0:T(8,128)} %broadcast_in_dim.9), calls=%async_computation.1 | async-start | bytes 262144 | tf_op jit(solution)/shard_map/all_to_all | solution.py:482
  160.3 0.7 copy-start.3
Sparse Core Ops, SparseCore 0:
  10.1 43.8 all-gather.2
  56.2 39.7 all-gather.4

commit v14 on v13

--- a/solution.py
+++ b/solution.py
@@ -435,14 +435,13 @@
     at = last - 1
     low_in, high_in = after(low[at], in_t), after(high[at], in_t)
     step(last, low_in[:half], high_in[half:])
-    total = part(pairs(last - 4, last - 1), after(total, low_in, high_in))
-    offsets = pairs(last - 1, last)
-    blocks = [at_z(offset) for offset in offsets] + [low[last], high[last]]
+    total = part(pairs(last - 4, last), after(total, low_in, high_in))
+    blocks = [low[last], high[last]]
     plan = dict(
         n_z=n_z,
         rows=rows,
-        blocks=[(offset, 0) for offset in offsets] + [(last, 0), (last, half)],
-        chunks=[slice(0, 4)],
+        blocks=[(last, 0), (last, half)],
+        chunks=[slice(0, 2)],
     )
     sums, mids = pl.pallas_call(
         functools.partial(hidden_kernel, plan),
@@ -461,7 +460,7 @@
             pltpu.VMEM((tokens, hidden), F32),
             pltpu.VMEM((sequences, 3 * RANK, hidden), F32),
         ]
-        + scratch((len(offsets) + 1) * rows, 4 * len(blocks) + 12),
+        + scratch(rows, 4 * len(blocks) + 12),
         compiler_params=params,
         name="hidden_side",
     )(

time: 235 us -> 234 us (level)
  transfers between devices with their start and end apart: 19 -> 19, of which waited for: 14 -> 13; matrix products, arithmetic and copies ran while one was open for 0% -> 0% of each run, Pallas kernels for 8% -> 8%
where the time goes in v14:
time: 234 us; the launch traced here: 233 us
  blocking collectives  87.1 us (37%)
  starting transfers between devices  67.9 us (29%)
  waiting for transfers between devices  30.4 us (13%)
  Pallas kernels  29.3 us (13%)
  between operations  15.1 us (6%)
    ppermute x8, starting transfers between devices, step(): high[k] = lax.ppermute(high_from, z_axes, ring(n_z, -1))  49.1 us
    all_to_all x1, blocking collectives, per_device(): lax.all_to_all(share.reshape(n_z, -1, 128), z_axes, 0, 0)  21.9 us
    ppermute x8, waiting for transfers between devices, step(): high[k] = lax.ppermute(high_from, z_axes, ring(n_z, -1))  18.3 us
    all_to_all x1, blocking collectives, per_device(): lax.all_to_all(jnp.broadcast_to(share, (n_z,) + share.shape), z_axes, 0, 0)  17 us
    ppermute x8, starting transfers between devices, step(): low[k] = lax.ppermute(low_from, z_axes, ring(n_z, 1))  15.3 us
    all_to_all x1, blocking collectives, per_device(): lax.all_to_all(out.reshape(n_y, -1, 128), 'y', 0, 0)  14.6 us
    all_gather x1, blocking collectives, per_device(): block = lax.all_gather(frozen_down_weight.T, 'y', axis=0, tiled=True)  13.4 us
    pallas_call x2, Pallas kernels, part(): pl.pallas_call(functools.partial(part_kernel, plan, before is None), out_...  11.3 us
  transfers between devices with their start and end apart: 19, of which 13 were waited for; matrix products, arithmetic and copies ran while one was open for 0% of the time, Pallas kernels for 8%

profile of v14, /device:TPU:32, one launch (start us, length us, event | category | flops | bytes accessed | tf_op | source)
XLA Modules:
  0.0 233.4 jit_solution(4672177112184356850)
XLA Ops:
  7.2 0.0 all-gather.3.cloned.1.call-start
  7.2 0.7 all-gather.3.cloned.1.call-update
  7.9 0.0 all-gather.5.cloned.1.call-start
  7.9 0.7 all-gather.5.cloned.1.call-update
  8.6 13.4 %all_gather.10.refs_0_ = bf16[256,896]{1,0:T(8,128)(2,1)S(1)} all-gather(bf16[64,896]{1,0:T(8,128)(2,1)} %bitcast.24), channel_id=1, replica_groups=mesh['z'=16,'y'=4,'x'=4,'c'=2] {'y'}, dimensions={0}, use_global_device_ids=true | all-gather | bytes 573440 | tf_op jit(solution)/shard_map/all_gather | solution.py:335
  22.0 6.9 %collective-permute-start.4 = (bf16[256,896]{1,0:T(8,128)(2,1)S(1)}, bf16[256,896]{1,0:T(8,128)(2,1)S(1)}, u32[]{:S(2)}, u32[]{:S(2)}) collective-permute-start(bf16[256,896]{1,0:T(8,128)(2,1)S(1)} %all_gather.10.refs_0_), channel_id=1, source_target_pairs={{0,480},{32,0},{64,32},{96,64},{128,96},{160,128},{192,160},{224,1... | collective-permute-start | bytes 1376264 | tf_op jit(solution)/shard_map/ppermute | solution.py:349
  28.9 1.9 collective-permute-start
  30.8 4.0 %collective-permute-done.4.refs_2_ = bf16[256,896]{1,0:T(8,128)(2,1)S(1)} collective-permute-done((bf16[256,896]{1,0:T(8,128)(2,1)S(1)}, bf16[256,896]{1,0:T(8,128)(2,1)S(1)}, u32[]{:S(2)}, u32[]{:S(2)}) %collective-permute-start.4) | collective-permute-done | bytes 458784 | tf_op jit(solution)/shard_map/ppermute | solution.py:349
  34.9 8.6 %collective-permute-start.5 = (bf16[256,896]{1,0:T(8,128)(2,1)S(1)}, bf16[256,896]{1,0:T(8,128)(2,1)S(1)}, u32[]{:S(2)}, u32[]{:S(2)}) collective-permute-start(bf16[256,896]{1,0:T(8,128)(2,1)S(1)} %collective-permute-done.4.refs_2_), channel_id=1, source_target_pairs={{0,480},{32,0},{64,32},{96,64},{128,96},{160,128},{192,160},{224,1... | collective-permute-start | bytes 1376264 | tf_op jit(solution)/shard_map/ppermute | solution.py:349
  43.5 0.5 collective-permute-done.refs_1_
  44.0 1.9 collective-permute-start.1
  45.9 4.7 %collective-permute-done.5.refs_4_ = bf16[256,896]{1,0:T(8,128)(2,1)S(1)} collective-permute-done((bf16[256,896]{1,0:T(8,128)(2,1)S(1)}, bf16[256,896]{1,0:T(8,128)(2,1)S(1)}, u32[]{:S(2)}, u32[]{:S(2)}) %collective-permute-start.5) | collective-permute-done | bytes 458784 | tf_op jit(solution)/shard_map/ppermute | solution.py:349
  50.7 5.7 %collective-permute-start.6 = (bf16[256,896]{1,0:T(8,128)(2,1)S(1)}, bf16[256,896]{1,0:T(8,128)(2,1)}, u32[]{:S(2)}, u32[]{:S(2)}) collective-permute-start(bf16[256,896]{1,0:T(8,128)(2,1)S(1)} %collective-permute-done.5.refs_4_), channel_id=1, source_target_pairs={{0,480},{32,0},{64,32},{96,64},{128,96},{160,128},{192,160},{224,1... | collective-permute-start | bytes 1376264 | tf_op jit(solution)/shard_map/ppermute | solution.py:349
  56.4 0.5 collective-permute-done.1.refs_3_
  56.9 1.9 collective-permute-start.2
  58.8 3.9 %collective-permute-done.6.refs_6_ = bf16[256,896]{1,0:T(8,128)(2,1)} collective-permute-done((bf16[256,896]{1,0:T(8,128)(2,1)S(1)}, bf16[256,896]{1,0:T(8,128)(2,1)}, u32[]{:S(2)}, u32[]{:S(2)}) %collective-permute-start.6) | collective-permute-done | bytes 458784 | tf_op jit(solution)/shard_map/ppermute | solution.py:349
  62.7 5.7 %collective-permute-start.11 = (bf16[256,896]{1,0:T(8,128)(2,1)}, bf16[256,896]{1,0:T(8,128)(2,1)S(1)}, u32[]{:S(2)}, u32[]{:S(2)}) collective-permute-start(bf16[256,896]{1,0:T(8,128)(2,1)} %collective-permute-done.6.refs_6_), channel_id=1, source_target_pairs={{0,480},{32,0},{64,32},{96,64},{128,96},{160,128},{192,160},{224,1... | collective-permute-start | bytes 1376264 | tf_op jit(solution)/shard_map/ppermute | solution.py:349
  68.4 0.6 collective-permute-done.2.refs_5_
  69.0 1.9 collective-permute-start.3
  70.9 0.0 all-gather.3.cloned.1.call-done.gradient_ref.refs_0_.refs_1_
  70.9 0.0 copy-done
  70.9 0.0 copy-done.8
  71.0 0.0 copy-done.9
  71.0 0.0 copy-done.11
  71.0 0.0 copy-done.13
  71.0 5.4 %part_product.2.refs_8_ = f32[512,896]{1,0:T(8,128)} custom-call(s32[1]{0:T(128)} %bitcast.z_ref, bf16[512,4096]{1,0:T(8,128)(2,1)} %all-gather.3.cloned.1.call-done.gradient_ref.refs_0_.refs_1_, bf16[256,896]{1,0:T(8,128)(2,1)} %copy-done, bf16[256,896]{1,0:T(8,128)(2,1)} %copy-done.9, bf16[256,896]{1,0:T(8,128)(2,1)} %copy-done.8, ...), custom_call_target="tpu_custom_call" | custom-call | flops 1644167168 | bytes 6291456 | tf_op jit(solution)/shard_map/part_product/pallas_call | solution.py:402
  76.4 0.0 collective-permute-done.11.refs_1_
  76.4 5.2 %collective-permute-start.12 = (bf16[256,896]{1,0:T(8,128)(2,1)S(1)}, bf16[256,896]{1,0:T(8,128)(2,1)S(1)}, u32[]{:S(2)}, u32[]{:S(2)}) collective-permute-start(bf16[256,896]{1,0:T(8,128)(2,1)S(1)} %collective-permute-done.11.refs_1_), channel_id=1, source_target_pairs={{0,480},{32,0},{64,32},{96,64},{128,96},{160,128},{192,160},{224,1... | collective-permute-start | bytes 1376264 | tf_op jit(solution)/shard_map/ppermute | solution.py:349
  81.6 0.0 collective-permute-done.3.refs_0_
  81.6 1.9 collective-permute-start.7
  83.6 4.1 %gradient_side.1 = (bf16[16,512]{1,0:T(8,128)(2,1)}, bf16[512,16]{1,0:T(8,128)(2,1)}, f32[4,128,128]{2,1,0:T(8,128)}) custom-call(bf16[512,4096]{1,0:T(8,128)(2,1)} %all-gather.3.cloned.1.call-done.gradient_ref.refs_0_.refs_1_, bf16[512,4096]{1,0:T(8,128)(2,1)} %all-gather.3.cloned.1.call-done.gradient_ref.refs_0_.refs_1_, bf16[48,4096]{1,0:T(8,128)(2,1)} %bitcast.16), custom_call_target="tpu_custom_call" | custom-call | flops 603979776 | bytes 5242880 | tf_op jit(solution)/shard_map/gradient_side/pallas_call | solution.py:354
  87.7 0.0 collective-permute-done.12.refs_3_
  87.7 5.2 %collective-permute-start.13 = (bf16[256,896]{1,0:T(8,128)(2,1)S(1)}, bf16[256,896]{1,0:T(8,128)(2,1)S(1)}, u32[]{:S(2)}, u32[]{:S(2)}) collective-permute-start(bf16[256,896]{1,0:T(8,128)(2,1)S(1)} %collective-permute-done.12.refs_3_), channel_id=1, source_target_pairs={{0,480},{32,0},{64,32},{96,64},{128,96},{160,128},{192,160},{224,1... | collective-permute-start | bytes 1376264 | tf_op jit(solution)/shard_map/ppermute | solution.py:349
  92.9 0.5 collective-permute-done.7.refs_2_
  93.4 1.9 collective-permute-start.8
  95.4 4.5 %collective-permute-done.13.refs_5_ = bf16[256,896]{1,0:T(8,128)(2,1)S(1)} collective-permute-done((bf16[256,896]{1,0:T(8,128)(2,1)S(1)}, bf16[256,896]{1,0:T(8,128)(2,1)S(1)}, u32[]{:S(2)}, u32[]{:S(2)}) %collective-permute-start.13) | collective-permute-done | bytes 458784 | tf_op jit(solution)/shard_map/ppermute | solution.py:349
  99.9 5.9 %collective-permute-start.14 = (bf16[256,896]{1,0:T(8,128)(2,1)S(1)}, bf16[256,896]{1,0:T(8,128)(2,1)S(1)}, u32[]{:S(2)}, u32[]{:S(2)}) collective-permute-start(bf16[256,896]{1,0:T(8,128)(2,1)S(1)} %collective-permute-done.13.refs_5_), channel_id=1, source_target_pairs={{0,480},{32,0},{64,32},{96,64},{128,96},{160,128},{192,160},{224,1... | collective-permute-start | bytes 1376264 | tf_op jit(solution)/shard_map/ppermute | solution.py:349
  105.8 0.8 collective-permute-done.8.refs_4_
  106.5 1.9 collective-permute-start.9
  108.5 0.0 all-gather.5.cloned.1.call-done.refs_0_.refs_1_
  108.5 4.1 %normed_side.1 = (bf16[32,512]{1,0:T(8,128)(2,1)}, bf16[512,32]{1,0:T(8,128)(2,1)}, f32[4,128,128]{2,1,0:T(8,128)}) custom-call(bf16[512,4096]{1,0:T(8,128)(2,1)} %all-gather.5.cloned.1.call-done.refs_0_.refs_1_, bf16[512,4096]{1,0:T(8,128)(2,1)} %all-gather.5.cloned.1.call-done.refs_0_.refs_1_, bf16[48,4096]{1,0:T(8,128)(2,1)} %bitcast.17), custom_call_target="tpu_custom_call" | custom-call | flops 671088640 | bytes 5242880 | tf_op jit(solution)/shard_map/normed_side/pallas_call | solution.py:354
  112.7 1.1 collective-permute-done.14.refs_7_
  113.8 5.9 %collective-permute-start.15 = (bf16[128,896]{1,0:T(8,128)(2,1)S(1)}, bf16[128,896]{1,0:T(8,128)(2,1)S(1)}, u32[]{:S(2)}, u32[]{:S(2)}) collective-permute-start(bf16[128,896]{1,0:T(8,128)(2,1)S(1)} %slice.16), channel_id=1, source_target_pairs={{0,480},{32,0},{64,32},{96,64},{128,96},{160,128},{192,160},{224,1... | collective-permute-start | bytes 688136 | tf_op jit(solution)/shard_map/ppermute | solution.py:349
  119.7 1.0 collective-permute-done.9.refs_6_
  120.7 1.9 collective-permute-start.10
  122.7 5.9 %part_product.3.refs_2_ = f32[512,896]{1,0:T(8,128)} custom-call(s32[1]{0:T(128)} %bitcast.z_ref, bf16[512,4096]{1,0:T(8,128)(2,1)} %all-gather.3.cloned.1.call-done.gradient_ref.refs_0_.refs_1_, bf16[256,896]{1,0:T(8,128)(2,1)} %copy-done.5, bf16[256,896]{1,0:T(8,128)(2,1)} %copy-done.4, bf16[256,896]{1,0:T(8,128)(2,1)} %copy-done.7, ...), custom_call_target="tpu_custom_call" | custom-call | flops 1879048192 | bytes 6291456 | tf_op jit(solution)/shard_map/part_product/pallas_call | solution.py:402
  128.6 0.0 collective-permute-done.15.refs_1_
  128.7 1.4 collective-permute-done.10.refs_0_
  130.0 0.7 copy-done.15
  130.7 7.2 %hidden_side.1 = (f32[4,48,896]{2,1,0:T(8,128)}, f32[64,512]{1,0:T(8,128)}) custom-call(s32[1]{0:T(128)} %bitcast.z_ref, bf16[512,4096]{1,0:T(8,128)(2,1)} %all-gather.3.cloned.1.call-done.gradient_ref.refs_0_.refs_1_, bf16[128,896]{1,0:T(8,128)(2,1)} %copy-done.15, bf16[128,896]{1,0:T(8,128)(2,1)} %copy-done.14, f32[512,896]{1,0:T(8,128)} %part_product.3.refs_2_, ...), custom_call_target="tpu_custom_call" | custom-call | tf_op jit(solution)/shard_map/hidden_side/pallas_call | solution.py:446
  137.9 0.0 copy-start.17
  137.9 0.0 copy-start.16
  137.9 11.0 %all_to_all.30 = f32[8,8,512]{2,1,0:T(8,128)S(1)} all-to-all(f32[8,8,512]{2,1,0:T(8,128)} %bitcast.23), channel_id=1, replica_groups=mesh['z'=16,'y'=4,'x'=4,'c'=2] {'x','c'}, dimensions={0} | all-to-all | bytes 262144 | tf_op jit(solution)/shard_map/all_to_all | solution.py:479
  148.9 0.7 broadcast_in_dim.9
  149.6 3.4 %all-to-all-start.1 = ((f32[8,8,512]{2,1,0:T(8,128)}), f32[8,8,512]{2,1,0:T(8,128)S(1)}, u32[]{:S(2)}, u32[]{:S(2)}) async-start(f32[8,8,512]{2,1,0:T(8,128)} %broadcast_in_dim.9), calls=%async_computation.1 | async-start | bytes 262144 | tf_op jit(solution)/shard_map/all_to_all | solution.py:481
  153.6 5.4 %all-to-all-done.1 = f32[8,8,512]{2,1,0:T(8,128)S(1)} async-done(((f32[8,8,512]{2,1,0:T(8,128)}), f32[8,8,512]{2,1,0:T(8,128)S(1)}, u32[]{:S(2)}, u32[]{:S(2)}) %all-to-all-start.1) | async-done | bytes 131104 | tf_op jit(solution)/shard_map/all_to_all | solution.py:481
  159.0 0.7 copy-done.3
  159.7 2.6 %clip_side.1 = f32[72,8,128]{2,1,0:T(8,128)} custom-call(f32[1]{0:T(128)} %copy.12.clip_ref, f32[64,512]{1,0:T(8,128)} %bitcast.22, f32[4,128,128]{2,1,0:T(8,128)} %get-tuple-element.27.normed_gram_hbm, f32[4,128,128]{2,1,0:T(8,128)} %get-tuple-element.28.gradient_gram_hbm, bf16[512,512]{1,0:T(8,128)(2,1)} %normed_hbm.1, bf16[512,512]{1,0:T(8,128)(2,1)} %gradient_hbm.1, ...), custom_call_target="tpu_custom_call" | custom-call | tf_op jit(solution)/shard_map/clip_side/pallas_call | solution.py:488
  162.3 14.6 %all_to_all.31 = f32[4,144,128]{2,1,0:T(8,128)S(1)} all-to-all(f32[4,144,128]{2,1,0:T(8,128)} %bitcast.18), channel_id=1, replica_groups=mesh['z'=16,'y'=4,'x'=4,'c'=2] {'y'}, dimensions={0} | all-to-all | bytes 589824 | tf_op jit(solution)/shard_map/all_to_all | solution.py:516
  176.9 21.9 %all_to_all.32 = f32[16,9,128]{2,1,0:T(8,128)S(1)} all-to-all(f32[16,9,128]{2,1,0:T(8,128)S(1)} %reshape.44), channel_id=1, replica_groups=mesh['z'=16,'y'=4,'x'=4,'c'=2] {'z'}, dimensions={0} | all-to-all | bytes 147456 | tf_op jit(solution)/shard_map/all_to_all | solution.py:517
  198.8 17.0 %all_to_all.33 = f32[16,9,128]{2,1,0:T(8,128)S(1)} all-to-all(f32[16,9,128]{2,1,0:T(8,128)S(1)} %broadcast_in_dim.10), channel_id=1, replica_groups=mesh['z'=16,'y'=4,'x'=4,'c'=2] {'z'}, dimensions={0} | all-to-all | bytes 147456 | tf_op jit(solution)/shard_map/all_to_all | solution.py:518
  215.9 9.2 %all_to_all.34 = f32[4,144,128]{2,1,0:T(8,128)S(1)} all-to-all(f32[4,144,128]{2,1,0:T(8,128)S(1)} %broadcast_in_dim.11), channel_id=1, replica_groups=mesh['z'=16,'y'=4,'x'=4,'c'=2] {'y'}, dimensions={0} | all-to-all | bytes 589824 | tf_op jit(solution)/shard_map/all_to_all | solution.py:521
  225.2 0.7 fusion.1
  225.8 0.7 fusion
  (37 shorter events, 0.2 us)
Async XLA Ops:
  7.2 63.8 %all-gather.3.cloned.1.call-start = ((), (), s32[]{:S(2)}) async-start(), calls=%async_computation.6 | async-start | bytes 4718592 | tf_op jit(solution)/shard_map/all_gather | solution.py:334
  7.9 100.6 %all-gather.5.cloned.1.call-start = ((), (), s32[]{:S(2)}) async-start(), calls=%async_computation.7 | async-start | bytes 4718592 | tf_op jit(solution)/shard_map/all_gather | solution.py:336
  22.0 48.9 %copy-start = (bf16[256,896]{1,0:T(8,128)(2,1)}, bf16[256,896]{1,0:T(8,128)(2,1)S(1)}, u32[]{:S(2)}) copy-start(bf16[256,896]{1,0:T(8,128)(2,1)S(1)} %all_gather.10.refs_0_) | copy-start | bytes 1376260
  22.0 12.8 %collective-permute-start.4 = (bf16[256,896]{1,0:T(8,128)(2,1)S(1)}, bf16[256,896]{1,0:T(8,128)(2,1)S(1)}, u32[]{:S(2)}, u32[]{:S(2)}) collective-permute-start(bf16[256,896]{1,0:T(8,128)(2,1)S(1)} %all_gather.10.refs_0_), channel_id=1, source_target_pairs={{0,480},{32,0},{64,32},{96,64},{128,96},{160,128},{192,160},{224,1... | collective-permute-start | bytes 1376264 | tf_op jit(solution)/shard_map/ppermute | solution.py:349
  28.9 15.1 %collective-permute-start = (bf16[256,896]{1,0:T(8,128)(2,1)S(1)}, bf16[256,896]{1,0:T(8,128)(2,1)S(1)}, u32[]{:S(2)}, u32[]{:S(2)}) collective-permute-start(bf16[256,896]{1,0:T(8,128)(2,1)S(1)} %all_gather.10.refs_0_), channel_id=1, source_target_pairs={{0,32},{32,64},{64,96},{96,128},{128,160},{160,192},{192,224},{224... | collective-permute-start | bytes 1376264 | tf_op jit(solution)/shard_map/ppermute | solution.py:348
  34.9 36.1 %copy-start.8 = (bf16[256,896]{1,0:T(8,128)(2,1)}, bf16[256,896]{1,0:T(8,128)(2,1)S(1)}, u32[]{:S(2)}) copy-start(bf16[256,896]{1,0:T(8,128)(2,1)S(1)} %collective-permute-done.4.refs_2_) | copy-start | bytes 1376260
  34.9 15.8 %collective-permute-start.5 = (bf16[256,896]{1,0:T(8,128)(2,1)S(1)}, bf16[256,896]{1,0:T(8,128)(2,1)S(1)}, u32[]{:S(2)}, u32[]{:S(2)}) collective-permute-start(bf16[256,896]{1,0:T(8,128)(2,1)S(1)} %collective-permute-done.4.refs_2_), channel_id=1, source_target_pairs={{0,480},{32,0},{64,32},{96,64},{128,96},{160,128},{192,160},{224,1... | collective-permute-start | bytes 1376264 | tf_op jit(solution)/shard_map/ppermute | solution.py:349
  44.0 27.0 %copy-start.9 = (bf16[256,896]{1,0:T(8,128)(2,1)}, bf16[256,896]{1,0:T(8,128)(2,1)S(1)}, u32[]{:S(2)}) copy-start(bf16[256,896]{1,0:T(8,128)(2,1)S(1)} %collective-permute-done.refs_1_) | copy-start | bytes 1376260
  44.0 12.9 %collective-permute-start.1 = (bf16[256,896]{1,0:T(8,128)(2,1)S(1)}, bf16[256,896]{1,0:T(8,128)(2,1)S(1)}, u32[]{:S(2)}, u32[]{:S(2)}) collective-permute-start(bf16[256,896]{1,0:T(8,128)(2,1)S(1)} %collective-permute-done.refs_1_), channel_id=1, source_target_pairs={{0,32},{32,64},{64,96},{96,128},{128,160},{160,192},{192,224},{224... | collective-permute-start | bytes 1376264 | tf_op jit(solution)/shard_map/ppermute | solution.py:348
  50.7 20.3 %copy-start.11 = (bf16[256,896]{1,0:T(8,128)(2,1)}, bf16[256,896]{1,0:T(8,128)(2,1)S(1)}, u32[]{:S(2)}) copy-start(bf16[256,896]{1,0:T(8,128)(2,1)S(1)} %collective-permute-done.5.refs_4_) | copy-start | bytes 1376260
  50.7 12.0 %collective-permute-start.6 = (bf16[256,896]{1,0:T(8,128)(2,1)S(1)}, bf16[256,896]{1,0:T(8,128)(2,1)}, u32[]{:S(2)}, u32[]{:S(2)}) collective-permute-start(bf16[256,896]{1,0:T(8,128)(2,1)S(1)} %collective-permute-done.5.refs_4_), channel_id=1, source_target_pairs={{0,480},{32,0},{64,32},{96,64},{128,96},{160,128},{192,160},{224,1... | collective-permute-start | bytes 1376264 | tf_op jit(solution)/shard_map/ppermute | solution.py:349
  56.9 14.1 %copy-start.13 = (bf16[256,896]{1,0:T(8,128)(2,1)}, bf16[256,896]{1,0:T(8,128)(2,1)S(1)}, u32[]{:S(2)}) copy-start(bf16[256,896]{1,0:T(8,128)(2,1)S(1)} %collective-permute-done.1.refs_3_) | copy-start | bytes 1376260
  56.9 12.1 %collective-permute-start.2 = (bf16[256,896]{1,0:T(8,128)(2,1)S(1)}, bf16[256,896]{1,0:T(8,128)(2,1)}, u32[]{:S(2)}, u32[]{:S(2)}) collective-permute-start(bf16[256,896]{1,0:T(8,128)(2,1)S(1)} %collective-permute-done.1.refs_3_), channel_id=1, source_target_pairs={{0,32},{32,64},{64,96},{96,128},{128,160},{160,192},{192,224},{224... | collective-permute-start | bytes 1376264 | tf_op jit(solution)/shard_map/ppermute | solution.py:348
  62.7 13.7 %collective-permute-start.11 = (bf16[256,896]{1,0:T(8,128)(2,1)}, bf16[256,896]{1,0:T(8,128)(2,1)S(1)}, u32[]{:S(2)}, u32[]{:S(2)}) collective-permute-start(bf16[256,896]{1,0:T(8,128)(2,1)} %collective-permute-done.6.refs_6_), channel_id=1, source_target_pairs={{0,480},{32,0},{64,32},{96,64},{128,96},{160,128},{192,160},{224,1... | collective-permute-start | bytes 1376264 | tf_op jit(solution)/shard_map/ppermute | solution.py:349
  69.0 12.6 %collective-permute-start.3 = (bf16[256,896]{1,0:T(8,128)(2,1)}, bf16[256,896]{1,0:T(8,128)(2,1)S(1)}, u32[]{:S(2)}, u32[]{:S(2)}) collective-permute-start(bf16[256,896]{1,0:T(8,128)(2,1)} %collective-permute-done.2.refs_5_), channel_id=1, source_target_pairs={{0,32},{32,64},{64,96},{96,128},{128,160},{160,192},{192,224},{224... | collective-permute-start | bytes 1376264 | tf_op jit(solution)/shard_map/ppermute | solution.py:348
  76.4 11.3 %copy-start.4 = (bf16[256,896]{1,0:T(8,128)(2,1)}, bf16[256,896]{1,0:T(8,128)(2,1)S(1)}, u32[]{:S(2)}) copy-start(bf16[256,896]{1,0:T(8,128)(2,1)S(1)} %collective-permute-done.11.refs_1_) | copy-start | bytes 1376260
  76.4 11.3 %collective-permute-start.12 = (bf16[256,896]{1,0:T(8,128)(2,1)S(1)}, bf16[256,896]{1,0:T(8,128)(2,1)S(1)}, u32[]{:S(2)}, u32[]{:S(2)}) collective-permute-start(bf16[256,896]{1,0:T(8,128)(2,1)S(1)} %collective-permute-done.11.refs_1_), channel_id=1, source_target_pairs={{0,480},{32,0},{64,32},{96,64},{128,96},{160,128},{192,160},{224,1... | collective-permute-start | bytes 1376264 | tf_op jit(solution)/shard_map/ppermute | solution.py:349
  81.6 6.0 %copy-start.5 = (bf16[256,896]{1,0:T(8,128)(2,1)}, bf16[256,896]{1,0:T(8,128)(2,1)S(1)}, u32[]{:S(2)}) copy-start(bf16[256,896]{1,0:T(8,128)(2,1)S(1)} %collective-permute-done.3.refs_0_) | copy-start | bytes 1376260
  81.6 11.8 %collective-permute-start.7 = (bf16[256,896]{1,0:T(8,128)(2,1)S(1)}, bf16[256,896]{1,0:T(8,128)(2,1)S(1)}, u32[]{:S(2)}, u32[]{:S(2)}) collective-permute-start(bf16[256,896]{1,0:T(8,128)(2,1)S(1)} %collective-permute-done.3.refs_0_), channel_id=1, source_target_pairs={{0,32},{32,64},{64,96},{96,128},{128,160},{160,192},{192,224},{224... | collective-permute-start | bytes 1376264 | tf_op jit(solution)/shard_map/ppermute | solution.py:348
  87.7 24.9 %copy-start.6 = (bf16[256,896]{1,0:T(8,128)(2,1)}, bf16[256,896]{1,0:T(8,128)(2,1)S(1)}, u32[]{:S(2)}) copy-start(bf16[256,896]{1,0:T(8,128)(2,1)S(1)} %collective-permute-done.12.refs_3_) | copy-start | bytes 1376260
  87.7 12.2 %collective-permute-start.13 = (bf16[256,896]{1,0:T(8,128)(2,1)S(1)}, bf16[256,896]{1,0:T(8,128)(2,1)S(1)}, u32[]{:S(2)}, u32[]{:S(2)}) collective-permute-start(bf16[256,896]{1,0:T(8,128)(2,1)S(1)} %collective-permute-done.12.refs_3_), channel_id=1, source_target_pairs={{0,480},{32,0},{64,32},{96,64},{128,96},{160,128},{192,160},{224,1... | collective-permute-start | bytes 1376264 | tf_op jit(solution)/shard_map/ppermute | solution.py:349
  93.4 19.2 %copy-start.7 = (bf16[256,896]{1,0:T(8,128)(2,1)}, bf16[256,896]{1,0:T(8,128)(2,1)S(1)}, u32[]{:S(2)}) copy-start(bf16[256,896]{1,0:T(8,128)(2,1)S(1)} %collective-permute-done.7.refs_2_) | copy-start | bytes 1376260
  93.4 13.1 %collective-permute-start.8 = (bf16[256,896]{1,0:T(8,128)(2,1)S(1)}, bf16[256,896]{1,0:T(8,128)(2,1)S(1)}, u32[]{:S(2)}, u32[]{:S(2)}) collective-permute-start(bf16[256,896]{1,0:T(8,128)(2,1)S(1)} %collective-permute-done.7.refs_2_), channel_id=1, source_target_pairs={{0,32},{32,64},{64,96},{96,128},{128,160},{160,192},{192,224},{224... | collective-permute-start | bytes 1376264 | tf_op jit(solution)/shard_map/ppermute | solution.py:348
  99.9 12.8 %copy-start.10 = (bf16[256,896]{1,0:T(8,128)(2,1)}, bf16[256,896]{1,0:T(8,128)(2,1)S(1)}, u32[]{:S(2)}) copy-start(bf16[256,896]{1,0:T(8,128)(2,1)S(1)} %collective-permute-done.13.refs_5_) | copy-start | bytes 1376260
  99.9 13.9 %collective-permute-start.14 = (bf16[256,896]{1,0:T(8,128)(2,1)S(1)}, bf16[256,896]{1,0:T(8,128)(2,1)S(1)}, u32[]{:S(2)}, u32[]{:S(2)}) collective-permute-start(bf16[256,896]{1,0:T(8,128)(2,1)S(1)} %collective-permute-done.13.refs_5_), channel_id=1, source_target_pairs={{0,480},{32,0},{64,32},{96,64},{128,96},{160,128},{192,160},{224,1... | collective-permute-start | bytes 1376264 | tf_op jit(solution)/shard_map/ppermute | solution.py:349
  106.5 6.1 %copy-start.12 = (bf16[256,896]{1,0:T(8,128)(2,1)}, bf16[256,896]{1,0:T(8,128)(2,1)S(1)}, u32[]{:S(2)}) copy-start(bf16[256,896]{1,0:T(8,128)(2,1)S(1)} %collective-permute-done.8.refs_4_) | copy-start | bytes 1376260
  106.5 14.2 %collective-permute-start.9 = (bf16[256,896]{1,0:T(8,128)(2,1)S(1)}, bf16[256,896]{1,0:T(8,128)(2,1)S(1)}, u32[]{:S(2)}, u32[]{:S(2)}) collective-permute-start(bf16[256,896]{1,0:T(8,128)(2,1)S(1)} %collective-permute-done.8.refs_4_), channel_id=1, source_target_pairs={{0,32},{32,64},{64,96},{96,128},{128,160},{160,192},{192,224},{224... | collective-permute-start | bytes 1376264 | tf_op jit(solution)/shard_map/ppermute | solution.py:348
  113.8 8.9 %copy-start.1 = (bf16[256,896]{1,0:T(8,128)(2,1)}, bf16[256,896]{1,0:T(8,128)(2,1)S(1)}, u32[]{:S(2)}) copy-start(bf16[256,896]{1,0:T(8,128)(2,1)S(1)} %collective-permute-done.14.refs_7_) | copy-start | bytes 1376260
  113.8 14.8 %collective-permute-start.15 = (bf16[128,896]{1,0:T(8,128)(2,1)S(1)}, bf16[128,896]{1,0:T(8,128)(2,1)S(1)}, u32[]{:S(2)}, u32[]{:S(2)}) collective-permute-start(bf16[128,896]{1,0:T(8,128)(2,1)S(1)} %slice.16), channel_id=1, source_target_pairs={{0,480},{32,0},{64,32},{96,64},{128,96},{160,128},{192,160},{224,1... | collective-permute-start | bytes 688136 | tf_op jit(solution)/shard_map/ppermute | solution.py:349
  120.7 2.0 copy-start.2
  120.7 9.3 %collective-permute-start.10 = (bf16[128,896]{1,0:T(8,128)(2,1)S(1)}, bf16[128,896]{1,0:T(8,128)(2,1)S(1)}, u32[]{:S(2)}, u32[]{:S(2)}) collective-permute-start(bf16[128,896]{1,0:T(8,128)(2,1)S(1)} %slice.15), channel_id=1, source_target_pairs={{0,32},{32,64},{64,96},{96,128},{128,160},{160,192},{192,224},{224... | collective-permute-start | bytes 688136 | tf_op jit(solution)/shard_map/ppermute | solution.py:348
  128.6 1.4 copy-start.14
  130.0 0.7 copy-start.15
  137.9 87.2 %copy-start.17 = (f32[3,16,512]{2,1,0:T(8,128)S(1)}, f32[3,16,512]{2,1,0:T(8,128)}, u32[]{:S(2)}) copy-start(f32[3,16,512]{2,1,0:T(8,128)} %param.18) | copy-start | bytes 294916
  137.9 87.9 %copy-start.16 = (f32[3,16,896]{2,1,0:T(8,128)S(1)}, f32[3,16,896]{2,1,0:T(8,128)}, u32[]{:S(2)}) copy-start(f32[3,16,896]{2,1,0:T(8,128)} %param.19) | copy-start | bytes 516100
  149.6 9.4 %all-to-all-start.1 = ((f32[8,8,512]{2,1,0:T(8,128)}), f32[8,8,512]{2,1,0:T(8,128)S(1)}, u32[]{:S(2)}, u32[]{:S(2)}) async-start(f32[8,8,512]{2,1,0:T(8,128)} %broadcast_in_dim.9), calls=%async_computation.1 | async-start | bytes 262144 | tf_op jit(solution)/shard_map/all_to_all | solution.py:481
  159.0 0.7 copy-start.3
Sparse Core Ops, SparseCore 0:
  10.1 43.8 all-gather.2
  56.2 39.7 all-gather.4

commit v15 on v14

--- a/solution.py
+++ b/solution.py
@@ -500,7 +500,7 @@
             pltpu.VMEM((3 * RANK, local_width), F32),
             pltpu.SemaphoreType.DMA((6,)),
         ],
-        compiler_params=params,
+        compiler_params=pltpu.CompilerParams(vmem_limit_bytes=8 * 2**20),
         name="clip_side",
     )(
         clipping_limit,

time: 234 us -> 233 us (level)
  no operation moved by 1% of the time
where the time goes in v15:
time: 233 us; the launch traced here: 232 us
  blocking collectives  86.8 us (37%)
  starting transfers between devices  67.9 us (29%)
  waiting for transfers between devices  30.4 us (13%)
  Pallas kernels  28.1 us (12%)
  between operations  15.1 us (6%)
  local copies, waits for them, and re-layouts  2.64 us (1%)
    ppermute x8, starting transfers between devices, step(): high[k] = lax.ppermute(high_from, z_axes, ring(n_z, -1))  49.1 us
    all_to_all x1, blocking collectives, per_device(): lax.all_to_all(share.reshape(n_z, -1, 128), z_axes, 0, 0)  21.8 us
    ppermute x8, waiting for transfers between devices, step(): high[k] = lax.ppermute(high_from, z_axes, ring(n_z, -1))  18.3 us
    all_to_all x1, blocking collectives, per_device(): lax.all_to_all(jnp.broadcast_to(share, (n_z,) + share.shape), z_axes, 0, 0)  17 us
    ppermute x8, starting transfers between devices, step(): low[k] = lax.ppermute(low_from, z_axes, ring(n_z, 1))  15.3 us
    all_to_all x1, blocking collectives, per_device(): lax.all_to_all(out.reshape(n_y, -1, 128), 'y', 0, 0)  14.4 us
    all_gather x1, blocking collectives, per_device(): block = lax.all_gather(frozen_down_weight.T, 'y', axis=0, tiled=True)  13.4 us
    pallas_call x2, Pallas kernels, part(): pl.pallas_call(functools.partial(part_kernel, plan, before is None), out_...  11.2 us
  transfers between devices with their start and end apart: 19, of which 13 were waited for; matrix products, arithmetic and copies ran while one was open for 0% of the time, Pallas kernels for 8%

profile of v15, /device:TPU:32, one launch (start us, length us, event | category | flops | bytes accessed | tf_op | source)
XLA Modules:
  0.0 232.4 jit_solution(17498333597029470165)
XLA Ops:
  7.2 0.0 all-gather.3.cloned.1.call-start
  7.2 0.7 all-gather.3.cloned.1.call-update
  7.9 0.0 all-gather.5.cloned.1.call-start
  7.9 0.7 all-gather.5.cloned.1.call-update
  8.6 13.4 %all_gather.10.refs_0_ = bf16[256,896]{1,0:T(8,128)(2,1)S(1)} all-gather(bf16[64,896]{1,0:T(8,128)(2,1)} %bitcast.24), channel_id=1, replica_groups=mesh['z'=16,'y'=4,'x'=4,'c'=2] {'y'}, dimensions={0}, use_global_device_ids=true | all-gather | bytes 573440 | tf_op jit(solution)/shard_map/all_gather | solution.py:335
  22.0 6.9 %collective-permute-start.4 = (bf16[256,896]{1,0:T(8,128)(2,1)S(1)}, bf16[256,896]{1,0:T(8,128)(2,1)S(1)}, u32[]{:S(2)}, u32[]{:S(2)}) collective-permute-start(bf16[256,896]{1,0:T(8,128)(2,1)S(1)} %all_gather.10.refs_0_), channel_id=1, source_target_pairs={{0,480},{32,0},{64,32},{96,64},{128,96},{160,128},{192,160},{224,1... | collective-permute-start | bytes 1376264 | tf_op jit(solution)/shard_map/ppermute | solution.py:349
  28.9 1.9 collective-permute-start
  30.8 4.0 %collective-permute-done.4.refs_2_ = bf16[256,896]{1,0:T(8,128)(2,1)S(1)} collective-permute-done((bf16[256,896]{1,0:T(8,128)(2,1)S(1)}, bf16[256,896]{1,0:T(8,128)(2,1)S(1)}, u32[]{:S(2)}, u32[]{:S(2)}) %collective-permute-start.4) | collective-permute-done | bytes 458784 | tf_op jit(solution)/shard_map/ppermute | solution.py:349
  34.9 8.6 %collective-permute-start.5 = (bf16[256,896]{1,0:T(8,128)(2,1)S(1)}, bf16[256,896]{1,0:T(8,128)(2,1)S(1)}, u32[]{:S(2)}, u32[]{:S(2)}) collective-permute-start(bf16[256,896]{1,0:T(8,128)(2,1)S(1)} %collective-permute-done.4.refs_2_), channel_id=1, source_target_pairs={{0,480},{32,0},{64,32},{96,64},{128,96},{160,128},{192,160},{224,1... | collective-permute-start | bytes 1376264 | tf_op jit(solution)/shard_map/ppermute | solution.py:349
  43.5 0.5 collective-permute-done.refs_1_
  44.0 1.9 collective-permute-start.1
  45.9 4.7 %collective-permute-done.5.refs_4_ = bf16[256,896]{1,0:T(8,128)(2,1)S(1)} collective-permute-done((bf16[256,896]{1,0:T(8,128)(2,1)S(1)}, bf16[256,896]{1,0:T(8,128)(2,1)S(1)}, u32[]{:S(2)}, u32[]{:S(2)}) %collective-permute-start.5) | collective-permute-done | bytes 458784 | tf_op jit(solution)/shard_map/ppermute | solution.py:349
  50.7 5.7 %collective-permute-start.6 = (bf16[256,896]{1,0:T(8,128)(2,1)S(1)}, bf16[256,896]{1,0:T(8,128)(2,1)}, u32[]{:S(2)}, u32[]{:S(2)}) collective-permute-start(bf16[256,896]{1,0:T(8,128)(2,1)S(1)} %collective-permute-done.5.refs_4_), channel_id=1, source_target_pairs={{0,480},{32,0},{64,32},{96,64},{128,96},{160,128},{192,160},{224,1... | collective-permute-start | bytes 1376264 | tf_op jit(solution)/shard_map/ppermute | solution.py:349
  56.4 0.5 collective-permute-done.1.refs_3_
  56.9 1.9 collective-permute-start.2
  58.8 3.9 %collective-permute-done.6.refs_6_ = bf16[256,896]{1,0:T(8,128)(2,1)} collective-permute-done((bf16[256,896]{1,0:T(8,128)(2,1)S(1)}, bf16[256,896]{1,0:T(8,128)(2,1)}, u32[]{:S(2)}, u32[]{:S(2)}) %collective-permute-start.6) | collective-permute-done | bytes 458784 | tf_op jit(solution)/shard_map/ppermute | solution.py:349
  62.7 5.7 %collective-permute-start.11 = (bf16[256,896]{1,0:T(8,128)(2,1)}, bf16[256,896]{1,0:T(8,128)(2,1)S(1)}, u32[]{:S(2)}, u32[]{:S(2)}) collective-permute-start(bf16[256,896]{1,0:T(8,128)(2,1)} %collective-permute-done.6.refs_6_), channel_id=1, source_target_pairs={{0,480},{32,0},{64,32},{96,64},{128,96},{160,128},{192,160},{224,1... | collective-permute-start | bytes 1376264 | tf_op jit(solution)/shard_map/ppermute | solution.py:349
  68.4 0.6 collective-permute-done.2.refs_5_
  69.0 1.9 collective-permute-start.3
  70.9 0.0 all-gather.3.cloned.1.call-done.gradient_ref.refs_0_.refs_1_
  70.9 0.0 copy-done.5
  70.9 0.0 copy-done.12
  71.0 0.0 copy-done.13
  71.0 0.0 copy-done.15
  71.0 0.0 copy-done.17
  71.0 5.4 %part_product.2.refs_8_ = f32[512,896]{1,0:T(8,128)} custom-call(s32[1]{0:T(128)} %bitcast.z_ref, bf16[512,4096]{1,0:T(8,128)(2,1)} %all-gather.3.cloned.1.call-done.gradient_ref.refs_0_.refs_1_, bf16[256,896]{1,0:T(8,128)(2,1)} %copy-done.5, bf16[256,896]{1,0:T(8,128)(2,1)} %copy-done.13, bf16[256,896]{1,0:T(8,128)(2,1)} %copy-done.12, ...), custom_call_target="tpu_custom_call" | custom-call | flops 1644167168 | bytes 6291456 | tf_op jit(solution)/shard_map/part_product/pallas_call | solution.py:402
  76.3 0.0 collective-permute-done.11.refs_1_
  76.4 5.2 %collective-permute-start.12 = (bf16[256,896]{1,0:T(8,128)(2,1)S(1)}, bf16[256,896]{1,0:T(8,128)(2,1)S(1)}, u32[]{:S(2)}, u32[]{:S(2)}) collective-permute-start(bf16[256,896]{1,0:T(8,128)(2,1)S(1)} %collective-permute-done.11.refs_1_), channel_id=1, source_target_pairs={{0,480},{32,0},{64,32},{96,64},{128,96},{160,128},{192,160},{224,1... | collective-permute-start | bytes 1376264 | tf_op jit(solution)/shard_map/ppermute | solution.py:349
  81.6 0.0 collective-permute-done.3.refs_0_
  81.6 1.9 collective-permute-start.7
  83.6 4.1 %gradient_side.1 = (bf16[16,512]{1,0:T(8,128)(2,1)}, bf16[512,16]{1,0:T(8,128)(2,1)}, f32[4,128,128]{2,1,0:T(8,128)}) custom-call(bf16[512,4096]{1,0:T(8,128)(2,1)} %all-gather.3.cloned.1.call-done.gradient_ref.refs_0_.refs_1_, bf16[512,4096]{1,0:T(8,128)(2,1)} %all-gather.3.cloned.1.call-done.gradient_ref.refs_0_.refs_1_, bf16[48,4096]{1,0:T(8,128)(2,1)} %bitcast.18), custom_call_target="tpu_custom_call" | custom-call | flops 603979776 | bytes 5242880 | tf_op jit(solution)/shard_map/gradient_side/pallas_call | solution.py:354
  87.7 0.0 collective-permute-done.12.refs_3_
  87.7 5.2 %collective-permute-start.13 = (bf16[256,896]{1,0:T(8,128)(2,1)S(1)}, bf16[256,896]{1,0:T(8,128)(2,1)S(1)}, u32[]{:S(2)}, u32[]{:S(2)}) collective-permute-start(bf16[256,896]{1,0:T(8,128)(2,1)S(1)} %collective-permute-done.12.refs_3_), channel_id=1, source_target_pairs={{0,480},{32,0},{64,32},{96,64},{128,96},{160,128},{192,160},{224,1... | collective-permute-start | bytes 1376264 | tf_op jit(solution)/shard_map/ppermute | solution.py:349
  92.9 0.5 collective-permute-done.7.refs_2_
  93.4 1.9 collective-permute-start.8
  95.3 4.5 %collective-permute-done.13.refs_5_ = bf16[256,896]{1,0:T(8,128)(2,1)S(1)} collective-permute-done((bf16[256,896]{1,0:T(8,128)(2,1)S(1)}, bf16[256,896]{1,0:T(8,128)(2,1)S(1)}, u32[]{:S(2)}, u32[]{:S(2)}) %collective-permute-start.13) | collective-permute-done | bytes 458784 | tf_op jit(solution)/shard_map/ppermute | solution.py:349
  99.9 5.9 %collective-permute-start.14 = (bf16[256,896]{1,0:T(8,128)(2,1)S(1)}, bf16[256,896]{1,0:T(8,128)(2,1)S(1)}, u32[]{:S(2)}, u32[]{:S(2)}) collective-permute-start(bf16[256,896]{1,0:T(8,128)(2,1)S(1)} %collective-permute-done.13.refs_5_), channel_id=1, source_target_pairs={{0,480},{32,0},{64,32},{96,64},{128,96},{160,128},{192,160},{224,1... | collective-permute-start | bytes 1376264 | tf_op jit(solution)/shard_map/ppermute | solution.py:349
  105.8 0.8 collective-permute-done.8.refs_4_
  106.5 1.9 collective-permute-start.9
  108.5 0.0 all-gather.5.cloned.1.call-done.refs_0_.refs_1_
  108.5 4.2 %normed_side.1 = (bf16[32,512]{1,0:T(8,128)(2,1)}, bf16[512,32]{1,0:T(8,128)(2,1)}, f32[4,128,128]{2,1,0:T(8,128)}) custom-call(bf16[512,4096]{1,0:T(8,128)(2,1)} %all-gather.5.cloned.1.call-done.refs_0_.refs_1_, bf16[512,4096]{1,0:T(8,128)(2,1)} %all-gather.5.cloned.1.call-done.refs_0_.refs_1_, bf16[48,4096]{1,0:T(8,128)(2,1)} %bitcast.19), custom_call_target="tpu_custom_call" | custom-call | flops 671088640 | bytes 5242880 | tf_op jit(solution)/shard_map/normed_side/pallas_call | solution.py:354
  112.7 1.1 collective-permute-done.14.refs_7_
  113.8 5.9 %collective-permute-start.15 = (bf16[128,896]{1,0:T(8,128)(2,1)S(1)}, bf16[128,896]{1,0:T(8,128)(2,1)S(1)}, u32[]{:S(2)}, u32[]{:S(2)}) collective-permute-start(bf16[128,896]{1,0:T(8,128)(2,1)S(1)} %slice.16), channel_id=1, source_target_pairs={{0,480},{32,0},{64,32},{96,64},{128,96},{160,128},{192,160},{224,1... | collective-permute-start | bytes 688136 | tf_op jit(solution)/shard_map/ppermute | solution.py:349
  119.7 1.0 collective-permute-done.9.refs_6_
  120.7 1.9 collective-permute-start.10
  122.7 5.9 %part_product.3.refs_2_ = f32[512,896]{1,0:T(8,128)} custom-call(s32[1]{0:T(128)} %bitcast.z_ref, bf16[512,4096]{1,0:T(8,128)(2,1)} %all-gather.3.cloned.1.call-done.gradient_ref.refs_0_.refs_1_, bf16[256,896]{1,0:T(8,128)(2,1)} %copy-done.9, bf16[256,896]{1,0:T(8,128)(2,1)} %copy-done.8, bf16[256,896]{1,0:T(8,128)(2,1)} %copy-done.11, ...), custom_call_target="tpu_custom_call" | custom-call | flops 1879048192 | bytes 6291456 | tf_op jit(solution)/shard_map/part_product/pallas_call | solution.py:402
  128.6 0.0 collective-permute-done.15.refs_1_
  128.6 1.4 collective-permute-done.10.refs_0_
  130.0 0.7 copy-done.19
  130.7 7.3 %hidden_side.1 = (f32[4,48,896]{2,1,0:T(8,128)}, f32[64,512]{1,0:T(8,128)}) custom-call(s32[1]{0:T(128)} %bitcast.z_ref, bf16[512,4096]{1,0:T(8,128)(2,1)} %all-gather.3.cloned.1.call-done.gradient_ref.refs_0_.refs_1_, bf16[128,896]{1,0:T(8,128)(2,1)} %copy-done.19, bf16[128,896]{1,0:T(8,128)(2,1)} %copy-done.18, f32[512,896]{1,0:T(8,128)} %part_product.3.refs_2_, ...), custom_call_target="tpu_custom_call" | custom-call | tf_op jit(solution)/shard_map/hidden_side/pallas_call | solution.py:446
  138.0 0.0 copy-start.21
  138.0 0.0 copy-start.20
  138.0 11.0 %all_to_all.30 = f32[8,8,512]{2,1,0:T(8,128)S(1)} all-to-all(f32[8,8,512]{2,1,0:T(8,128)} %bitcast.23), channel_id=1, replica_groups=mesh['z'=16,'y'=4,'x'=4,'c'=2] {'x','c'}, dimensions={0} | all-to-all | bytes 262144 | tf_op jit(solution)/shard_map/all_to_all | solution.py:479
  149.0 0.7 broadcast_in_dim.9
  149.7 3.4 %all-to-all-start.1 = ((f32[8,8,512]{2,1,0:T(8,128)}), f32[8,8,512]{2,1,0:T(8,128)S(1)}, u32[]{:S(2)}, u32[]{:S(2)}) async-start(f32[8,8,512]{2,1,0:T(8,128)} %broadcast_in_dim.9), calls=%async_computation.1 | async-start | bytes 262144 | tf_op jit(solution)/shard_map/all_to_all | solution.py:481
  153.7 5.4 %all-to-all-done.1 = f32[8,8,512]{2,1,0:T(8,128)S(1)} async-done(((f32[8,8,512]{2,1,0:T(8,128)}), f32[8,8,512]{2,1,0:T(8,128)S(1)}, u32[]{:S(2)}, u32[]{:S(2)}) %all-to-all-start.1) | async-done | bytes 131104 | tf_op jit(solution)/shard_map/all_to_all | solution.py:481
  159.1 1.1 copy-done.2
  160.2 1.3 clip_side.1
  161.5 14.4 %all_to_all.31 = f32[4,144,128]{2,1,0:T(8,128)S(1)} all-to-all(f32[4,144,128]{2,1,0:T(8,128)S(1)} %bitcast.16), channel_id=1, replica_groups=mesh['z'=16,'y'=4,'x'=4,'c'=2] {'y'}, dimensions={0} | all-to-all | bytes 589824 | tf_op jit(solution)/shard_map/all_to_all | solution.py:516
  176.0 21.8 %all_to_all.32 = f32[16,9,128]{2,1,0:T(8,128)S(1)} all-to-all(f32[16,9,128]{2,1,0:T(8,128)S(1)} %reshape.44), channel_id=1, replica_groups=mesh['z'=16,'y'=4,'x'=4,'c'=2] {'z'}, dimensions={0} | all-to-all | bytes 147456 | tf_op jit(solution)/shard_map/all_to_all | solution.py:517
  197.8 17.0 %all_to_all.33 = f32[16,9,128]{2,1,0:T(8,128)S(1)} all-to-all(f32[16,9,128]{2,1,0:T(8,128)S(1)} %broadcast_in_dim.10), channel_id=1, replica_groups=mesh['z'=16,'y'=4,'x'=4,'c'=2] {'z'}, dimensions={0} | all-to-all | bytes 147456 | tf_op jit(solution)/shard_map/all_to_all | solution.py:518
  214.9 9.2 %all_to_all.34 = f32[4,144,128]{2,1,0:T(8,128)S(1)} all-to-all(f32[4,144,128]{2,1,0:T(8,128)S(1)} %broadcast_in_dim.11), channel_id=1, replica_groups=mesh['z'=16,'y'=4,'x'=4,'c'=2] {'y'}, dimensions={0} | all-to-all | bytes 589824 | tf_op jit(solution)/shard_map/all_to_all | solution.py:521
  224.2 0.7 fusion.1
  224.8 0.7 fusion
  (45 shorter events, 0.2 us)
Async XLA Ops:
  7.2 63.8 %all-gather.3.cloned.1.call-start = ((), (), s32[]{:S(2)}) async-start(), calls=%async_computation.6 | async-start | bytes 4718592 | tf_op jit(solution)/shard_map/all_gather | solution.py:334
  7.9 100.6 %all-gather.5.cloned.1.call-start = ((), (), s32[]{:S(2)}) async-start(), calls=%async_computation.7 | async-start | bytes 4718592 | tf_op jit(solution)/shard_map/all_gather | solution.py:336
  22.0 48.9 %copy-start.5 = (bf16[256,896]{1,0:T(8,128)(2,1)}, bf16[256,896]{1,0:T(8,128)(2,1)S(1)}, u32[]{:S(2)}) copy-start(bf16[256,896]{1,0:T(8,128)(2,1)S(1)} %all_gather.10.refs_0_) | copy-start | bytes 1376260
  22.0 12.8 %collective-permute-start.4 = (bf16[256,896]{1,0:T(8,128)(2,1)S(1)}, bf16[256,896]{1,0:T(8,128)(2,1)S(1)}, u32[]{:S(2)}, u32[]{:S(2)}) collective-permute-start(bf16[256,896]{1,0:T(8,128)(2,1)S(1)} %all_gather.10.refs_0_), channel_id=1, source_target_pairs={{0,480},{32,0},{64,32},{96,64},{128,96},{160,128},{192,160},{224,1... | collective-permute-start | bytes 1376264 | tf_op jit(solution)/shard_map/ppermute | solution.py:349
  28.9 15.1 %collective-permute-start = (bf16[256,896]{1,0:T(8,128)(2,1)S(1)}, bf16[256,896]{1,0:T(8,128)(2,1)S(1)}, u32[]{:S(2)}, u32[]{:S(2)}) collective-permute-start(bf16[256,896]{1,0:T(8,128)(2,1)S(1)} %all_gather.10.refs_0_), channel_id=1, source_target_pairs={{0,32},{32,64},{64,96},{96,128},{128,160},{160,192},{192,224},{224... | collective-permute-start | bytes 1376264 | tf_op jit(solution)/shard_map/ppermute | solution.py:348
  34.9 36.1 %copy-start.12 = (bf16[256,896]{1,0:T(8,128)(2,1)}, bf16[256,896]{1,0:T(8,128)(2,1)S(1)}, u32[]{:S(2)}) copy-start(bf16[256,896]{1,0:T(8,128)(2,1)S(1)} %collective-permute-done.4.refs_2_) | copy-start | bytes 1376260
  34.9 15.8 %collective-permute-start.5 = (bf16[256,896]{1,0:T(8,128)(2,1)S(1)}, bf16[256,896]{1,0:T(8,128)(2,1)S(1)}, u32[]{:S(2)}, u32[]{:S(2)}) collective-permute-start(bf16[256,896]{1,0:T(8,128)(2,1)S(1)} %collective-permute-done.4.refs_2_), channel_id=1, source_target_pairs={{0,480},{32,0},{64,32},{96,64},{128,96},{160,128},{192,160},{224,1... | collective-permute-start | bytes 1376264 | tf_op jit(solution)/shard_map/ppermute | solution.py:349
  44.0 27.0 %copy-start.13 = (bf16[256,896]{1,0:T(8,128)(2,1)}, bf16[256,896]{1,0:T(8,128)(2,1)S(1)}, u32[]{:S(2)}) copy-start(bf16[256,896]{1,0:T(8,128)(2,1)S(1)} %collective-permute-done.refs_1_) | copy-start | bytes 1376260
  44.0 12.9 %collective-permute-start.1 = (bf16[256,896]{1,0:T(8,128)(2,1)S(1)}, bf16[256,896]{1,0:T(8,128)(2,1)S(1)}, u32[]{:S(2)}, u32[]{:S(2)}) collective-permute-start(bf16[256,896]{1,0:T(8,128)(2,1)S(1)} %collective-permute-done.refs_1_), channel_id=1, source_target_pairs={{0,32},{32,64},{64,96},{96,128},{128,160},{160,192},{192,224},{224... | collective-permute-start | bytes 1376264 | tf_op jit(solution)/shard_map/ppermute | solution.py:348
  50.7 20.3 %copy-start.15 = (bf16[256,896]{1,0:T(8,128)(2,1)}, bf16[256,896]{1,0:T(8,128)(2,1)S(1)}, u32[]{:S(2)}) copy-start(bf16[256,896]{1,0:T(8,128)(2,1)S(1)} %collective-permute-done.5.refs_4_) | copy-start | bytes 1376260
  50.7 12.0 %collective-permute-start.6 = (bf16[256,896]{1,0:T(8,128)(2,1)S(1)}, bf16[256,896]{1,0:T(8,128)(2,1)}, u32[]{:S(2)}, u32[]{:S(2)}) collective-permute-start(bf16[256,896]{1,0:T(8,128)(2,1)S(1)} %collective-permute-done.5.refs_4_), channel_id=1, source_target_pairs={{0,480},{32,0},{64,32},{96,64},{128,96},{160,128},{192,160},{224,1... | collective-permute-start | bytes 1376264 | tf_op jit(solution)/shard_map/ppermute | solution.py:349
  56.9 14.1 %copy-start.17 = (bf16[256,896]{1,0:T(8,128)(2,1)}, bf16[256,896]{1,0:T(8,128)(2,1)S(1)}, u32[]{:S(2)}) copy-start(bf16[256,896]{1,0:T(8,128)(2,1)S(1)} %collective-permute-done.1.refs_3_) | copy-start | bytes 1376260
  56.9 12.1 %collective-permute-start.2 = (bf16[256,896]{1,0:T(8,128)(2,1)S(1)}, bf16[256,896]{1,0:T(8,128)(2,1)}, u32[]{:S(2)}, u32[]{:S(2)}) collective-permute-start(bf16[256,896]{1,0:T(8,128)(2,1)S(1)} %collective-permute-done.1.refs_3_), channel_id=1, source_target_pairs={{0,32},{32,64},{64,96},{96,128},{128,160},{160,192},{192,224},{224... | collective-permute-start | bytes 1376264 | tf_op jit(solution)/shard_map/ppermute | solution.py:348
  62.7 13.7 %collective-permute-start.11 = (bf16[256,896]{1,0:T(8,128)(2,1)}, bf16[256,896]{1,0:T(8,128)(2,1)S(1)}, u32[]{:S(2)}, u32[]{:S(2)}) collective-permute-start(bf16[256,896]{1,0:T(8,128)(2,1)} %collective-permute-done.6.refs_6_), channel_id=1, source_target_pairs={{0,480},{32,0},{64,32},{96,64},{128,96},{160,128},{192,160},{224,1... | collective-permute-start | bytes 1376264 | tf_op jit(solution)/shard_map/ppermute | solution.py:349
  69.0 12.6 %collective-permute-start.3 = (bf16[256,896]{1,0:T(8,128)(2,1)}, bf16[256,896]{1,0:T(8,128)(2,1)S(1)}, u32[]{:S(2)}, u32[]{:S(2)}) collective-permute-start(bf16[256,896]{1,0:T(8,128)(2,1)} %collective-permute-done.2.refs_5_), channel_id=1, source_target_pairs={{0,32},{32,64},{64,96},{96,128},{128,160},{160,192},{192,224},{224... | collective-permute-start | bytes 1376264 | tf_op jit(solution)/shard_map/ppermute | solution.py:348
  76.4 11.3 %copy-start.8 = (bf16[256,896]{1,0:T(8,128)(2,1)}, bf16[256,896]{1,0:T(8,128)(2,1)S(1)}, u32[]{:S(2)}) copy-start(bf16[256,896]{1,0:T(8,128)(2,1)S(1)} %collective-permute-done.11.refs_1_) | copy-start | bytes 1376260
  76.4 11.3 %collective-permute-start.12 = (bf16[256,896]{1,0:T(8,128)(2,1)S(1)}, bf16[256,896]{1,0:T(8,128)(2,1)S(1)}, u32[]{:S(2)}, u32[]{:S(2)}) collective-permute-start(bf16[256,896]{1,0:T(8,128)(2,1)S(1)} %collective-permute-done.11.refs_1_), channel_id=1, source_target_pairs={{0,480},{32,0},{64,32},{96,64},{128,96},{160,128},{192,160},{224,1... | collective-permute-start | bytes 1376264 | tf_op jit(solution)/shard_map/ppermute | solution.py:349
  81.6 6.1 %copy-start.9 = (bf16[256,896]{1,0:T(8,128)(2,1)}, bf16[256,896]{1,0:T(8,128)(2,1)S(1)}, u32[]{:S(2)}) copy-start(bf16[256,896]{1,0:T(8,128)(2,1)S(1)} %collective-permute-done.3.refs_0_) | copy-start | bytes 1376260
  81.6 11.8 %collective-permute-start.7 = (bf16[256,896]{1,0:T(8,128)(2,1)S(1)}, bf16[256,896]{1,0:T(8,128)(2,1)S(1)}, u32[]{:S(2)}, u32[]{:S(2)}) collective-permute-start(bf16[256,896]{1,0:T(8,128)(2,1)S(1)} %collective-permute-done.3.refs_0_), channel_id=1, source_target_pairs={{0,32},{32,64},{64,96},{96,128},{128,160},{160,192},{192,224},{224... | collective-permute-start | bytes 1376264 | tf_op jit(solution)/shard_map/ppermute | solution.py:348
  87.7 25.0 %copy-start.10 = (bf16[256,896]{1,0:T(8,128)(2,1)}, bf16[256,896]{1,0:T(8,128)(2,1)S(1)}, u32[]{:S(2)}) copy-start(bf16[256,896]{1,0:T(8,128)(2,1)S(1)} %collective-permute-done.12.refs_3_) | copy-start | bytes 1376260
  87.7 12.2 %collective-permute-start.13 = (bf16[256,896]{1,0:T(8,128)(2,1)S(1)}, bf16[256,896]{1,0:T(8,128)(2,1)S(1)}, u32[]{:S(2)}, u32[]{:S(2)}) collective-permute-start(bf16[256,896]{1,0:T(8,128)(2,1)S(1)} %collective-permute-done.12.refs_3_), channel_id=1, source_target_pairs={{0,480},{32,0},{64,32},{96,64},{128,96},{160,128},{192,160},{224,1... | collective-permute-start | bytes 1376264 | tf_op jit(solution)/shard_map/ppermute | solution.py:349
  93.4 19.2 %copy-start.11 = (bf16[256,896]{1,0:T(8,128)(2,1)}, bf16[256,896]{1,0:T(8,128)(2,1)S(1)}, u32[]{:S(2)}) copy-start(bf16[256,896]{1,0:T(8,128)(2,1)S(1)} %collective-permute-done.7.refs_2_) | copy-start | bytes 1376260
  93.4 13.1 %collective-permute-start.8 = (bf16[256,896]{1,0:T(8,128)(2,1)S(1)}, bf16[256,896]{1,0:T(8,128)(2,1)S(1)}, u32[]{:S(2)}, u32[]{:S(2)}) collective-permute-start(bf16[256,896]{1,0:T(8,128)(2,1)S(1)} %collective-permute-done.7.refs_2_), channel_id=1, source_target_pairs={{0,32},{32,64},{64,96},{96,128},{128,160},{160,192},{192,224},{224... | collective-permute-start | bytes 1376264 | tf_op jit(solution)/shard_map/ppermute | solution.py:348
  99.9 12.8 %copy-start.14 = (bf16[256,896]{1,0:T(8,128)(2,1)}, bf16[256,896]{1,0:T(8,128)(2,1)S(1)}, u32[]{:S(2)}) copy-start(bf16[256,896]{1,0:T(8,128)(2,1)S(1)} %collective-permute-done.13.refs_5_) | copy-start | bytes 1376260
  99.9 13.9 %collective-permute-start.14 = (bf16[256,896]{1,0:T(8,128)(2,1)S(1)}, bf16[256,896]{1,0:T(8,128)(2,1)S(1)}, u32[]{:S(2)}, u32[]{:S(2)}) collective-permute-start(bf16[256,896]{1,0:T(8,128)(2,1)S(1)} %collective-permute-done.13.refs_5_), channel_id=1, source_target_pairs={{0,480},{32,0},{64,32},{96,64},{128,96},{160,128},{192,160},{224,1... | collective-permute-start | bytes 1376264 | tf_op jit(solution)/shard_map/ppermute | solution.py:349
  106.5 6.1 %copy-start.16 = (bf16[256,896]{1,0:T(8,128)(2,1)}, bf16[256,896]{1,0:T(8,128)(2,1)S(1)}, u32[]{:S(2)}) copy-start(bf16[256,896]{1,0:T(8,128)(2,1)S(1)} %collective-permute-done.8.refs_4_) | copy-start | bytes 1376260
  106.5 14.2 %collective-permute-start.9 = (bf16[256,896]{1,0:T(8,128)(2,1)S(1)}, bf16[256,896]{1,0:T(8,128)(2,1)S(1)}, u32[]{:S(2)}, u32[]{:S(2)}) collective-permute-start(bf16[256,896]{1,0:T(8,128)(2,1)S(1)} %collective-permute-done.8.refs_4_), channel_id=1, source_target_pairs={{0,32},{32,64},{64,96},{96,128},{128,160},{160,192},{192,224},{224... | collective-permute-start | bytes 1376264 | tf_op jit(solution)/shard_map/ppermute | solution.py:348
  113.8 8.9 %copy-start.6 = (bf16[256,896]{1,0:T(8,128)(2,1)}, bf16[256,896]{1,0:T(8,128)(2,1)S(1)}, u32[]{:S(2)}) copy-start(bf16[256,896]{1,0:T(8,128)(2,1)S(1)} %collective-permute-done.14.refs_7_) | copy-start | bytes 1376260
  113.8 14.8 %collective-permute-start.15 = (bf16[128,896]{1,0:T(8,128)(2,1)S(1)}, bf16[128,896]{1,0:T(8,128)(2,1)S(1)}, u32[]{:S(2)}, u32[]{:S(2)}) collective-permute-start(bf16[128,896]{1,0:T(8,128)(2,1)S(1)} %slice.16), channel_id=1, source_target_pairs={{0,480},{32,0},{64,32},{96,64},{128,96},{160,128},{192,160},{224,1... | collective-permute-start | bytes 688136 | tf_op jit(solution)/shard_map/ppermute | solution.py:349
  120.7 2.0 copy-start.7
  120.7 9.3 %collective-permute-start.10 = (bf16[128,896]{1,0:T(8,128)(2,1)S(1)}, bf16[128,896]{1,0:T(8,128)(2,1)S(1)}, u32[]{:S(2)}, u32[]{:S(2)}) collective-permute-start(bf16[128,896]{1,0:T(8,128)(2,1)S(1)} %slice.15), channel_id=1, source_target_pairs={{0,32},{32,64},{64,96},{96,128},{128,160},{160,192},{192,224},{224... | collective-permute-start | bytes 688136 | tf_op jit(solution)/shard_map/ppermute | solution.py:348
  128.6 1.4 copy-start.18
  130.0 0.7 copy-start.19
  130.7 28.4 %copy-start = (bf16[512,512]{1,0:T(8,128)(2,1)S(1)}, bf16[512,512]{1,0:T(8,128)(2,1)}, u32[]{:S(2)}) copy-start(bf16[512,512]{1,0:T(8,128)(2,1)} %gradient_hbm.1) | copy-start | bytes 1572868
  130.7 28.4 %copy-start.1 = (bf16[512,512]{1,0:T(8,128)(2,1)S(1)}, bf16[512,512]{1,0:T(8,128)(2,1)}, u32[]{:S(2)}) copy-start(bf16[512,512]{1,0:T(8,128)(2,1)} %normed_hbm.1) | copy-start | bytes 1572868
  130.7 28.4 %copy-start.3 = (f32[4,128,128]{2,1,0:T(8,128)S(1)}, f32[4,128,128]{2,1,0:T(8,128)}, u32[]{:S(2)}) copy-start(f32[4,128,128]{2,1,0:T(8,128)} %get-tuple-element.28.gradient_gram_hbm) | copy-start | bytes 786436
  130.7 28.4 %copy-start.4 = (f32[4,128,128]{2,1,0:T(8,128)S(1)}, f32[4,128,128]{2,1,0:T(8,128)}, u32[]{:S(2)}) copy-start(f32[4,128,128]{2,1,0:T(8,128)} %get-tuple-element.27.normed_gram_hbm) | copy-start | bytes 786436
  138.0 86.2 %copy-start.21 = (f32[3,16,512]{2,1,0:T(8,128)S(1)}, f32[3,16,512]{2,1,0:T(8,128)}, u32[]{:S(2)}) copy-start(f32[3,16,512]{2,1,0:T(8,128)} %param.18) | copy-start | bytes 294916
  138.0 86.8 %copy-start.20 = (f32[3,16,896]{2,1,0:T(8,128)S(1)}, f32[3,16,896]{2,1,0:T(8,128)}, u32[]{:S(2)}) copy-start(f32[3,16,896]{2,1,0:T(8,128)} %param.19) | copy-start | bytes 516100
  149.7 9.4 %all-to-all-start.1 = ((f32[8,8,512]{2,1,0:T(8,128)}), f32[8,8,512]{2,1,0:T(8,128)S(1)}, u32[]{:S(2)}, u32[]{:S(2)}) async-start(f32[8,8,512]{2,1,0:T(8,128)} %broadcast_in_dim.9), calls=%async_computation.1 | async-start | bytes 262144 | tf_op jit(solution)/shard_map/all_to_all | solution.py:481
  159.1 1.1 copy-start.2
Sparse Core Ops, SparseCore 0:
  10.1 43.8 all-gather.2
  56.2 39.7 all-gather.4
